TPU v7x, 32 devices: a whole 2x2x4 slice. The times are simulated.
32 devices in a mesh: groups: 2 (over x), dp: 16 (over z, y, core).
Axes of the slice: x: 2, y: 2, z: 4, core: 2. Of those that a mesh axis runs over, the one named last changes fastest.
Arguments:
- queries: bfloat16 [32, 256, 1536], P(('groups', 'dp')), parts along dimension 0, may hold values from -8 to 8
- key_rows: bfloat16 [32, 256, 1536], P(('groups', 'dp')), parts along dimension 0, may hold values from -8 to 8
- value_rows: bfloat16 [32, 256, 1536], P(('groups', 'dp')), parts along dimension 0, may hold values from -24 to 24
- stream: bfloat16 [32, 256, 1536], P(('groups', 'dp')), parts along dimension 0, may hold values from -3 to 3
- earlier: bfloat16 [32, 256, 1536], P(('groups', 'dp')), parts along dimension 0, may hold values from -6 to 6
- out_weight: bfloat16 [1536, 1536], P('dp'), may hold values from -0.15625 to 0.15625
- pred_weight: bfloat16 [768, 1536], P('dp'), may hold values from -0.21875 to 0.21875
- decoder_hidden: bfloat16 [32, 8, 256, 768], P(('groups', 'dp')), parts along dimension 0, may hold values from -6 to 6
- kept_index: int32 [32, 8, 64], P(('groups', 'dp')), parts along dimension 0, may hold values from 0 to 255, as said below
Outputs:
- targets: float32 [32, 256, 1536], P(('groups', 'dp')), parts along dimension 0
- pred_grad: float32 [1536, 1536], P(('groups', 'dp')), parts along dimension 0
There are 2 independent parts, one for each index of `groups`. A program takes and returns all parts, laid end to end along the dimension named above; an argument that names none is the same for every part. Nothing has to cross between parts.
Inputs may be any that keep to these rules, and one draw needn't show every extreme that they name: `kept_index`: within one clone of one image the 64 entries are distinct patch numbers.
All inputs are finite; a program needn't handle non-finite values.
Results may differ from a plain program's by a relative error of at most 0.002.
Values may be sent and summed in bfloat16 or wider, within the bound.
No kernel may reach another device: no remote copies, remote signals or barrier semaphores. Data moves between devices by JAX's collectives and lax.ppermute only.
A program may use at most 128 MiB of HBM per device.

v0:
```python
import math

import jax
import jax.numpy as jnp
from jax import lax
from jax.sharding import PartitionSpec as P

HEADS = 24
TOP_K = 10


def on_device(
    queries,
    key_rows,
    value_rows,
    stream,
    earlier,
    out_weight,
    pred_weight,
    decoder_hidden,
    kept_index,
):
    images, patches, model_width = queries.shape
    head_size = model_width // HEADS
    clones = decoder_hidden.shape[1]
    dec_width = decoder_hidden.shape[3]
    dec_rows = decoder_hidden.reshape(images * clones * patches, dec_width)
    full_out, full_pred = (
        lax.all_gather(out_weight, "dp", axis=0, tiled=True),
        lax.all_gather(pred_weight, "dp", axis=0, tiled=True),
    )
    query_split = queries.reshape(images, patches, HEADS, head_size)
    key_split = key_rows.reshape(images, patches, HEADS, head_size)
    value_split = value_rows.reshape(images, patches, HEADS, head_size)
    scores = jnp.einsum(
        "iphd,ikhd->ihpk", query_split, key_split, preferred_element_type=jnp.float32
    ) / math.sqrt(head_size)
    attn_probs = jax.nn.softmax(scores, axis=-1).astype(jnp.bfloat16)
    mixed = jnp.einsum(
        "ihpk,ikhd->iphd", attn_probs, value_split, preferred_element_type=jnp.float32
    )
    mixed = mixed.reshape(images * patches, model_width).astype(jnp.bfloat16)
    branch = jnp.dot(mixed, full_out, preferred_element_type=jnp.float32)
    predicted = jnp.dot(dec_rows, full_pred, preferred_element_type=jnp.float32)
    layer_out = stream.astype(jnp.float32) + branch.reshape(images, patches, model_width)
    center = jnp.mean(layer_out, axis=1, keepdims=True)
    spread = jnp.mean((layer_out - center) ** 2, axis=1, keepdims=True)
    normed = (layer_out - center) / jnp.sqrt(spread + 1e-05)
    blend = ((TOP_K - 1) * earlier.astype(jnp.float32) + normed) / TOP_K
    middle = jnp.mean(blend, axis=2, keepdims=True)
    breadth = jnp.mean((blend - middle) ** 2, axis=2, keepdims=True)
    targets = (blend - middle) / jnp.sqrt(breadth + 1e-06)
    positions = jnp.arange(patches, dtype=jnp.int32)
    covered = jnp.any(kept_index[:, :, :, None] == positions[None, None, None, :], axis=2)
    masked = jnp.where(covered, 0.0, 1.0).astype(jnp.float32)
    errors = predicted.reshape(images, clones, patches, model_width) - targets[:, None]
    scaled = 2.0 / (math.sqrt(model_width) * clones) * masked[:, :, :, None] * errors
    scaled = scaled.reshape(images * clones * patches, model_width).astype(jnp.bfloat16)
    rows_here = pred_weight.shape[0]
    complete = lax.dot_general(
        dec_rows, scaled, (((0,), (0,)), ((), ())), preferred_element_type=jnp.float32
    )
    summed = lax.psum(complete, "dp")
    pred_grad = lax.dynamic_slice_in_dim(summed, lax.axis_index("dp") * rows_here, rows_here, 0)
    return (targets, pred_grad)


def solution(mesh):
    return jax.shard_map(
        on_device,
        mesh=mesh,
        in_specs=(
            P(("groups", "dp"), None, None),
            P(("groups", "dp"), None, None),
            P(("groups", "dp"), None, None),
            P(("groups", "dp"), None, None),
            P(("groups", "dp"), None, None),
            P("dp", None),
            P("dp", None),
            P(("groups", "dp"), None, None, None),
            P(("groups", "dp"), None, None),
        ),
        out_specs=(P(("groups", "dp"), None, None), P(("groups", "dp"), None)),
        check_vma=False,
    )
```

profile of v0, /device:TPU:0, one launch (start us, length us, event | category | flops | bytes accessed | tf_op | source)
XLA Modules:
  0.0 255.0 jit_solution(14090135868582322472)
XLA Ops:
  7.2 0.0 copy-start
  7.2 0.0 all-gather.3.cloned.1.call-start
  7.2 0.7 all-gather.3.cloned.1.call-update
  7.9 0.0 all-gather.5.cloned.1.call-start
  8.0 0.7 all-gather.5.cloned.1.call-update
  8.7 0.0 copy-start.3
  8.7 0.0 all-reduce.2.cloned.1.call-start
  8.7 2.3 copy.25
  11.0 2.3 copy.23
  13.3 2.3 copy.24
  15.6 0.0 copy-done.3
  15.6 0.2 fusion.26
  15.7 6.2 %fusion.29 = (f32[24,256]{1,0:T(8,128)S(1)}, f32[24,256,256]{1,2,0:T(8,128)}) fusion(bf16[256,24,64]{0,2,1:T(8,128)(2,1)} %bitcast.46, bf16[256,24,64]{0,2,1:T(8,128)(2,1)} %bitcast.47), kind=kOutput, calls=%fused_computation.34 | convolution fusion | flops 206045440 | bytes 7888896 | tf_op jit(solution)/shard_map/sub | solution.py:38
  22.0 4.6 %fusion.15 = bf16[24,256,64]{1,2,0:T(8,128)(2,1)} fusion(bf16[256,24,64]{0,2,1:T(8,128)(2,1)} %bitcast.45, f32[24,256,256]{1,2,0:T(8,128)} %get-tuple-element.11, f32[24,256]{1,0:T(8,128)S(1)} %get-tuple-element.10), kind=kOutput, calls=%fused_computation.22 | convolution fusion | flops 204865536 | bytes 7888896 | tf_op jit(solution)/shard_map/ihpk,ikhd->iphd/dot_general | solution.py:39
  26.6 39.9 %all-gather.3.cloned.1.call-done = bf16[1536,1536]{1,0:T(8,128)(2,1)} async-done(((bf16[96,1536]{1,0:T(8,128)(2,1)}), bf16[1536,1536]{1,0:T(8,128)(2,1)}) %all-gather.3.cloned.1.call-update) | async-done | bytes 4718608 | tf_op jit(solution)/shard_map/all_gather | solution.py:29
  66.4 0.0 copy-start.2
  66.4 4.3 %fusion.30 = (f32[1536]{0:T(1024)S(1)}, f32[1,256,1536]{2,1,0:T(8,128)S(1)}) fusion(bf16[256,1536]{0,1:T(8,128)(2,1)} %bitcast.44, bf16[1536,1536]{1,0:T(8,128)(2,1)} %all-gather.3.cloned.1.call-done, bf16[1,256,1536]{2,1,0:T(8,128)(2,1)} %param.12), kind=kOutput, calls=%fused_computation.35 | convolution fusion | flops 1209137664 | bytes 7870464 | tf_op jit(solution)/shard_map/dot_general | solution.py:43
  70.7 0.2 multiply_reduce_fusion.2
  70.9 0.0 copy-done.2
  70.9 0.4 fusion.28
  71.4 0.0 copy-start.1
  71.4 0.3 multiply_reduce_fusion.1
  71.7 0.8 copy-done.1
  72.5 1.4 fusion.38
  73.9 35.6 %all-gather.5.cloned.1.call-done = bf16[768,1536]{1,0:T(8,128)(2,1)} async-done(((bf16[48,1536]{1,0:T(8,128)(2,1)}), bf16[768,1536]{1,0:T(8,128)(2,1)}) %all-gather.5.cloned.1.call-update) | async-done | bytes 2359312 | tf_op jit(solution)/shard_map/all_gather | solution.py:30
  109.5 0.0 copy-done
  109.5 18.3 %fusion.7 = f32[768,1536]{0,1:T(8,128)} fusion(f32[256,1536]{1,0:T(8,128)} %fusion.38, f32[8,256]{1,0:T(8,128)S(1)} %select_multiply_fusion, bf16[1,8,256,768]{3,2,1,0:T(8,128)(2,1)S(1)} %copy-done, bf16[768,1536]{1,0:T(8,128)(2,1)} %all-gather.5.cloned.1.call-done), kind=kOutput, calls=%fused_computation.9 | convolution fusion | flops 9673113600 | bytes 11804672 | tf_op jit(solution)/shard_map/dot_general | solution.py:60
  127.8 0.0 all-reduce.2.cloned.1.call-update
  127.8 2.7 %subtract_divide_fusion = f32[1,256,1536]{2,1,0:T(8,128)} fusion(f32[1,256,1536]{2,1,0:T(8,128)} %copy-done.1, f32[256]{0:T(256)S(1)} %add_sqrt_fusion.1, f32[256]{0:T(256)S(1)} %broadcast_multiply_fusion.1), kind=kLoop, calls=%fused_computation.21 | loop fusion | flops 786432 | bytes 3147776 | tf_op jit(solution)/shard_map/div | solution.py:52
  130.6 113.2 %all-reduce.2.cloned.1.call-done = f32[768,1536]{0,1:T(8,128)} async-done(((f32[768,1536]{0,1:T(8,128)}), f32[768,1536]{0,1:T(8,128)}) %all-reduce.2.cloned.1.call-update) | async-done | bytes 4718608 | tf_op jit(solution)/shard_map/psum | solution.py:63
  243.8 2.6 %constant_dynamic-slice_fusion = f32[48,1536]{0,1:T(8,128)} fusion(f32[768,1536]{0,1:T(8,128)} %all-reduce.2.cloned.1.call-done, s32[]{:T(128)S(6)} %select_n.15), kind=kLoop, calls=%fused_computation.31 | loop fusion | bytes 589828 | tf_op jit(solution)/shard_map/dynamic_slice | solution.py:64
  246.3 2.1 copy.28
  (5 shorter events, 0.0 us)
Async XLA Ops:
  7.2 102.3 %copy-start = (bf16[1,8,256,768]{3,2,1,0:T(8,128)(2,1)S(1)}, bf16[1,8,256,768]{3,2,1,0:T(8,128)(2,1)}, u32[]{:S(2)}) copy-start(bf16[1,8,256,768]{3,2,1,0:T(8,128)(2,1)} %param.16) | copy-start | bytes 9437188
  7.2 59.2 %all-gather.3.cloned.1.call-start = ((), (), s32[]{:S(2)}) async-start(), calls=%async_computation | async-start | bytes 5013504 | tf_op jit(solution)/shard_map/all_gather | solution.py:29
  7.9 101.6 %all-gather.5.cloned.1.call-start = ((), (), s32[]{:S(2)}) async-start(), calls=%async_computation.1 | async-start | bytes 2506752 | tf_op jit(solution)/shard_map/all_gather | solution.py:30
  8.7 6.9 %copy-start.3 = (s32[1,8,64]{2,1,0:T(8,128)S(1)}, s32[1,8,64]{2,1,0:T(8,128)}, u32[]{:S(2)}) copy-start(s32[1,8,64]{2,1,0:T(8,128)} %param.17) | copy-start | bytes 6148
  8.7 235.1 %all-reduce.2.cloned.1.call-start = ((), (), s32[]{:S(2)}) async-start(), calls=%async_computation.2 | async-start | bytes 9437184 | tf_op jit(solution)/shard_map/psum | solution.py:63
  66.4 4.5 %copy-start.2 = (bf16[1,256,1536]{2,1,0:T(8,128)(2,1)S(1)}, bf16[1,256,1536]{2,1,0:T(8,128)(2,1)}, u32[]{:S(2)}) copy-start(bf16[1,256,1536]{2,1,0:T(8,128)(2,1)} %param.13) | copy-start | bytes 2359300
  71.4 1.1 copy-start.1
Sparse Core Ops, SparseCore 0:
  10.3 56.0 all-gather.2
  68.7 40.7 all-gather.4
  128.0 115.7 all-reduce.1
where the time goes:
time: 255 us
  waiting for transfers between devices  190 us (75%)
  matrix products  33.4 us (13%)
  between operations  13.8 us (5%)
  local copies, waits for them, and re-layouts  12.3 us (5%)
  other arithmetic  5.24 us (2%)
    psum x1, waiting for transfers between devices, on_device(): summed = lax.psum(complete, 'dp')  113 us
    all_gather x1, waiting for transfers between devices, on_device(): lax.all_gather(out_weight, 'dp', axis=0, tiled=True)  39.9 us
    all_gather x1, waiting for transfers between devices, on_device(): lax.all_gather(pred_weight, 'dp', axis=0, tiled=True)  35.6 us
    dot_general x1, matrix products, on_device(): lax.dot_general(dec_rows, scaled, (((0,), (0,)), ((), ())), preferred_ele...  18.3 us
    unnamed x12, local copies, waits for them, and re-layouts  9.76 us
    sub x1, matrix products, on_device(): attn_probs = jax.nn.softmax(scores, axis=-1).astype(jnp.bfloat16)  6.23 us
  transfers between devices with their start and end apart: 3, of which 3 were waited for; matrix products, arithmetic and copies ran while one was open for 11% of the time, Pallas kernels for 0%

commit v1 on v0

v1 whole, which is shorter than its diff:
```python
import functools
import math

import jax
import jax.numpy as jnp
from jax import lax
from jax.experimental import pallas as pl
from jax.experimental.pallas import tpu as pltpu
from jax.sharding import PartitionSpec as P

HEADS = 24
TOP_K = 10
AXES = ("groups", "dp")
VMEM = 48 * 1024 * 1024
CORE, NEXT_Y, NEXT_Z, FAR_Z = 1, 2, 4, 8
TAIL = 16


def call(kernel, out_shape, *, name, grid=(1,), in_specs, out_specs, scratch=(), flops=0, nbytes=0):
    return pl.pallas_call(
        kernel,
        out_shape=out_shape,
        grid_spec=pltpu.PrefetchScalarGridSpec(
            num_scalar_prefetch=1,
            grid=grid,
            in_specs=in_specs,
            out_specs=out_specs,
            scratch_shapes=scratch,
        ),
        compiler_params=pltpu.CompilerParams(vmem_limit_bytes=VMEM),
        cost_estimate=pl.CostEstimate(flops=flops, bytes_accessed=nbytes, transcendentals=0),
        name=name,
    )


def whole(shape):
    return pl.BlockSpec(shape, lambda i, s: (0,) * len(shape))


def contract_rows(a, b):
    return lax.dot_general(a, b, (((0,), (0,)), ((), ())), preferred_element_type=jnp.float32)


def attention_kernel(where_ref, q_ref, k_ref, v_ref, out_ref, *, size):
    mixed = []
    for j in range(q_ref.shape[1] // size):
        cols = slice(j * size, (j + 1) * size)
        q = q_ref[:, cols] * jnp.asarray(1.0 / math.sqrt(size), q_ref.dtype)
        scores = lax.dot_general(
            q, k_ref[:, cols], (((1,), (1,)), ((), ())), preferred_element_type=jnp.float32
        )
        top = jnp.max(scores, axis=1, keepdims=True)
        weights = jnp.exp(scores - top)
        weights = weights / jnp.sum(weights, axis=1, keepdims=True)
        mixed.append(
            jnp.dot(weights.astype(jnp.bfloat16), v_ref[:, cols], preferred_element_type=jnp.float32)
        )
    out_ref[...] = jnp.concatenate(mixed, axis=1).astype(out_ref.dtype)


def attention(where, q, k, v):
    patches, width = q.shape
    size = width // HEADS
    lanes = 2 * size
    spec = pl.BlockSpec((patches, lanes), lambda i, s: (0, i))
    return call(
        functools.partial(attention_kernel, size=size),
        jax.ShapeDtypeStruct((patches, width), jnp.bfloat16),
        name="attention",
        grid=(width // lanes,),
        in_specs=[spec] * 3,
        out_specs=spec,
        flops=4 * patches * patches * width * 4,
        nbytes=8 * patches * width,
    )(where, q, k, v)


def gram_kernel(where_ref, hidden_ref, kept_ref, gram_ref, sum_ref, total):
    step = pl.program_id(0)
    patches = hidden_ref.shape[2]
    kept = kept_ref[pl.ds(step, 1), :]
    positions = lax.broadcasted_iota(jnp.int32, (patches, kept.shape[1]), 0)
    covered = jnp.max(jnp.where(positions == kept, 1.0, 0.0), axis=1, keepdims=True)
    rows = hidden_ref[0, 0]
    rows = jnp.where(covered > 0.5, jnp.zeros_like(rows), rows)

    @pl.when(step == 0)
    def _():
        gram_ref[...] = jnp.zeros_like(gram_ref)
        total[...] = jnp.zeros_like(total)

    gram_ref[...] += contract_rows(rows, rows)
    total[...] += rows.astype(jnp.float32)

    @pl.when(step == pl.num_programs(0) - 1)
    def _():
        sum_ref[...] = total[...].astype(sum_ref.dtype)


def gram(where, hidden, kept):
    _, clones, patches, width = hidden.shape
    return call(
        gram_kernel,
        (
            jax.ShapeDtypeStruct((width, width), jnp.float32),
            jax.ShapeDtypeStruct((patches, width), jnp.bfloat16),
        ),
        name="gram",
        grid=(clones,),
        in_specs=[
            pl.BlockSpec((1, 1, patches, width), lambda i, s: (0, i, 0, 0)),
            whole(kept.shape),
        ],
        out_specs=(whole((width, width)), whole((patches, width))),
        scratch=[pltpu.VMEM((patches, width), jnp.float32)],
        flops=2 * clones * patches * width * width,
        nbytes=2 * clones * patches * width + 4 * width * width,
    )(where, hidden, kept)


def put_in_order(where_ref, pieces, full):
    core, chip = where_ref[0], where_ref[1]
    if len(pieces) == 1:
        full[...] = pieces[0][...]
        return
    for k, piece in enumerate(pieces):
        rows = piece.shape[0] // 2
        base = (chip ^ k) * 2
        for j in range(2):
            at = pl.multiple_of((base + (core ^ j)) * rows, rows)
            full[pl.ds(at, rows), :] = piece[j * rows : (j + 1) * rows, :]


def branch_kernel(
    where_ref, mixed_own, mixed_other, stream_own, earlier_own, others, *rest
):
    *pieces, blend_ref, stats_ref, full = rest
    put_in_order(where_ref, pieces, full)
    patches, half = stream_own.shape
    streams = (stream_own[...], others[0])
    earliers = (earlier_own[...], others[1])
    for i, mixed in enumerate((mixed_own, mixed_other)):
        layer_out = streams[i].astype(jnp.float32) + jnp.dot(
            mixed[...], full[...], preferred_element_type=jnp.float32
        )
        center = jnp.mean(layer_out, axis=0, keepdims=True)
        away = layer_out - center
        spread = jnp.mean(away * away, axis=0, keepdims=True)
        normed = away / jnp.sqrt(spread + 1e-05)
        blend = ((TOP_K - 1) * earliers[i].astype(jnp.float32) + normed) / TOP_K
        rows = slice(i * patches, (i + 1) * patches)
        blend_ref[rows, :] = blend
        middle = jnp.mean(blend, axis=1, keepdims=True)
        off = blend - middle
        squares = jnp.sum(off * off, axis=1, keepdims=True)
        lane = lax.broadcasted_iota(jnp.int32, (patches, 128), 1)
        stats_ref[rows, :] = jnp.where(lane < 64, middle, squares)


def branch(where, mixed_own, mixed_other, stream, earlier, others, pieces):
    patches, width = mixed_own.shape
    half = width // 2
    own_half = pl.BlockSpec((patches, half), lambda i, s: (0, s[0]))
    return call(
        branch_kernel,
        (
            jax.ShapeDtypeStruct((2 * patches, half), jnp.float32),
            jax.ShapeDtypeStruct((2 * patches, 128), jnp.float32),
        ),
        name="branch",
        in_specs=[whole((patches, width))] * 2
        + [own_half] * 2
        + [whole((2, patches, half))]
        + [whole(p.shape) for p in pieces],
        out_specs=(whole((2 * patches, half)), whole((2 * patches, 128))),
        scratch=[pltpu.VMEM((width, half), jnp.bfloat16)],
        flops=4 * patches * width * half,
        nbytes=12 * patches * width + 2 * width * half,
    )(where, mixed_own, mixed_other, stream, earlier, others, *pieces)


def predict_kernel(where_ref, gram_own, gram_other, *rest):
    *pieces, out_ref, full = rest
    put_in_order(where_ref, pieces, full)
    both = gram_own[...] + gram_other[...]
    high = both.astype(jnp.bfloat16)
    low = (both - high.astype(jnp.float32)).astype(jnp.bfloat16)
    out_ref[...] = jnp.dot(high, full[...], preferred_element_type=jnp.float32) + jnp.dot(
        low, full[...], preferred_element_type=jnp.float32
    )


def predict(where, gram_own, gram_other, pieces):
    width, half = gram_own.shape[0], pieces[0].shape[1]
    return call(
        predict_kernel,
        jax.ShapeDtypeStruct((width, half), jnp.float32),
        name="predict",
        in_specs=[whole((width, width))] * 2 + [whole(p.shape) for p in pieces],
        out_specs=whole((width, half)),
        scratch=[pltpu.VMEM((width, half), jnp.bfloat16)],
        flops=4 * width * width * half,
        nbytes=8 * width * width + 6 * width * half,
    )(where, gram_own, gram_other, *pieces)


def encode(values, out_ref):
    rows = values.shape[0]
    top = jnp.max(jnp.abs(values), axis=0, keepdims=True)
    power = jnp.ceil(jnp.log2(jnp.maximum(top, 1e-30))) - 15.0
    codes = jnp.clip(jnp.round(values * jnp.exp2(-power)), -32767.0, 32767.0)
    out_ref[:rows, :] = codes.astype(jnp.int32).astype(jnp.int16)
    out_ref[rows:, :] = jnp.broadcast_to(power, (TAIL, values.shape[1])).astype(jnp.int32).astype(jnp.int16)


def decode(codes):
    rows = codes.shape[0] - TAIL
    power = codes[rows:, :].astype(jnp.int32).astype(jnp.float32)[:1]
    return codes[:rows, :].astype(jnp.int32).astype(jnp.float32) * jnp.exp2(power)


def targets_kernel(where_ref, blend, stats, stats_other, sum_own, sum_other, product, own_ref, other_ref, grad_ref):
    patches, width = blend.shape[0] // 2, 2 * blend.shape[1]
    results = []
    for i, (out, features) in enumerate(((own_ref, sum_own), (other_ref, sum_other))):
        mine = stats[i * patches : (i + 1) * patches, :]
        theirs = stats_other[(1 - i) * patches : (2 - i) * patches, :]
        gap = mine[:, :1] - theirs[:, :1]
        middle = 0.5 * (mine[:, :1] + theirs[:, :1])
        squares = mine[:, 64:65] + theirs[:, 64:65] + (width / 4) * gap * gap
        root = 1.0 / jnp.sqrt(squares / width + 1e-06)
        target = (blend[i * patches : (i + 1) * patches, :] - middle) * root
        out[...] = target
        results.append(contract_rows(features[...], target.astype(jnp.bfloat16)))
    grad = product[...] - (results[0] + results[1])
    if len(grad_ref.shape) == 3:
        chips, rows = grad_ref.shape[0], grad_ref.shape[1] - TAIL
        for k in range(chips):
            encode(grad[k * rows : (k + 1) * rows, :], grad_ref.at[k])
    else:
        grad_ref[...] = grad


def targets_and_term(where, blend, stats, stats_other, sum_own, sum_other, product, grad_shape):
    patches, half = blend.shape[0] // 2, blend.shape[1]
    width = product.shape[0]
    inputs = (blend, stats, stats_other, sum_own, sum_other, product)
    return call(
        targets_kernel,
        (
            jax.ShapeDtypeStruct((patches, half), jnp.float32),
            jax.ShapeDtypeStruct((patches, half), jnp.float32),
            grad_shape,
        ),
        name="targets",
        in_specs=[whole(x.shape) for x in inputs],
        out_specs=(whole((patches, half)), whole((patches, half)), whole(grad_shape.shape)),
        flops=4 * patches * width * half,
        nbytes=16 * patches * half + 6 * width * half,
    )(where, *inputs)


def sum_kernel(where_ref, codes, out_ref, *, scale):
    total = decode(codes[0])
    for k in range(1, codes.shape[0]):
        total = total + decode(codes[k])
    out_ref[...] = (total * scale).reshape(out_ref.shape)


def sum_terms(where, codes, scale):
    chips, rows, half = codes.shape
    shape = (2, (rows - TAIL) // 2, half)
    return call(
        functools.partial(sum_kernel, scale=scale),
        jax.ShapeDtypeStruct(shape, jnp.float32),
        name="sum_terms",
        in_specs=[whole(codes.shape)],
        out_specs=whole(shape),
        flops=chips * rows * half,
        nbytes=2 * chips * rows * half,
    )(where, codes)


def on_device(
    mesh_shape,
    queries,
    key_rows,
    value_rows,
    stream,
    earlier,
    out_weight,
    pred_weight,
    decoder_hidden,
    kept_index,
):
    groups, parts = mesh_shape["groups"], mesh_shape["dp"]
    chips = parts // 2
    _, patches, width = queries.shape
    clones = decoder_hidden.shape[1]
    half = width // 2
    me = lax.axis_index("dp")
    core, chip = me % 2, me // 2
    where = jnp.stack([core, chip]).astype(jnp.int32)
    same_core = [[2 * k + j for k in range(chips)] for j in range(2)]

    def swap(x, bits):
        pairs = [(g * parts + i, g * parts + (i ^ bits)) for g in range(groups) for i in range(parts)]
        return lax.ppermute(x, AXES, pairs)

    def my_half(x):
        return lax.dynamic_slice_in_dim(x, core * half, half, axis=-1)

    def other_half(x):
        return lax.dynamic_slice_in_dim(x, (1 - core) * half, half, axis=-1)

    out_piece = jnp.concatenate([my_half(out_weight), swap(other_half(out_weight), CORE)], axis=0)
    pred_piece = jnp.concatenate([my_half(pred_weight), swap(other_half(pred_weight), CORE)], axis=0)

    def gathered(piece):
        rows = piece.shape[0] // 2
        got = lax.all_gather(piece, "dp", axis_index_groups=same_core).reshape(chips, 2, rows, half)
        got = jnp.where(core == 0, got, got[:, ::-1])
        return [got.reshape(chips * 2 * rows, half)]

    by_pairs = chips == 8
    if by_pairs:
        z1, z2, y0 = swap(out_piece, NEXT_Z), swap(out_piece, FAR_Z), swap(out_piece, NEXT_Y)
        z3 = swap(z2, NEXT_Z)
        y1, y2, y3 = swap(z1, NEXT_Y), swap(z2, NEXT_Y), swap(z3, NEXT_Y)
        out_pieces = [out_piece, y0, z1, y1, z2, y2, z3, y3]
    else:
        out_pieces = gathered(out_piece)
    pred_pieces = gathered(pred_piece)

    mixed_own = attention(where, queries[0], key_rows[0], value_rows[0])
    gram_own, sum_own = gram(where, decoder_hidden, kept_index[0])
    mixed_other = swap(mixed_own, CORE)
    others = swap(jnp.concatenate([other_half(stream), other_half(earlier)], axis=0), CORE)
    sum_other = swap(sum_own, CORE)
    gram_other = swap(gram_own, CORE)

    blend, stats = branch(where, mixed_own, mixed_other, stream[0], earlier[0], others, out_pieces)
    stats_other = swap(stats, CORE)
    product = predict(where, gram_own, gram_other, pred_pieces)

    dec = product.shape[0]
    rows = dec // chips
    if by_pairs:
        grad_shape = jax.ShapeDtypeStruct((chips, rows + TAIL, half), jnp.int16)
    else:
        grad_shape = jax.ShapeDtypeStruct((dec, half), jnp.float32)
    target_own, target_other, term = targets_and_term(
        where, blend, stats, stats_other, sum_own, sum_other, product, grad_shape
    )
    target_rest = swap(target_other, CORE)
    scale = 2.0 / (math.sqrt(width) * clones)
    if by_pairs:
        codes = lax.all_to_all(term, "dp", 0, 0, axis_index_groups=same_core)
        summed = sum_terms(where, codes, scale)
    else:
        summed = lax.psum_scatter(
            term, "dp", scatter_dimension=0, tiled=True, axis_index_groups=same_core
        )
        summed = (summed * scale).reshape(2, rows // 2, half)

    def side_by_side(mine, theirs):
        return jnp.where(
            core == 0,
            jnp.concatenate([mine, theirs], axis=1),
            jnp.concatenate([theirs, mine], axis=1),
        )

    targets = side_by_side(target_own, target_rest)[None]
    keep = lax.dynamic_index_in_dim(summed, core, 0, keepdims=False)
    send = lax.dynamic_index_in_dim(summed, 1 - core, 0, keepdims=False)
    return targets, side_by_side(keep, swap(send, CORE))


def solution(mesh):
    by_image = P(AXES, None, None)
    return jax.shard_map(
        functools.partial(on_device, dict(mesh.shape)),
        mesh=mesh,
        in_specs=(
            by_image,
            by_image,
            by_image,
            by_image,
            by_image,
            P("dp", None),
            P("dp", None),
            P(AXES, None, None, None),
            by_image,
        ),
        out_specs=(by_image, P(AXES, None)),
        check_vma=False,
    )
```

time: 255 us -> 150 us (0.59)
  waiting for transfers between devices: 190 us -> 59.1 us
  Pallas kernels: 0 us -> 35.7 us
  matrix products: 33.4 us -> 0 us
  starting transfers between devices: 0.11 us -> 19 us
  other arithmetic: 5.24 us -> 8.1 us
    psum x1 -> x0, waiting for transfers between devices: 113 us -> none  [on_device(): summed = lax.psum(complete, 'dp')]
    all_gather x2 -> x1, waiting for transfers between devices: 75.5 us -> 0.01 us  [gathered(): lax.all_gather(piece, 'dp', axis_index_groups=same_core)]
    pallas_call x0 -> x6, Pallas kernels: none -> 35.7 us  [the longest x1 13.5 us: attention(): call(functools.partial(attention_kernel, size=size), jax.ShapeDtypeStruct...]
    all_to_all x0 -> x1, waiting for transfers between devices: none -> 33.2 us  [on_device(): codes = lax.all_to_all(term, 'dp', 0, 0, axis_index_groups=same_core)]
    dot_general x3 -> x0, matrix products: 27.2 us -> none  [the longest x1 18.3 us: on_device(): lax.dot_general(dec_rows, scaled, (((0,), (0,)), ((), ())), preferred_ele...]
    ppermute x0 -> x16, waiting for transfers between devices: none -> 25.8 us  [swap(): return lax.ppermute(x, AXES, pairs)]
    ppermute x0 -> x16, starting transfers between devices: none -> 13.8 us  [swap(): return lax.ppermute(x, AXES, pairs)]
    sub x1 -> x0, matrix products: 6.23 us -> none  [on_device(): attn_probs = jax.nn.softmax(scores, axis=-1).astype(jnp.bfloat16)]
  transfers between devices with their start and end apart: 3 -> 18, of which waited for: 3 -> 6; matrix products, arithmetic and copies ran while one was open for 11% -> 6% of each run, Pallas kernels for 0% -> 21%
where the time goes in v1:
time: 150 us
  waiting for transfers between devices  59.1 us (39%)
  Pallas kernels  35.7 us (24%)
  starting transfers between devices  19 us (13%)
  between operations  14.2 us (9%)
  local copies, waits for them, and re-layouts  13.7 us (9%)
  other arithmetic  8.1 us (5%)
    all_to_all x1, waiting for transfers between devices, on_device(): codes = lax.all_to_all(term, 'dp', 0, 0, axis_index_groups=same_core)  33.2 us
    ppermute x16, waiting for transfers between devices, swap(): return lax.ppermute(x, AXES, pairs)  25.8 us
    ppermute x16, starting transfers between devices, swap(): return lax.ppermute(x, AXES, pairs)  13.8 us
    pallas_call x1, Pallas kernels, attention(): call(functools.partial(attention_kernel, size=size), jax.ShapeDtypeStruct...  13.5 us
    unnamed x36, local copies, waits for them, and re-layouts  11 us
    pallas_call x1, Pallas kernels, gram(): call(gram_kernel, (jax.ShapeDtypeStruct((width, width), jnp.float32), jax...  6.42 us
    pallas_call x1, Pallas kernels, branch(): call(branch_kernel, (jax.ShapeDtypeStruct((2 * patches, half), jnp.float3...  5.64 us
    all_to_all x1, starting transfers between devices, on_device(): codes = lax.all_to_all(term, 'dp', 0, 0, axis_index_groups=same_core)  5.19 us
  transfers between devices with their start and end apart: 18, of which 6 were waited for; matrix products, arithmetic and copies ran while one was open for 6% of the time, Pallas kernels for 21%

profile of v1, /device:TPU:0, one launch (start us, length us, event | category | flops | bytes accessed | tf_op | source)
XLA Modules:
  0.0 149.8 jit_solution(18046054606205373560)
XLA Ops:
  7.2 0.0 all-gather.3.cloned.1.call-start
  7.2 1.6 %constant_dynamic-slice_fusion.1 = (bf16[48,768]{1,0:T(8,128)(2,1)S(1)}, bf16[48,768]{1,0:T(8,128)(2,1)}) fusion(bf16[48,1536]{1,0:T(8,128)(2,1)} %param.15, s32[]{:T(128)S(6)} %select_n.63, s32[]{:T(128)S(6)} %select_n.62), kind=kLoop, calls=%fused_computation.9 | loop fusion | bytes 294920 | tf_op jit(solution)/shard_map/dynamic_slice | solution.py:311
  8.8 0.5 collective-permute-start.13
  9.3 0.1 pad_add_fusion.where_ref
  9.3 1.9 %copy-done.12 = bf16[1,8,256,768]{3,2,1,0:T(8,128)(2,1)S(1)} copy-done((bf16[1,8,256,768]{3,2,1,0:T(8,128)(2,1)S(1)}, bf16[1,8,256,768]{3,2,1,0:T(8,128)(2,1)}, u32[]{:S(2)}) %copy-start.12) | copy-done | bytes 3145752
  11.2 0.7 copy-done.16
  11.9 6.4 %gram.1 = (f32[768,768]{1,0:T(8,128)S(1)}, bf16[256,768]{1,0:T(8,128)(2,1)S(1)}) custom-call(s32[2]{0:T(128)S(1)} %pad_add_fusion.where_ref, bf16[1,8,256,768]{3,2,1,0:T(8,128)(2,1)S(1)} %copy-done.12, s32[8,64]{1,0:T(8,128)S(1)} %bitcast.23), custom_call_target="tpu_custom_call" | custom-call | flops 2415919104 | bytes 5505024 | tf_op jit(solution)/shard_map/gram/pallas_call | solution.py:102
  18.4 0.7 copy-done.4
  19.1 0.1 collective-permute-start.12
  19.1 0.0 collective-permute-done.13
  19.2 1.6 %pad_maximum_fusion.2 = bf16[96,768]{1,0:T(8,128)(2,1)} fusion(bf16[48,768]{1,0:T(8,128)(2,1)} %collective-permute-done.13, bf16[48,768]{1,0:T(8,128)(2,1)S(1)} %get-tuple-element.20), kind=kLoop, calls=%fused_computation.5 | loop fusion | flops 294912 | bytes 294912 | tf_op jit(solution)/shard_map/concatenate | solution.py:317
  20.8 0.0 all-gather.3.cloned.1.call-update
  20.8 0.5 collective-permute-start.2
  21.3 2.5 %collective-permute-done.2 = bf16[96,768]{1,0:T(8,128)(2,1)S(1)} collective-permute-done((bf16[96,768]{1,0:T(8,128)(2,1)S(1)}, bf16[96,768]{1,0:T(8,128)(2,1)S(1)}, u32[]{:S(2)}, u32[]{:S(2)}) %collective-permute-start.2) | collective-permute-done | bytes 147488 | tf_op jit(solution)/shard_map/ppermute | solution.py:308
  23.9 0.0 copy-start.13
  23.9 0.0 copy-start.14
  23.9 0.0 copy-start.15
  23.9 3.8 %collective-permute-start.6 = (bf16[192,768]{1,0:T(8,128)(2,1)S(1)}, bf16[192,768]{1,0:T(8,128)(2,1)}, u32[]{:S(2)}, u32[]{:S(2)}) collective-permute-start(bf16[192,768]{1,0:T(8,128)(2,1)S(1)} %pad_maximum_fusion.1.rest_0_), channel_id=1, source_target_pairs={{0,8},{1,9},{2,10},{3,11},{4,12},{5,13},{6,14},{7,15},{8,0},{9,1},... | collective-permute-start | bytes 884744 | tf_op jit(solution)/shard_map/ppermute | solution.py:308
  27.7 1.0 constant_dynamic-slice_fusion.4
  28.8 0.9 pad_maximum_fusion
  29.7 0.1 collective-permute-start.1
  29.8 1.6 %collective-permute-start.4 = (bf16[192,768]{1,0:T(8,128)(2,1)S(1)}, bf16[192,768]{1,0:T(8,128)(2,1)S(1)}, u32[]{:S(2)}, u32[]{:S(2)}) collective-permute-start(bf16[192,768]{1,0:T(8,128)(2,1)S(1)} %pad_maximum_fusion.1.rest_0_), channel_id=1, source_target_pairs={{0,4},{1,5},{2,6},{3,7},{4,0},{5,1},{6,2},{7,3},{8,12},{9,13},{10,... | collective-permute-start | bytes 884744 | tf_op jit(solution)/shard_map/ppermute | solution.py:308
  31.4 1.5 %collective-permute-start.3 = (bf16[192,768]{1,0:T(8,128)(2,1)S(1)}, bf16[192,768]{1,0:T(8,128)(2,1)S(1)}, u32[]{:S(2)}, u32[]{:S(2)}) collective-permute-start(bf16[192,768]{1,0:T(8,128)(2,1)S(1)} %pad_maximum_fusion.1.rest_0_), channel_id=1, source_target_pairs={{0,2},{1,3},{2,0},{3,1},{4,6},{5,7},{6,4},{7,5},{8,10},{9,11},{10,... | collective-permute-start | bytes 884744 | tf_op jit(solution)/shard_map/ppermute | solution.py:308
  32.9 13.5 %attention.1.mixed_own = bf16[256,1536]{1,0:T(8,128)(2,1)} custom-call(s32[2]{0:T(128)S(1)} %pad_add_fusion.where_ref, bf16[256,1536]{1,0:T(8,128)(2,1)S(1)} %bitcast.20, bf16[256,1536]{1,0:T(8,128)(2,1)S(1)} %bitcast.21, bf16[256,1536]{1,0:T(8,128)(2,1)S(1)} %bitcast.22), custom_call_target="tpu_custom_call" | custom-call | flops 1610612736 | bytes 3145728 | tf_op jit(solution)/shard_map/attention/pallas_call | solution.py:66
  46.4 0.0 collective-permute-done.6.rest_4_
  46.4 0.0 collective-permute-start
  46.4 2.6 %collective-permute-done.4.rest_2_ = bf16[192,768]{1,0:T(8,128)(2,1)S(1)} collective-permute-done((bf16[192,768]{1,0:T(8,128)(2,1)S(1)}, bf16[192,768]{1,0:T(8,128)(2,1)S(1)}, u32[]{:S(2)}, u32[]{:S(2)}) %collective-permute-start.4) | collective-permute-done | bytes 294944 | tf_op jit(solution)/shard_map/ppermute | solution.py:308
  49.0 0.0 collective-permute-start.8
  49.0 0.0 collective-permute-done.3.rest_1_
  49.0 0.7 copy-done.8
  49.8 1.6 %collective-permute-start.5 = (bf16[192,768]{1,0:T(8,128)(2,1)S(1)}, bf16[192,768]{1,0:T(8,128)(2,1)S(1)}, u32[]{:S(2)}, u32[]{:S(2)}) collective-permute-start(bf16[192,768]{1,0:T(8,128)(2,1)S(1)} %collective-permute-done.4.rest_2_), channel_id=1, source_target_pairs={{0,2},{1,3},{2,0},{3,1},{4,6},{5,7},{6,4},{7,5},{8,10},{9,11},{10,... | collective-permute-start | bytes 884744 | tf_op jit(solution)/shard_map/ppermute | solution.py:308
  51.3 0.7 copy-done.6
  52.1 9.0 %collective-permute-done.8.rest_6_ = bf16[192,768]{1,0:T(8,128)(2,1)} collective-permute-done((bf16[192,768]{1,0:T(8,128)(2,1)}, bf16[192,768]{1,0:T(8,128)(2,1)}, u32[]{:S(2)}, u32[]{:S(2)}) %collective-permute-start.8) | collective-permute-done | bytes 294944 | tf_op jit(solution)/shard_map/ppermute | solution.py:308
  61.1 1.6 %collective-permute-start.7 = (bf16[192,768]{1,0:T(8,128)(2,1)}, bf16[192,768]{1,0:T(8,128)(2,1)}, u32[]{:S(2)}, u32[]{:S(2)}) collective-permute-start(bf16[192,768]{1,0:T(8,128)(2,1)} %collective-permute-done.6.rest_4_), channel_id=1, source_target_pairs={{0,2},{1,3},{2,0},{3,1},{4,6},{5,7},{6,4},{7,5},{8,10},{9,11},{10,... | collective-permute-start | bytes 884744 | tf_op jit(solution)/shard_map/ppermute | solution.py:308
  62.7 0.0 collective-permute-done.5.rest_3_
  62.7 0.7 copy-done.10
  63.4 2.4 %collective-permute-start.9 = (bf16[192,768]{1,0:T(8,128)(2,1)}, bf16[192,768]{1,0:T(8,128)(2,1)}, u32[]{:S(2)}, u32[]{:S(2)}) collective-permute-start(bf16[192,768]{1,0:T(8,128)(2,1)} %collective-permute-done.8.rest_6_), channel_id=1, source_target_pairs={{0,2},{1,3},{2,0},{3,1},{4,6},{5,7},{6,4},{7,5},{8,10},{9,11},{10,... | collective-permute-start | bytes 884744 | tf_op jit(solution)/shard_map/ppermute | solution.py:308
  65.8 6.9 %collective-permute-done.7.rest_5_ = bf16[192,768]{1,0:T(8,128)(2,1)} collective-permute-done((bf16[192,768]{1,0:T(8,128)(2,1)}, bf16[192,768]{1,0:T(8,128)(2,1)}, u32[]{:S(2)}, u32[]{:S(2)}) %collective-permute-start.7) | collective-permute-done | bytes 294944 | tf_op jit(solution)/shard_map/ppermute | solution.py:308
  72.7 0.0 collective-permute-start.11
  72.7 0.0 collective-permute-done.1.others
  72.7 0.0 collective-permute-done.mixed_other
  72.7 4.7 %collective-permute-done.9.rest_7_ = bf16[192,768]{1,0:T(8,128)(2,1)} collective-permute-done((bf16[192,768]{1,0:T(8,128)(2,1)}, bf16[192,768]{1,0:T(8,128)(2,1)}, u32[]{:S(2)}, u32[]{:S(2)}) %collective-permute-start.9) | collective-permute-done | bytes 294944 | tf_op jit(solution)/shard_map/ppermute | solution.py:308
  77.4 1.1 copy-done.2
  78.5 1.0 copy-done.7
  79.5 1.0 copy-done.9
  80.5 1.0 copy-done.11
  81.4 5.6 %branch.1 = (f32[512,768]{1,0:T(8,128)}, f32[512,128]{1,0:T(8,128)}) custom-call(s32[2]{0:T(128)S(1)} %pad_add_fusion.where_ref, bf16[256,1536]{1,0:T(8,128)(2,1)} %attention.1.mixed_own, bf16[256,1536]{1,0:T(8,128)(2,1)} %collective-permute-done.mixed_other, bf16[256,1536]{1,0:T(8,128)(2,1)S(1)} %bitcast.17, bf16[256,1536]{1,0:T(8,128)(2,1)S(1)} %bitcast.18, ...), custom_call_target="tpu_custom_call" | custom-call | flops 1207959552 | bytes 7077888 | tf_op jit(solution)/shard_map/branch/pallas_call | solution.py:164
  87.1 0.0 collective-permute-start.10
  87.1 1.9 %reverse_select_fusion = bf16[8,2,48,768]{3,2,1,0:T(8,128)(2,1)S(1)} fusion(bf16[8,2,48,768]{3,2,1,0:T(8,128)(2,1)} %bitcast.24, pred[]{:T(512)S(6)} %eq.4), kind=kLoop, calls=%fused_computation | loop fusion | flops 589824 | bytes 2359297 | tf_op jit(solution)/shard_map/jit(_where)/select_n | solution.py:322
  89.0 0.0 collective-permute-done.12.gram_other
  89.0 0.0 copy-start.3
  89.0 4.3 %predict.1.product = f32[768,768]{1,0:T(8,128)S(1)} custom-call(s32[2]{0:T(128)S(1)} %pad_add_fusion.where_ref, f32[768,768]{1,0:T(8,128)S(1)} %get-tuple-element.12.gram_own, f32[768,768]{1,0:T(8,128)} %collective-permute-done.12.gram_other, bf16[768,768]{1,0:T(8,128)(2,1)S(1)} %bitcast.16), custom_call_target="tpu_custom_call" | custom-call | flops 1811939328 | bytes 8257536 | tf_op jit(solution)/shard_map/predict/pallas_call | solution.py:195
  93.3 1.4 copy-done
  94.8 0.0 collective-permute-done.11.sum_other
  94.8 0.0 collective-permute-done.10.stats_other
  94.8 5.0 %targets.1 = (f32[256,768]{1,0:T(8,128)S(1)}, f32[256,768]{1,0:T(8,128)S(1)}, s16[8,112,768]{2,1,0:T(8,128)(2,1)}) custom-call(s32[2]{0:T(128)S(1)} %pad_add_fusion.where_ref, f32[512,768]{1,0:T(8,128)S(1)} %copy-done.3, f32[512,128]{1,0:T(8,128)} %get-tuple-element.10.stats, f32[512,128]{1,0:T(8,128)S(1)} %collective-permute-done.10.stats_other, ...), custom_call_target="tpu_custom_call" | custom-call | flops 603979776 | bytes 6684672 | tf_op jit(solution)/shard_map/targets/pallas_call | solution.py:248
  99.7 5.2 %all-to-all-start = ((s16[8,112,768]{2,1,0:T(8,128)(2,1)}), s16[8,112,768]{2,1,0:T(8,128)(2,1)S(1)}, u32[]{:S(2)}, u32[]{:S(2)}) async-start(s16[8,112,768]{2,1,0:T(8,128)(2,1)} %get-tuple-element.15), calls=%async_computation | async-start | bytes 2752512 | tf_op jit(solution)/shard_map/all_to_all | solution.py:358
  104.9 0.2 collective-permute-start.14
  105.2 33.2 %all-to-all-done.codes = s16[8,112,768]{2,1,0:T(8,128)(2,1)S(1)} async-done(((s16[8,112,768]{2,1,0:T(8,128)(2,1)}), s16[8,112,768]{2,1,0:T(8,128)(2,1)S(1)}, u32[]{:S(2)}, u32[]{:S(2)}) %all-to-all-start) | async-done | bytes 1376288 | tf_op jit(solution)/shard_map/all_to_all | solution.py:358
  138.4 0.9 sum_terms.1
  139.3 0.1 collective-permute-start.15
  139.4 2.8 %maximum_select_fusion = f32[1,256,1536]{2,1,0:T(8,128)} fusion(f32[1,256,768]{2,1,0:T(8,128)} %bitcast.11, f32[1,256,768]{2,1,0:T(8,128)S(1)} %bitcast.19, pred[]{:T(512)S(6)} %eq.4), kind=kLoop, calls=%fused_computation.1 | loop fusion | flops 1179648 | bytes 3145729 | tf_op jit(solution)/shard_map/jit(_where)/select_n | solution.py:367
  142.2 0.0 collective-permute-done.15
  142.2 0.7 maximum_select_fusion.1
  (26 shorter events, 0.1 us)
Async XLA Ops:
  7.2 79.9 %all-gather.3.cloned.1.call-start = ((), (), s32[]{:S(2)}) async-start(), calls=%async_computation.1 | async-start | bytes 1327104 | tf_op jit(solution)/shard_map/all_gather | solution.py:321
  8.8 10.3 %collective-permute-start.13 = (bf16[48,768]{1,0:T(8,128)(2,1)}, bf16[48,768]{1,0:T(8,128)(2,1)}, u32[]{:S(2)}, u32[]{:S(2)}) collective-permute-start(bf16[48,768]{1,0:T(8,128)(2,1)} %get-tuple-element.21), channel_id=1, source_target_pairs={{0,1},{1,0},{2,3},{3,2},{4,5},{5,4},{6,7},{7,6},{8,9},{9,8},{10,11... | collective-permute-start | bytes 221192 | tf_op jit(solution)/shard_map/ppermute | solution.py:308
  9.3 1.9 %copy-start.12 = (bf16[1,8,256,768]{3,2,1,0:T(8,128)(2,1)S(1)}, bf16[1,8,256,768]{3,2,1,0:T(8,128)(2,1)}, u32[]{:S(2)}) copy-start(bf16[1,8,256,768]{3,2,1,0:T(8,128)(2,1)} %hidden_ref.1) | copy-start | bytes 9437188
  11.2 0.7 copy-start.16
  11.9 8.9 %copy-start.17 = (bf16[96,1536]{1,0:T(8,128)(2,1)S(1)}, bf16[96,1536]{1,0:T(8,128)(2,1)}, u32[]{:S(2)}) copy-start(bf16[96,1536]{1,0:T(8,128)(2,1)} %param.14) | copy-start | bytes 884740
  18.3 0.7 copy-start.4
  19.1 8.6 %copy-start.1 = (bf16[1,256,1536]{2,1,0:T(8,128)(2,1)S(1)}, bf16[1,256,1536]{2,1,0:T(8,128)(2,1)}, u32[]{:S(2)}) copy-start(bf16[1,256,1536]{2,1,0:T(8,128)(2,1)} %param.12) | copy-start | bytes 2359300
  19.1 69.9 %collective-permute-start.12 = (f32[768,768]{1,0:T(8,128)S(1)}, f32[768,768]{1,0:T(8,128)}, u32[]{:S(2)}, u32[]{:S(2)}) collective-permute-start(f32[768,768]{1,0:T(8,128)S(1)} %get-tuple-element.12.gram_own), channel_id=1, source_target_pairs={{0,1},{1,0},{2,3},{3,2},{4,5},{5,4},{6,7},{7,6},{8,9},{9,8},{10,11... | collective-permute-start | bytes 7077896 | tf_op jit(solution)/shard_map/ppermute | solution.py:308
  20.8 3.0 %collective-permute-start.2 = (bf16[96,768]{1,0:T(8,128)(2,1)S(1)}, bf16[96,768]{1,0:T(8,128)(2,1)S(1)}, u32[]{:S(2)}, u32[]{:S(2)}) collective-permute-start(bf16[96,768]{1,0:T(8,128)(2,1)S(1)} %get-tuple-element.19), channel_id=1, source_target_pairs={{0,1},{1,0},{2,3},{3,2},{4,5},{5,4},{6,7},{7,6},{8,9},{9,8},{10,11... | collective-permute-start | bytes 442376 | tf_op jit(solution)/shard_map/ppermute | solution.py:308
  23.9 9.0 %copy-start.13 = (bf16[1,256,1536]{2,1,0:T(8,128)(2,1)S(1)}, bf16[1,256,1536]{2,1,0:T(8,128)(2,1)}, u32[]{:S(2)}) copy-start(bf16[1,256,1536]{2,1,0:T(8,128)(2,1)} %param.9) | copy-start | bytes 2359300
  23.9 9.0 %copy-start.14 = (bf16[1,256,1536]{2,1,0:T(8,128)(2,1)S(1)}, bf16[1,256,1536]{2,1,0:T(8,128)(2,1)}, u32[]{:S(2)}) copy-start(bf16[1,256,1536]{2,1,0:T(8,128)(2,1)} %param.10) | copy-start | bytes 2359300
  23.9 9.0 %copy-start.15 = (bf16[1,256,1536]{2,1,0:T(8,128)(2,1)S(1)}, bf16[1,256,1536]{2,1,0:T(8,128)(2,1)}, u32[]{:S(2)}) copy-start(bf16[1,256,1536]{2,1,0:T(8,128)(2,1)} %param.11) | copy-start | bytes 2359300
  23.9 22.5 %collective-permute-start.6 = (bf16[192,768]{1,0:T(8,128)(2,1)S(1)}, bf16[192,768]{1,0:T(8,128)(2,1)}, u32[]{:S(2)}, u32[]{:S(2)}) collective-permute-start(bf16[192,768]{1,0:T(8,128)(2,1)S(1)} %pad_maximum_fusion.1.rest_0_), channel_id=1, source_target_pairs={{0,8},{1,9},{2,10},{3,11},{4,12},{5,13},{6,14},{7,15},{8,0},{9,1},... | collective-permute-start | bytes 884744 | tf_op jit(solution)/shard_map/ppermute | solution.py:308
  29.7 43.0 %collective-permute-start.1 = (bf16[2,256,768]{2,1,0:T(8,128)(2,1)}, bf16[2,256,768]{2,1,0:T(8,128)(2,1)}, u32[]{:S(2)}, u32[]{:S(2)}) collective-permute-start(bf16[2,256,768]{2,1,0:T(8,128)(2,1)} %pad_maximum_fusion), channel_id=1, source_target_pairs={{0,1},{1,0},{2,3},{3,2},{4,5},{5,4},{6,7},{7,6},{8,9},{9,8},{10,11... | collective-permute-start | bytes 2359304 | tf_op jit(solution)/shard_map/ppermute | solution.py:308
  29.8 19.3 %collective-permute-start.4 = (bf16[192,768]{1,0:T(8,128)(2,1)S(1)}, bf16[192,768]{1,0:T(8,128)(2,1)S(1)}, u32[]{:S(2)}, u32[]{:S(2)}) collective-permute-start(bf16[192,768]{1,0:T(8,128)(2,1)S(1)} %pad_maximum_fusion.1.rest_0_), channel_id=1, source_target_pairs={{0,4},{1,5},{2,6},{3,7},{4,0},{5,1},{6,2},{7,3},{8,12},{9,13},{10,... | collective-permute-start | bytes 884744 | tf_op jit(solution)/shard_map/ppermute | solution.py:308
  31.4 17.7 %collective-permute-start.3 = (bf16[192,768]{1,0:T(8,128)(2,1)S(1)}, bf16[192,768]{1,0:T(8,128)(2,1)S(1)}, u32[]{:S(2)}, u32[]{:S(2)}) collective-permute-start(bf16[192,768]{1,0:T(8,128)(2,1)S(1)} %pad_maximum_fusion.1.rest_0_), channel_id=1, source_target_pairs={{0,2},{1,3},{2,0},{3,1},{4,6},{5,7},{6,4},{7,5},{8,10},{9,11},{10,... | collective-permute-start | bytes 884744 | tf_op jit(solution)/shard_map/ppermute | solution.py:308
  46.4 26.3 %collective-permute-start = (bf16[256,1536]{1,0:T(8,128)(2,1)}, bf16[256,1536]{1,0:T(8,128)(2,1)}, u32[]{:S(2)}, u32[]{:S(2)}) collective-permute-start(bf16[256,1536]{1,0:T(8,128)(2,1)} %attention.1.mixed_own), channel_id=1, source_target_pairs={{0,1},{1,0},{2,3},{3,2},{4,5},{5,4},{6,7},{7,6},{8,9},{9,8},{10,11... | collective-permute-start | bytes 2359304 | tf_op jit(solution)/shard_map/ppermute | solution.py:308
  49.0 12.0 %collective-permute-start.8 = (bf16[192,768]{1,0:T(8,128)(2,1)}, bf16[192,768]{1,0:T(8,128)(2,1)}, u32[]{:S(2)}, u32[]{:S(2)}) collective-permute-start(bf16[192,768]{1,0:T(8,128)(2,1)} %collective-permute-done.6.rest_4_), channel_id=1, source_target_pairs={{0,4},{1,5},{2,6},{3,7},{4,0},{5,1},{6,2},{7,3},{8,12},{9,13},{10,... | collective-permute-start | bytes 884744 | tf_op jit(solution)/shard_map/ppermute | solution.py:308
  49.0 0.7 copy-start.8
  49.8 12.9 %collective-permute-start.5 = (bf16[192,768]{1,0:T(8,128)(2,1)S(1)}, bf16[192,768]{1,0:T(8,128)(2,1)S(1)}, u32[]{:S(2)}, u32[]{:S(2)}) collective-permute-start(bf16[192,768]{1,0:T(8,128)(2,1)S(1)} %collective-permute-done.4.rest_2_), channel_id=1, source_target_pairs={{0,2},{1,3},{2,0},{3,1},{4,6},{5,7},{6,4},{7,5},{8,10},{9,11},{10,... | collective-permute-start | bytes 884744 | tf_op jit(solution)/shard_map/ppermute | solution.py:308
  51.3 0.7 copy-start.6
  61.1 11.6 %collective-permute-start.7 = (bf16[192,768]{1,0:T(8,128)(2,1)}, bf16[192,768]{1,0:T(8,128)(2,1)}, u32[]{:S(2)}, u32[]{:S(2)}) collective-permute-start(bf16[192,768]{1,0:T(8,128)(2,1)} %collective-permute-done.6.rest_4_), channel_id=1, source_target_pairs={{0,2},{1,3},{2,0},{3,1},{4,6},{5,7},{6,4},{7,5},{8,10},{9,11},{10,... | collective-permute-start | bytes 884744 | tf_op jit(solution)/shard_map/ppermute | solution.py:308
  62.7 0.7 copy-start.10
  63.4 14.0 %collective-permute-start.9 = (bf16[192,768]{1,0:T(8,128)(2,1)}, bf16[192,768]{1,0:T(8,128)(2,1)}, u32[]{:S(2)}, u32[]{:S(2)}) collective-permute-start(bf16[192,768]{1,0:T(8,128)(2,1)} %collective-permute-done.8.rest_6_), channel_id=1, source_target_pairs={{0,2},{1,3},{2,0},{3,1},{4,6},{5,7},{6,4},{7,5},{8,10},{9,11},{10,... | collective-permute-start | bytes 884744 | tf_op jit(solution)/shard_map/ppermute | solution.py:308
  72.7 22.1 %collective-permute-start.11 = (bf16[256,768]{1,0:T(8,128)(2,1)}, bf16[256,768]{1,0:T(8,128)(2,1)}, u32[]{:S(2)}, u32[]{:S(2)}) collective-permute-start(bf16[256,768]{1,0:T(8,128)(2,1)} %copy-done.4), channel_id=1, source_target_pairs={{0,1},{1,0},{2,3},{3,2},{4,5},{5,4},{6,7},{7,6},{8,9},{9,8},{10,11... | collective-permute-start | bytes 1179656 | tf_op jit(solution)/shard_map/ppermute | solution.py:308
  77.4 1.1 copy-start.2
  78.5 1.0 copy-start.7
  79.5 1.0 copy-start.9
  80.5 1.0 copy-start.11
  87.1 7.7 %collective-permute-start.10 = (f32[512,128]{1,0:T(8,128)}, f32[512,128]{1,0:T(8,128)S(1)}, u32[]{:S(2)}, u32[]{:S(2)}) collective-permute-start(f32[512,128]{1,0:T(8,128)} %get-tuple-element.10.stats), channel_id=1, source_target_pairs={{0,1},{1,0},{2,3},{3,2},{4,5},{5,4},{6,7},{7,6},{8,9},{9,8},{10,11... | collective-permute-start | bytes 786440 | tf_op jit(solution)/shard_map/ppermute | solution.py:308
  89.0 5.8 %copy-start.3 = (f32[512,768]{1,0:T(8,128)S(1)}, f32[512,768]{1,0:T(8,128)}, u32[]{:S(2)}) copy-start(f32[512,768]{1,0:T(8,128)} %get-tuple-element.9.blend) | copy-start | bytes 4718596
  89.0 5.8 %copy-start.5 = (bf16[256,768]{1,0:T(8,128)(2,1)S(1)}, bf16[256,768]{1,0:T(8,128)(2,1)}, u32[]{:S(2)}) copy-start(bf16[256,768]{1,0:T(8,128)(2,1)} %copy-done.4) | copy-start | bytes 1179652
  93.3 1.4 copy-start
  99.7 38.7 %all-to-all-start = ((s16[8,112,768]{2,1,0:T(8,128)(2,1)}), s16[8,112,768]{2,1,0:T(8,128)(2,1)S(1)}, u32[]{:S(2)}, u32[]{:S(2)}) async-start(s16[8,112,768]{2,1,0:T(8,128)(2,1)} %get-tuple-element.15), calls=%async_computation | async-start | bytes 2752512 | tf_op jit(solution)/shard_map/all_to_all | solution.py:358
  104.9 34.5 %collective-permute-start.14 = (f32[256,768]{1,0:T(8,128)S(1)}, f32[256,768]{1,0:T(8,128)}, u32[]{:S(2)}, u32[]{:S(2)}) collective-permute-start(f32[256,768]{1,0:T(8,128)S(1)} %get-tuple-element.14), channel_id=1, source_target_pairs={{0,1},{1,0},{2,3},{3,2},{4,5},{5,4},{6,7},{7,6},{8,9},{9,8},{10,11... | collective-permute-start | bytes 2359304 | tf_op jit(solution)/shard_map/ppermute | solution.py:308
  139.3 2.9 %collective-permute-start.15 = (f32[48,768]{1,0:T(8,128)S(1)}, f32[48,768]{1,0:T(8,128)S(1)}, u32[]{:S(2)}, u32[]{:S(2)}) collective-permute-start(f32[48,768]{1,0:T(8,128)S(1)} %get-tuple-element.17), channel_id=1, source_target_pairs={{0,1},{1,0},{2,3},{3,2},{4,5},{5,4},{6,7},{7,6},{8,9},{9,8},{10,11... | collective-permute-start | bytes 442376 | tf_op jit(solution)/shard_map/ppermute | solution.py:308
Sparse Core Ops, SparseCore 0:
  20.9 54.7 all-gather.2

commit v2 on v1

v2 whole, which is shorter than its diff:
```python
import functools
import math

import jax
import jax.numpy as jnp
from jax import lax
from jax.experimental import pallas as pl
from jax.experimental.pallas import tpu as pltpu
from jax.sharding import PartitionSpec as P

HEADS = 24
TOP_K = 10
AXES = ("groups", "dp")
VMEM = 56 * 1024 * 1024
CORE, NEXT_Y, NEXT_Z, FAR_Z = 1, 2, 4, 8
LINE = 4
CUTS = 2
TAIL = 16


def call(kernel, out_shape, *, name, grid=(1,), in_specs, out_specs, scratch=(), flops=0, nbytes=0):
    return pl.pallas_call(
        kernel,
        out_shape=out_shape,
        grid_spec=pltpu.PrefetchScalarGridSpec(
            num_scalar_prefetch=1,
            grid=grid,
            in_specs=in_specs,
            out_specs=out_specs,
            scratch_shapes=scratch,
        ),
        compiler_params=pltpu.CompilerParams(vmem_limit_bytes=VMEM),
        cost_estimate=pl.CostEstimate(flops=flops, bytes_accessed=nbytes, transcendentals=0),
        name=name,
    )


def whole(shape):
    return pl.BlockSpec(shape, lambda i, s: (0,) * len(shape))


def contract_rows(a, b):
    return lax.dot_general(a, b, (((0,), (0,)), ((), ())), preferred_element_type=jnp.float32)


def attention_kernel(where_ref, q_ref, k_ref, v_ref, out_ref, *, size):
    mixed = []
    for j in range(q_ref.shape[1] // size):
        cols = slice(j * size, (j + 1) * size)
        q = q_ref[:, cols] * jnp.asarray(1.0 / math.sqrt(size), q_ref.dtype)
        scores = lax.dot_general(
            k_ref[:, cols], q, (((1,), (1,)), ((), ())), preferred_element_type=jnp.float32
        )
        weights = jnp.exp(scores - jnp.max(scores, axis=0, keepdims=True))
        weights = weights * (1.0 / jnp.sum(weights, axis=0, keepdims=True))
        mixed.append(contract_rows(weights.astype(jnp.bfloat16), v_ref[:, cols]))
    out_ref[...] = jnp.concatenate(mixed, axis=1).astype(out_ref.dtype)


def attention(where, q, k, v):
    patches, width = q.shape
    return call(
        functools.partial(attention_kernel, size=width // HEADS),
        jax.ShapeDtypeStruct((patches, width), jnp.bfloat16),
        name="attention",
        in_specs=[whole((patches, width))] * 3,
        out_specs=whole((patches, width)),
        flops=4 * patches * patches * width * 4,
        nbytes=8 * patches * width,
    )(where, q, k, v)


def gram_kernel(where_ref, hidden_ref, kept_ref, *rest, parted):
    *gram_refs, sum_ref, rows_all, total = rest
    clones, patches = hidden_ref.shape[1], hidden_ref.shape[2]
    positions = lax.broadcasted_iota(jnp.int32, (patches, kept_ref.shape[1]), 0)
    sums = None
    for i in range(clones):
        kept = kept_ref[i : i + 1, :]
        covered = jnp.max(jnp.where(positions == kept, 1.0, 0.0), axis=1, keepdims=True)
        rows = hidden_ref[0, i]
        rows = jnp.where(covered > 0.5, jnp.zeros_like(rows), rows)
        rows_all[i * patches : (i + 1) * patches, :] = rows
        wide = rows.astype(jnp.float32)
        sums = wide if sums is None else sums + wide
    sum_ref[...] = sums.astype(sum_ref.dtype)
    if not parted:
        gram_refs[0][...] = contract_rows(rows_all[...], rows_all[...])
        return
    total[...] = contract_rows(rows_all[...], rows_all[...])
    mine, theirs = gram_refs
    core = where_ref[0]
    chips, rows = parted
    for k in range(chips):
        for ref, c in ((mine, core), (theirs, 1 - core)):
            at = pl.multiple_of((2 * k + c) * rows, rows)
            ref[k * rows : (k + 1) * rows, :] = total[pl.ds(at, rows), :]


def gram(where, hidden, kept, parted):
    _, clones, patches, width = hidden.shape
    grams = [(width // 2, width)] * 2 if parted else [(width, width)]
    return call(
        functools.partial(gram_kernel, parted=parted),
        tuple(jax.ShapeDtypeStruct(g, jnp.float32) for g in grams)
        + (jax.ShapeDtypeStruct((patches, width), jnp.bfloat16),),
        name="gram",
        in_specs=[whole(hidden.shape), whole(kept.shape)],
        out_specs=tuple(whole(g) for g in grams) + (whole((patches, width)),),
        scratch=[
            pltpu.VMEM((clones * patches, width), jnp.bfloat16),
            pltpu.VMEM((width, width), jnp.float32),
        ],
        flops=2 * clones * patches * width * width,
        nbytes=2 * clones * patches * width + 4 * width * width,
    )(where, hidden, kept)


def put_in_order(where_ref, pieces, full):
    core, chip = where_ref[0], where_ref[1]
    if len(pieces) == 1:
        full[...] = pieces[0][...]
        return
    for k, piece in enumerate(pieces):
        rows = piece.shape[0] // 2
        base = (chip ^ k) * 2
        for j in range(2):
            at = pl.multiple_of((base + (core ^ j)) * rows, rows)
            full[pl.ds(at, rows), :] = piece[j * rows : (j + 1) * rows, :]


def branch_kernel(
    where_ref, mixed_own, mixed_other, stream_own, earlier_own, others, *rest
):
    *pieces, blend_ref, stats_ref, full = rest
    put_in_order(where_ref, pieces, full)
    patches, half = stream_own.shape
    streams = (stream_own[...], others[0])
    earliers = (earlier_own[...], others[1])
    for i, mixed in enumerate((mixed_own, mixed_other)):
        layer_out = streams[i].astype(jnp.float32) + jnp.dot(
            mixed[...], full[...], preferred_element_type=jnp.float32
        )
        center = jnp.mean(layer_out, axis=0, keepdims=True)
        away = layer_out - center
        spread = jnp.mean(away * away, axis=0, keepdims=True)
        normed = away / jnp.sqrt(spread + 1e-05)
        blend = ((TOP_K - 1) * earliers[i].astype(jnp.float32) + normed) / TOP_K
        rows = slice(i * patches, (i + 1) * patches)
        blend_ref[rows, :] = blend
        middle = jnp.mean(blend, axis=1, keepdims=True)
        off = blend - middle
        squares = jnp.sum(off * off, axis=1, keepdims=True)
        lane = lax.broadcasted_iota(jnp.int32, (patches, 128), 1)
        stats_ref[rows, :] = jnp.where(lane < 64, middle, squares)


def branch(where, mixed_own, mixed_other, stream, earlier, others, pieces):
    patches, width = mixed_own.shape
    half = width // 2
    own_half = pl.BlockSpec((patches, half), lambda i, s: (0, s[0]))
    return call(
        branch_kernel,
        (
            jax.ShapeDtypeStruct((2 * patches, half), jnp.float32),
            jax.ShapeDtypeStruct((2 * patches, 128), jnp.float32),
        ),
        name="branch",
        in_specs=[whole((patches, width))] * 2
        + [own_half] * 2
        + [whole((2, patches, half))]
        + [whole(p.shape) for p in pieces],
        out_specs=(whole((2 * patches, half)), whole((2 * patches, 128))),
        scratch=[pltpu.VMEM((width, half), jnp.bfloat16)],
        flops=4 * patches * width * half,
        nbytes=12 * patches * width + 2 * width * half,
    )(where, mixed_own, mixed_other, stream, earlier, others, *pieces)


def encode(values, out_ref):
    rows = values.shape[0]
    top = jnp.max(jnp.abs(values), axis=0, keepdims=True)
    power = jnp.ceil(jnp.log2(jnp.maximum(top, 1e-30))) - 15.0
    codes = jnp.clip(jnp.round(values * jnp.exp2(-power)), -32767.0, 32767.0)
    out_ref[:rows, :] = codes.astype(jnp.int32).astype(jnp.int16)
    out_ref[rows:, :] = jnp.broadcast_to(power, (TAIL, values.shape[1])).astype(jnp.int32).astype(jnp.int16)


def decode(codes):
    rows = codes.shape[0] - TAIL
    power = codes[rows:, :].astype(jnp.int32).astype(jnp.float32)[:1]
    return codes[:rows, :].astype(jnp.int32).astype(jnp.float32) * jnp.exp2(power)


def halve(values, where_ref, send_ref, keep_ref):
    rows = keep_ref.shape[0] // LINE
    y = where_ref[1] % 2

    def blocks(of):
        return [values[pl.ds(pl.multiple_of((2 * z + of) * rows, rows), rows), :] for z in range(LINE)]

    keep_ref[...] = jnp.concatenate(blocks(y), axis=0)
    encode(jnp.concatenate(blocks(1 - y), axis=0), send_ref)


def halved_shapes(rows, width):
    return (
        jax.ShapeDtypeStruct((rows // 2 + TAIL, width), jnp.int16),
        jax.ShapeDtypeStruct((rows // 2, width), jnp.float32),
    )


def first_kernel(where_ref, mine, theirs, send_ref, keep_ref, total):
    total[...] = mine[...] + theirs[...]
    halve(total, where_ref, send_ref, keep_ref)


def first_step(where, mine, theirs):
    shapes = halved_shapes(*mine.shape)
    return call(
        first_kernel,
        shapes,
        name="first_step",
        in_specs=[whole(mine.shape)] * 2,
        out_specs=tuple(whole(x.shape) for x in shapes),
        scratch=[pltpu.VMEM(mine.shape, jnp.float32)],
        flops=mine.size,
        nbytes=11 * mine.size,
    )(where, mine, theirs)


def second_kernel(where_ref, keep, codes, own_ref, *rest):
    *send_refs, total = rest
    rows = own_ref.shape[0]
    z = where_ref[1] // 2
    total[...] = keep[...] + decode(codes[...])

    def block(of):
        return total[pl.ds(pl.multiple_of(of * rows, rows), rows), :]

    own_ref[...] = block(z)
    for m, ref in enumerate(send_refs):
        encode(block(z ^ (m + 1)), ref)


def second_step(where, keep, codes):
    rows, width = keep.shape[0] // LINE, keep.shape[1]
    shapes = (jax.ShapeDtypeStruct((rows, width), jnp.float32),) + (
        jax.ShapeDtypeStruct((rows + TAIL, width), jnp.int16),
    ) * (LINE - 1)
    return call(
        second_kernel,
        shapes,
        name="second_step",
        in_specs=[whole(keep.shape), whole(codes.shape)],
        out_specs=tuple(whole(x.shape) for x in shapes),
        scratch=[pltpu.VMEM(keep.shape, jnp.float32)],
        flops=keep.size,
        nbytes=9 * keep.size,
    )(where, keep, codes)


def last_kernel(where_ref, own, c1, c2, c3, *out_refs, scale):
    total = own[...] + (decode(c1[...]) + (decode(c2[...]) + decode(c3[...])))
    if scale is None:
        (pair,) = out_refs
        rows = total.shape[0]
        high = total.astype(jnp.bfloat16)
        pair[:rows, :] = high
        pair[rows:, :] = (total - high.astype(jnp.float32)).astype(jnp.bfloat16)
        return
    keep, send = out_refs
    rows = keep.shape[0]
    first, second = total[:rows, :] * scale, total[rows:, :] * scale
    mine_first = where_ref[0] == 0
    keep[...] = jnp.where(mine_first, first, second)
    send[...] = jnp.where(mine_first, second, first)


def last_step(where, own, codes, scale=None):
    rows, width = own.shape
    if scale is None:
        shapes = (jax.ShapeDtypeStruct((2 * rows, width), jnp.bfloat16),)
    else:
        shapes = (jax.ShapeDtypeStruct((rows // 2, width), jnp.float32),) * 2
    return call(
        functools.partial(last_kernel, scale=scale),
        shapes,
        name="last_step",
        in_specs=[whole(own.shape)] + [whole(c.shape) for c in codes],
        out_specs=tuple(whole(x.shape) for x in shapes),
        flops=8 * own.size,
        nbytes=14 * own.size,
    )(where, own, *codes)


def targets_kernel(where_ref, blend, stats, stats_other, sum_own, sum_other, grams, weights, own_ref, other_ref, *rest, width):
    patches = own_ref.shape[0]
    grad = contract_rows(grams[...], weights[...])
    for i, (out, features) in enumerate(((own_ref, sum_own), (other_ref, sum_other))):
        mine = stats[i * patches : (i + 1) * patches, :]
        theirs = stats_other[(1 - i) * patches : (2 - i) * patches, :]
        gap = mine[:, :1] - theirs[:, :1]
        middle = 0.5 * (mine[:, :1] + theirs[:, :1])
        squares = mine[:, 64:65] + theirs[:, 64:65] + (width / 4) * gap * gap
        root = 1.0 / jnp.sqrt(squares / width + 1e-06)
        target = (blend[i * patches : (i + 1) * patches, :] - middle) * root
        out[...] = target
        grad = grad - contract_rows(features[...], target.astype(jnp.bfloat16))
    if len(rest) == 1:
        rest[0][...] = grad
        return
    send_ref, keep_ref, total = rest
    total[...] = grad
    halve(total, where_ref, send_ref, keep_ref)


def targets_and_term(where, blend, stats, stats_other, sum_own, sum_other, grams, weights, cut, coded):
    j, n = cut
    patches, columns = blend.shape[0] // 2, blend.shape[1] // n
    dec = grams.shape[1]
    shapes = (jax.ShapeDtypeStruct((patches, columns), jnp.float32),) * 2
    if coded:
        shapes += halved_shapes(dec, columns)
    else:
        shapes += (jax.ShapeDtypeStruct((dec, columns), jnp.float32),)

    def part(x):
        return pl.BlockSpec((x.shape[0], columns), lambda i, s: (0, j))

    inputs = (blend, stats, stats_other, sum_own, sum_other, grams, weights)
    return call(
        functools.partial(targets_kernel, width=2 * blend.shape[1]),
        shapes,
        name="targets",
        in_specs=[part(blend)] + [whole(x.shape) for x in inputs[1:-1]] + [part(weights)],
        out_specs=tuple(whole(x.shape) for x in shapes),
        scratch=[pltpu.VMEM((dec, columns), jnp.float32)] if coded else [],
        flops=4 * patches * dec * columns,
        nbytes=16 * patches * columns + 6 * dec * columns,
    )(where, *inputs)


def after(x, *others):
    return lax.optimization_barrier((x,) + others)[0]


def on_device(
    mesh_shape,
    queries,
    key_rows,
    value_rows,
    stream,
    earlier,
    out_weight,
    pred_weight,
    decoder_hidden,
    kept_index,
):
    groups, parts = mesh_shape["groups"], mesh_shape["dp"]
    chips = parts // 2
    patches, width = queries.shape[1:]
    clones, dec = decoder_hidden.shape[1], decoder_hidden.shape[3]
    half = width // 2
    scale = 2.0 / (math.sqrt(width) * clones)
    me = lax.axis_index("dp")
    core, chip = me % 2, me // 2
    where = jnp.stack([core, chip]).astype(jnp.int32)
    same_core = [[2 * k + j for k in range(chips)] for j in range(2)]
    by_pairs = chips == 2 * LINE

    def swap(x, bits):
        pairs = [(g * parts + i, g * parts + (i ^ bits)) for g in range(groups) for i in range(parts)]
        return lax.ppermute(x, AXES, pairs)

    def my_half(x):
        return lax.dynamic_slice_in_dim(x, core * half, half, axis=-1)

    def other_half(x):
        return lax.dynamic_slice_in_dim(x, (1 - core) * half, half, axis=-1)

    def side_by_side(mine, theirs):
        return jnp.where(
            core == 0,
            jnp.concatenate(mine + theirs, axis=1),
            jnp.concatenate(theirs + mine, axis=1),
        )

    out_piece = jnp.concatenate([my_half(out_weight), swap(other_half(out_weight), CORE)], axis=0)
    if by_pairs:
        z1, z2, y0 = swap(out_piece, NEXT_Z), swap(out_piece, FAR_Z), swap(out_piece, NEXT_Y)
        z3 = swap(z2, NEXT_Z)
        y1, y2, y3 = swap(z1, NEXT_Y), swap(z2, NEXT_Y), swap(z3, NEXT_Y)
        out_pieces = [out_piece, y0, z1, y1, z2, y2, z3, y3]
    else:
        rows = out_weight.shape[0]
        got = lax.all_gather(out_piece, "dp", axis_index_groups=same_core).reshape(chips, 2, rows, half)
        out_pieces = [jnp.where(core == 0, got, got[:, ::-1]).reshape(width, half)]

    hidden = after(decoder_hidden, out_piece)
    if by_pairs:
        gram_mine, gram_theirs, sum_own = gram(where, hidden, kept_index[0], (chips, dec // parts))
        send, keep = first_step(where, gram_mine, swap(gram_theirs, CORE))
        own, *codes = second_step(where, keep, swap(send, NEXT_Y))
        codes = [swap(c, NEXT_Z * (m + 1)) for m, c in enumerate(codes)]
        (gram_rows,) = last_step(where, own, codes)
    else:
        gram_all, sum_own = gram(where, hidden, kept_index[0], None)
        gram_rows = lax.psum_scatter(gram_all, "dp", scatter_dimension=0, tiled=True)
        high = gram_rows.astype(jnp.bfloat16)
        low = (gram_rows - high.astype(jnp.float32)).astype(jnp.bfloat16)
        gram_rows = jnp.concatenate([high, low], axis=0)
    grams = jnp.concatenate([gram_rows, swap(gram_rows, CORE)], axis=0)
    pred = after(pred_weight, out_piece)
    pred_mine, pred_theirs = my_half(pred), swap(other_half(pred), CORE)
    weights = jnp.concatenate([pred_mine, pred_mine, pred_theirs, pred_theirs], axis=0)

    mixed_own = attention(where, after(queries, out_piece)[0], key_rows[0], value_rows[0])
    mixed_other = swap(mixed_own, CORE)
    others = jnp.concatenate([other_half(after(stream, out_piece)), other_half(earlier)], axis=0)
    others = swap(others, CORE)
    sum_other = swap(sum_own, CORE)

    blend, stats = branch(where, mixed_own, mixed_other, stream[0], earlier[0], others, out_pieces)
    stats_other = swap(stats, CORE)

    def term(cut, coded):
        return targets_and_term(
            where, blend, stats, stats_other, sum_own, sum_other, grams, weights, cut, coded
        )

    if not by_pairs:
        target_own, target_other, total = term((0, 1), False)
        targets = side_by_side([target_own], [swap(target_other, CORE)])[None]
        summed = lax.psum_scatter(
            total, "dp", scatter_dimension=0, tiled=True, axis_index_groups=same_core
        )
        summed = (summed * scale).reshape(2, dec // parts, half)
        keep = lax.dynamic_index_in_dim(summed, core, 0, keepdims=False)
        send = lax.dynamic_index_in_dim(summed, 1 - core, 0, keepdims=False)
        return targets, side_by_side([keep], [swap(send, CORE)])

    steps = [term((j, CUTS), True) for j in range(CUTS)]
    received = [swap(send, NEXT_Y) for _, _, send, _ in steps]
    targets = side_by_side([s[0] for s in steps], [swap(s[1], CORE) for s in steps])[None]
    received[-1] = after(received[-1], targets)
    mine, theirs = [], []
    for (_, _, _, keep), codes in zip(steps, received):
        own, *codes = second_step(where, keep, codes)
        codes = [swap(c, NEXT_Z * (m + 1)) for m, c in enumerate(codes)]
        keep, send = last_step(where, own, codes, scale)
        mine.append(keep)
        theirs.append(swap(send, CORE))
    return targets, side_by_side(mine, theirs)


def solution(mesh):
    by_image = P(AXES, None, None)
    return jax.shard_map(
        functools.partial(on_device, dict(mesh.shape)),
        mesh=mesh,
        in_specs=(
            by_image,
            by_image,
            by_image,
            by_image,
            by_image,
            P("dp", None),
            P("dp", None),
            P(AXES, None, None, None),
            by_image,
        ),
        out_specs=(by_image, P(AXES, None)),
        check_vma=False,
    )
```

time: 150 us -> 127 us (0.85)
  waiting for transfers between devices: 59.1 us -> 37.2 us
  between operations: 14.2 us -> 0.91 us
  Pallas kernels: 35.7 us -> 48.7 us
  starting transfers between devices: 19 us -> 25.8 us
  local copies, waits for them, and re-layouts: 13.7 us -> 7.46 us
  other arithmetic: 8.1 us -> 6.4 us
    all_to_all x1 -> x0, waiting for transfers between devices: 33.2 us -> none  [on_device(): codes = lax.all_to_all(term, 'dp', 0, 0, axis_index_groups=same_core)]
    pallas_call x5 -> x11, Pallas kernels: 30.1 us -> 42.2 us  [the longest x2 9.4 us: targets_and_term(): call(functools.partial(targets_kernel, width=2 * blend.shape[1]), shapes,...]
    ppermute x16 -> x31, starting transfers between devices: 13.8 us -> 25.8 us  [swap(): return lax.ppermute(x, AXES, pairs)]
    ppermute x16 -> x31, waiting for transfers between devices: 25.8 us -> 37.2 us  [swap(): return lax.ppermute(x, AXES, pairs)]
    all_to_all x1 -> x0, starting transfers between devices: 5.19 us -> none  [on_device(): codes = lax.all_to_all(term, 'dp', 0, 0, axis_index_groups=same_core)]
    unnamed x36 -> x64, local copies, waits for them, and re-layouts: 11 us -> 6.38 us
    select_n x3 -> x2, other arithmetic: 5.44 us -> 4.22 us  [side_by_side(): jnp.where(core == 0, jnp.concatenate(mine + theirs, axis=1), jnp.concaten...]
  transfers between devices with their start and end apart: 18 -> 31, of which waited for: 6 -> 10; matrix products, arithmetic and copies ran while one was open for 6% -> 4% of each run, Pallas kernels for 21% -> 29%
where the time goes in v2:
time: 127 us; the launch traced here: 126 us
  Pallas kernels  48.7 us (38%)
  waiting for transfers between devices  37.2 us (29%)
  starting transfers between devices  25.8 us (20%)
  local copies, waits for them, and re-layouts  7.46 us (6%)
  other arithmetic  6.4 us (5%)
    ppermute x31, waiting for transfers between devices, swap(): return lax.ppermute(x, AXES, pairs)  37.2 us
    ppermute x31, starting transfers between devices, swap(): return lax.ppermute(x, AXES, pairs)  25.8 us
    pallas_call x2, Pallas kernels, targets_and_term(): call(functools.partial(targets_kernel, width=2 * blend.shape[1]), shapes,...  9.4 us
    pallas_call x3, Pallas kernels, second_step(): call(second_kernel, shapes, name='second_step', in_specs=[whole(keep.shap...  8.25 us
    pallas_call x1, Pallas kernels, gram(): call(functools.partial(gram_kernel, parted=parted), tuple((jax.ShapeDtype...  7.64 us
    pallas_call x3, Pallas kernels, last_step(): call(functools.partial(last_kernel, scale=scale), shapes, name='last_step...  7.36 us
    pallas_call x1, Pallas kernels, branch(): call(branch_kernel, (jax.ShapeDtypeStruct((2 * patches, half), jnp.float3...  6.48 us
    unnamed x64, local copies, waits for them, and re-layouts  6.38 us
  transfers between devices with their start and end apart: 31, of which 10 were waited for; matrix products, arithmetic and copies ran while one was open for 4% of the time, Pallas kernels for 29%

profile of v2, /device:TPU:0, one launch (start us, length us, event | category | flops | bytes accessed | tf_op | source)
XLA Modules:
  0.0 126.5 jit_solution(5453829286516199110)
XLA Ops:
  0.7 1.0 constant_dynamic-slice_fusion.5
  1.7 0.5 collective-permute-start
  2.2 0.6 pad_add_fusion.where_ref
  2.8 0.4 collective-permute-done
  3.2 7.6 %gram.1 = (f32[384,768]{1,0:T(8,128)}, f32[384,768]{1,0:T(8,128)}, bf16[256,768]{1,0:T(8,128)(2,1)}) custom-call(s32[2]{0:T(128)} %pad_add_fusion.where_ref, bf16[1,8,256,768]{3,2,1,0:T(8,128)(2,1)} %hidden_ref, s32[8,64]{1,0:T(8,128)} %bitcast.21), custom_call_target="tpu_custom_call" | custom-call | flops 2415919104 | bytes 5505024 | tf_op jit(solution)/shard_map/gram/pallas_call | solution.py:103
  10.9 0.4 collective-permute-start.12
  11.3 2.8 %collective-permute-start.4 = (bf16[192,768]{1,0:T(8,128)(2,1)S(1)}, bf16[192,768]{1,0:T(8,128)(2,1)S(1)}, u32[]{:S(2)}, u32[]{:S(2)}) collective-permute-start(bf16[192,768]{1,0:T(8,128)(2,1)S(1)} %pad_maximum_fusion.1.rest_0_), channel_id=1, source_target_pairs={{0,4},{1,5},{2,6},{3,7},{4,0},{5,1},{6,2},{7,3},{8,12},{9,13},{10,... | collective-permute-start | bytes 884744 | tf_op jit(solution)/shard_map/ppermute | solution.py:374
  14.1 2.6 %collective-permute-start.6 = (bf16[192,768]{1,0:T(8,128)(2,1)S(1)}, bf16[192,768]{1,0:T(8,128)(2,1)S(1)}, u32[]{:S(2)}, u32[]{:S(2)}) collective-permute-start(bf16[192,768]{1,0:T(8,128)(2,1)S(1)} %pad_maximum_fusion.1.rest_0_), channel_id=1, source_target_pairs={{0,8},{1,9},{2,10},{3,11},{4,12},{5,13},{6,14},{7,15},{8,0},{9,1},... | collective-permute-start | bytes 884744 | tf_op jit(solution)/shard_map/ppermute | solution.py:374
  16.7 6.1 %attention.1.mixed_own = bf16[256,1536]{1,0:T(8,128)(2,1)} custom-call(s32[2]{0:T(128)} %pad_add_fusion.where_ref, bf16[256,1536]{1,0:T(8,128)(2,1)} %bitcast.18, bf16[256,1536]{1,0:T(8,128)(2,1)} %bitcast.19, bf16[256,1536]{1,0:T(8,128)(2,1)} %bitcast.20), custom_call_target="tpu_custom_call" | custom-call | flops 1610612736 | bytes 3145728 | tf_op jit(solution)/shard_map/attention/pallas_call | solution.py:62
  22.8 1.0 copy-done.5
  23.8 3.5 %first_step.1 = (s16[208,768]{1,0:T(8,128)(2,1)}, f32[192,768]{1,0:T(8,128)}) custom-call(s32[2]{0:T(128)} %pad_add_fusion.where_ref, f32[384,768]{1,0:T(8,128)} %get-tuple-element.44.mine, f32[384,768]{1,0:T(8,128)} %copy-done.5), custom_call_target="tpu_custom_call" | custom-call | flops 294912 | bytes 3244032 | tf_op jit(solution)/shard_map/first_step/pallas_call | solution.py:220
  27.3 1.5 %collective-permute-start.13 = (s16[208,768]{1,0:T(8,128)(2,1)}, s16[208,768]{1,0:T(8,128)(2,1)S(1)}, u32[]{:S(2)}, u32[]{:S(2)}) collective-permute-start(s16[208,768]{1,0:T(8,128)(2,1)} %get-tuple-element.47), channel_id=1, source_target_pairs={{0,2},{1,3},{2,0},{3,1},{4,6},{5,7},{6,4},{7,5},{8,10},{9,11},{10,... | collective-permute-start | bytes 958472 | tf_op jit(solution)/shard_map/ppermute | solution.py:374
  28.9 0.3 collective-permute-start.2
  29.2 0.6 collective-permute-start.3
  29.8 0.6 collective-permute-done.6.rest_4_
  30.3 1.5 %collective-permute-start.5 = (bf16[192,768]{1,0:T(8,128)(2,1)S(1)}, bf16[192,768]{1,0:T(8,128)(2,1)S(1)}, u32[]{:S(2)}, u32[]{:S(2)}) collective-permute-start(bf16[192,768]{1,0:T(8,128)(2,1)S(1)} %collective-permute-done.4.rest_2_), channel_id=1, source_target_pairs={{0,2},{1,3},{2,0},{3,1},{4,6},{5,7},{6,4},{7,5},{8,10},{9,11},{10,... | collective-permute-start | bytes 884744 | tf_op jit(solution)/shard_map/ppermute | solution.py:374
  31.9 6.0 %collective-permute-done.13.codes = s16[208,768]{1,0:T(8,128)(2,1)S(1)} collective-permute-done((s16[208,768]{1,0:T(8,128)(2,1)}, s16[208,768]{1,0:T(8,128)(2,1)S(1)}, u32[]{:S(2)}, u32[]{:S(2)}) %collective-permute-start.13) | collective-permute-done | bytes 319520 | tf_op jit(solution)/shard_map/ppermute | solution.py:374
  37.8 0.4 collective-permute-start.8
  38.3 0.3 copy-done.11
  38.6 2.8 %second_step.3 = (f32[48,768]{1,0:T(8,128)}, s16[64,768]{1,0:T(8,128)(2,1)}, s16[64,768]{1,0:T(8,128)(2,1)}, s16[64,768]{1,0:T(8,128)(2,1)}) custom-call(s32[2]{0:T(128)} %pad_add_fusion.where_ref, f32[192,768]{1,0:T(8,128)} %get-tuple-element.46.keep, s16[208,768]{1,0:T(8,128)(2,1)} %copy-done.11), custom_call_target="tpu_custom_call" | custom-call | flops 147456 | bytes 1327104 | tf_op jit(solution)/shard_map/second_step/pallas_call | solution.py:251
  41.3 2.8 %collective-permute-done.3.rest_1_ = bf16[192,768]{1,0:T(8,128)(2,1)S(1)} collective-permute-done((bf16[192,768]{1,0:T(8,128)(2,1)S(1)}, bf16[192,768]{1,0:T(8,128)(2,1)S(1)}, u32[]{:S(2)}, u32[]{:S(2)}) %collective-permute-start.3) | collective-permute-done | bytes 294944 | tf_op jit(solution)/shard_map/ppermute | solution.py:374
  44.2 0.4 collective-permute-start.14
  44.6 5.5 %collective-permute-done.5.rest_3_ = bf16[192,768]{1,0:T(8,128)(2,1)S(1)} collective-permute-done((bf16[192,768]{1,0:T(8,128)(2,1)S(1)}, bf16[192,768]{1,0:T(8,128)(2,1)S(1)}, u32[]{:S(2)}, u32[]{:S(2)}) %collective-permute-start.5) | collective-permute-done | bytes 294944 | tf_op jit(solution)/shard_map/ppermute | solution.py:374
  50.1 0.3 collective-permute-start.15
  50.4 1.5 %collective-permute-start.7 = (bf16[192,768]{1,0:T(8,128)(2,1)S(1)}, bf16[192,768]{1,0:T(8,128)(2,1)S(1)}, u32[]{:S(2)}, u32[]{:S(2)}) collective-permute-start(bf16[192,768]{1,0:T(8,128)(2,1)S(1)} %collective-permute-done.6.rest_4_), channel_id=1, source_target_pairs={{0,2},{1,3},{2,0},{3,1},{4,6},{5,7},{6,4},{7,5},{8,10},{9,11},{10,... | collective-permute-start | bytes 884744 | tf_op jit(solution)/shard_map/ppermute | solution.py:374
  52.0 0.5 collective-permute-start.9
  52.5 5.2 %collective-permute-done.15.c2 = s16[64,768]{1,0:T(8,128)(2,1)S(1)} collective-permute-done((s16[64,768]{1,0:T(8,128)(2,1)}, s16[64,768]{1,0:T(8,128)(2,1)S(1)}, u32[]{:S(2)}, u32[]{:S(2)}) %collective-permute-start.15) | collective-permute-done | bytes 98336 | tf_op jit(solution)/shard_map/ppermute | solution.py:374
  57.6 0.3 collective-permute-start.16
  57.9 6.3 %collective-permute-done.16.c3 = s16[64,768]{1,0:T(8,128)(2,1)S(1)} collective-permute-done((s16[64,768]{1,0:T(8,128)(2,1)}, s16[64,768]{1,0:T(8,128)(2,1)S(1)}, u32[]{:S(2)}, u32[]{:S(2)}) %collective-permute-start.16) | collective-permute-done | bytes 98336 | tf_op jit(solution)/shard_map/ppermute | solution.py:374
  64.3 0.6 copy-done.24
  64.9 2.5 %last_step.3 = bf16[96,768]{1,0:T(8,128)(2,1)} custom-call(s32[2]{0:T(128)} %pad_add_fusion.where_ref, f32[48,768]{1,0:T(8,128)} %get-tuple-element.48.own, s16[64,768]{1,0:T(8,128)(2,1)} %copy-done.22, s16[64,768]{1,0:T(8,128)(2,1)} %copy-done.23, s16[64,768]{1,0:T(8,128)(2,1)} %copy-done.24), custom_call_target="tpu_custom_call" | custom-call | flops 294912 | bytes 516096 | tf_op jit(solution)/shard_map/last_step/pallas_call | solution.py:286
  67.4 0.5 collective-permute-start.17
  67.9 0.1 copy-done.19
  68.0 0.3 copy-done.7
  68.3 0.4 copy-done.8
  68.8 0.1 copy-done.20
  68.9 6.5 %branch.1 = (f32[512,768]{1,0:T(8,128)}, f32[512,128]{1,0:T(8,128)}) custom-call(s32[2]{0:T(128)} %pad_add_fusion.where_ref, bf16[256,1536]{1,0:T(8,128)(2,1)} %attention.1.mixed_own, bf16[256,1536]{1,0:T(8,128)(2,1)} %copy-done.7, bf16[256,1536]{1,0:T(8,128)(2,1)} %bitcast.12, bf16[256,1536]{1,0:T(8,128)(2,1)} %bitcast.13, bf16[2,256,768]{2,1,0:T(8,128)(2,1)} %copy-done.8, ...), custom_call_target="tpu_custom_call" | custom-call | flops 1207959552 | bytes 7077888 | tf_op jit(solution)/shard_map/branch/pallas_call | solution.py:162
  75.3 0.2 collective-permute-start.10
  75.6 0.7 pad_maximum_fusion.3.weights
  76.3 0.7 pad_maximum_fusion.2.grams
  77.1 0.7 copy-done.3
  77.9 4.6 %targets.3 = (f32[256,384]{1,0:T(8,128)}, f32[256,384]{1,0:T(8,128)}, s16[400,384]{1,0:T(8,128)(2,1)}, f32[384,384]{1,0:T(8,128)}) custom-call(s32[2]{0:T(128)} %pad_add_fusion.where_ref, f32[512,768]{1,0:T(8,128)} %get-tuple-element.40.blend, f32[512,128]{1,0:T(8,128)} %get-tuple-element.41.stats, f32[512,128]{1,0:T(8,128)} %copy-done.6, ...), custom_call_target="tpu_custom_call" | custom-call | flops 301989888 | bytes 3342336 | tf_op jit(solution)/shard_map/targets/pallas_call | solution.py:332
  82.6 0.3 collective-permute-start.20
  82.9 4.8 %targets.2 = (f32[256,384]{1,0:T(8,128)}, f32[256,384]{1,0:T(8,128)}, s16[400,384]{1,0:T(8,128)(2,1)}, f32[384,384]{1,0:T(8,128)}) custom-call(s32[2]{0:T(128)} %pad_add_fusion.where_ref, f32[512,768]{1,0:T(8,128)} %get-tuple-element.40.blend, f32[512,128]{1,0:T(8,128)} %get-tuple-element.41.stats, f32[512,128]{1,0:T(8,128)} %copy-done.6, ...), custom_call_target="tpu_custom_call" | custom-call | flops 301989888 | bytes 3342336 | tf_op jit(solution)/shard_map/targets/pallas_call | solution.py:332
  87.7 0.2 collective-permute-start.19
  87.9 1.5 %collective-permute-start.21 = (s16[400,384]{1,0:T(8,128)(2,1)}, s16[400,384]{1,0:T(8,128)(2,1)S(1)}, u32[]{:S(2)}, u32[]{:S(2)}) collective-permute-start(s16[400,384]{1,0:T(8,128)(2,1)} %get-tuple-element.58), channel_id=1, source_target_pairs={{0,2},{1,3},{2,0},{3,1},{4,6},{5,7},{6,4},{7,5},{8,10},{9,11},{10,... | collective-permute-start | bytes 921608 | tf_op jit(solution)/shard_map/ppermute | solution.py:374
  89.4 0.5 collective-permute-start.25
  89.9 8.3 %collective-permute-done.21.codes = s16[400,384]{1,0:T(8,128)(2,1)S(1)} collective-permute-done((s16[400,384]{1,0:T(8,128)(2,1)}, s16[400,384]{1,0:T(8,128)(2,1)S(1)}, u32[]{:S(2)}, u32[]{:S(2)}) %collective-permute-start.21) | collective-permute-done | bytes 307232 | tf_op jit(solution)/shard_map/ppermute | solution.py:374
  98.2 0.7 copy-done.13
  98.9 2.7 %second_step.4 = (f32[96,384]{1,0:T(8,128)}, s16[112,384]{1,0:T(8,128)(2,1)}, s16[112,384]{1,0:T(8,128)(2,1)}, s16[112,384]{1,0:T(8,128)(2,1)}) custom-call(s32[2]{0:T(128)} %pad_add_fusion.where_ref, f32[384,384]{1,0:T(8,128)} %get-tuple-element.57.keep, s16[400,384]{1,0:T(8,128)(2,1)} %copy-done.13), custom_call_target="tpu_custom_call" | custom-call | flops 147456 | bytes 1327104 | tf_op jit(solution)/shard_map/second_step/pallas_call | solution.py:251
  101.7 1.0 collective-permute-start.23
  102.6 3.4 %collective-permute-start.24 = (s16[112,384]{1,0:T(8,128)(2,1)}, s16[112,384]{1,0:T(8,128)(2,1)S(1)}, u32[]{:S(2)}, u32[]{:S(2)}) collective-permute-start(s16[112,384]{1,0:T(8,128)(2,1)} %get-tuple-element.62), channel_id=1, source_target_pairs={{0,12},{1,13},{2,14},{3,15},{4,8},{5,9},{6,10},{7,11},{8,4},{9,5},... | collective-permute-start | bytes 258056 | tf_op jit(solution)/shard_map/ppermute | solution.py:374
  106.1 2.5 %maximum_select_fusion = f32[1,256,1536]{2,1,0:T(8,128)} fusion(f32[1,256,384]{2,1,0:T(8,128)S(1)} %bitcast.15, f32[1,256,384]{2,1,0:T(8,128)S(1)} %bitcast.17, f32[1,256,384]{2,1,0:T(8,128)S(1)} %bitcast.14, f32[1,256,384]{2,1,0:T(8,128)} %bitcast.16, pred[]{:T(512)S(6)} %eq.6), kind=kLoop, calls=%fused_computation | loop fusion | flops 2752512 | bytes 3145729 | tf_op jit(solution)/shard_map/jit(_where)/select_n | solution.py:383
  108.6 0.7 copy-done.12
  109.3 2.7 %second_step.5 = (f32[96,384]{1,0:T(8,128)}, s16[112,384]{1,0:T(8,128)(2,1)}, s16[112,384]{1,0:T(8,128)(2,1)}, s16[112,384]{1,0:T(8,128)(2,1)}) custom-call(s32[2]{0:T(128)} %pad_add_fusion.where_ref, f32[384,384]{1,0:T(8,128)} %get-tuple-element.64.keep, s16[400,384]{1,0:T(8,128)(2,1)} %copy-done.12), custom_call_target="tpu_custom_call" | custom-call | flops 147456 | bytes 1327104 | tf_op jit(solution)/shard_map/second_step/pallas_call | solution.py:251
  112.0 1.0 collective-permute-start.27
  113.0 3.4 %collective-permute-start.28 = (s16[112,384]{1,0:T(8,128)(2,1)}, s16[112,384]{1,0:T(8,128)(2,1)S(1)}, u32[]{:S(2)}, u32[]{:S(2)}) collective-permute-start(s16[112,384]{1,0:T(8,128)(2,1)} %get-tuple-element.70), channel_id=1, source_target_pairs={{0,12},{1,13},{2,14},{3,15},{4,8},{5,9},{6,10},{7,11},{8,4},{9,5},... | collective-permute-start | bytes 258056 | tf_op jit(solution)/shard_map/ppermute | solution.py:374
  116.4 0.6 copy-done.26
  117.1 2.4 %last_step.4 = (f32[48,384]{1,0:T(8,128)}, f32[48,384]{1,0:T(8,128)}) custom-call(s32[2]{0:T(128)} %pad_add_fusion.where_ref, f32[96,384]{1,0:T(8,128)} %get-tuple-element.59.own, s16[112,384]{1,0:T(8,128)(2,1)} %copy-done.25, s16[112,384]{1,0:T(8,128)(2,1)} %copy-done.26, s16[112,384]{1,0:T(8,128)(2,1)} %copy-done.27), custom_call_target="tpu_custom_call" | custom-call | flops 294912 | bytes 516096 | tf_op jit(solution)/shard_map/last_step/pallas_call | solution.py:286
  119.5 0.6 collective-permute-done.27.c2
  120.2 0.6 copy-done.29
  120.8 2.5 %last_step.5 = (f32[48,384]{1,0:T(8,128)}, f32[48,384]{1,0:T(8,128)}) custom-call(s32[2]{0:T(128)} %pad_add_fusion.where_ref, f32[96,384]{1,0:T(8,128)} %get-tuple-element.67.own, s16[112,384]{1,0:T(8,128)(2,1)} %copy-done.28, s16[112,384]{1,0:T(8,128)(2,1)} %copy-done.29, s16[112,384]{1,0:T(8,128)(2,1)} %copy-done.30), custom_call_target="tpu_custom_call" | custom-call | flops 294912 | bytes 516096 | tf_op jit(solution)/shard_map/last_step/pallas_call | solution.py:286
  123.3 1.5 %collective-permute-done.30 = f32[48,384]{1,0:T(8,128)S(1)} collective-permute-done((f32[48,384]{1,0:T(8,128)}, f32[48,384]{1,0:T(8,128)S(1)}, u32[]{:S(2)}, u32[]{:S(2)}) %collective-permute-start.30) | collective-permute-done | bytes 73760 | tf_op jit(solution)/shard_map/ppermute | solution.py:374
  124.7 1.7 %maximum_select_fusion.1 = f32[48,1536]{1,0:T(8,128)} fusion(f32[48,384]{1,0:T(8,128)S(1)} %collective-permute-done.30, f32[48,384]{1,0:T(8,128)S(1)} %collective-permute-done.29, f32[48,384]{1,0:T(8,128)} %get-tuple-element.71, f32[48,384]{1,0:T(8,128)} %get-tuple-element.63, pred[]{:T(512)S(6)} %eq.6), kind=kLoop, calls=%fused_computation.5 | loop fusion | flops 516096 | bytes 589825 | tf_op jit(solution)/shard_map/jit(_where)/select_n | solution.py:383
  (85 shorter events, 0.5 us)
Async XLA Ops:
  1.7 1.5 %collective-permute-start = (bf16[96,768]{1,0:T(8,128)(2,1)S(1)}, bf16[96,768]{1,0:T(8,128)(2,1)S(1)}, u32[]{:S(2)}, u32[]{:S(2)}) collective-permute-start(bf16[96,768]{1,0:T(8,128)(2,1)S(1)} %get-tuple-element.75), channel_id=1, source_target_pairs={{0,1},{1,0},{2,3},{3,2},{4,5},{5,4},{6,7},{7,6},{8,9},{9,8},{10,11... | collective-permute-start | bytes 442376 | tf_op jit(solution)/shard_map/ppermute | solution.py:374
  3.2 26.0 %copy-start.4 = (bf16[192,768]{1,0:T(8,128)(2,1)}, bf16[192,768]{1,0:T(8,128)(2,1)S(1)}, u32[]{:S(2)}) copy-start(bf16[192,768]{1,0:T(8,128)(2,1)S(1)} %pad_maximum_fusion.1.rest_0_) | copy-start | bytes 884740
  3.2 8.0 %copy-start.1 = (bf16[1,256,1536]{2,1,0:T(8,128)(2,1)S(1)}, bf16[1,256,1536]{2,1,0:T(8,128)(2,1)}, u32[]{:S(2)}) copy-start(bf16[1,256,1536]{2,1,0:T(8,128)(2,1)} %param.13) | copy-start | bytes 2359300
  10.9 11.9 %collective-permute-start.12 = (f32[384,768]{1,0:T(8,128)}, f32[384,768]{1,0:T(8,128)S(1)}, u32[]{:S(2)}, u32[]{:S(2)}) collective-permute-start(f32[384,768]{1,0:T(8,128)} %get-tuple-element.45), channel_id=1, source_target_pairs={{0,1},{1,0},{2,3},{3,2},{4,5},{5,4},{6,7},{7,6},{8,9},{9,8},{10,11... | collective-permute-start | bytes 3538952 | tf_op jit(solution)/shard_map/ppermute | solution.py:374
  11.3 17.9 %collective-permute-start.4 = (bf16[192,768]{1,0:T(8,128)(2,1)S(1)}, bf16[192,768]{1,0:T(8,128)(2,1)S(1)}, u32[]{:S(2)}, u32[]{:S(2)}) collective-permute-start(bf16[192,768]{1,0:T(8,128)(2,1)S(1)} %pad_maximum_fusion.1.rest_0_), channel_id=1, source_target_pairs={{0,4},{1,5},{2,6},{3,7},{4,0},{5,1},{6,2},{7,3},{8,12},{9,13},{10,... | collective-permute-start | bytes 884744 | tf_op jit(solution)/shard_map/ppermute | solution.py:374
  14.1 16.3 %collective-permute-start.6 = (bf16[192,768]{1,0:T(8,128)(2,1)S(1)}, bf16[192,768]{1,0:T(8,128)(2,1)S(1)}, u32[]{:S(2)}, u32[]{:S(2)}) collective-permute-start(bf16[192,768]{1,0:T(8,128)(2,1)S(1)} %pad_maximum_fusion.1.rest_0_), channel_id=1, source_target_pairs={{0,8},{1,9},{2,10},{3,11},{4,12},{5,13},{6,14},{7,15},{8,0},{9,1},... | collective-permute-start | bytes 884744 | tf_op jit(solution)/shard_map/ppermute | solution.py:374
  16.7 6.1 %copy-start = (bf16[1,256,1536]{2,1,0:T(8,128)(2,1)S(1)}, bf16[1,256,1536]{2,1,0:T(8,128)(2,1)}, u32[]{:S(2)}) copy-start(bf16[1,256,1536]{2,1,0:T(8,128)(2,1)} %param.12) | copy-start | bytes 2359300
  22.7 44.6 %collective-permute-start.1 = (bf16[256,1536]{1,0:T(8,128)(2,1)}, bf16[256,1536]{1,0:T(8,128)(2,1)S(1)}, u32[]{:S(2)}, u32[]{:S(2)}) collective-permute-start(bf16[256,1536]{1,0:T(8,128)(2,1)} %attention.1.mixed_own), channel_id=1, source_target_pairs={{0,1},{1,0},{2,3},{3,2},{4,5},{5,4},{6,7},{7,6},{8,9},{9,8},{10,11... | collective-permute-start | bytes 2359304 | tf_op jit(solution)/shard_map/ppermute | solution.py:374
  22.8 1.0 copy-start.5
  27.3 37.0 %copy-start.2 = (bf16[256,768]{1,0:T(8,128)(2,1)S(1)}, bf16[256,768]{1,0:T(8,128)(2,1)}, u32[]{:S(2)}) copy-start(bf16[256,768]{1,0:T(8,128)(2,1)} %get-tuple-element.43.sum_own) | copy-start | bytes 1179652
  27.3 37.0 %copy-start.21 = (bf16[48,1536]{1,0:T(8,128)(2,1)S(1)}, bf16[48,1536]{1,0:T(8,128)(2,1)}, u32[]{:S(2)}) copy-start(bf16[48,1536]{1,0:T(8,128)(2,1)} %param.15) | copy-start | bytes 442372
  27.3 10.5 %collective-permute-start.13 = (s16[208,768]{1,0:T(8,128)(2,1)}, s16[208,768]{1,0:T(8,128)(2,1)S(1)}, u32[]{:S(2)}, u32[]{:S(2)}) collective-permute-start(s16[208,768]{1,0:T(8,128)(2,1)} %get-tuple-element.47), channel_id=1, source_target_pairs={{0,2},{1,3},{2,0},{3,1},{4,6},{5,7},{6,4},{7,5},{8,10},{9,11},{10,... | collective-permute-start | bytes 958472 | tf_op jit(solution)/shard_map/ppermute | solution.py:374
  28.9 39.0 %collective-permute-start.2 = (bf16[2,256,768]{2,1,0:T(8,128)(2,1)S(1)}, bf16[2,256,768]{2,1,0:T(8,128)(2,1)S(1)}, u32[]{:S(2)}, u32[]{:S(2)}) collective-permute-start(bf16[2,256,768]{2,1,0:T(8,128)(2,1)S(1)} %pad_maximum_fusion), channel_id=1, source_target_pairs={{0,1},{1,0},{2,3},{3,2},{4,5},{5,4},{6,7},{7,6},{8,9},{9,8},{10,11... | collective-permute-start | bytes 2359304 | tf_op jit(solution)/shard_map/ppermute | solution.py:374
  29.2 38.7 %copy-start.14 = (bf16[192,768]{1,0:T(8,128)(2,1)}, bf16[192,768]{1,0:T(8,128)(2,1)S(1)}, u32[]{:S(2)}) copy-start(bf16[192,768]{1,0:T(8,128)(2,1)S(1)} %collective-permute-done.4.rest_2_) | copy-start | bytes 884740
  29.2 15.0 %collective-permute-start.3 = (bf16[192,768]{1,0:T(8,128)(2,1)S(1)}, bf16[192,768]{1,0:T(8,128)(2,1)S(1)}, u32[]{:S(2)}, u32[]{:S(2)}) collective-permute-start(bf16[192,768]{1,0:T(8,128)(2,1)S(1)} %pad_maximum_fusion.1.rest_0_), channel_id=1, source_target_pairs={{0,2},{1,3},{2,0},{3,1},{4,6},{5,7},{6,4},{7,5},{8,10},{9,11},{10,... | collective-permute-start | bytes 884744 | tf_op jit(solution)/shard_map/ppermute | solution.py:374
  30.3 37.6 %copy-start.15 = (bf16[192,768]{1,0:T(8,128)(2,1)}, bf16[192,768]{1,0:T(8,128)(2,1)S(1)}, u32[]{:S(2)}) copy-start(bf16[192,768]{1,0:T(8,128)(2,1)S(1)} %collective-permute-done.6.rest_4_) | copy-start | bytes 884740
  30.3 19.8 %collective-permute-start.5 = (bf16[192,768]{1,0:T(8,128)(2,1)S(1)}, bf16[192,768]{1,0:T(8,128)(2,1)S(1)}, u32[]{:S(2)}, u32[]{:S(2)}) collective-permute-start(bf16[192,768]{1,0:T(8,128)(2,1)S(1)} %collective-permute-done.4.rest_2_), channel_id=1, source_target_pairs={{0,2},{1,3},{2,0},{3,1},{4,6},{5,7},{6,4},{7,5},{8,10},{9,11},{10,... | collective-permute-start | bytes 884744 | tf_op jit(solution)/shard_map/ppermute | solution.py:374
  37.8 0.7 copy-start.11
  37.8 12.6 %collective-permute-start.8 = (bf16[192,768]{1,0:T(8,128)(2,1)S(1)}, bf16[192,768]{1,0:T(8,128)(2,1)S(1)}, u32[]{:S(2)}, u32[]{:S(2)}) collective-permute-start(bf16[192,768]{1,0:T(8,128)(2,1)S(1)} %collective-permute-done.6.rest_4_), channel_id=1, source_target_pairs={{0,4},{1,5},{2,6},{3,7},{4,0},{5,1},{6,2},{7,3},{8,12},{9,13},{10,... | collective-permute-start | bytes 884744 | tf_op jit(solution)/shard_map/ppermute | solution.py:374
  44.2 23.7 %copy-start.16 = (bf16[192,768]{1,0:T(8,128)(2,1)}, bf16[192,768]{1,0:T(8,128)(2,1)S(1)}, u32[]{:S(2)}) copy-start(bf16[192,768]{1,0:T(8,128)(2,1)S(1)} %collective-permute-done.3.rest_1_) | copy-start | bytes 884740
  44.2 7.8 %collective-permute-start.14 = (s16[64,768]{1,0:T(8,128)(2,1)}, s16[64,768]{1,0:T(8,128)(2,1)S(1)}, u32[]{:S(2)}, u32[]{:S(2)}) collective-permute-start(s16[64,768]{1,0:T(8,128)(2,1)} %get-tuple-element.49), channel_id=1, source_target_pairs={{0,4},{1,5},{2,6},{3,7},{4,0},{5,1},{6,2},{7,3},{8,12},{9,13},{10,... | collective-permute-start | bytes 294920 | tf_op jit(solution)/shard_map/ppermute | solution.py:374
  50.1 17.8 %copy-start.17 = (bf16[192,768]{1,0:T(8,128)(2,1)}, bf16[192,768]{1,0:T(8,128)(2,1)S(1)}, u32[]{:S(2)}) copy-start(bf16[192,768]{1,0:T(8,128)(2,1)S(1)} %collective-permute-done.5.rest_3_) | copy-start | bytes 884740
  50.1 7.5 %collective-permute-start.15 = (s16[64,768]{1,0:T(8,128)(2,1)}, s16[64,768]{1,0:T(8,128)(2,1)S(1)}, u32[]{:S(2)}, u32[]{:S(2)}) collective-permute-start(s16[64,768]{1,0:T(8,128)(2,1)} %get-tuple-element.50), channel_id=1, source_target_pairs={{0,8},{1,9},{2,10},{3,11},{4,12},{5,13},{6,14},{7,15},{8,0},{9,1},... | collective-permute-start | bytes 294920 | tf_op jit(solution)/shard_map/ppermute | solution.py:374
  50.4 17.5 %copy-start.18 = (bf16[192,768]{1,0:T(8,128)(2,1)}, bf16[192,768]{1,0:T(8,128)(2,1)S(1)}, u32[]{:S(2)}) copy-start(bf16[192,768]{1,0:T(8,128)(2,1)S(1)} %collective-permute-done.8.rest_6_) | copy-start | bytes 884740
  50.4 16.9 %collective-permute-start.7 = (bf16[192,768]{1,0:T(8,128)(2,1)S(1)}, bf16[192,768]{1,0:T(8,128)(2,1)S(1)}, u32[]{:S(2)}, u32[]{:S(2)}) collective-permute-start(bf16[192,768]{1,0:T(8,128)(2,1)S(1)} %collective-permute-done.6.rest_4_), channel_id=1, source_target_pairs={{0,2},{1,3},{2,0},{3,1},{4,6},{5,7},{6,4},{7,5},{8,10},{9,11},{10,... | collective-permute-start | bytes 884744 | tf_op jit(solution)/shard_map/ppermute | solution.py:374
  52.0 12.4 %copy-start.22 = (s16[64,768]{1,0:T(8,128)(2,1)}, s16[64,768]{1,0:T(8,128)(2,1)S(1)}, u32[]{:S(2)}) copy-start(s16[64,768]{1,0:T(8,128)(2,1)S(1)} %collective-permute-done.14.c1) | copy-start | bytes 294916
  52.0 15.9 %collective-permute-start.9 = (bf16[192,768]{1,0:T(8,128)(2,1)S(1)}, bf16[192,768]{1,0:T(8,128)(2,1)S(1)}, u32[]{:S(2)}, u32[]{:S(2)}) collective-permute-start(bf16[192,768]{1,0:T(8,128)(2,1)S(1)} %collective-permute-done.8.rest_6_), channel_id=1, source_target_pairs={{0,2},{1,3},{2,0},{3,1},{4,6},{5,7},{6,4},{7,5},{8,10},{9,11},{10,... | collective-permute-start | bytes 884744 | tf_op jit(solution)/shard_map/ppermute | solution.py:374
  57.6 6.7 %copy-start.23 = (s16[64,768]{1,0:T(8,128)(2,1)}, s16[64,768]{1,0:T(8,128)(2,1)S(1)}, u32[]{:S(2)}) copy-start(s16[64,768]{1,0:T(8,128)(2,1)S(1)} %collective-permute-done.15.c2) | copy-start | bytes 294916
  57.6 6.6 %collective-permute-start.16 = (s16[64,768]{1,0:T(8,128)(2,1)}, s16[64,768]{1,0:T(8,128)(2,1)S(1)}, u32[]{:S(2)}, u32[]{:S(2)}) collective-permute-start(s16[64,768]{1,0:T(8,128)(2,1)} %get-tuple-element.51), channel_id=1, source_target_pairs={{0,12},{1,13},{2,14},{3,15},{4,8},{5,9},{6,10},{7,11},{8,4},{9,5},... | collective-permute-start | bytes 294920 | tf_op jit(solution)/shard_map/ppermute | solution.py:374
  64.3 0.6 copy-start.24
  64.3 12.8 %collective-permute-start.11 = (bf16[256,768]{1,0:T(8,128)(2,1)S(1)}, bf16[256,768]{1,0:T(8,128)(2,1)S(1)}, u32[]{:S(2)}, u32[]{:S(2)}) collective-permute-start(bf16[256,768]{1,0:T(8,128)(2,1)S(1)} %copy-done.2), channel_id=1, source_target_pairs={{0,1},{1,0},{2,3},{3,2},{4,5},{5,4},{6,7},{7,6},{8,9},{9,8},{10,11... | collective-permute-start | bytes 1179656 | tf_op jit(solution)/shard_map/ppermute | solution.py:374
  67.3 0.7 copy-start.19
  67.3 8.2 %collective-permute-start.18 = (bf16[48,768]{1,0:T(8,128)(2,1)S(1)}, bf16[48,768]{1,0:T(8,128)(2,1)S(1)}, u32[]{:S(2)}, u32[]{:S(2)}) collective-permute-start(bf16[48,768]{1,0:T(8,128)(2,1)S(1)} %get-tuple-element.77), channel_id=1, source_target_pairs={{0,1},{1,0},{2,3},{3,2},{4,5},{5,4},{6,7},{7,6},{8,9},{9,8},{10,11... | collective-permute-start | bytes 221192 | tf_op jit(solution)/shard_map/ppermute | solution.py:374
  67.4 1.0 copy-start.7
  67.4 9.0 %collective-permute-start.17 = (bf16[96,768]{1,0:T(8,128)(2,1)}, bf16[96,768]{1,0:T(8,128)(2,1)S(1)}, u32[]{:S(2)}, u32[]{:S(2)}) collective-permute-start(bf16[96,768]{1,0:T(8,128)(2,1)} %last_step.3), channel_id=1, source_target_pairs={{0,1},{1,0},{2,3},{3,2},{4,5},{5,4},{6,7},{7,6},{8,9},{9,8},{10,11... | collective-permute-start | bytes 442376 | tf_op jit(solution)/shard_map/ppermute | solution.py:374
  67.9 0.9 copy-start.8
  67.9 1.0 copy-start.20
  68.9 7.5 %copy-start.9 = (bf16[96,768]{1,0:T(8,128)(2,1)S(1)}, bf16[96,768]{1,0:T(8,128)(2,1)}, u32[]{:S(2)}) copy-start(bf16[96,768]{1,0:T(8,128)(2,1)} %last_step.3) | copy-start | bytes 442372
  75.3 1.7 %collective-permute-start.10 = (f32[512,128]{1,0:T(8,128)}, f32[512,128]{1,0:T(8,128)S(1)}, u32[]{:S(2)}, u32[]{:S(2)}) collective-permute-start(f32[512,128]{1,0:T(8,128)} %get-tuple-element.41.stats), channel_id=1, source_target_pairs={{0,1},{1,0},{2,3},{3,2},{4,5},{5,4},{6,7},{7,6},{8,9},{9,8},{10,11... | collective-permute-start | bytes 786440 | tf_op jit(solution)/shard_map/ppermute | solution.py:374
  77.1 0.8 copy-start.3
  77.1 0.8 copy-start.6
  82.6 6.9 %copy-start.31 = (s16[400,384]{1,0:T(8,128)(2,1)S(1)}, s16[400,384]{1,0:T(8,128)(2,1)}, u32[]{:S(2)}) copy-start(s16[400,384]{1,0:T(8,128)(2,1)} %get-tuple-element.65) | copy-start | bytes 921604
  82.6 23.5 %copy-start.10 = (f32[256,384]{1,0:T(8,128)S(1)}, f32[256,384]{1,0:T(8,128)}, u32[]{:S(2)}) copy-start(f32[256,384]{1,0:T(8,128)} %get-tuple-element.54) | copy-start | bytes 1179652
  82.6 20.1 %collective-permute-start.20 = (f32[256,384]{1,0:T(8,128)}, f32[256,384]{1,0:T(8,128)S(1)}, u32[]{:S(2)}, u32[]{:S(2)}) collective-permute-start(f32[256,384]{1,0:T(8,128)} %get-tuple-element.56), channel_id=1, source_target_pairs={{0,1},{1,0},{2,3},{3,2},{4,5},{5,4},{6,7},{7,6},{8,9},{9,8},{10,11... | collective-permute-start | bytes 1179656 | tf_op jit(solution)/shard_map/ppermute | solution.py:374
  87.7 18.4 %collective-permute-start.19 = (f32[256,384]{1,0:T(8,128)}, f32[256,384]{1,0:T(8,128)S(1)}, u32[]{:S(2)}, u32[]{:S(2)}) collective-permute-start(f32[256,384]{1,0:T(8,128)} %get-tuple-element.55), channel_id=1, source_target_pairs={{0,1},{1,0},{2,3},{3,2},{4,5},{5,4},{6,7},{7,6},{8,9},{9,8},{10,11... | collective-permute-start | bytes 1179656 | tf_op jit(solution)/shard_map/ppermute | solution.py:374
  87.9 10.3 %collective-permute-start.21 = (s16[400,384]{1,0:T(8,128)(2,1)}, s16[400,384]{1,0:T(8,128)(2,1)S(1)}, u32[]{:S(2)}, u32[]{:S(2)}) collective-permute-start(s16[400,384]{1,0:T(8,128)(2,1)} %get-tuple-element.58), channel_id=1, source_target_pairs={{0,2},{1,3},{2,0},{3,1},{4,6},{5,7},{6,4},{7,5},{8,10},{9,11},{10,... | collective-permute-start | bytes 921608 | tf_op jit(solution)/shard_map/ppermute | solution.py:374
  89.4 19.1 %collective-permute-start.25 = (s16[400,384]{1,0:T(8,128)(2,1)S(1)}, s16[400,384]{1,0:T(8,128)(2,1)S(1)}, u32[]{:S(2)}, u32[]{:S(2)}) collective-permute-start(s16[400,384]{1,0:T(8,128)(2,1)S(1)} %copy-done.31), channel_id=1, source_target_pairs={{0,2},{1,3},{2,0},{3,1},{4,6},{5,7},{6,4},{7,5},{8,10},{9,11},{10,... | collective-permute-start | bytes 921608 | tf_op jit(solution)/shard_map/ppermute | solution.py:374
  98.2 0.7 copy-start.13
  101.7 11.3 %collective-permute-start.22 = (s16[112,384]{1,0:T(8,128)(2,1)}, s16[112,384]{1,0:T(8,128)(2,1)S(1)}, u32[]{:S(2)}, u32[]{:S(2)}) collective-permute-start(s16[112,384]{1,0:T(8,128)(2,1)} %get-tuple-element.60), channel_id=1, source_target_pairs={{0,4},{1,5},{2,6},{3,7},{4,0},{5,1},{6,2},{7,3},{8,12},{9,13},{10,... | collective-permute-start | bytes 258056 | tf_op jit(solution)/shard_map/ppermute | solution.py:374
  101.7 14.7 %collective-permute-start.23 = (s16[112,384]{1,0:T(8,128)(2,1)}, s16[112,384]{1,0:T(8,128)(2,1)S(1)}, u32[]{:S(2)}, u32[]{:S(2)}) collective-permute-start(s16[112,384]{1,0:T(8,128)(2,1)} %get-tuple-element.61), channel_id=1, source_target_pairs={{0,8},{1,9},{2,10},{3,11},{4,12},{5,13},{6,14},{7,15},{8,0},{9,1},... | collective-permute-start | bytes 258056 | tf_op jit(solution)/shard_map/ppermute | solution.py:374
  102.6 13.8 %collective-permute-start.24 = (s16[112,384]{1,0:T(8,128)(2,1)}, s16[112,384]{1,0:T(8,128)(2,1)S(1)}, u32[]{:S(2)}, u32[]{:S(2)}) collective-permute-start(s16[112,384]{1,0:T(8,128)(2,1)} %get-tuple-element.62), channel_id=1, source_target_pairs={{0,12},{1,13},{2,14},{3,15},{4,8},{5,9},{6,10},{7,11},{8,4},{9,5},... | collective-permute-start | bytes 258056 | tf_op jit(solution)/shard_map/ppermute | solution.py:374
  108.6 0.7 copy-start.12
  112.0 7.5 %collective-permute-start.26 = (s16[112,384]{1,0:T(8,128)(2,1)}, s16[112,384]{1,0:T(8,128)(2,1)S(1)}, u32[]{:S(2)}, u32[]{:S(2)}) collective-permute-start(s16[112,384]{1,0:T(8,128)(2,1)} %get-tuple-element.68), channel_id=1, source_target_pairs={{0,4},{1,5},{2,6},{3,7},{4,0},{5,1},{6,2},{7,3},{8,12},{9,13},{10,... | collective-permute-start | bytes 258056 | tf_op jit(solution)/shard_map/ppermute | solution.py:374
  112.0 8.1 %collective-permute-start.27 = (s16[112,384]{1,0:T(8,128)(2,1)}, s16[112,384]{1,0:T(8,128)(2,1)S(1)}, u32[]{:S(2)}, u32[]{:S(2)}) collective-permute-start(s16[112,384]{1,0:T(8,128)(2,1)} %get-tuple-element.69), channel_id=1, source_target_pairs={{0,8},{1,9},{2,10},{3,11},{4,12},{5,13},{6,14},{7,15},{8,0},{9,1},... | collective-permute-start | bytes 258056 | tf_op jit(solution)/shard_map/ppermute | solution.py:374
  113.0 3.5 %copy-start.25 = (s16[112,384]{1,0:T(8,128)(2,1)}, s16[112,384]{1,0:T(8,128)(2,1)S(1)}, u32[]{:S(2)}) copy-start(s16[112,384]{1,0:T(8,128)(2,1)S(1)} %collective-permute-done.22.c1) | copy-start | bytes 258052
  113.0 7.2 %collective-permute-start.28 = (s16[112,384]{1,0:T(8,128)(2,1)}, s16[112,384]{1,0:T(8,128)(2,1)S(1)}, u32[]{:S(2)}, u32[]{:S(2)}) collective-permute-start(s16[112,384]{1,0:T(8,128)(2,1)} %get-tuple-element.70), channel_id=1, source_target_pairs={{0,12},{1,13},{2,14},{3,15},{4,8},{5,9},{6,10},{7,11},{8,4},{9,5},... | collective-permute-start | bytes 258056 | tf_op jit(solution)/shard_map/ppermute | solution.py:374
  116.4 0.7 copy-start.26
  116.4 0.7 copy-start.27
  119.5 3.8 %collective-permute-start.29 = (f32[48,384]{1,0:T(8,128)}, f32[48,384]{1,0:T(8,128)S(1)}, u32[]{:S(2)}, u32[]{:S(2)}) collective-permute-start(f32[48,384]{1,0:T(8,128)} %get-tuple-element.72), channel_id=1, source_target_pairs={{0,1},{1,0},{2,3},{3,2},{4,5},{5,4},{6,7},{7,6},{8,9},{9,8},{10,11... | collective-permute-start | bytes 221192 | tf_op jit(solution)/shard_map/ppermute | solution.py:374
  119.5 0.6 copy-start.28
  120.1 0.6 copy-start.29
  120.2 0.6 copy-start.30
  123.3 1.5 %collective-permute-start.30 = (f32[48,384]{1,0:T(8,128)}, f32[48,384]{1,0:T(8,128)S(1)}, u32[]{:S(2)}, u32[]{:S(2)}) collective-permute-start(f32[48,384]{1,0:T(8,128)} %get-tuple-element.73), channel_id=1, source_target_pairs={{0,1},{1,0},{2,3},{3,2},{4,5},{5,4},{6,7},{7,6},{8,9},{9,8},{10,11... | collective-permute-start | bytes 221192 | tf_op jit(solution)/shard_map/ppermute | solution.py:374

commit v3 on v2

--- a/solution.py
+++ b/solution.py
@@ -11,32 +11,38 @@
 HEADS = 24
 TOP_K = 10
 AXES = ("groups", "dp")
-VMEM = 56 * 1024 * 1024
+VMEM = 24 * 1024 * 1024
+COST = 1000
 CORE, NEXT_Y, NEXT_Z, FAR_Z = 1, 2, 4, 8
 LINE = 4
 CUTS = 2
 TAIL = 16
 
 
-def call(kernel, out_shape, *, name, grid=(1,), in_specs, out_specs, scratch=(), flops=0, nbytes=0):
-    return pl.pallas_call(
-        kernel,
-        out_shape=out_shape,
-        grid_spec=pltpu.PrefetchScalarGridSpec(
-            num_scalar_prefetch=1,
-            grid=grid,
-            in_specs=in_specs,
-            out_specs=out_specs,
+def call(kernel, out_shape, name, scratch=()):
+    held = pl.BlockSpec(memory_space=pltpu.VMEM)
+
+    def run(where, *arrays):
+        return pl.pallas_call(
+            kernel,
+            out_shape=tuple(out_shape),
+            in_specs=[pl.BlockSpec(memory_space=pltpu.SMEM)] + [held] * len(arrays),
+            out_specs=(held,) * len(out_shape),
             scratch_shapes=scratch,
-        ),
-        compiler_params=pltpu.CompilerParams(vmem_limit_bytes=VMEM),
-        cost_estimate=pl.CostEstimate(flops=flops, bytes_accessed=nbytes, transcendentals=0),
-        name=name,
-    )
-
-
-def whole(shape):
-    return pl.BlockSpec(shape, lambda i, s: (0,) * len(shape))
+            compiler_params=pltpu.CompilerParams(vmem_limit_bytes=VMEM),
+            cost_estimate=pl.CostEstimate(flops=COST, bytes_accessed=COST, transcendentals=0),
+            name=name,
+        )(where, *arrays)
+
+    return run
+
+
+def f32(*shape):
+    return jax.ShapeDtypeStruct(shape, jnp.float32)
+
+
+def bf16(*shape):
+    return jax.ShapeDtypeStruct(shape, jnp.bfloat16)
 
 
 def contract_rows(a, b):
@@ -58,16 +64,8 @@
 
 
 def attention(where, q, k, v):
-    patches, width = q.shape
-    return call(
-        functools.partial(attention_kernel, size=width // HEADS),
-        jax.ShapeDtypeStruct((patches, width), jnp.bfloat16),
-        name="attention",
-        in_specs=[whole((patches, width))] * 3,
-        out_specs=whole((patches, width)),
-        flops=4 * patches * patches * width * 4,
-        nbytes=8 * patches * width,
-    )(where, q, k, v)
+    kernel = functools.partial(attention_kernel, size=q.shape[1] // HEADS)
+    return call(kernel, [bf16(*q.shape)], "attention")(where, q, k, v)[0]
 
 
 def gram_kernel(where_ref, hidden_ref, kept_ref, *rest, parted):
@@ -99,21 +97,10 @@
 
 def gram(where, hidden, kept, parted):
     _, clones, patches, width = hidden.shape
-    grams = [(width // 2, width)] * 2 if parted else [(width, width)]
-    return call(
-        functools.partial(gram_kernel, parted=parted),
-        tuple(jax.ShapeDtypeStruct(g, jnp.float32) for g in grams)
-        + (jax.ShapeDtypeStruct((patches, width), jnp.bfloat16),),
-        name="gram",
-        in_specs=[whole(hidden.shape), whole(kept.shape)],
-        out_specs=tuple(whole(g) for g in grams) + (whole((patches, width)),),
-        scratch=[
-            pltpu.VMEM((clones * patches, width), jnp.bfloat16),
-            pltpu.VMEM((width, width), jnp.float32),
-        ],
-        flops=2 * clones * patches * width * width,
-        nbytes=2 * clones * patches * width + 4 * width * width,
-    )(where, hidden, kept)
+    grams = [f32(width // 2, width)] * 2 if parted else [f32(width, width)]
+    scratch = [pltpu.VMEM((clones * patches, width), jnp.bfloat16), pltpu.VMEM((width, width), jnp.float32)]
+    kernel = functools.partial(gram_kernel, parted=parted)
+    return call(kernel, grams + [bf16(patches, width)], "gram", scratch)(where, hidden, kept)
 
 
 def put_in_order(where_ref, pieces, full):
@@ -129,14 +116,13 @@
             full[pl.ds(at, rows), :] = piece[j * rows : (j + 1) * rows, :]
 
 
-def branch_kernel(
-    where_ref, mixed_own, mixed_other, stream_own, earlier_own, others, *rest
-):
+def branch_kernel(where_ref, mixed_own, mixed_other, stream, earlier, others, *rest):
     *pieces, blend_ref, stats_ref, full = rest
     put_in_order(where_ref, pieces, full)
-    patches, half = stream_own.shape
-    streams = (stream_own[...], others[0])
-    earliers = (earlier_own[...], others[1])
+    patches, half = stream.shape[0], blend_ref.shape[1]
+    columns = pl.ds(pl.multiple_of(where_ref[0] * half, half), half)
+    streams = (stream[:, columns], others[0])
+    earliers = (earlier[:, columns], others[1])
     for i, mixed in enumerate((mixed_own, mixed_other)):
         layer_out = streams[i].astype(jnp.float32) + jnp.dot(
             mixed[...], full[...], preferred_element_type=jnp.float32
@@ -144,8 +130,8 @@
         center = jnp.mean(layer_out, axis=0, keepdims=True)
         away = layer_out - center
         spread = jnp.mean(away * away, axis=0, keepdims=True)
-        normed = away / jnp.sqrt(spread + 1e-05)
-        blend = ((TOP_K - 1) * earliers[i].astype(jnp.float32) + normed) / TOP_K
+        normed = away * (1.0 / jnp.sqrt(spread + 1e-05))
+        blend = ((TOP_K - 1) * earliers[i].astype(jnp.float32) + normed) * (1.0 / TOP_K)
         rows = slice(i * patches, (i + 1) * patches)
         blend_ref[rows, :] = blend
         middle = jnp.mean(blend, axis=1, keepdims=True)
@@ -155,26 +141,12 @@
         stats_ref[rows, :] = jnp.where(lane < 64, middle, squares)
 
 
-def branch(where, mixed_own, mixed_other, stream, earlier, others, pieces):
+def branch(where, mixed_own, *others):
     patches, width = mixed_own.shape
     half = width // 2
-    own_half = pl.BlockSpec((patches, half), lambda i, s: (0, s[0]))
-    return call(
-        branch_kernel,
-        (
-            jax.ShapeDtypeStruct((2 * patches, half), jnp.float32),
-            jax.ShapeDtypeStruct((2 * patches, 128), jnp.float32),
-        ),
-        name="branch",
-        in_specs=[whole((patches, width))] * 2
-        + [own_half] * 2
-        + [whole((2, patches, half))]
-        + [whole(p.shape) for p in pieces],
-        out_specs=(whole((2 * patches, half)), whole((2 * patches, 128))),
-        scratch=[pltpu.VMEM((width, half), jnp.bfloat16)],
-        flops=4 * patches * width * half,
-        nbytes=12 * patches * width + 2 * width * half,
-    )(where, mixed_own, mixed_other, stream, earlier, others, *pieces)
+    shapes = [f32(2 * patches, half), f32(2 * patches, 128)]
+    scratch = [pltpu.VMEM((width, half), jnp.bfloat16)]
+    return call(branch_kernel, shapes, "branch", scratch)(where, mixed_own, *others)
 
 
 def encode(values, out_ref):
@@ -204,10 +176,7 @@
 
 
 def halved_shapes(rows, width):
-    return (
-        jax.ShapeDtypeStruct((rows // 2 + TAIL, width), jnp.int16),
-        jax.ShapeDtypeStruct((rows // 2, width), jnp.float32),
-    )
+    return [jax.ShapeDtypeStruct((rows // 2 + TAIL, width), jnp.int16), f32(rows // 2, width)]
 
 
 def first_kernel(where_ref, mine, theirs, send_ref, keep_ref, total):
@@ -216,17 +185,8 @@
 
 
 def first_step(where, mine, theirs):
-    shapes = halved_shapes(*mine.shape)
-    return call(
-        first_kernel,
-        shapes,
-        name="first_step",
-        in_specs=[whole(mine.shape)] * 2,
-        out_specs=tuple(whole(x.shape) for x in shapes),
-        scratch=[pltpu.VMEM(mine.shape, jnp.float32)],
-        flops=mine.size,
-        nbytes=11 * mine.size,
-    )(where, mine, theirs)
+    scratch = [pltpu.VMEM(mine.shape, jnp.float32)]
+    return call(first_kernel, halved_shapes(*mine.shape), "first_step", scratch)(where, mine, theirs)
 
 
 def second_kernel(where_ref, keep, codes, own_ref, *rest):
@@ -245,19 +205,9 @@
 
 def second_step(where, keep, codes):
     rows, width = keep.shape[0] // LINE, keep.shape[1]
-    shapes = (jax.ShapeDtypeStruct((rows, width), jnp.float32),) + (
-        jax.ShapeDtypeStruct((rows + TAIL, width), jnp.int16),
-    ) * (LINE - 1)
-    return call(
-        second_kernel,
-        shapes,
-        name="second_step",
-        in_specs=[whole(keep.shape), whole(codes.shape)],
-        out_specs=tuple(whole(x.shape) for x in shapes),
-        scratch=[pltpu.VMEM(keep.shape, jnp.float32)],
-        flops=keep.size,
-        nbytes=9 * keep.size,
-    )(where, keep, codes)
+    shapes = [f32(rows, width)] + [jax.ShapeDtypeStruct((rows + TAIL, width), jnp.int16)] * (LINE - 1)
+    scratch = [pltpu.VMEM(keep.shape, jnp.float32)]
+    return call(second_kernel, shapes, "second_step", scratch)(where, keep, codes)
 
 
 def last_kernel(where_ref, own, c1, c2, c3, *out_refs, scale):
@@ -279,32 +229,22 @@
 
 def last_step(where, own, codes, scale=None):
     rows, width = own.shape
-    if scale is None:
-        shapes = (jax.ShapeDtypeStruct((2 * rows, width), jnp.bfloat16),)
-    else:
-        shapes = (jax.ShapeDtypeStruct((rows // 2, width), jnp.float32),) * 2
-    return call(
-        functools.partial(last_kernel, scale=scale),
-        shapes,
-        name="last_step",
-        in_specs=[whole(own.shape)] + [whole(c.shape) for c in codes],
-        out_specs=tuple(whole(x.shape) for x in shapes),
-        flops=8 * own.size,
-        nbytes=14 * own.size,
-    )(where, own, *codes)
-
-
-def targets_kernel(where_ref, blend, stats, stats_other, sum_own, sum_other, grams, weights, own_ref, other_ref, *rest, width):
-    patches = own_ref.shape[0]
-    grad = contract_rows(grams[...], weights[...])
+    shapes = [bf16(2 * rows, width)] if scale is None else [f32(rows // 2, width)] * 2
+    return call(functools.partial(last_kernel, scale=scale), shapes, "last_step")(where, own, *codes)
+
+
+def targets_kernel(where_ref, blend, stats, stats_other, sum_own, sum_other, grams, weights, own_ref, other_ref, *rest, cut, width):
+    patches, columns = own_ref.shape
+    cols = slice(cut * columns, (cut + 1) * columns)
+    grad = contract_rows(grams[...], weights[:, cols])
     for i, (out, features) in enumerate(((own_ref, sum_own), (other_ref, sum_other))):
         mine = stats[i * patches : (i + 1) * patches, :]
         theirs = stats_other[(1 - i) * patches : (2 - i) * patches, :]
         gap = mine[:, :1] - theirs[:, :1]
         middle = 0.5 * (mine[:, :1] + theirs[:, :1])
         squares = mine[:, 64:65] + theirs[:, 64:65] + (width / 4) * gap * gap
-        root = 1.0 / jnp.sqrt(squares / width + 1e-06)
-        target = (blend[i * patches : (i + 1) * patches, :] - middle) * root
+        root = 1.0 / jnp.sqrt(squares * (1.0 / width) + 1e-06)
+        target = (blend[i * patches : (i + 1) * patches, cols] - middle) * root
         out[...] = target
         grad = grad - contract_rows(features[...], target.astype(jnp.bfloat16))
     if len(rest) == 1:
@@ -319,26 +259,13 @@
     j, n = cut
     patches, columns = blend.shape[0] // 2, blend.shape[1] // n
     dec = grams.shape[1]
-    shapes = (jax.ShapeDtypeStruct((patches, columns), jnp.float32),) * 2
-    if coded:
-        shapes += halved_shapes(dec, columns)
-    else:
-        shapes += (jax.ShapeDtypeStruct((dec, columns), jnp.float32),)
-
-    def part(x):
-        return pl.BlockSpec((x.shape[0], columns), lambda i, s: (0, j))
-
-    inputs = (blend, stats, stats_other, sum_own, sum_other, grams, weights)
-    return call(
-        functools.partial(targets_kernel, width=2 * blend.shape[1]),
-        shapes,
-        name="targets",
-        in_specs=[part(blend)] + [whole(x.shape) for x in inputs[1:-1]] + [part(weights)],
-        out_specs=tuple(whole(x.shape) for x in shapes),
-        scratch=[pltpu.VMEM((dec, columns), jnp.float32)] if coded else [],
-        flops=4 * patches * dec * columns,
-        nbytes=16 * patches * columns + 6 * dec * columns,
-    )(where, *inputs)
+    shapes = [f32(patches, columns)] * 2
+    shapes += halved_shapes(dec, columns) if coded else [f32(dec, columns)]
+    kernel = functools.partial(targets_kernel, cut=j, width=2 * blend.shape[1])
+    scratch = [pltpu.VMEM((dec, columns), jnp.float32)] if coded else []
+    return call(kernel, shapes, "targets", scratch)(
+        where, blend, stats, stats_other, sum_own, sum_other, grams, weights
+    )
 
 
 def after(x, *others):
@@ -421,7 +348,7 @@
     others = swap(others, CORE)
     sum_other = swap(sum_own, CORE)
 
-    blend, stats = branch(where, mixed_own, mixed_other, stream[0], earlier[0], others, out_pieces)
+    blend, stats = branch(where, mixed_own, mixed_other, stream[0], earlier[0], others, *out_pieces)
     stats_other = swap(stats, CORE)
 
     def term(cut, coded):

time: 127 us -> 110 us (0.87)
  Pallas kernels: 48.7 us -> 21 us
  waiting for transfers between devices: 37.2 us -> 47.5 us
  starting transfers between devices: 25.8 us -> 33.1 us
  local copies, waits for them, and re-layouts: 7.46 us -> 3.68 us
  other arithmetic: 6.4 us -> 3.7 us
    pallas_call x12, Pallas kernels: 48.7 us -> 21 us  [run(): pl.pallas_call(kernel, out_shape=tuple(out_shape), in_specs=[pl.BlockSpec...]
    ppermute x31, waiting for transfers between devices: 37.2 us -> 47.5 us  [swap(): return lax.ppermute(x, AXES, pairs)]
    ppermute x31, starting transfers between devices: 25.8 us -> 33.1 us  [swap(): return lax.ppermute(x, AXES, pairs)]
    unnamed x64 -> x16, local copies, waits for them, and re-layouts: 6.38 us -> 2.6 us
  transfers between devices with their start and end apart: 31 -> 31, of which waited for: 10 -> 13; matrix products, arithmetic and copies ran while one was open for 4% -> 3% of each run, Pallas kernels for 29% -> 13%
where the time goes in v3:
time: 110 us
  waiting for transfers between devices  47.5 us (43%)
  starting transfers between devices  33.1 us (30%)
  Pallas kernels  21 us (19%)
  other arithmetic  3.7 us (3%)
  local copies, waits for them, and re-layouts  3.68 us (3%)
    ppermute x31, waiting for transfers between devices, swap(): return lax.ppermute(x, AXES, pairs)  47.5 us
    ppermute x31, starting transfers between devices, swap(): return lax.ppermute(x, AXES, pairs)  33.1 us
    pallas_call x12, Pallas kernels, run(): pl.pallas_call(kernel, out_shape=tuple(out_shape), in_specs=[pl.BlockSpec...  21 us
    select_n x2, other arithmetic, side_by_side(): jnp.where(core == 0, jnp.concatenate(mine + theirs, axis=1), jnp.concaten...  3.49 us
    unnamed x16, local copies, waits for them, and re-layouts  2.6 us
  transfers between devices with their start and end apart: 31, of which 13 were waited for; matrix products, arithmetic and copies ran while one was open for 3% of the time, Pallas kernels for 13%

profile of v3, /device:TPU:0, one launch (start us, length us, event | category | flops | bytes accessed | tf_op | source)
XLA Modules:
  0.0 109.9 jit_solution(2385025953094236011)
XLA Ops:
  0.7 1.0 constant_dynamic-slice_fusion.5
  1.7 0.5 collective-permute-start
  2.2 0.1 pad_add_fusion.where_ref
  2.3 0.9 collective-permute-done
  3.2 0.0 copy-start
  3.2 1.9 %copy-done = bf16[1,8,256,768]{3,2,1,0:T(8,128)(2,1)S(1)} copy-done((bf16[1,8,256,768]{3,2,1,0:T(8,128)(2,1)S(1)}, bf16[1,8,256,768]{3,2,1,0:T(8,128)(2,1)}, u32[]{:S(2)}) %copy-start) | copy-done | bytes 3145752
  5.1 0.7 copy-done.6
  5.8 4.2 %gram.1 = (f32[384,768]{1,0:T(8,128)S(1)}, f32[384,768]{1,0:T(8,128)S(1)}, bf16[256,768]{1,0:T(8,128)(2,1)S(1)}) custom-call(s32[2]{0:T(128)S(1)} %pad_add_fusion.where_ref, bf16[1,8,256,768]{3,2,1,0:T(8,128)(2,1)S(1)} %copy-done, s32[8,64]{1,0:T(8,128)S(1)} %bitcast.19), custom_call_target="tpu_custom_call" | custom-call | flops 1000 | bytes 1000 | tf_op jit(solution)/shard_map/gram/pallas_call | solution.py:26
  10.0 0.4 collective-permute-start.12
  10.4 3.7 %collective-permute-start.6 = (bf16[192,768]{1,0:T(8,128)(2,1)S(1)}, bf16[192,768]{1,0:T(8,128)(2,1)S(1)}, u32[]{:S(2)}, u32[]{:S(2)}) collective-permute-start(bf16[192,768]{1,0:T(8,128)(2,1)S(1)} %pad_maximum_fusion.1.rest_0_), channel_id=1, source_target_pairs={{0,8},{1,9},{2,10},{3,11},{4,12},{5,13},{6,14},{7,15},{8,0},{9,1},... | collective-permute-start | bytes 884744 | tf_op jit(solution)/shard_map/ppermute | solution.py:301
  14.2 1.6 %collective-permute-start.3 = (bf16[192,768]{1,0:T(8,128)(2,1)S(1)}, bf16[192,768]{1,0:T(8,128)(2,1)S(1)}, u32[]{:S(2)}, u32[]{:S(2)}) collective-permute-start(bf16[192,768]{1,0:T(8,128)(2,1)S(1)} %pad_maximum_fusion.1.rest_0_), channel_id=1, source_target_pairs={{0,2},{1,3},{2,0},{3,1},{4,6},{5,7},{6,4},{7,5},{8,10},{9,11},{10,... | collective-permute-start | bytes 884744 | tf_op jit(solution)/shard_map/ppermute | solution.py:301
  15.8 1.6 %collective-permute-start.4 = (bf16[192,768]{1,0:T(8,128)(2,1)S(1)}, bf16[192,768]{1,0:T(8,128)(2,1)S(1)}, u32[]{:S(2)}, u32[]{:S(2)}) collective-permute-start(bf16[192,768]{1,0:T(8,128)(2,1)S(1)} %pad_maximum_fusion.1.rest_0_), channel_id=1, source_target_pairs={{0,4},{1,5},{2,6},{3,7},{4,0},{5,1},{6,2},{7,3},{8,12},{9,13},{10,... | collective-permute-start | bytes 884744 | tf_op jit(solution)/shard_map/ppermute | solution.py:301
  17.4 3.5 %attention.1.mixed_own = bf16[256,1536]{1,0:T(8,128)(2,1)S(1)} custom-call(s32[2]{0:T(128)S(1)} %pad_add_fusion.where_ref, bf16[256,1536]{1,0:T(8,128)(2,1)S(1)} %bitcast.14, bf16[256,1536]{1,0:T(8,128)(2,1)S(1)} %bitcast.15, bf16[256,1536]{1,0:T(8,128)(2,1)S(1)} %bitcast.16), custom_call_target="tpu_custom_call" | custom-call | flops 1000 | bytes 1000 | tf_op jit(solution)/shard_map/attention/pallas_call | solution.py:26
  20.8 0.1 collective-permute-start.1
  21.0 7.1 %collective-permute-done.6.rest_4_ = bf16[192,768]{1,0:T(8,128)(2,1)S(1)} collective-permute-done((bf16[192,768]{1,0:T(8,128)(2,1)S(1)}, bf16[192,768]{1,0:T(8,128)(2,1)S(1)}, u32[]{:S(2)}, u32[]{:S(2)}) %collective-permute-start.6) | collective-permute-done | bytes 294944 | tf_op jit(solution)/shard_map/ppermute | solution.py:301
  28.1 0.7 collective-permute-start.8
  28.8 0.1 pad_maximum_fusion
  28.9 0.0 collective-permute-done.12.theirs
  28.9 0.1 collective-permute-start.2
  29.0 0.0 copy-start.7
  29.0 0.9 first_step.1
  29.9 1.5 %collective-permute-start.13 = (s16[208,768]{1,0:T(8,128)(2,1)S(1)}, s16[208,768]{1,0:T(8,128)(2,1)S(1)}, u32[]{:S(2)}, u32[]{:S(2)}) collective-permute-start(s16[208,768]{1,0:T(8,128)(2,1)S(1)} %get-tuple-element.47), channel_id=1, source_target_pairs={{0,2},{1,3},{2,0},{3,1},{4,6},{5,7},{6,4},{7,5},{8,10},{9,11},{10,... | collective-permute-start | bytes 958472 | tf_op jit(solution)/shard_map/ppermute | solution.py:301
  31.4 0.6 collective-permute-start.5
  32.0 4.8 %collective-permute-done.8.rest_6_ = bf16[192,768]{1,0:T(8,128)(2,1)S(1)} collective-permute-done((bf16[192,768]{1,0:T(8,128)(2,1)S(1)}, bf16[192,768]{1,0:T(8,128)(2,1)S(1)}, u32[]{:S(2)}, u32[]{:S(2)}) %collective-permute-start.8) | collective-permute-done | bytes 294944 | tf_op jit(solution)/shard_map/ppermute | solution.py:301
  36.7 1.3 %collective-permute-start.7 = (bf16[192,768]{1,0:T(8,128)(2,1)S(1)}, bf16[192,768]{1,0:T(8,128)(2,1)S(1)}, u32[]{:S(2)}, u32[]{:S(2)}) collective-permute-start(bf16[192,768]{1,0:T(8,128)(2,1)S(1)} %collective-permute-done.6.rest_4_), channel_id=1, source_target_pairs={{0,2},{1,3},{2,0},{3,1},{4,6},{5,7},{6,4},{7,5},{8,10},{9,11},{10,... | collective-permute-start | bytes 884744 | tf_op jit(solution)/shard_map/ppermute | solution.py:301
  38.1 2.2 %collective-permute-done.13.codes = s16[208,768]{1,0:T(8,128)(2,1)S(1)} collective-permute-done((s16[208,768]{1,0:T(8,128)(2,1)S(1)}, s16[208,768]{1,0:T(8,128)(2,1)S(1)}, u32[]{:S(2)}, u32[]{:S(2)}) %collective-permute-start.13) | collective-permute-done | bytes 319520 | tf_op jit(solution)/shard_map/ppermute | solution.py:301
  40.3 1.5 %collective-permute-start.9 = (bf16[192,768]{1,0:T(8,128)(2,1)S(1)}, bf16[192,768]{1,0:T(8,128)(2,1)S(1)}, u32[]{:S(2)}, u32[]{:S(2)}) collective-permute-start(bf16[192,768]{1,0:T(8,128)(2,1)S(1)} %collective-permute-done.8.rest_6_), channel_id=1, source_target_pairs={{0,2},{1,3},{2,0},{3,1},{4,6},{5,7},{6,4},{7,5},{8,10},{9,11},{10,... | collective-permute-start | bytes 884744 | tf_op jit(solution)/shard_map/ppermute | solution.py:301
  41.8 0.8 second_step.3
  42.6 4.0 %collective-permute-done.5.rest_3_ = bf16[192,768]{1,0:T(8,128)(2,1)S(1)} collective-permute-done((bf16[192,768]{1,0:T(8,128)(2,1)S(1)}, bf16[192,768]{1,0:T(8,128)(2,1)S(1)}, u32[]{:S(2)}, u32[]{:S(2)}) %collective-permute-start.5) | collective-permute-done | bytes 294944 | tf_op jit(solution)/shard_map/ppermute | solution.py:301
  46.6 1.3 %collective-permute-start.14 = (s16[64,768]{1,0:T(8,128)(2,1)S(1)}, s16[64,768]{1,0:T(8,128)(2,1)S(1)}, u32[]{:S(2)}, u32[]{:S(2)}) collective-permute-start(s16[64,768]{1,0:T(8,128)(2,1)S(1)} %get-tuple-element.49), channel_id=1, source_target_pairs={{0,4},{1,5},{2,6},{3,7},{4,0},{5,1},{6,2},{7,3},{8,12},{9,13},{10,... | collective-permute-start | bytes 294920 | tf_op jit(solution)/shard_map/ppermute | solution.py:301
  47.9 5.0 %collective-permute-done.7.rest_5_ = bf16[192,768]{1,0:T(8,128)(2,1)S(1)} collective-permute-done((bf16[192,768]{1,0:T(8,128)(2,1)S(1)}, bf16[192,768]{1,0:T(8,128)(2,1)S(1)}, u32[]{:S(2)}, u32[]{:S(2)}) %collective-permute-start.7) | collective-permute-done | bytes 294944 | tf_op jit(solution)/shard_map/ppermute | solution.py:301
  52.9 3.4 %collective-permute-start.15 = (s16[64,768]{1,0:T(8,128)(2,1)S(1)}, s16[64,768]{1,0:T(8,128)(2,1)S(1)}, u32[]{:S(2)}, u32[]{:S(2)}) collective-permute-start(s16[64,768]{1,0:T(8,128)(2,1)S(1)} %get-tuple-element.50), channel_id=1, source_target_pairs={{0,8},{1,9},{2,10},{3,11},{4,12},{5,13},{6,14},{7,15},{8,0},{9,1},... | collective-permute-start | bytes 294920 | tf_op jit(solution)/shard_map/ppermute | solution.py:301
  56.3 4.4 %collective-permute-done.15.c2 = s16[64,768]{1,0:T(8,128)(2,1)S(1)} collective-permute-done((s16[64,768]{1,0:T(8,128)(2,1)S(1)}, s16[64,768]{1,0:T(8,128)(2,1)S(1)}, u32[]{:S(2)}, u32[]{:S(2)}) %collective-permute-start.15) | collective-permute-done | bytes 98336 | tf_op jit(solution)/shard_map/ppermute | solution.py:301
  60.7 2.5 %collective-permute-start.16 = (s16[64,768]{1,0:T(8,128)(2,1)S(1)}, s16[64,768]{1,0:T(8,128)(2,1)S(1)}, u32[]{:S(2)}, u32[]{:S(2)}) collective-permute-start(s16[64,768]{1,0:T(8,128)(2,1)S(1)} %get-tuple-element.51), channel_id=1, source_target_pairs={{0,12},{1,13},{2,14},{3,15},{4,8},{5,9},{6,10},{7,11},{8,4},{9,5},... | collective-permute-start | bytes 294920 | tf_op jit(solution)/shard_map/ppermute | solution.py:301
  63.2 3.9 %collective-permute-done.16.c3 = s16[64,768]{1,0:T(8,128)(2,1)S(1)} collective-permute-done((s16[64,768]{1,0:T(8,128)(2,1)S(1)}, s16[64,768]{1,0:T(8,128)(2,1)S(1)}, u32[]{:S(2)}, u32[]{:S(2)}) %collective-permute-start.16) | collective-permute-done | bytes 98336 | tf_op jit(solution)/shard_map/ppermute | solution.py:301
  67.1 0.6 last_step.3
  67.8 0.6 collective-permute-start.17
  68.3 2.8 %branch.1 = (f32[512,768]{1,0:T(8,128)S(1)}, f32[512,128]{1,0:T(8,128)S(1)}) custom-call(s32[2]{0:T(128)S(1)} %pad_add_fusion.where_ref, bf16[256,1536]{1,0:T(8,128)(2,1)S(1)} %attention.1.mixed_own, bf16[256,1536]{1,0:T(8,128)(2,1)S(1)} %collective-permute-done.1.mixed_other, bf16[256,1536]{1,0:T(8,128)(2,1)S(1)} %bitcast.12, ...), custom_call_target="tpu_custom_call" | custom-call | flops 1000 | bytes 1000 | tf_op jit(solution)/shard_map/branch/pallas_call | solution.py:26
  71.1 0.1 collective-permute-start.10
  71.3 1.4 %collective-permute-done.10.stats_other = f32[512,128]{1,0:T(8,128)S(1)} collective-permute-done((f32[512,128]{1,0:T(8,128)S(1)}, f32[512,128]{1,0:T(8,128)S(1)}, u32[]{:S(2)}, u32[]{:S(2)}) %collective-permute-start.10) | collective-permute-done | bytes 262176 | tf_op jit(solution)/shard_map/ppermute | solution.py:301
  72.7 2.6 %targets.3 = (f32[256,384]{1,0:T(8,128)S(1)}, f32[256,384]{1,0:T(8,128)S(1)}, s16[400,384]{1,0:T(8,128)(2,1)}, f32[384,384]{1,0:T(8,128)S(1)}) custom-call(s32[2]{0:T(128)S(1)} %pad_add_fusion.where_ref, f32[512,768]{1,0:T(8,128)S(1)} %get-tuple-element.40.blend, f32[512,128]{1,0:T(8,128)S(1)} %get-tuple-element.41.stats, ...), custom_call_target="tpu_custom_call" | custom-call | flops 1000 | bytes 1000 | tf_op jit(solution)/shard_map/targets/pallas_call | solution.py:26
  75.3 0.1 collective-permute-start.20
  75.5 2.8 %targets.2 = (f32[256,384]{1,0:T(8,128)S(1)}, f32[256,384]{1,0:T(8,128)S(1)}, s16[400,384]{1,0:T(8,128)(2,1)}, f32[384,384]{1,0:T(8,128)S(1)}) custom-call(s32[2]{0:T(128)S(1)} %pad_add_fusion.where_ref, f32[512,768]{1,0:T(8,128)S(1)} %get-tuple-element.40.blend, f32[512,128]{1,0:T(8,128)S(1)} %get-tuple-element.41.stats, ...), custom_call_target="tpu_custom_call" | custom-call | flops 1000 | bytes 1000 | tf_op jit(solution)/shard_map/targets/pallas_call | solution.py:26
  78.3 0.4 collective-permute-start.19
  78.6 1.4 %collective-permute-start.21 = (s16[400,384]{1,0:T(8,128)(2,1)}, s16[400,384]{1,0:T(8,128)(2,1)S(1)}, u32[]{:S(2)}, u32[]{:S(2)}) collective-permute-start(s16[400,384]{1,0:T(8,128)(2,1)} %get-tuple-element.58), channel_id=1, source_target_pairs={{0,2},{1,3},{2,0},{3,1},{4,6},{5,7},{6,4},{7,5},{8,10},{9,11},{10,... | collective-permute-start | bytes 921608 | tf_op jit(solution)/shard_map/ppermute | solution.py:301
  80.1 0.6 collective-permute-start.25
  80.7 8.3 %collective-permute-done.21.codes = s16[400,384]{1,0:T(8,128)(2,1)S(1)} collective-permute-done((s16[400,384]{1,0:T(8,128)(2,1)}, s16[400,384]{1,0:T(8,128)(2,1)S(1)}, u32[]{:S(2)}, u32[]{:S(2)}) %collective-permute-start.21) | collective-permute-done | bytes 307232 | tf_op jit(solution)/shard_map/ppermute | solution.py:301
  89.0 0.8 second_step.4
  89.8 0.1 collective-permute-start.22
  89.9 3.1 %collective-permute-start.23 = (s16[112,384]{1,0:T(8,128)(2,1)S(1)}, s16[112,384]{1,0:T(8,128)(2,1)S(1)}, u32[]{:S(2)}, u32[]{:S(2)}) collective-permute-start(s16[112,384]{1,0:T(8,128)(2,1)S(1)} %get-tuple-element.61), channel_id=1, source_target_pairs={{0,8},{1,9},{2,10},{3,11},{4,12},{5,13},{6,14},{7,15},{8,0},{9,1},... | collective-permute-start | bytes 258056 | tf_op jit(solution)/shard_map/ppermute | solution.py:301
  92.9 1.3 %collective-permute-start.24 = (s16[112,384]{1,0:T(8,128)(2,1)S(1)}, s16[112,384]{1,0:T(8,128)(2,1)S(1)}, u32[]{:S(2)}, u32[]{:S(2)}) collective-permute-start(s16[112,384]{1,0:T(8,128)(2,1)S(1)} %get-tuple-element.62), channel_id=1, source_target_pairs={{0,12},{1,13},{2,14},{3,15},{4,8},{5,9},{6,10},{7,11},{8,4},{9,5},... | collective-permute-start | bytes 258056 | tf_op jit(solution)/shard_map/ppermute | solution.py:301
  94.2 2.8 %maximum_select_fusion = f32[1,256,1536]{2,1,0:T(8,128)} fusion(f32[1,256,384]{2,1,0:T(8,128)} %bitcast.11, f32[1,256,384]{2,1,0:T(8,128)} %bitcast.10, f32[1,256,384]{2,1,0:T(8,128)S(1)} %bitcast.17, f32[1,256,384]{2,1,0:T(8,128)S(1)} %bitcast.18, pred[]{:T(512)S(6)} %eq.6), kind=kLoop, calls=%fused_computation | loop fusion | flops 2752512 | bytes 3145729 | tf_op jit(solution)/shard_map/jit(_where)/select_n | solution.py:310
  97.0 0.8 second_step.5
  97.8 0.1 collective-permute-start.26
  97.9 3.1 %collective-permute-start.27 = (s16[112,384]{1,0:T(8,128)(2,1)S(1)}, s16[112,384]{1,0:T(8,128)(2,1)S(1)}, u32[]{:S(2)}, u32[]{:S(2)}) collective-permute-start(s16[112,384]{1,0:T(8,128)(2,1)S(1)} %get-tuple-element.69), channel_id=1, source_target_pairs={{0,8},{1,9},{2,10},{3,11},{4,12},{5,13},{6,14},{7,15},{8,0},{9,1},... | collective-permute-start | bytes 258056 | tf_op jit(solution)/shard_map/ppermute | solution.py:301
  100.9 1.3 %collective-permute-start.28 = (s16[112,384]{1,0:T(8,128)(2,1)S(1)}, s16[112,384]{1,0:T(8,128)(2,1)S(1)}, u32[]{:S(2)}, u32[]{:S(2)}) collective-permute-start(s16[112,384]{1,0:T(8,128)(2,1)S(1)} %get-tuple-element.70), channel_id=1, source_target_pairs={{0,12},{1,13},{2,14},{3,15},{4,8},{5,9},{6,10},{7,11},{8,4},{9,5},... | collective-permute-start | bytes 258056 | tf_op jit(solution)/shard_map/ppermute | solution.py:301
  102.3 0.6 last_step.4
  102.9 0.1 collective-permute-start.29
  103.0 2.2 %collective-permute-done.27.c2 = s16[112,384]{1,0:T(8,128)(2,1)S(1)} collective-permute-done((s16[112,384]{1,0:T(8,128)(2,1)S(1)}, s16[112,384]{1,0:T(8,128)(2,1)S(1)}, u32[]{:S(2)}, u32[]{:S(2)}) %collective-permute-start.27) | collective-permute-done | bytes 86048 | tf_op jit(solution)/shard_map/ppermute | solution.py:301
  105.2 2.0 %collective-permute-done.28.c3 = s16[112,384]{1,0:T(8,128)(2,1)S(1)} collective-permute-done((s16[112,384]{1,0:T(8,128)(2,1)S(1)}, s16[112,384]{1,0:T(8,128)(2,1)S(1)}, u32[]{:S(2)}, u32[]{:S(2)}) %collective-permute-start.28) | collective-permute-done | bytes 86048 | tf_op jit(solution)/shard_map/ppermute | solution.py:301
  107.2 0.6 last_step.5
  107.8 0.1 collective-permute-start.30
  107.9 1.2 %collective-permute-done.30 = f32[48,384]{1,0:T(8,128)S(1)} collective-permute-done((f32[48,384]{1,0:T(8,128)S(1)}, f32[48,384]{1,0:T(8,128)S(1)}, u32[]{:S(2)}, u32[]{:S(2)}) %collective-permute-start.30) | collective-permute-done | bytes 73760 | tf_op jit(solution)/shard_map/ppermute | solution.py:301
  109.2 0.7 maximum_select_fusion.1
  (37 shorter events, 0.2 us)
Async XLA Ops:
  1.7 1.5 %collective-permute-start = (bf16[96,768]{1,0:T(8,128)(2,1)S(1)}, bf16[96,768]{1,0:T(8,128)(2,1)S(1)}, u32[]{:S(2)}, u32[]{:S(2)}) collective-permute-start(bf16[96,768]{1,0:T(8,128)(2,1)S(1)} %get-tuple-element.75), channel_id=1, source_target_pairs={{0,1},{1,0},{2,3},{3,2},{4,5},{5,4},{6,7},{7,6},{8,9},{9,8},{10,11... | collective-permute-start | bytes 442376 | tf_op jit(solution)/shard_map/ppermute | solution.py:301
  3.2 1.9 %copy-start = (bf16[1,8,256,768]{3,2,1,0:T(8,128)(2,1)S(1)}, bf16[1,8,256,768]{3,2,1,0:T(8,128)(2,1)}, u32[]{:S(2)}) copy-start(bf16[1,8,256,768]{3,2,1,0:T(8,128)(2,1)} %hidden_ref) | copy-start | bytes 9437188
  5.1 0.7 copy-start.6
  5.8 8.4 %copy-start.2 = (bf16[1,256,1536]{2,1,0:T(8,128)(2,1)S(1)}, bf16[1,256,1536]{2,1,0:T(8,128)(2,1)}, u32[]{:S(2)}) copy-start(bf16[1,256,1536]{2,1,0:T(8,128)(2,1)} %param.13) | copy-start | bytes 2359300
  5.8 11.6 %copy-start.3 = (bf16[1,256,1536]{2,1,0:T(8,128)(2,1)S(1)}, bf16[1,256,1536]{2,1,0:T(8,128)(2,1)}, u32[]{:S(2)}) copy-start(bf16[1,256,1536]{2,1,0:T(8,128)(2,1)} %param.9) | copy-start | bytes 2359300
  5.8 11.6 %copy-start.4 = (bf16[1,256,1536]{2,1,0:T(8,128)(2,1)S(1)}, bf16[1,256,1536]{2,1,0:T(8,128)(2,1)}, u32[]{:S(2)}) copy-start(bf16[1,256,1536]{2,1,0:T(8,128)(2,1)} %param.10) | copy-start | bytes 2359300
  5.8 11.6 %copy-start.5 = (bf16[1,256,1536]{2,1,0:T(8,128)(2,1)S(1)}, bf16[1,256,1536]{2,1,0:T(8,128)(2,1)}, u32[]{:S(2)}) copy-start(bf16[1,256,1536]{2,1,0:T(8,128)(2,1)} %param.11) | copy-start | bytes 2359300
  10.0 18.9 %collective-permute-start.12 = (f32[384,768]{1,0:T(8,128)S(1)}, f32[384,768]{1,0:T(8,128)S(1)}, u32[]{:S(2)}, u32[]{:S(2)}) collective-permute-start(f32[384,768]{1,0:T(8,128)S(1)} %get-tuple-element.45), channel_id=1, source_target_pairs={{0,1},{1,0},{2,3},{3,2},{4,5},{5,4},{6,7},{7,6},{8,9},{9,8},{10,11... | collective-permute-start | bytes 3538952 | tf_op jit(solution)/shard_map/ppermute | solution.py:301
  10.4 17.7 %collective-permute-start.6 = (bf16[192,768]{1,0:T(8,128)(2,1)S(1)}, bf16[192,768]{1,0:T(8,128)(2,1)S(1)}, u32[]{:S(2)}, u32[]{:S(2)}) collective-permute-start(bf16[192,768]{1,0:T(8,128)(2,1)S(1)} %pad_maximum_fusion.1.rest_0_), channel_id=1, source_target_pairs={{0,8},{1,9},{2,10},{3,11},{4,12},{5,13},{6,14},{7,15},{8,0},{9,1},... | collective-permute-start | bytes 884744 | tf_op jit(solution)/shard_map/ppermute | solution.py:301
  14.2 15.7 %collective-permute-start.3 = (bf16[192,768]{1,0:T(8,128)(2,1)S(1)}, bf16[192,768]{1,0:T(8,128)(2,1)S(1)}, u32[]{:S(2)}, u32[]{:S(2)}) collective-permute-start(bf16[192,768]{1,0:T(8,128)(2,1)S(1)} %pad_maximum_fusion.1.rest_0_), channel_id=1, source_target_pairs={{0,2},{1,3},{2,0},{3,1},{4,6},{5,7},{6,4},{7,5},{8,10},{9,11},{10,... | collective-permute-start | bytes 884744 | tf_op jit(solution)/shard_map/ppermute | solution.py:301
  15.8 15.6 %collective-permute-start.4 = (bf16[192,768]{1,0:T(8,128)(2,1)S(1)}, bf16[192,768]{1,0:T(8,128)(2,1)S(1)}, u32[]{:S(2)}, u32[]{:S(2)}) collective-permute-start(bf16[192,768]{1,0:T(8,128)(2,1)S(1)} %pad_maximum_fusion.1.rest_0_), channel_id=1, source_target_pairs={{0,4},{1,5},{2,6},{3,7},{4,0},{5,1},{6,2},{7,3},{8,12},{9,13},{10,... | collective-permute-start | bytes 884744 | tf_op jit(solution)/shard_map/ppermute | solution.py:301
  17.4 3.5 %copy-start.1 = (bf16[1,256,1536]{2,1,0:T(8,128)(2,1)S(1)}, bf16[1,256,1536]{2,1,0:T(8,128)(2,1)}, u32[]{:S(2)}) copy-start(bf16[1,256,1536]{2,1,0:T(8,128)(2,1)} %param.12) | copy-start | bytes 2359300
  20.8 46.9 %collective-permute-start.1 = (bf16[256,1536]{1,0:T(8,128)(2,1)S(1)}, bf16[256,1536]{1,0:T(8,128)(2,1)S(1)}, u32[]{:S(2)}, u32[]{:S(2)}) collective-permute-start(bf16[256,1536]{1,0:T(8,128)(2,1)S(1)} %attention.1.mixed_own), channel_id=1, source_target_pairs={{0,1},{1,0},{2,3},{3,2},{4,5},{5,4},{6,7},{7,6},{8,9},{9,8},{10,11... | collective-permute-start | bytes 2359304 | tf_op jit(solution)/shard_map/ppermute | solution.py:301
  28.1 8.6 %collective-permute-start.8 = (bf16[192,768]{1,0:T(8,128)(2,1)S(1)}, bf16[192,768]{1,0:T(8,128)(2,1)S(1)}, u32[]{:S(2)}, u32[]{:S(2)}) collective-permute-start(bf16[192,768]{1,0:T(8,128)(2,1)S(1)} %collective-permute-done.6.rest_4_), channel_id=1, source_target_pairs={{0,4},{1,5},{2,6},{3,7},{4,0},{5,1},{6,2},{7,3},{8,12},{9,13},{10,... | collective-permute-start | bytes 884744 | tf_op jit(solution)/shard_map/ppermute | solution.py:301
  28.9 39.5 %collective-permute-start.2 = (bf16[2,256,768]{2,1,0:T(8,128)(2,1)S(1)}, bf16[2,256,768]{2,1,0:T(8,128)(2,1)S(1)}, u32[]{:S(2)}, u32[]{:S(2)}) collective-permute-start(bf16[2,256,768]{2,1,0:T(8,128)(2,1)S(1)} %pad_maximum_fusion), channel_id=1, source_target_pairs={{0,1},{1,0},{2,3},{3,2},{4,5},{5,4},{6,7},{7,6},{8,9},{9,8},{10,11... | collective-permute-start | bytes 2359304 | tf_op jit(solution)/shard_map/ppermute | solution.py:301
  29.0 34.2 %copy-start.7 = (bf16[48,1536]{1,0:T(8,128)(2,1)S(1)}, bf16[48,1536]{1,0:T(8,128)(2,1)}, u32[]{:S(2)}) copy-start(bf16[48,1536]{1,0:T(8,128)(2,1)} %param.15) | copy-start | bytes 442372
  29.9 10.4 %collective-permute-start.13 = (s16[208,768]{1,0:T(8,128)(2,1)S(1)}, s16[208,768]{1,0:T(8,128)(2,1)S(1)}, u32[]{:S(2)}, u32[]{:S(2)}) collective-permute-start(s16[208,768]{1,0:T(8,128)(2,1)S(1)} %get-tuple-element.47), channel_id=1, source_target_pairs={{0,2},{1,3},{2,0},{3,1},{4,6},{5,7},{6,4},{7,5},{8,10},{9,11},{10,... | collective-permute-start | bytes 958472 | tf_op jit(solution)/shard_map/ppermute | solution.py:301
  31.4 15.2 %collective-permute-start.5 = (bf16[192,768]{1,0:T(8,128)(2,1)S(1)}, bf16[192,768]{1,0:T(8,128)(2,1)S(1)}, u32[]{:S(2)}, u32[]{:S(2)}) collective-permute-start(bf16[192,768]{1,0:T(8,128)(2,1)S(1)} %collective-permute-done.4.rest_2_), channel_id=1, source_target_pairs={{0,2},{1,3},{2,0},{3,1},{4,6},{5,7},{6,4},{7,5},{8,10},{9,11},{10,... | collective-permute-start | bytes 884744 | tf_op jit(solution)/shard_map/ppermute | solution.py:301
  36.7 16.2 %collective-permute-start.7 = (bf16[192,768]{1,0:T(8,128)(2,1)S(1)}, bf16[192,768]{1,0:T(8,128)(2,1)S(1)}, u32[]{:S(2)}, u32[]{:S(2)}) collective-permute-start(bf16[192,768]{1,0:T(8,128)(2,1)S(1)} %collective-permute-done.6.rest_4_), channel_id=1, source_target_pairs={{0,2},{1,3},{2,0},{3,1},{4,6},{5,7},{6,4},{7,5},{8,10},{9,11},{10,... | collective-permute-start | bytes 884744 | tf_op jit(solution)/shard_map/ppermute | solution.py:301
  40.3 28.1 %collective-permute-start.9 = (bf16[192,768]{1,0:T(8,128)(2,1)S(1)}, bf16[192,768]{1,0:T(8,128)(2,1)S(1)}, u32[]{:S(2)}, u32[]{:S(2)}) collective-permute-start(bf16[192,768]{1,0:T(8,128)(2,1)S(1)} %collective-permute-done.8.rest_6_), channel_id=1, source_target_pairs={{0,2},{1,3},{2,0},{3,1},{4,6},{5,7},{6,4},{7,5},{8,10},{9,11},{10,... | collective-permute-start | bytes 884744 | tf_op jit(solution)/shard_map/ppermute | solution.py:301
  46.6 9.7 %collective-permute-start.14 = (s16[64,768]{1,0:T(8,128)(2,1)S(1)}, s16[64,768]{1,0:T(8,128)(2,1)S(1)}, u32[]{:S(2)}, u32[]{:S(2)}) collective-permute-start(s16[64,768]{1,0:T(8,128)(2,1)S(1)} %get-tuple-element.49), channel_id=1, source_target_pairs={{0,4},{1,5},{2,6},{3,7},{4,0},{5,1},{6,2},{7,3},{8,12},{9,13},{10,... | collective-permute-start | bytes 294920 | tf_op jit(solution)/shard_map/ppermute | solution.py:301
  52.9 7.8 %collective-permute-start.15 = (s16[64,768]{1,0:T(8,128)(2,1)S(1)}, s16[64,768]{1,0:T(8,128)(2,1)S(1)}, u32[]{:S(2)}, u32[]{:S(2)}) collective-permute-start(s16[64,768]{1,0:T(8,128)(2,1)S(1)} %get-tuple-element.50), channel_id=1, source_target_pairs={{0,8},{1,9},{2,10},{3,11},{4,12},{5,13},{6,14},{7,15},{8,0},{9,1},... | collective-permute-start | bytes 294920 | tf_op jit(solution)/shard_map/ppermute | solution.py:301
  56.3 14.9 %collective-permute-start.11 = (bf16[256,768]{1,0:T(8,128)(2,1)S(1)}, bf16[256,768]{1,0:T(8,128)(2,1)S(1)}, u32[]{:S(2)}, u32[]{:S(2)}) collective-permute-start(bf16[256,768]{1,0:T(8,128)(2,1)S(1)} %get-tuple-element.43.sum_own), channel_id=1, source_target_pairs={{0,1},{1,0},{2,3},{3,2},{4,5},{5,4},{6,7},{7,6},{8,9},{9,8},{10,11... | collective-permute-start | bytes 1179656 | tf_op jit(solution)/shard_map/ppermute | solution.py:301
  60.7 6.4 %collective-permute-start.16 = (s16[64,768]{1,0:T(8,128)(2,1)S(1)}, s16[64,768]{1,0:T(8,128)(2,1)S(1)}, u32[]{:S(2)}, u32[]{:S(2)}) collective-permute-start(s16[64,768]{1,0:T(8,128)(2,1)S(1)} %get-tuple-element.51), channel_id=1, source_target_pairs={{0,12},{1,13},{2,14},{3,15},{4,8},{5,9},{6,10},{7,11},{8,4},{9,5},... | collective-permute-start | bytes 294920 | tf_op jit(solution)/shard_map/ppermute | solution.py:301
  67.1 4.1 %collective-permute-start.18 = (bf16[48,768]{1,0:T(8,128)(2,1)S(1)}, bf16[48,768]{1,0:T(8,128)(2,1)S(1)}, u32[]{:S(2)}, u32[]{:S(2)}) collective-permute-start(bf16[48,768]{1,0:T(8,128)(2,1)S(1)} %get-tuple-element.77), channel_id=1, source_target_pairs={{0,1},{1,0},{2,3},{3,2},{4,5},{5,4},{6,7},{7,6},{8,9},{9,8},{10,11... | collective-permute-start | bytes 221192 | tf_op jit(solution)/shard_map/ppermute | solution.py:301
  67.8 3.5 %collective-permute-start.17 = (bf16[96,768]{1,0:T(8,128)(2,1)S(1)}, bf16[96,768]{1,0:T(8,128)(2,1)S(1)}, u32[]{:S(2)}, u32[]{:S(2)}) collective-permute-start(bf16[96,768]{1,0:T(8,128)(2,1)S(1)} %last_step.3), channel_id=1, source_target_pairs={{0,1},{1,0},{2,3},{3,2},{4,5},{5,4},{6,7},{7,6},{8,9},{9,8},{10,11... | collective-permute-start | bytes 442376 | tf_op jit(solution)/shard_map/ppermute | solution.py:301
  71.1 1.6 %collective-permute-start.10 = (f32[512,128]{1,0:T(8,128)S(1)}, f32[512,128]{1,0:T(8,128)S(1)}, u32[]{:S(2)}, u32[]{:S(2)}) collective-permute-start(f32[512,128]{1,0:T(8,128)S(1)} %get-tuple-element.41.stats), channel_id=1, source_target_pairs={{0,1},{1,0},{2,3},{3,2},{4,5},{5,4},{6,7},{7,6},{8,9},{9,8},{10,11... | collective-permute-start | bytes 786440 | tf_op jit(solution)/shard_map/ppermute | solution.py:301
  75.3 17.6 %collective-permute-start.20 = (f32[256,384]{1,0:T(8,128)S(1)}, f32[256,384]{1,0:T(8,128)}, u32[]{:S(2)}, u32[]{:S(2)}) collective-permute-start(f32[256,384]{1,0:T(8,128)S(1)} %get-tuple-element.56), channel_id=1, source_target_pairs={{0,1},{1,0},{2,3},{3,2},{4,5},{5,4},{6,7},{7,6},{8,9},{9,8},{10,11... | collective-permute-start | bytes 1179656 | tf_op jit(solution)/shard_map/ppermute | solution.py:301
  78.3 16.0 %collective-permute-start.19 = (f32[256,384]{1,0:T(8,128)S(1)}, f32[256,384]{1,0:T(8,128)}, u32[]{:S(2)}, u32[]{:S(2)}) collective-permute-start(f32[256,384]{1,0:T(8,128)S(1)} %get-tuple-element.55), channel_id=1, source_target_pairs={{0,1},{1,0},{2,3},{3,2},{4,5},{5,4},{6,7},{7,6},{8,9},{9,8},{10,11... | collective-permute-start | bytes 1179656 | tf_op jit(solution)/shard_map/ppermute | solution.py:301
  78.6 10.3 %collective-permute-start.21 = (s16[400,384]{1,0:T(8,128)(2,1)}, s16[400,384]{1,0:T(8,128)(2,1)S(1)}, u32[]{:S(2)}, u32[]{:S(2)}) collective-permute-start(s16[400,384]{1,0:T(8,128)(2,1)} %get-tuple-element.58), channel_id=1, source_target_pairs={{0,2},{1,3},{2,0},{3,1},{4,6},{5,7},{6,4},{7,5},{8,10},{9,11},{10,... | collective-permute-start | bytes 921608 | tf_op jit(solution)/shard_map/ppermute | solution.py:301
  80.1 16.9 %collective-permute-start.25 = (s16[400,384]{1,0:T(8,128)(2,1)}, s16[400,384]{1,0:T(8,128)(2,1)S(1)}, u32[]{:S(2)}, u32[]{:S(2)}) collective-permute-start(s16[400,384]{1,0:T(8,128)(2,1)} %get-tuple-element.65), channel_id=1, source_target_pairs={{0,2},{1,3},{2,0},{3,1},{4,6},{5,7},{6,4},{7,5},{8,10},{9,11},{10,... | collective-permute-start | bytes 921608 | tf_op jit(solution)/shard_map/ppermute | solution.py:301
  89.8 11.2 %collective-permute-start.22 = (s16[112,384]{1,0:T(8,128)(2,1)S(1)}, s16[112,384]{1,0:T(8,128)(2,1)S(1)}, u32[]{:S(2)}, u32[]{:S(2)}) collective-permute-start(s16[112,384]{1,0:T(8,128)(2,1)S(1)} %get-tuple-element.60), channel_id=1, source_target_pairs={{0,4},{1,5},{2,6},{3,7},{4,0},{5,1},{6,2},{7,3},{8,12},{9,13},{10,... | collective-permute-start | bytes 258056 | tf_op jit(solution)/shard_map/ppermute | solution.py:301
  89.9 12.4 %collective-permute-start.23 = (s16[112,384]{1,0:T(8,128)(2,1)S(1)}, s16[112,384]{1,0:T(8,128)(2,1)S(1)}, u32[]{:S(2)}, u32[]{:S(2)}) collective-permute-start(s16[112,384]{1,0:T(8,128)(2,1)S(1)} %get-tuple-element.61), channel_id=1, source_target_pairs={{0,8},{1,9},{2,10},{3,11},{4,12},{5,13},{6,14},{7,15},{8,0},{9,1},... | collective-permute-start | bytes 258056 | tf_op jit(solution)/shard_map/ppermute | solution.py:301
  92.9 9.4 %collective-permute-start.24 = (s16[112,384]{1,0:T(8,128)(2,1)S(1)}, s16[112,384]{1,0:T(8,128)(2,1)S(1)}, u32[]{:S(2)}, u32[]{:S(2)}) collective-permute-start(s16[112,384]{1,0:T(8,128)(2,1)S(1)} %get-tuple-element.62), channel_id=1, source_target_pairs={{0,12},{1,13},{2,14},{3,15},{4,8},{5,9},{6,10},{7,11},{8,4},{9,5},... | collective-permute-start | bytes 258056 | tf_op jit(solution)/shard_map/ppermute | solution.py:301
  97.8 5.2 %collective-permute-start.26 = (s16[112,384]{1,0:T(8,128)(2,1)S(1)}, s16[112,384]{1,0:T(8,128)(2,1)S(1)}, u32[]{:S(2)}, u32[]{:S(2)}) collective-permute-start(s16[112,384]{1,0:T(8,128)(2,1)S(1)} %get-tuple-element.68), channel_id=1, source_target_pairs={{0,4},{1,5},{2,6},{3,7},{4,0},{5,1},{6,2},{7,3},{8,12},{9,13},{10,... | collective-permute-start | bytes 258056 | tf_op jit(solution)/shard_map/ppermute | solution.py:301
  97.9 7.3 %collective-permute-start.27 = (s16[112,384]{1,0:T(8,128)(2,1)S(1)}, s16[112,384]{1,0:T(8,128)(2,1)S(1)}, u32[]{:S(2)}, u32[]{:S(2)}) collective-permute-start(s16[112,384]{1,0:T(8,128)(2,1)S(1)} %get-tuple-element.69), channel_id=1, source_target_pairs={{0,8},{1,9},{2,10},{3,11},{4,12},{5,13},{6,14},{7,15},{8,0},{9,1},... | collective-permute-start | bytes 258056 | tf_op jit(solution)/shard_map/ppermute | solution.py:301
  100.9 6.3 %collective-permute-start.28 = (s16[112,384]{1,0:T(8,128)(2,1)S(1)}, s16[112,384]{1,0:T(8,128)(2,1)S(1)}, u32[]{:S(2)}, u32[]{:S(2)}) collective-permute-start(s16[112,384]{1,0:T(8,128)(2,1)S(1)} %get-tuple-element.70), channel_id=1, source_target_pairs={{0,12},{1,13},{2,14},{3,15},{4,8},{5,9},{6,10},{7,11},{8,4},{9,5},... | collective-permute-start | bytes 258056 | tf_op jit(solution)/shard_map/ppermute | solution.py:301
  102.9 5.0 %collective-permute-start.29 = (f32[48,384]{1,0:T(8,128)S(1)}, f32[48,384]{1,0:T(8,128)S(1)}, u32[]{:S(2)}, u32[]{:S(2)}) collective-permute-start(f32[48,384]{1,0:T(8,128)S(1)} %get-tuple-element.72), channel_id=1, source_target_pairs={{0,1},{1,0},{2,3},{3,2},{4,5},{5,4},{6,7},{7,6},{8,9},{9,8},{10,11... | collective-permute-start | bytes 221192 | tf_op jit(solution)/shard_map/ppermute | solution.py:301
  107.8 1.3 %collective-permute-start.30 = (f32[48,384]{1,0:T(8,128)S(1)}, f32[48,384]{1,0:T(8,128)S(1)}, u32[]{:S(2)}, u32[]{:S(2)}) collective-permute-start(f32[48,384]{1,0:T(8,128)S(1)} %get-tuple-element.73), channel_id=1, source_target_pairs={{0,1},{1,0},{2,3},{3,2},{4,5},{5,4},{6,7},{7,6},{8,9},{9,8},{10,11... | collective-permute-start | bytes 221192 | tf_op jit(solution)/shard_map/ppermute | solution.py:301

commit v4 on v3

--- a/solution.py
+++ b/solution.py
@@ -19,7 +19,7 @@
 TAIL = 16
 
 
-def call(kernel, out_shape, name, scratch=()):
+def call(kernel, out_shape, name, scratch=(), cost=COST):
     held = pl.BlockSpec(memory_space=pltpu.VMEM)
 
     def run(where, *arrays):
@@ -30,7 +30,7 @@
             out_specs=(held,) * len(out_shape),
             scratch_shapes=scratch,
             compiler_params=pltpu.CompilerParams(vmem_limit_bytes=VMEM),
-            cost_estimate=pl.CostEstimate(flops=COST, bytes_accessed=COST, transcendentals=0),
+            cost_estimate=pl.CostEstimate(flops=0, bytes_accessed=cost, transcendentals=0),
             name=name,
         )(where, *arrays)
 
@@ -49,7 +49,7 @@
     return lax.dot_general(a, b, (((0,), (0,)), ((), ())), preferred_element_type=jnp.float32)
 
 
-def attention_kernel(where_ref, q_ref, k_ref, v_ref, out_ref, *, size):
+def attention_kernel(where_ref, q_ref, k_ref, v_ref, stream, earlier, out_ref, *bundle, size):
     mixed = []
     for j in range(q_ref.shape[1] // size):
         cols = slice(j * size, (j + 1) * size)
@@ -60,12 +60,21 @@
         weights = jnp.exp(scores - jnp.max(scores, axis=0, keepdims=True))
         weights = weights * (1.0 / jnp.sum(weights, axis=0, keepdims=True))
         mixed.append(contract_rows(weights.astype(jnp.bfloat16), v_ref[:, cols]))
-    out_ref[...] = jnp.concatenate(mixed, axis=1).astype(out_ref.dtype)
-
-
-def attention(where, q, k, v):
-    kernel = functools.partial(attention_kernel, size=q.shape[1] // HEADS)
-    return call(kernel, [bf16(*q.shape)], "attention")(where, q, k, v)[0]
+    half = bundle[0].shape[1]
+    mixed = jnp.concatenate(mixed, axis=1).astype(out_ref.dtype)
+    out_ref[...] = mixed
+    theirs = pl.ds(pl.multiple_of((1 - where_ref[0]) * half, half), half)
+    bundle[0][...] = mixed[:, :half]
+    bundle[1][...] = mixed[:, half:]
+    bundle[2][...] = stream[:, theirs]
+    bundle[3][...] = earlier[:, theirs]
+
+
+def attention(where, q, k, v, stream, earlier):
+    patches, width = q.shape
+    kernel = functools.partial(attention_kernel, size=width // HEADS)
+    shapes = [bf16(patches, width)] + [bf16(patches, width // 2)] * 4
+    return call(kernel, shapes, "attention")(where, q, k, v, stream, earlier)
 
 
 def gram_kernel(where_ref, hidden_ref, kept_ref, *rest, parted):
@@ -116,16 +125,18 @@
             full[pl.ds(at, rows), :] = piece[j * rows : (j + 1) * rows, :]
 
 
-def branch_kernel(where_ref, mixed_own, mixed_other, stream, earlier, others, *rest):
+def branch_kernel(where_ref, mixed_own, stream, earlier, *rest):
+    others, rest = rest[:4], rest[4:]
     *pieces, blend_ref, stats_ref, full = rest
     put_in_order(where_ref, pieces, full)
     patches, half = stream.shape[0], blend_ref.shape[1]
     columns = pl.ds(pl.multiple_of(where_ref[0] * half, half), half)
-    streams = (stream[:, columns], others[0])
-    earliers = (earlier[:, columns], others[1])
-    for i, mixed in enumerate((mixed_own, mixed_other)):
+    mixeds = (mixed_own[...], jnp.concatenate([others[0][...], others[1][...]], axis=1))
+    streams = (stream[:, columns], others[2][...])
+    earliers = (earlier[:, columns], others[3][...])
+    for i in range(2):
         layer_out = streams[i].astype(jnp.float32) + jnp.dot(
-            mixed[...], full[...], preferred_element_type=jnp.float32
+            mixeds[i], full[...], preferred_element_type=jnp.float32
         )
         center = jnp.mean(layer_out, axis=0, keepdims=True)
         away = layer_out - center
@@ -179,14 +190,14 @@
     return [jax.ShapeDtypeStruct((rows // 2 + TAIL, width), jnp.int16), f32(rows // 2, width)]
 
 
-def first_kernel(where_ref, mine, theirs, send_ref, keep_ref, total):
-    total[...] = mine[...] + theirs[...]
+def first_kernel(where_ref, mine, t0, t1, send_ref, keep_ref, total):
+    total[...] = mine[...] + jnp.concatenate([t0[...], t1[...]], axis=0)
     halve(total, where_ref, send_ref, keep_ref)
 
 
 def first_step(where, mine, theirs):
     scratch = [pltpu.VMEM(mine.shape, jnp.float32)]
-    return call(first_kernel, halved_shapes(*mine.shape), "first_step", scratch)(where, mine, theirs)
+    return call(first_kernel, halved_shapes(*mine.shape), "first_step", scratch)(where, mine, *theirs)
 
 
 def second_kernel(where_ref, keep, codes, own_ref, *rest):
@@ -313,47 +324,51 @@
             jnp.concatenate(theirs + mine, axis=1),
         )
 
-    out_piece = jnp.concatenate([my_half(out_weight), swap(other_half(out_weight), CORE)], axis=0)
+    rows = out_weight.shape[0]
+    got = swap(jnp.concatenate([other_half(out_weight), other_half(pred_weight)], axis=0), CORE)
+    out_piece = jnp.concatenate([my_half(out_weight), got[:rows]], axis=0)
+    pred_mine, pred_theirs = my_half(pred_weight), got[rows:]
+    weights = jnp.concatenate([pred_mine, pred_mine, pred_theirs, pred_theirs], axis=0)
+
+    def attend(*anchors):
+        q = after(queries, *anchors) if anchors else queries
+        return attention(where, q[0], key_rows[0], value_rows[0], stream[0], earlier[0])
+
     if by_pairs:
-        z1, z2, y0 = swap(out_piece, NEXT_Z), swap(out_piece, FAR_Z), swap(out_piece, NEXT_Y)
+        z2, z1, y0 = swap(out_piece, FAR_Z), swap(out_piece, NEXT_Z), swap(out_piece, NEXT_Y)
+        y1, y2 = swap(z1, NEXT_Y), swap(after(z2, y0), NEXT_Y)
         z3 = swap(z2, NEXT_Z)
-        y1, y2, y3 = swap(z1, NEXT_Y), swap(z2, NEXT_Y), swap(z3, NEXT_Y)
+        y3 = swap(after(z3, y1), NEXT_Y)
         out_pieces = [out_piece, y0, z1, y1, z2, y2, z3, y3]
+        hidden = decoder_hidden
+        gram_mine, gram_theirs, sum_own = gram(where, hidden, kept_index[0], (chips, dec // parts))
+        sum_other = swap(sum_own, CORE)
+        gram_theirs = [swap(g, CORE) for g in jnp.split(gram_theirs, 2)]
+        mixed_own, *bundle = attend(z3)
+        others = [swap(b, CORE) for b in bundle]
+        send, keep = first_step(where, after(gram_mine, y0), gram_theirs)
+        own, *codes = second_step(where, after(keep, z3,y1), swap(send, NEXT_Y))
+        codes = [swap(c, NEXT_Z * (m + 1)) for m, c in enumerate(codes)]
+        (gram_rows,) = last_step(where, after(own, y2), codes)
     else:
-        rows = out_weight.shape[0]
         got = lax.all_gather(out_piece, "dp", axis_index_groups=same_core).reshape(chips, 2, rows, half)
         out_pieces = [jnp.where(core == 0, got, got[:, ::-1]).reshape(width, half)]
-
-    hidden = after(decoder_hidden, out_piece)
-    if by_pairs:
-        gram_mine, gram_theirs, sum_own = gram(where, hidden, kept_index[0], (chips, dec // parts))
-        send, keep = first_step(where, gram_mine, swap(gram_theirs, CORE))
-        own, *codes = second_step(where, keep, swap(send, NEXT_Y))
-        codes = [swap(c, NEXT_Z * (m + 1)) for m, c in enumerate(codes)]
-        (gram_rows,) = last_step(where, own, codes)
-    else:
-        gram_all, sum_own = gram(where, hidden, kept_index[0], None)
+        gram_all, sum_own = gram(where, decoder_hidden, kept_index[0], None)
+        sum_other = swap(sum_own, CORE)
+        mixed_own, *bundle = attend()
+        others = [swap(b, CORE) for b in bundle]
         gram_rows = lax.psum_scatter(gram_all, "dp", scatter_dimension=0, tiled=True)
         high = gram_rows.astype(jnp.bfloat16)
         low = (gram_rows - high.astype(jnp.float32)).astype(jnp.bfloat16)
         gram_rows = jnp.concatenate([high, low], axis=0)
     grams = jnp.concatenate([gram_rows, swap(gram_rows, CORE)], axis=0)
-    pred = after(pred_weight, out_piece)
-    pred_mine, pred_theirs = my_half(pred), swap(other_half(pred), CORE)
-    weights = jnp.concatenate([pred_mine, pred_mine, pred_theirs, pred_theirs], axis=0)
-
-    mixed_own = attention(where, after(queries, out_piece)[0], key_rows[0], value_rows[0])
-    mixed_other = swap(mixed_own, CORE)
-    others = jnp.concatenate([other_half(after(stream, out_piece)), other_half(earlier)], axis=0)
-    others = swap(others, CORE)
-    sum_other = swap(sum_own, CORE)
-
-    blend, stats = branch(where, mixed_own, mixed_other, stream[0], earlier[0], others, *out_pieces)
+
+    blend, stats = branch(where, mixed_own, stream[0], earlier[0], *others, *out_pieces)
     stats_other = swap(stats, CORE)
 
-    def term(cut, coded):
+    def term(cut, coded, *before):
         return targets_and_term(
-            where, blend, stats, stats_other, sum_own, sum_other, grams, weights, cut, coded
+            where, blend, stats, after(stats_other, *before), sum_own, sum_other, grams, weights, cut, coded
         )
 
     if not by_pairs:
@@ -367,14 +382,18 @@
         send = lax.dynamic_index_in_dim(summed, 1 - core, 0, keepdims=False)
         return targets, side_by_side([keep], [swap(send, CORE)])
 
-    steps = [term((j, CUTS), True) for j in range(CUTS)]
-    received = [swap(send, NEXT_Y) for _, _, send, _ in steps]
-    targets = side_by_side([s[0] for s in steps], [swap(s[1], CORE) for s in steps])[None]
-    received[-1] = after(received[-1], targets)
+    steps, rest, received = [], [], []
+    for j in range(CUTS):
+        steps.append(term((j, CUTS), True, *rest))
+        rest.append(swap(steps[j][1], CORE))
+        received.append(swap(steps[j][2], NEXT_Y))
+    targets = side_by_side([s[0] for s in steps], rest)[None]
     mine, theirs = [], []
-    for (_, _, _, keep), codes in zip(steps, received):
-        own, *codes = second_step(where, keep, codes)
+    for j in range(CUTS):
+        own, *codes = second_step(where, steps[j][3], received[j])
         codes = [swap(c, NEXT_Z * (m + 1)) for m, c in enumerate(codes)]
+        if j == 0:
+            own = after(own, targets)
         keep, send = last_step(where, own, codes, scale)
         mine.append(keep)
         theirs.append(swap(send, CORE))

time: 110 us -> 91.5 us (0.83)
  waiting for transfers between devices: 47.5 us -> 31.7 us
  starting transfers between devices: 33.1 us -> 31.1 us
  Pallas kernels: 21 us -> 19.6 us
    ppermute x31 -> x33, waiting for transfers between devices: 47.5 us -> 31.7 us  [swap(): return lax.ppermute(x, AXES, pairs)]
    ppermute x31 -> x33, starting transfers between devices: 33.1 us -> 31.1 us  [swap(): return lax.ppermute(x, AXES, pairs)]
    pallas_call x12, Pallas kernels: 21 us -> 19.6 us  [run(): pl.pallas_call(kernel, out_shape=tuple(out_shape), in_specs=[pl.BlockSpec...]
    unnamed x16 -> x14, local copies, waits for them, and re-layouts: 2.6 us -> 2.59 us
  transfers between devices with their start and end apart: 31 -> 33, of which waited for: 13 -> 12; matrix products, arithmetic and copies ran while one was open for 3% -> 3% of each run, Pallas kernels for 13% -> 19%
where the time goes in v4:
time: 91.5 us; the launch traced here: 91.3 us
  waiting for transfers between devices  31.7 us (35%)
  starting transfers between devices  31.1 us (34%)
  Pallas kernels  19.6 us (21%)
  local copies, waits for them, and re-layouts  4.63 us (5%)
  other arithmetic  3.38 us (4%)
    ppermute x33, waiting for transfers between devices, swap(): return lax.ppermute(x, AXES, pairs)  31.7 us
    ppermute x33, starting transfers between devices, swap(): return lax.ppermute(x, AXES, pairs)  31.1 us
    pallas_call x12, Pallas kernels, run(): pl.pallas_call(kernel, out_shape=tuple(out_shape), in_specs=[pl.BlockSpec...  19.6 us
    select_n x2, other arithmetic, side_by_side(): jnp.where(core == 0, jnp.concatenate(mine + theirs, axis=1), jnp.concaten...  3.22 us
    unnamed x14, local copies, waits for them, and re-layouts  2.59 us
    dynamic_slice x2, local copies, waits for them, and re-layouts, my_half(): return lax.dynamic_slice_in_dim(x, core * half, half, axis=-1)  1.95 us
  transfers between devices with their start and end apart: 33, of which 12 were waited for; matrix products, arithmetic and copies ran while one was open for 3% of the time, Pallas kernels for 19%

profile of v4, /device:TPU:0, one launch (start us, length us, event | category | flops | bytes accessed | tf_op | source)
XLA Modules:
  0.0 91.3 jit_solution(8076415602564069983)
XLA Ops:
  0.7 1.0 %constant_dynamic-slice_fusion.3 = (bf16[96,768]{1,0:T(8,128)(2,1)S(1)}, bf16[96,768]{1,0:T(8,128)(2,1)S(1)}) fusion(bf16[96,1536]{1,0:T(8,128)(2,1)} %param.14, s32[]{:T(128)S(6)} %select_n.45, s32[]{:T(128)S(6)} %select_n.46), kind=kLoop, calls=%fused_computation.9 | loop fusion | bytes 589832 | tf_op jit(solution)/shard_map/dynamic_slice | solution.py:315
  1.7 0.9 %constant_dynamic-slice_fusion = (bf16[48,768]{1,0:T(8,128)(2,1)S(1)}, bf16[48,768]{1,0:T(8,128)(2,1)S(1)}) fusion(bf16[48,1536]{1,0:T(8,128)(2,1)} %param.15, s32[]{:T(128)S(6)} %select_n.45, s32[]{:T(128)S(6)} %select_n.46), kind=kLoop, calls=%fused_computation.6 | loop fusion | bytes 294920 | tf_op jit(solution)/shard_map/dynamic_slice | solution.py:315
  2.6 0.5 collective-permute-start
  3.1 0.1 pad_add_fusion.where_ref
  3.2 1.9 %copy-done.2 = bf16[1,8,256,768]{3,2,1,0:T(8,128)(2,1)S(1)} copy-done((bf16[1,8,256,768]{3,2,1,0:T(8,128)(2,1)S(1)}, bf16[1,8,256,768]{3,2,1,0:T(8,128)(2,1)}, u32[]{:S(2)}) %copy-start.2) | copy-done | bytes 3145752
  5.1 0.7 copy-done.6
  5.8 4.2 %gram.1 = (f32[384,768]{1,0:T(8,128)S(1)}, f32[384,768]{1,0:T(8,128)S(1)}, bf16[256,768]{1,0:T(8,128)(2,1)S(1)}) custom-call(s32[2]{0:T(128)S(1)} %pad_add_fusion.where_ref, bf16[1,8,256,768]{3,2,1,0:T(8,128)(2,1)S(1)} %copy-done.2, s32[8,64]{1,0:T(8,128)S(1)} %bitcast.21), custom_call_target="tpu_custom_call" | custom-call | bytes 1000 | tf_op jit(solution)/shard_map/gram/pallas_call | solution.py:26
  10.0 0.1 fusion
  10.1 0.1 collective-permute-start.14
  10.2 0.5 collective-permute-start.15
  10.7 2.7 %collective-permute-start.7 = (bf16[192,768]{1,0:T(8,128)(2,1)S(1)}, bf16[192,768]{1,0:T(8,128)(2,1)S(1)}, u32[]{:S(2)}, u32[]{:S(2)}) collective-permute-start(bf16[192,768]{1,0:T(8,128)(2,1)S(1)} %pad_maximum_fusion.rest_4_), channel_id=1, source_target_pairs={{0,2},{1,3},{2,0},{3,1},{4,6},{5,7},{6,4},{7,5},{8,10},{9,11},{10,... | collective-permute-start | bytes 884744 | tf_op jit(solution)/shard_map/ppermute | solution.py:312
  13.4 2.6 %collective-permute-start.1 = (bf16[192,768]{1,0:T(8,128)(2,1)S(1)}, bf16[192,768]{1,0:T(8,128)(2,1)S(1)}, u32[]{:S(2)}, u32[]{:S(2)}) collective-permute-start(bf16[192,768]{1,0:T(8,128)(2,1)S(1)} %pad_maximum_fusion.rest_4_), channel_id=1, source_target_pairs={{0,8},{1,9},{2,10},{3,11},{4,12},{5,13},{6,14},{7,15},{8,0},{9,1},... | collective-permute-start | bytes 884744 | tf_op jit(solution)/shard_map/ppermute | solution.py:312
  15.9 1.6 %collective-permute-start.8 = (bf16[192,768]{1,0:T(8,128)(2,1)S(1)}, bf16[192,768]{1,0:T(8,128)(2,1)S(1)}, u32[]{:S(2)}, u32[]{:S(2)}) collective-permute-start(bf16[192,768]{1,0:T(8,128)(2,1)S(1)} %pad_maximum_fusion.rest_4_), channel_id=1, source_target_pairs={{0,4},{1,5},{2,6},{3,7},{4,0},{5,1},{6,2},{7,3},{8,12},{9,13},{10,... | collective-permute-start | bytes 884744 | tf_op jit(solution)/shard_map/ppermute | solution.py:312
  17.5 3.4 %collective-permute-done.7.rest_5_ = bf16[192,768]{1,0:T(8,128)(2,1)S(1)} collective-permute-done((bf16[192,768]{1,0:T(8,128)(2,1)S(1)}, bf16[192,768]{1,0:T(8,128)(2,1)S(1)}, u32[]{:S(2)}, u32[]{:S(2)}) %collective-permute-start.7) | collective-permute-done | bytes 294944 | tf_op jit(solution)/shard_map/ppermute | solution.py:312
  21.0 0.9 first_step.1
  21.9 1.8 %collective-permute-start.16 = (s16[208,768]{1,0:T(8,128)(2,1)S(1)}, s16[208,768]{1,0:T(8,128)(2,1)S(1)}, u32[]{:S(2)}, u32[]{:S(2)}) collective-permute-start(s16[208,768]{1,0:T(8,128)(2,1)S(1)} %get-tuple-element.62), channel_id=1, source_target_pairs={{0,2},{1,3},{2,0},{3,1},{4,6},{5,7},{6,4},{7,5},{8,10},{9,11},{10,... | collective-permute-start | bytes 958472 | tf_op jit(solution)/shard_map/ppermute | solution.py:312
  23.7 6.0 %collective-permute-done.1.rest_8_ = bf16[192,768]{1,0:T(8,128)(2,1)S(1)} collective-permute-done((bf16[192,768]{1,0:T(8,128)(2,1)S(1)}, bf16[192,768]{1,0:T(8,128)(2,1)S(1)}, u32[]{:S(2)}, u32[]{:S(2)}) %collective-permute-start.1) | collective-permute-done | bytes 294944 | tf_op jit(solution)/shard_map/ppermute | solution.py:312
  29.8 0.6 collective-permute-start.2
  30.3 0.5 collective-permute-start.9
  30.9 1.5 %collective-permute-start.10 = (bf16[192,768]{1,0:T(8,128)(2,1)S(1)}, bf16[192,768]{1,0:T(8,128)(2,1)S(1)}, u32[]{:S(2)}, u32[]{:S(2)}) collective-permute-start(bf16[192,768]{1,0:T(8,128)(2,1)S(1)} %collective-permute-done.1.rest_8_), channel_id=1, source_target_pairs={{0,2},{1,3},{2,0},{3,1},{4,6},{5,7},{6,4},{7,5},{8,10},{9,11},{10,... | collective-permute-start | bytes 884744 | tf_op jit(solution)/shard_map/ppermute | solution.py:312
  32.4 5.6 %collective-permute-done.2.rest_10_ = bf16[192,768]{1,0:T(8,128)(2,1)S(1)} collective-permute-done((bf16[192,768]{1,0:T(8,128)(2,1)S(1)}, bf16[192,768]{1,0:T(8,128)(2,1)S(1)}, u32[]{:S(2)}, u32[]{:S(2)}) %collective-permute-start.2) | collective-permute-done | bytes 294944 | tf_op jit(solution)/shard_map/ppermute | solution.py:312
  37.9 2.3 %collective-permute-done.9.rest_7_ = bf16[192,768]{1,0:T(8,128)(2,1)S(1)} collective-permute-done((bf16[192,768]{1,0:T(8,128)(2,1)S(1)}, bf16[192,768]{1,0:T(8,128)(2,1)S(1)}, u32[]{:S(2)}, u32[]{:S(2)}) %collective-permute-start.9) | collective-permute-done | bytes 294944 | tf_op jit(solution)/shard_map/ppermute | solution.py:312
  40.3 0.0 collective-permute-done.16.codes
  40.3 0.8 second_step.3
  41.1 1.5 %collective-permute-start.17 = (s16[64,768]{1,0:T(8,128)(2,1)S(1)}, s16[64,768]{1,0:T(8,128)(2,1)S(1)}, u32[]{:S(2)}, u32[]{:S(2)}) collective-permute-start(s16[64,768]{1,0:T(8,128)(2,1)S(1)} %get-tuple-element.65), channel_id=1, source_target_pairs={{0,4},{1,5},{2,6},{3,7},{4,0},{5,1},{6,2},{7,3},{8,12},{9,13},{10,... | collective-permute-start | bytes 294920 | tf_op jit(solution)/shard_map/ppermute | solution.py:312
  42.6 2.0 %collective-permute-start.18 = (s16[64,768]{1,0:T(8,128)(2,1)S(1)}, s16[64,768]{1,0:T(8,128)(2,1)S(1)}, u32[]{:S(2)}, u32[]{:S(2)}) collective-permute-start(s16[64,768]{1,0:T(8,128)(2,1)S(1)} %get-tuple-element.66), channel_id=1, source_target_pairs={{0,8},{1,9},{2,10},{3,11},{4,12},{5,13},{6,14},{7,15},{8,0},{9,1},... | collective-permute-start | bytes 294920 | tf_op jit(solution)/shard_map/ppermute | solution.py:312
  44.6 1.4 %collective-permute-start.19 = (s16[64,768]{1,0:T(8,128)(2,1)S(1)}, s16[64,768]{1,0:T(8,128)(2,1)S(1)}, u32[]{:S(2)}, u32[]{:S(2)}) collective-permute-start(s16[64,768]{1,0:T(8,128)(2,1)S(1)} %get-tuple-element.67), channel_id=1, source_target_pairs={{0,12},{1,13},{2,14},{3,15},{4,8},{5,9},{6,10},{7,11},{8,4},{9,5},... | collective-permute-start | bytes 294920 | tf_op jit(solution)/shard_map/ppermute | solution.py:312
  46.0 0.5 collective-permute-start.11
  46.5 3.5 %attention.1 = (bf16[256,1536]{1,0:T(8,128)(2,1)S(1)}, bf16[256,768]{1,0:T(8,128)(2,1)S(1)}, bf16[256,768]{1,0:T(8,128)(2,1)S(1)}, bf16[256,768]{1,0:T(8,128)(2,1)S(1)}, bf16[256,768]{1,0:T(8,128)(2,1)S(1)}) custom-call(s32[2]{0:T(128)S(1)} %pad_add_fusion.where_ref, bf16[256,1536]{1,0:T(8,128)(2,1)S(1)} %bitcast.16, bf16[256,1536]{1,0:T(8,128)(2,1)S(1)} %bitcast.17, ...), custom_call_target="tpu_custom_call" | custom-call | bytes 1000 | tf_op jit(solution)/shard_map/attention/pallas_call | solution.py:26
  50.0 0.1 collective-permute-start.3
  50.1 0.5 collective-permute-start.4
  50.6 1.0 %collective-permute-done.18.c2 = s16[64,768]{1,0:T(8,128)(2,1)S(1)} collective-permute-done((s16[64,768]{1,0:T(8,128)(2,1)S(1)}, s16[64,768]{1,0:T(8,128)(2,1)S(1)}, u32[]{:S(2)}, u32[]{:S(2)}) %collective-permute-start.18) | collective-permute-done | bytes 98336 | tf_op jit(solution)/shard_map/ppermute | solution.py:312
  51.6 0.5 collective-permute-start.6
  52.1 0.6 collective-permute-done.11.rest_11_
  52.7 0.6 last_step.3
  53.4 0.6 collective-permute-start.20
  53.9 2.8 %branch.1 = (f32[512,768]{1,0:T(8,128)S(1)}, f32[512,128]{1,0:T(8,128)S(1)}) custom-call(s32[2]{0:T(128)S(1)} %pad_add_fusion.where_ref, bf16[256,1536]{1,0:T(8,128)(2,1)S(1)} %get-tuple-element.47.mixed_own, bf16[256,1536]{1,0:T(8,128)(2,1)S(1)} %bitcast.13, bf16[256,1536]{1,0:T(8,128)(2,1)S(1)} %bitcast.15, ...), custom_call_target="tpu_custom_call" | custom-call | bytes 1000 | tf_op jit(solution)/shard_map/branch/pallas_call | solution.py:26
  56.7 0.1 collective-permute-start.12
  56.9 1.4 %collective-permute-done.12.stats_other = f32[512,128]{1,0:T(8,128)S(1)} collective-permute-done((f32[512,128]{1,0:T(8,128)S(1)}, f32[512,128]{1,0:T(8,128)S(1)}, u32[]{:S(2)}, u32[]{:S(2)}) %collective-permute-start.12) | collective-permute-done | bytes 262176 | tf_op jit(solution)/shard_map/ppermute | solution.py:312
  58.3 1.9 %targets.2 = (f32[256,384]{1,0:T(8,128)S(1)}, f32[256,384]{1,0:T(8,128)S(1)}, s16[400,384]{1,0:T(8,128)(2,1)S(1)}, f32[384,384]{1,0:T(8,128)S(1)}) custom-call(s32[2]{0:T(128)S(1)} %pad_add_fusion.where_ref, f32[512,768]{1,0:T(8,128)S(1)} %get-tuple-element.54.blend, f32[512,128]{1,0:T(8,128)S(1)} %get-tuple-element.55.stats, ...), custom_call_target="tpu_custom_call" | custom-call | bytes 1000 | tf_op jit(solution)/shard_map/targets/pallas_call | solution.py:26
  60.2 0.2 collective-permute-start.21
  60.4 1.1 %collective-permute-start.23 = (s16[400,384]{1,0:T(8,128)(2,1)S(1)}, s16[400,384]{1,0:T(8,128)(2,1)S(1)}, u32[]{:S(2)}, u32[]{:S(2)}) collective-permute-start(s16[400,384]{1,0:T(8,128)(2,1)S(1)} %get-tuple-element.74), channel_id=1, source_target_pairs={{0,2},{1,3},{2,0},{3,1},{4,6},{5,7},{6,4},{7,5},{8,10},{9,11},{10,... | collective-permute-start | bytes 921608 | tf_op jit(solution)/shard_map/ppermute | solution.py:312
  61.5 0.5 collective-permute-done.21
  62.0 2.1 %targets.3 = (f32[256,384]{1,0:T(8,128)S(1)}, f32[256,384]{1,0:T(8,128)S(1)}, s16[400,384]{1,0:T(8,128)(2,1)S(1)}, f32[384,384]{1,0:T(8,128)S(1)}) custom-call(s32[2]{0:T(128)S(1)} %pad_add_fusion.where_ref, f32[512,768]{1,0:T(8,128)S(1)} %get-tuple-element.54.blend, f32[512,128]{1,0:T(8,128)S(1)} %get-tuple-element.55.stats, ...), custom_call_target="tpu_custom_call" | custom-call | bytes 1000 | tf_op jit(solution)/shard_map/targets/pallas_call | solution.py:26
  64.1 0.2 collective-permute-start.22
  64.3 1.1 %collective-permute-start.27 = (s16[400,384]{1,0:T(8,128)(2,1)S(1)}, s16[400,384]{1,0:T(8,128)(2,1)S(1)}, u32[]{:S(2)}, u32[]{:S(2)}) collective-permute-start(s16[400,384]{1,0:T(8,128)(2,1)S(1)} %get-tuple-element.82), channel_id=1, source_target_pairs={{0,2},{1,3},{2,0},{3,1},{4,6},{5,7},{6,4},{7,5},{8,10},{9,11},{10,... | collective-permute-start | bytes 921608 | tf_op jit(solution)/shard_map/ppermute | solution.py:312
  65.3 5.2 %collective-permute-done.23.codes = s16[400,384]{1,0:T(8,128)(2,1)S(1)} collective-permute-done((s16[400,384]{1,0:T(8,128)(2,1)S(1)}, s16[400,384]{1,0:T(8,128)(2,1)S(1)}, u32[]{:S(2)}, u32[]{:S(2)}) %collective-permute-start.23) | collective-permute-done | bytes 307232 | tf_op jit(solution)/shard_map/ppermute | solution.py:312
  70.5 0.8 second_step.4
  71.3 1.0 %collective-permute-start.24 = (s16[112,384]{1,0:T(8,128)(2,1)S(1)}, s16[112,384]{1,0:T(8,128)(2,1)S(1)}, u32[]{:S(2)}, u32[]{:S(2)}) collective-permute-start(s16[112,384]{1,0:T(8,128)(2,1)S(1)} %get-tuple-element.77), channel_id=1, source_target_pairs={{0,4},{1,5},{2,6},{3,7},{4,0},{5,1},{6,2},{7,3},{8,12},{9,13},{10,... | collective-permute-start | bytes 258056 | tf_op jit(solution)/shard_map/ppermute | solution.py:312
  72.3 2.2 %collective-permute-start.25 = (s16[112,384]{1,0:T(8,128)(2,1)S(1)}, s16[112,384]{1,0:T(8,128)(2,1)S(1)}, u32[]{:S(2)}, u32[]{:S(2)}) collective-permute-start(s16[112,384]{1,0:T(8,128)(2,1)S(1)} %get-tuple-element.78), channel_id=1, source_target_pairs={{0,8},{1,9},{2,10},{3,11},{4,12},{5,13},{6,14},{7,15},{8,0},{9,1},... | collective-permute-start | bytes 258056 | tf_op jit(solution)/shard_map/ppermute | solution.py:312
  74.5 1.2 %collective-permute-start.26 = (s16[112,384]{1,0:T(8,128)(2,1)S(1)}, s16[112,384]{1,0:T(8,128)(2,1)S(1)}, u32[]{:S(2)}, u32[]{:S(2)}) collective-permute-start(s16[112,384]{1,0:T(8,128)(2,1)S(1)} %get-tuple-element.79), channel_id=1, source_target_pairs={{0,12},{1,13},{2,14},{3,15},{4,8},{5,9},{6,10},{7,11},{8,4},{9,5},... | collective-permute-start | bytes 258056 | tf_op jit(solution)/shard_map/ppermute | solution.py:312
  75.8 0.8 collective-permute-done.27.codes
  76.5 0.8 second_step.5
  77.3 1.0 %collective-permute-start.28 = (s16[112,384]{1,0:T(8,128)(2,1)S(1)}, s16[112,384]{1,0:T(8,128)(2,1)S(1)}, u32[]{:S(2)}, u32[]{:S(2)}) collective-permute-start(s16[112,384]{1,0:T(8,128)(2,1)S(1)} %get-tuple-element.84), channel_id=1, source_target_pairs={{0,4},{1,5},{2,6},{3,7},{4,0},{5,1},{6,2},{7,3},{8,12},{9,13},{10,... | collective-permute-start | bytes 258056 | tf_op jit(solution)/shard_map/ppermute | solution.py:312
  78.4 2.2 %collective-permute-start.29 = (s16[112,384]{1,0:T(8,128)(2,1)S(1)}, s16[112,384]{1,0:T(8,128)(2,1)S(1)}, u32[]{:S(2)}, u32[]{:S(2)}) collective-permute-start(s16[112,384]{1,0:T(8,128)(2,1)S(1)} %get-tuple-element.85), channel_id=1, source_target_pairs={{0,8},{1,9},{2,10},{3,11},{4,12},{5,13},{6,14},{7,15},{8,0},{9,1},... | collective-permute-start | bytes 258056 | tf_op jit(solution)/shard_map/ppermute | solution.py:312
  80.6 1.2 %collective-permute-start.30 = (s16[112,384]{1,0:T(8,128)(2,1)S(1)}, s16[112,384]{1,0:T(8,128)(2,1)S(1)}, u32[]{:S(2)}, u32[]{:S(2)}) collective-permute-start(s16[112,384]{1,0:T(8,128)(2,1)S(1)} %get-tuple-element.86), channel_id=1, source_target_pairs={{0,12},{1,13},{2,14},{3,15},{4,8},{5,9},{6,10},{7,11},{8,4},{9,5},... | collective-permute-start | bytes 258056 | tf_op jit(solution)/shard_map/ppermute | solution.py:312
  81.8 2.5 %maximum_select_fusion = f32[1,256,1536]{2,1,0:T(8,128)} fusion(f32[1,256,384]{2,1,0:T(8,128)} %bitcast.11, f32[1,256,384]{2,1,0:T(8,128)S(1)} %bitcast.22, f32[1,256,384]{2,1,0:T(8,128)S(1)} %bitcast.20, f32[1,256,384]{2,1,0:T(8,128)S(1)} %bitcast.19, pred[]{:T(512)S(6)} %eq.6), kind=kLoop, calls=%fused_computation | loop fusion | flops 2752512 | bytes 3145729 | tf_op jit(solution)/shard_map/jit(_where)/select_n | solution.py:321
  84.3 0.6 last_step.4
  84.9 0.1 collective-permute-start.31
  85.0 3.5 %collective-permute-done.29.c2 = s16[112,384]{1,0:T(8,128)(2,1)S(1)} collective-permute-done((s16[112,384]{1,0:T(8,128)(2,1)S(1)}, s16[112,384]{1,0:T(8,128)(2,1)S(1)}, u32[]{:S(2)}, u32[]{:S(2)}) %collective-permute-start.29) | collective-permute-done | bytes 86048 | tf_op jit(solution)/shard_map/ppermute | solution.py:312
  88.6 0.6 last_step.5
  89.2 0.1 collective-permute-start.32
  89.3 1.2 %collective-permute-done.32 = f32[48,384]{1,0:T(8,128)S(1)} collective-permute-done((f32[48,384]{1,0:T(8,128)S(1)}, f32[48,384]{1,0:T(8,128)S(1)}, u32[]{:S(2)}, u32[]{:S(2)}) %collective-permute-start.32) | collective-permute-done | bytes 73760 | tf_op jit(solution)/shard_map/ppermute | solution.py:312
  90.5 0.7 maximum_select_fusion.1
  (40 shorter events, 0.2 us)
Async XLA Ops:
  2.6 8.0 %collective-permute-start = (bf16[144,768]{1,0:T(8,128)(2,1)S(1)}, bf16[144,768]{1,0:T(8,128)(2,1)S(1)}, u32[]{:S(2)}, u32[]{:S(2)}) collective-permute-start(bf16[144,768]{1,0:T(8,128)(2,1)S(1)} %pad_maximum_fusion.3), channel_id=1, source_target_pairs={{0,1},{1,0},{2,3},{3,2},{4,5},{5,4},{6,7},{7,6},{8,9},{9,8},{10,11... | collective-permute-start | bytes 663560 | tf_op jit(solution)/shard_map/ppermute | solution.py:312
  3.2 1.9 %copy-start.2 = (bf16[1,8,256,768]{3,2,1,0:T(8,128)(2,1)S(1)}, bf16[1,8,256,768]{3,2,1,0:T(8,128)(2,1)}, u32[]{:S(2)}) copy-start(bf16[1,8,256,768]{3,2,1,0:T(8,128)(2,1)} %hidden_ref.1) | copy-start | bytes 9437188
  5.1 0.7 copy-start.6
  10.1 10.9 %collective-permute-start.14 = (f32[192,768]{1,0:T(8,128)S(1)}, f32[192,768]{1,0:T(8,128)S(1)}, u32[]{:S(2)}, u32[]{:S(2)}) collective-permute-start(f32[192,768]{1,0:T(8,128)S(1)} %get-tuple-element.91), channel_id=1, source_target_pairs={{0,1},{1,0},{2,3},{3,2},{4,5},{5,4},{6,7},{7,6},{8,9},{9,8},{10,11... | collective-permute-start | bytes 1769480 | tf_op jit(solution)/shard_map/ppermute | solution.py:312
  10.2 10.8 %collective-permute-start.15 = (f32[192,768]{1,0:T(8,128)S(1)}, f32[192,768]{1,0:T(8,128)S(1)}, u32[]{:S(2)}, u32[]{:S(2)}) collective-permute-start(f32[192,768]{1,0:T(8,128)S(1)} %get-tuple-element.90), channel_id=1, source_target_pairs={{0,1},{1,0},{2,3},{3,2},{4,5},{5,4},{6,7},{7,6},{8,9},{9,8},{10,11... | collective-permute-start | bytes 1769480 | tf_op jit(solution)/shard_map/ppermute | solution.py:312
  10.7 35.8 %copy-start.5 = (bf16[1,256,1536]{2,1,0:T(8,128)(2,1)S(1)}, bf16[1,256,1536]{2,1,0:T(8,128)(2,1)}, u32[]{:S(2)}) copy-start(bf16[1,256,1536]{2,1,0:T(8,128)(2,1)} %param.11) | copy-start | bytes 2359300
  10.7 10.3 %collective-permute-start.7 = (bf16[192,768]{1,0:T(8,128)(2,1)S(1)}, bf16[192,768]{1,0:T(8,128)(2,1)S(1)}, u32[]{:S(2)}, u32[]{:S(2)}) collective-permute-start(bf16[192,768]{1,0:T(8,128)(2,1)S(1)} %pad_maximum_fusion.rest_4_), channel_id=1, source_target_pairs={{0,2},{1,3},{2,0},{3,1},{4,6},{5,7},{6,4},{7,5},{8,10},{9,11},{10,... | collective-permute-start | bytes 884744 | tf_op jit(solution)/shard_map/ppermute | solution.py:312
  13.4 16.4 %collective-permute-start.1 = (bf16[192,768]{1,0:T(8,128)(2,1)S(1)}, bf16[192,768]{1,0:T(8,128)(2,1)S(1)}, u32[]{:S(2)}, u32[]{:S(2)}) collective-permute-start(bf16[192,768]{1,0:T(8,128)(2,1)S(1)} %pad_maximum_fusion.rest_4_), channel_id=1, source_target_pairs={{0,8},{1,9},{2,10},{3,11},{4,12},{5,13},{6,14},{7,15},{8,0},{9,1},... | collective-permute-start | bytes 884744 | tf_op jit(solution)/shard_map/ppermute | solution.py:312
  15.9 14.4 %collective-permute-start.8 = (bf16[192,768]{1,0:T(8,128)(2,1)S(1)}, bf16[192,768]{1,0:T(8,128)(2,1)S(1)}, u32[]{:S(2)}, u32[]{:S(2)}) collective-permute-start(bf16[192,768]{1,0:T(8,128)(2,1)S(1)} %pad_maximum_fusion.rest_4_), channel_id=1, source_target_pairs={{0,4},{1,5},{2,6},{3,7},{4,0},{5,1},{6,2},{7,3},{8,12},{9,13},{10,... | collective-permute-start | bytes 884744 | tf_op jit(solution)/shard_map/ppermute | solution.py:312
  21.0 25.5 %copy-start = (bf16[1,256,1536]{2,1,0:T(8,128)(2,1)S(1)}, bf16[1,256,1536]{2,1,0:T(8,128)(2,1)}, u32[]{:S(2)}) copy-start(bf16[1,256,1536]{2,1,0:T(8,128)(2,1)} %param.12) | copy-start | bytes 2359300
  21.0 25.5 %copy-start.1 = (bf16[1,256,1536]{2,1,0:T(8,128)(2,1)S(1)}, bf16[1,256,1536]{2,1,0:T(8,128)(2,1)}, u32[]{:S(2)}) copy-start(bf16[1,256,1536]{2,1,0:T(8,128)(2,1)} %param.13) | copy-start | bytes 2359300
  21.0 25.5 %copy-start.3 = (bf16[1,256,1536]{2,1,0:T(8,128)(2,1)S(1)}, bf16[1,256,1536]{2,1,0:T(8,128)(2,1)}, u32[]{:S(2)}) copy-start(bf16[1,256,1536]{2,1,0:T(8,128)(2,1)} %param.9) | copy-start | bytes 2359300
  21.0 25.5 %copy-start.4 = (bf16[1,256,1536]{2,1,0:T(8,128)(2,1)S(1)}, bf16[1,256,1536]{2,1,0:T(8,128)(2,1)}, u32[]{:S(2)}) copy-start(bf16[1,256,1536]{2,1,0:T(8,128)(2,1)} %param.10) | copy-start | bytes 2359300
  21.9 18.4 %collective-permute-start.16 = (s16[208,768]{1,0:T(8,128)(2,1)S(1)}, s16[208,768]{1,0:T(8,128)(2,1)S(1)}, u32[]{:S(2)}, u32[]{:S(2)}) collective-permute-start(s16[208,768]{1,0:T(8,128)(2,1)S(1)} %get-tuple-element.62), channel_id=1, source_target_pairs={{0,2},{1,3},{2,0},{3,1},{4,6},{5,7},{6,4},{7,5},{8,10},{9,11},{10,... | collective-permute-start | bytes 958472 | tf_op jit(solution)/shard_map/ppermute | solution.py:312
  29.8 8.2 %collective-permute-start.2 = (bf16[192,768]{1,0:T(8,128)(2,1)S(1)}, bf16[192,768]{1,0:T(8,128)(2,1)S(1)}, u32[]{:S(2)}, u32[]{:S(2)}) collective-permute-start(bf16[192,768]{1,0:T(8,128)(2,1)S(1)} %collective-permute-done.1.rest_8_), channel_id=1, source_target_pairs={{0,4},{1,5},{2,6},{3,7},{4,0},{5,1},{6,2},{7,3},{8,12},{9,13},{10,... | collective-permute-start | bytes 884744 | tf_op jit(solution)/shard_map/ppermute | solution.py:312
  30.3 9.9 %collective-permute-start.9 = (bf16[192,768]{1,0:T(8,128)(2,1)S(1)}, bf16[192,768]{1,0:T(8,128)(2,1)S(1)}, u32[]{:S(2)}, u32[]{:S(2)}) collective-permute-start(bf16[192,768]{1,0:T(8,128)(2,1)S(1)} %collective-permute-done.8.rest_6_), channel_id=1, source_target_pairs={{0,2},{1,3},{2,0},{3,1},{4,6},{5,7},{6,4},{7,5},{8,10},{9,11},{10,... | collective-permute-start | bytes 884744 | tf_op jit(solution)/shard_map/ppermute | solution.py:312
  30.9 19.1 %collective-permute-start.10 = (bf16[192,768]{1,0:T(8,128)(2,1)S(1)}, bf16[192,768]{1,0:T(8,128)(2,1)S(1)}, u32[]{:S(2)}, u32[]{:S(2)}) collective-permute-start(bf16[192,768]{1,0:T(8,128)(2,1)S(1)} %collective-permute-done.1.rest_8_), channel_id=1, source_target_pairs={{0,2},{1,3},{2,0},{3,1},{4,6},{5,7},{6,4},{7,5},{8,10},{9,11},{10,... | collective-permute-start | bytes 884744 | tf_op jit(solution)/shard_map/ppermute | solution.py:312
  41.1 9.0 %collective-permute-start.17 = (s16[64,768]{1,0:T(8,128)(2,1)S(1)}, s16[64,768]{1,0:T(8,128)(2,1)S(1)}, u32[]{:S(2)}, u32[]{:S(2)}) collective-permute-start(s16[64,768]{1,0:T(8,128)(2,1)S(1)} %get-tuple-element.65), channel_id=1, source_target_pairs={{0,4},{1,5},{2,6},{3,7},{4,0},{5,1},{6,2},{7,3},{8,12},{9,13},{10,... | collective-permute-start | bytes 294920 | tf_op jit(solution)/shard_map/ppermute | solution.py:312
  42.6 8.9 %collective-permute-start.18 = (s16[64,768]{1,0:T(8,128)(2,1)S(1)}, s16[64,768]{1,0:T(8,128)(2,1)S(1)}, u32[]{:S(2)}, u32[]{:S(2)}) collective-permute-start(s16[64,768]{1,0:T(8,128)(2,1)S(1)} %get-tuple-element.66), channel_id=1, source_target_pairs={{0,8},{1,9},{2,10},{3,11},{4,12},{5,13},{6,14},{7,15},{8,0},{9,1},... | collective-permute-start | bytes 294920 | tf_op jit(solution)/shard_map/ppermute | solution.py:312
  44.6 7.0 %collective-permute-start.19 = (s16[64,768]{1,0:T(8,128)(2,1)S(1)}, s16[64,768]{1,0:T(8,128)(2,1)S(1)}, u32[]{:S(2)}, u32[]{:S(2)}) collective-permute-start(s16[64,768]{1,0:T(8,128)(2,1)S(1)} %get-tuple-element.67), channel_id=1, source_target_pairs={{0,12},{1,13},{2,14},{3,15},{4,8},{5,9},{6,10},{7,11},{8,4},{9,5},... | collective-permute-start | bytes 294920 | tf_op jit(solution)/shard_map/ppermute | solution.py:312
  46.0 6.7 %collective-permute-start.11 = (bf16[192,768]{1,0:T(8,128)(2,1)S(1)}, bf16[192,768]{1,0:T(8,128)(2,1)S(1)}, u32[]{:S(2)}, u32[]{:S(2)}) collective-permute-start(bf16[192,768]{1,0:T(8,128)(2,1)S(1)} %collective-permute-done.2.rest_10_), channel_id=1, source_target_pairs={{0,2},{1,3},{2,0},{3,1},{4,6},{5,7},{6,4},{7,5},{8,10},{9,11},{10,... | collective-permute-start | bytes 884744 | tf_op jit(solution)/shard_map/ppermute | solution.py:312
  50.0 3.4 %collective-permute-start.3 = (bf16[256,768]{1,0:T(8,128)(2,1)S(1)}, bf16[256,768]{1,0:T(8,128)(2,1)S(1)}, u32[]{:S(2)}, u32[]{:S(2)}) collective-permute-start(bf16[256,768]{1,0:T(8,128)(2,1)S(1)} %get-tuple-element.48), channel_id=1, source_target_pairs={{0,1},{1,0},{2,3},{3,2},{4,5},{5,4},{6,7},{7,6},{8,9},{9,8},{10,11... | collective-permute-start | bytes 1179656 | tf_op jit(solution)/shard_map/ppermute | solution.py:312
  50.1 3.8 %collective-permute-start.4 = (bf16[256,768]{1,0:T(8,128)(2,1)S(1)}, bf16[256,768]{1,0:T(8,128)(2,1)S(1)}, u32[]{:S(2)}, u32[]{:S(2)}) collective-permute-start(bf16[256,768]{1,0:T(8,128)(2,1)S(1)} %get-tuple-element.49), channel_id=1, source_target_pairs={{0,1},{1,0},{2,3},{3,2},{4,5},{5,4},{6,7},{7,6},{8,9},{9,8},{10,11... | collective-permute-start | bytes 1179656 | tf_op jit(solution)/shard_map/ppermute | solution.py:312
  51.6 2.4 %collective-permute-start.5 = (bf16[256,768]{1,0:T(8,128)(2,1)S(1)}, bf16[256,768]{1,0:T(8,128)(2,1)S(1)}, u32[]{:S(2)}, u32[]{:S(2)}) collective-permute-start(bf16[256,768]{1,0:T(8,128)(2,1)S(1)} %get-tuple-element.50), channel_id=1, source_target_pairs={{0,1},{1,0},{2,3},{3,2},{4,5},{5,4},{6,7},{7,6},{8,9},{9,8},{10,11... | collective-permute-start | bytes 1179656 | tf_op jit(solution)/shard_map/ppermute | solution.py:312
  51.6 2.4 %collective-permute-start.6 = (bf16[256,768]{1,0:T(8,128)(2,1)S(1)}, bf16[256,768]{1,0:T(8,128)(2,1)S(1)}, u32[]{:S(2)}, u32[]{:S(2)}) collective-permute-start(bf16[256,768]{1,0:T(8,128)(2,1)S(1)} %get-tuple-element.51), channel_id=1, source_target_pairs={{0,1},{1,0},{2,3},{3,2},{4,5},{5,4},{6,7},{7,6},{8,9},{9,8},{10,11... | collective-permute-start | bytes 1179656 | tf_op jit(solution)/shard_map/ppermute | solution.py:312
  52.7 5.6 %collective-permute-start.13 = (bf16[256,768]{1,0:T(8,128)(2,1)S(1)}, bf16[256,768]{1,0:T(8,128)(2,1)S(1)}, u32[]{:S(2)}, u32[]{:S(2)}) collective-permute-start(bf16[256,768]{1,0:T(8,128)(2,1)S(1)} %get-tuple-element.56.sum_own), channel_id=1, source_target_pairs={{0,1},{1,0},{2,3},{3,2},{4,5},{5,4},{6,7},{7,6},{8,9},{9,8},{10,11... | collective-permute-start | bytes 1179656 | tf_op jit(solution)/shard_map/ppermute | solution.py:312
  53.4 3.5 %collective-permute-start.20 = (bf16[96,768]{1,0:T(8,128)(2,1)S(1)}, bf16[96,768]{1,0:T(8,128)(2,1)S(1)}, u32[]{:S(2)}, u32[]{:S(2)}) collective-permute-start(bf16[96,768]{1,0:T(8,128)(2,1)S(1)} %last_step.3), channel_id=1, source_target_pairs={{0,1},{1,0},{2,3},{3,2},{4,5},{5,4},{6,7},{7,6},{8,9},{9,8},{10,11... | collective-permute-start | bytes 442376 | tf_op jit(solution)/shard_map/ppermute | solution.py:312
  56.7 1.6 %collective-permute-start.12 = (f32[512,128]{1,0:T(8,128)S(1)}, f32[512,128]{1,0:T(8,128)S(1)}, u32[]{:S(2)}, u32[]{:S(2)}) collective-permute-start(f32[512,128]{1,0:T(8,128)S(1)} %get-tuple-element.55.stats), channel_id=1, source_target_pairs={{0,1},{1,0},{2,3},{3,2},{4,5},{5,4},{6,7},{7,6},{8,9},{9,8},{10,11... | collective-permute-start | bytes 786440 | tf_op jit(solution)/shard_map/ppermute | solution.py:312
  60.2 1.8 %collective-permute-start.21 = (f32[256,384]{1,0:T(8,128)S(1)}, f32[256,384]{1,0:T(8,128)S(1)}, u32[]{:S(2)}, u32[]{:S(2)}) collective-permute-start(f32[256,384]{1,0:T(8,128)S(1)} %get-tuple-element.69), channel_id=1, source_target_pairs={{0,1},{1,0},{2,3},{3,2},{4,5},{5,4},{6,7},{7,6},{8,9},{9,8},{10,11... | collective-permute-start | bytes 1179656 | tf_op jit(solution)/shard_map/ppermute | solution.py:312
  60.4 10.1 %collective-permute-start.23 = (s16[400,384]{1,0:T(8,128)(2,1)S(1)}, s16[400,384]{1,0:T(8,128)(2,1)S(1)}, u32[]{:S(2)}, u32[]{:S(2)}) collective-permute-start(s16[400,384]{1,0:T(8,128)(2,1)S(1)} %get-tuple-element.74), channel_id=1, source_target_pairs={{0,2},{1,3},{2,0},{3,1},{4,6},{5,7},{6,4},{7,5},{8,10},{9,11},{10,... | collective-permute-start | bytes 921608 | tf_op jit(solution)/shard_map/ppermute | solution.py:312
  64.1 16.5 %collective-permute-start.22 = (f32[256,384]{1,0:T(8,128)S(1)}, f32[256,384]{1,0:T(8,128)}, u32[]{:S(2)}, u32[]{:S(2)}) collective-permute-start(f32[256,384]{1,0:T(8,128)S(1)} %get-tuple-element.72), channel_id=1, source_target_pairs={{0,1},{1,0},{2,3},{3,2},{4,5},{5,4},{6,7},{7,6},{8,9},{9,8},{10,11... | collective-permute-start | bytes 1179656 | tf_op jit(solution)/shard_map/ppermute | solution.py:312
  64.3 12.3 %collective-permute-start.27 = (s16[400,384]{1,0:T(8,128)(2,1)S(1)}, s16[400,384]{1,0:T(8,128)(2,1)S(1)}, u32[]{:S(2)}, u32[]{:S(2)}) collective-permute-start(s16[400,384]{1,0:T(8,128)(2,1)S(1)} %get-tuple-element.82), channel_id=1, source_target_pairs={{0,2},{1,3},{2,0},{3,1},{4,6},{5,7},{6,4},{7,5},{8,10},{9,11},{10,... | collective-permute-start | bytes 921608 | tf_op jit(solution)/shard_map/ppermute | solution.py:312
  71.3 7.0 %collective-permute-start.24 = (s16[112,384]{1,0:T(8,128)(2,1)S(1)}, s16[112,384]{1,0:T(8,128)(2,1)S(1)}, u32[]{:S(2)}, u32[]{:S(2)}) collective-permute-start(s16[112,384]{1,0:T(8,128)(2,1)S(1)} %get-tuple-element.77), channel_id=1, source_target_pairs={{0,4},{1,5},{2,6},{3,7},{4,0},{5,1},{6,2},{7,3},{8,12},{9,13},{10,... | collective-permute-start | bytes 258056 | tf_op jit(solution)/shard_map/ppermute | solution.py:312
  72.3 11.9 %collective-permute-start.25 = (s16[112,384]{1,0:T(8,128)(2,1)S(1)}, s16[112,384]{1,0:T(8,128)(2,1)S(1)}, u32[]{:S(2)}, u32[]{:S(2)}) collective-permute-start(s16[112,384]{1,0:T(8,128)(2,1)S(1)} %get-tuple-element.78), channel_id=1, source_target_pairs={{0,8},{1,9},{2,10},{3,11},{4,12},{5,13},{6,14},{7,15},{8,0},{9,1},... | collective-permute-start | bytes 258056 | tf_op jit(solution)/shard_map/ppermute | solution.py:312
  74.5 9.8 %collective-permute-start.26 = (s16[112,384]{1,0:T(8,128)(2,1)S(1)}, s16[112,384]{1,0:T(8,128)(2,1)S(1)}, u32[]{:S(2)}, u32[]{:S(2)}) collective-permute-start(s16[112,384]{1,0:T(8,128)(2,1)S(1)} %get-tuple-element.79), channel_id=1, source_target_pairs={{0,12},{1,13},{2,14},{3,15},{4,8},{5,9},{6,10},{7,11},{8,4},{9,5},... | collective-permute-start | bytes 258056 | tf_op jit(solution)/shard_map/ppermute | solution.py:312
  77.3 7.7 %collective-permute-start.28 = (s16[112,384]{1,0:T(8,128)(2,1)S(1)}, s16[112,384]{1,0:T(8,128)(2,1)S(1)}, u32[]{:S(2)}, u32[]{:S(2)}) collective-permute-start(s16[112,384]{1,0:T(8,128)(2,1)S(1)} %get-tuple-element.84), channel_id=1, source_target_pairs={{0,4},{1,5},{2,6},{3,7},{4,0},{5,1},{6,2},{7,3},{8,12},{9,13},{10,... | collective-permute-start | bytes 258056 | tf_op jit(solution)/shard_map/ppermute | solution.py:312
  78.4 10.2 %collective-permute-start.29 = (s16[112,384]{1,0:T(8,128)(2,1)S(1)}, s16[112,384]{1,0:T(8,128)(2,1)S(1)}, u32[]{:S(2)}, u32[]{:S(2)}) collective-permute-start(s16[112,384]{1,0:T(8,128)(2,1)S(1)} %get-tuple-element.85), channel_id=1, source_target_pairs={{0,8},{1,9},{2,10},{3,11},{4,12},{5,13},{6,14},{7,15},{8,0},{9,1},... | collective-permute-start | bytes 258056 | tf_op jit(solution)/shard_map/ppermute | solution.py:312
  80.6 8.0 %collective-permute-start.30 = (s16[112,384]{1,0:T(8,128)(2,1)S(1)}, s16[112,384]{1,0:T(8,128)(2,1)S(1)}, u32[]{:S(2)}, u32[]{:S(2)}) collective-permute-start(s16[112,384]{1,0:T(8,128)(2,1)S(1)} %get-tuple-element.86), channel_id=1, source_target_pairs={{0,12},{1,13},{2,14},{3,15},{4,8},{5,9},{6,10},{7,11},{8,4},{9,5},... | collective-permute-start | bytes 258056 | tf_op jit(solution)/shard_map/ppermute | solution.py:312
  84.9 4.3 %collective-permute-start.31 = (f32[48,384]{1,0:T(8,128)S(1)}, f32[48,384]{1,0:T(8,128)S(1)}, u32[]{:S(2)}, u32[]{:S(2)}) collective-permute-start(f32[48,384]{1,0:T(8,128)S(1)} %get-tuple-element.88), channel_id=1, source_target_pairs={{0,1},{1,0},{2,3},{3,2},{4,5},{5,4},{6,7},{7,6},{8,9},{9,8},{10,11... | collective-permute-start | bytes 221192 | tf_op jit(solution)/shard_map/ppermute | solution.py:312
  89.2 1.3 %collective-permute-start.32 = (f32[48,384]{1,0:T(8,128)S(1)}, f32[48,384]{1,0:T(8,128)S(1)}, u32[]{:S(2)}, u32[]{:S(2)}) collective-permute-start(f32[48,384]{1,0:T(8,128)S(1)} %get-tuple-element.89), channel_id=1, source_target_pairs={{0,1},{1,0},{2,3},{3,2},{4,5},{5,4},{6,7},{7,6},{8,9},{9,8},{10,11... | collective-permute-start | bytes 221192 | tf_op jit(solution)/shard_map/ppermute | solution.py:312

commit v5 on v4

--- a/solution.py
+++ b/solution.py
@@ -19,7 +19,7 @@
 TAIL = 16
 
 
-def call(kernel, out_shape, name, scratch=(), cost=COST):
+def call(kernel, out_shape, name, scratch=()):
     held = pl.BlockSpec(memory_space=pltpu.VMEM)
 
     def run(where, *arrays):
@@ -30,7 +30,7 @@
             out_specs=(held,) * len(out_shape),
             scratch_shapes=scratch,
             compiler_params=pltpu.CompilerParams(vmem_limit_bytes=VMEM),
-            cost_estimate=pl.CostEstimate(flops=0, bytes_accessed=cost, transcendentals=0),
+            cost_estimate=pl.CostEstimate(flops=COST, bytes_accessed=COST, transcendentals=0),
             name=name,
         )(where, *arrays)
 
@@ -79,7 +79,7 @@
 
 def gram_kernel(where_ref, hidden_ref, kept_ref, *rest, parted):
     *gram_refs, sum_ref, rows_all, total = rest
-    clones, patches = hidden_ref.shape[1], hidden_ref.shape[2]
+    clones, patches = hidden_ref.shape[1:3]
     positions = lax.broadcasted_iota(jnp.int32, (patches, kept_ref.shape[1]), 0)
     sums = None
     for i in range(clones):
@@ -95,21 +95,40 @@
         gram_refs[0][...] = contract_rows(rows_all[...], rows_all[...])
         return
     total[...] = contract_rows(rows_all[...], rows_all[...])
-    mine, theirs = gram_refs
+    mine, *theirs = gram_refs
     core = where_ref[0]
     chips, rows = parted
     for k in range(chips):
-        for ref, c in ((mine, core), (theirs, 1 - core)):
-            at = pl.multiple_of((2 * k + c) * rows, rows)
-            ref[k * rows : (k + 1) * rows, :] = total[pl.ds(at, rows), :]
+        at = pl.multiple_of((2 * k + core) * rows, rows)
+        mine[k * rows : (k + 1) * rows, :] = total[pl.ds(at, rows), :]
+        at = pl.multiple_of((2 * k + 1 - core) * rows, rows)
+        part = k // (chips // len(theirs))
+        here = (k % (chips // len(theirs))) * rows
+        theirs[part][here : here + rows, :] = total[pl.ds(at, rows), :]
 
 
 def gram(where, hidden, kept, parted):
     _, clones, patches, width = hidden.shape
-    grams = [f32(width // 2, width)] * 2 if parted else [f32(width, width)]
-    scratch = [pltpu.VMEM((clones * patches, width), jnp.bfloat16), pltpu.VMEM((width, width), jnp.float32)]
+    grams = [f32(width // 2, width)] + [f32(width // 4, width)] * 2 if parted else [f32(width, width)]
+    scratch = [
+        pltpu.VMEM((clones * patches, width), jnp.bfloat16),
+        pltpu.VMEM((width, width), jnp.float32),
+    ]
     kernel = functools.partial(gram_kernel, parted=parted)
-    return call(kernel, grams + [bf16(patches, width)], "gram", scratch)(where, hidden, kept)
+    shapes = grams + [bf16(patches, width)]
+    return call(kernel, shapes, "gram", scratch)(where, hidden, kept)
+
+
+def cut_kernel(where_ref, own, other, out_ref):
+    rows, half = own.shape[0], out_ref.shape[1]
+    columns = pl.ds(pl.multiple_of(where_ref[0] * half, half), half)
+    out_ref[:rows, :] = own[:, columns]
+    out_ref[rows:, :] = other[:, columns]
+
+
+def cut(where, own, other):
+    rows, width = own.shape
+    return call(cut_kernel, [bf16(2 * rows, width // 2)], "cut")(where, own, other)[0]
 
 
 def put_in_order(where_ref, pieces, full):
@@ -244,10 +263,15 @@
     return call(functools.partial(last_kernel, scale=scale), shapes, "last_step")(where, own, *codes)
 
 
-def targets_kernel(where_ref, blend, stats, stats_other, sum_own, sum_other, grams, weights, own_ref, other_ref, *rest, cut, width):
+def targets_kernel(where_ref, blend, stats, stats_other, sum_own, sum_other, gram_own, gram_other, weights, own_ref, other_ref, *rest, cut, width):
     patches, columns = own_ref.shape
     cols = slice(cut * columns, (cut + 1) * columns)
-    grad = contract_rows(grams[...], weights[:, cols])
+    rows = weights.shape[0] // 2
+    mine, theirs = weights[:rows, cols], weights[rows:, cols]
+    grad = contract_rows(
+        jnp.concatenate([gram_own[...], gram_other[...]], axis=0),
+        jnp.concatenate([mine, mine, theirs, theirs], axis=0),
+    )
     for i, (out, features) in enumerate(((own_ref, sum_own), (other_ref, sum_other))):
         mine = stats[i * patches : (i + 1) * patches, :]
         theirs = stats_other[(1 - i) * patches : (2 - i) * patches, :]
@@ -266,16 +290,16 @@
     halve(total, where_ref, send_ref, keep_ref)
 
 
-def targets_and_term(where, blend, stats, stats_other, sum_own, sum_other, grams, weights, cut, coded):
-    j, n = cut
+def targets_and_term(where, blend, stats, stats_other, sum_own, sum_other, grams, weights, part, coded):
+    j, n = part
     patches, columns = blend.shape[0] // 2, blend.shape[1] // n
-    dec = grams.shape[1]
+    dec = grams[0].shape[1]
     shapes = [f32(patches, columns)] * 2
     shapes += halved_shapes(dec, columns) if coded else [f32(dec, columns)]
     kernel = functools.partial(targets_kernel, cut=j, width=2 * blend.shape[1])
     scratch = [pltpu.VMEM((dec, columns), jnp.float32)] if coded else []
     return call(kernel, shapes, "targets", scratch)(
-        where, blend, stats, stats_other, sum_own, sum_other, grams, weights
+        where, blend, stats, stats_other, sum_own, sum_other, *grams, weights
     )
 
 
@@ -311,12 +335,6 @@
         pairs = [(g * parts + i, g * parts + (i ^ bits)) for g in range(groups) for i in range(parts)]
         return lax.ppermute(x, AXES, pairs)
 
-    def my_half(x):
-        return lax.dynamic_slice_in_dim(x, core * half, half, axis=-1)
-
-    def other_half(x):
-        return lax.dynamic_slice_in_dim(x, (1 - core) * half, half, axis=-1)
-
     def side_by_side(mine, theirs):
         return jnp.where(
             core == 0,
@@ -325,35 +343,36 @@
         )
 
     rows = out_weight.shape[0]
-    got = swap(jnp.concatenate([other_half(out_weight), other_half(pred_weight)], axis=0), CORE)
-    out_piece = jnp.concatenate([my_half(out_weight), got[:rows]], axis=0)
-    pred_mine, pred_theirs = my_half(pred_weight), got[rows:]
-    weights = jnp.concatenate([pred_mine, pred_mine, pred_theirs, pred_theirs], axis=0)
+    if by_pairs:
+        gram_mine, *gram_theirs, sum_own = gram(where, decoder_hidden, kept_index[0], (chips, dec // parts))
+    else:
+        gram_all, sum_own = gram(where, decoder_hidden, kept_index[0], None)
+    out_piece = cut(where, after(out_weight, sum_own), swap(out_weight, CORE))
+    pred_piece = cut(where, pred_weight, swap(pred_weight, CORE))
 
     def attend(*anchors):
         q = after(queries, *anchors) if anchors else queries
         return attention(where, q[0], key_rows[0], value_rows[0], stream[0], earlier[0])
 
     if by_pairs:
-        z2, z1, y0 = swap(out_piece, FAR_Z), swap(out_piece, NEXT_Z), swap(out_piece, NEXT_Y)
-        y1, y2 = swap(z1, NEXT_Y), swap(after(z2, y0), NEXT_Y)
-        z3 = swap(z2, NEXT_Z)
-        y3 = swap(after(z3, y1), NEXT_Y)
+        z1, z2, y0 = swap(out_piece, NEXT_Z), swap(out_piece, FAR_Z), swap(out_piece, NEXT_Y)
+        sum_other = swap(sum_own, CORE)
+        gram_theirs = [swap(g, CORE) for g in gram_theirs]
+        send, keep = first_step(where, after(gram_mine, y0), gram_theirs)
+        y1 = swap(z1, NEXT_Y)
+        z3 = swap(after(z2, send), NEXT_Z)
+        y2 = swap(after(z2, y0), NEXT_Y)
+        own, *codes = second_step(where, after(keep, z2), swap(send, NEXT_Y))
+        y3 = swap(after(z3, y1, own), NEXT_Y)
         out_pieces = [out_piece, y0, z1, y1, z2, y2, z3, y3]
-        hidden = decoder_hidden
-        gram_mine, gram_theirs, sum_own = gram(where, hidden, kept_index[0], (chips, dec // parts))
-        sum_other = swap(sum_own, CORE)
-        gram_theirs = [swap(g, CORE) for g in jnp.split(gram_theirs, 2)]
-        mixed_own, *bundle = attend(z3)
+        mixed_own, *bundle = attend(z3, pred_piece)
         others = [swap(b, CORE) for b in bundle]
-        send, keep = first_step(where, after(gram_mine, y0), gram_theirs)
-        own, *codes = second_step(where, after(keep, z3,y1), swap(send, NEXT_Y))
         codes = [swap(c, NEXT_Z * (m + 1)) for m, c in enumerate(codes)]
         (gram_rows,) = last_step(where, after(own, y2), codes)
+        mixed_own = after(mixed_own, gram_rows)
     else:
         got = lax.all_gather(out_piece, "dp", axis_index_groups=same_core).reshape(chips, 2, rows, half)
         out_pieces = [jnp.where(core == 0, got, got[:, ::-1]).reshape(width, half)]
-        gram_all, sum_own = gram(where, decoder_hidden, kept_index[0], None)
         sum_other = swap(sum_own, CORE)
         mixed_own, *bundle = attend()
         others = [swap(b, CORE) for b in bundle]
@@ -361,14 +380,14 @@
         high = gram_rows.astype(jnp.bfloat16)
         low = (gram_rows - high.astype(jnp.float32)).astype(jnp.bfloat16)
         gram_rows = jnp.concatenate([high, low], axis=0)
-    grams = jnp.concatenate([gram_rows, swap(gram_rows, CORE)], axis=0)
+    grams = [gram_rows, swap(gram_rows, CORE)]
 
     blend, stats = branch(where, mixed_own, stream[0], earlier[0], *others, *out_pieces)
     stats_other = swap(stats, CORE)
 
-    def term(cut, coded, *before):
+    def term(part, coded, *before):
         return targets_and_term(
-            where, blend, stats, after(stats_other, *before), sum_own, sum_other, grams, weights, cut, coded
+            where, blend, stats, after(stats_other, *before), sum_own, sum_other, grams, pred_piece, part, coded
         )
 
     if not by_pairs:

time: 91.5 us -> 89.4 us (0.977)
  waiting for transfers between devices: 31.7 us -> 26.3 us
  starting transfers between devices: 31.1 us -> 35.7 us
  local copies, waits for them, and re-layouts: 4.63 us -> 2.6 us
    ppermute x33 -> x34, waiting for transfers between devices: 31.7 us -> 26.3 us  [swap(): return lax.ppermute(x, AXES, pairs)]
    ppermute x33 -> x34, starting transfers between devices: 31.1 us -> 35.7 us  [swap(): return lax.ppermute(x, AXES, pairs)]
    dynamic_slice x2 -> x0, local copies, waits for them, and re-layouts: 1.95 us -> none  [my_half(): return lax.dynamic_slice_in_dim(x, core * half, half, axis=-1)]
    pallas_call x12 -> x14, Pallas kernels: 19.6 us -> 20.5 us  [run(): pl.pallas_call(kernel, out_shape=tuple(out_shape), in_specs=[pl.BlockSpec...]
    unnamed x14 -> x18, local copies, waits for them, and re-layouts: 2.59 us -> 2.6 us
  transfers between devices with their start and end apart: 33 -> 34, of which waited for: 12 -> 10; matrix products, arithmetic and copies ran while one was open for 3% -> 3% of each run, Pallas kernels for 19% -> 21%
where the time goes in v5:
time: 89.4 us; the launch traced here: 89.2 us
  starting transfers between devices  35.7 us (40%)
  waiting for transfers between devices  26.3 us (29%)
  Pallas kernels  20.5 us (23%)
  other arithmetic  3.3 us (4%)
  local copies, waits for them, and re-layouts  2.6 us (3%)
  between operations  0.91 us (1%)
    ppermute x34, starting transfers between devices, swap(): return lax.ppermute(x, AXES, pairs)  35.7 us
    ppermute x34, waiting for transfers between devices, swap(): return lax.ppermute(x, AXES, pairs)  26.3 us
    pallas_call x14, Pallas kernels, run(): pl.pallas_call(kernel, out_shape=tuple(out_shape), in_specs=[pl.BlockSpec...  20.5 us
    select_n x2, other arithmetic, side_by_side(): jnp.where(core == 0, jnp.concatenate(mine + theirs, axis=1), jnp.concaten...  3.22 us
    unnamed x18, local copies, waits for them, and re-layouts  2.6 us
  transfers between devices with their start and end apart: 34, of which 10 were waited for; matrix products, arithmetic and copies ran while one was open for 3% of the time, Pallas kernels for 21%

profile of v5, /device:TPU:0, one launch (start us, length us, event | category | flops | bytes accessed | tf_op | source)
XLA Modules:
  0.0 89.2 jit_solution(11313775230055845763)
XLA Ops:
  0.6 0.5 collective-permute-start
  1.1 0.1 pad_add_fusion.where_ref
  1.2 1.9 %copy-done.2 = bf16[1,8,256,768]{3,2,1,0:T(8,128)(2,1)S(1)} copy-done((bf16[1,8,256,768]{3,2,1,0:T(8,128)(2,1)S(1)}, bf16[1,8,256,768]{3,2,1,0:T(8,128)(2,1)}, u32[]{:S(2)}) %copy-start.2) | copy-done | bytes 3145752
  3.1 0.7 copy-done.8
  3.8 4.2 %gram.1 = (f32[384,768]{1,0:T(8,128)S(1)}, f32[192,768]{1,0:T(8,128)S(1)}, f32[192,768]{1,0:T(8,128)S(1)}, bf16[256,768]{1,0:T(8,128)(2,1)S(1)}) custom-call(s32[2]{0:T(128)S(1)} %pad_add_fusion.where_ref, bf16[1,8,256,768]{3,2,1,0:T(8,128)(2,1)S(1)} %copy-done.2, s32[8,64]{1,0:T(8,128)S(1)} %bitcast.21), custom_call_target="tpu_custom_call" | custom-call | flops 1000 | bytes 1000 | tf_op jit(solution)/shard_map/gram/pallas_call | solution.py:26
  8.0 0.1 collective-permute-start.3
  8.1 0.4 collective-permute-start.4
  8.6 0.6 cut.2.rest_4_
  9.2 2.7 %collective-permute-start.2 = (bf16[192,768]{1,0:T(8,128)(2,1)S(1)}, bf16[192,768]{1,0:T(8,128)(2,1)S(1)}, u32[]{:S(2)}, u32[]{:S(2)}) collective-permute-start(bf16[192,768]{1,0:T(8,128)(2,1)S(1)} %cut.2.rest_4_), channel_id=1, source_target_pairs={{0,2},{1,3},{2,0},{3,1},{4,6},{5,7},{6,4},{7,5},{8,10},{9,11},{10,... | collective-permute-start | bytes 884744 | tf_op jit(solution)/shard_map/ppermute | solution.py:336
  11.8 2.6 %collective-permute-start.1 = (bf16[192,768]{1,0:T(8,128)(2,1)S(1)}, bf16[192,768]{1,0:T(8,128)(2,1)S(1)}, u32[]{:S(2)}, u32[]{:S(2)}) collective-permute-start(bf16[192,768]{1,0:T(8,128)(2,1)S(1)} %cut.2.rest_4_), channel_id=1, source_target_pairs={{0,8},{1,9},{2,10},{3,11},{4,12},{5,13},{6,14},{7,15},{8,0},{9,1},... | collective-permute-start | bytes 884744 | tf_op jit(solution)/shard_map/ppermute | solution.py:336
  14.4 1.6 %collective-permute-start.16 = (bf16[192,768]{1,0:T(8,128)(2,1)S(1)}, bf16[192,768]{1,0:T(8,128)(2,1)S(1)}, u32[]{:S(2)}, u32[]{:S(2)}) collective-permute-start(bf16[192,768]{1,0:T(8,128)(2,1)S(1)} %cut.2.rest_4_), channel_id=1, source_target_pairs={{0,4},{1,5},{2,6},{3,7},{4,0},{5,1},{6,2},{7,3},{8,12},{9,13},{10,... | collective-permute-start | bytes 884744 | tf_op jit(solution)/shard_map/ppermute | solution.py:336
  16.0 3.5 %collective-permute-done.2.rest_5_ = bf16[192,768]{1,0:T(8,128)(2,1)S(1)} collective-permute-done((bf16[192,768]{1,0:T(8,128)(2,1)S(1)}, bf16[192,768]{1,0:T(8,128)(2,1)S(1)}, u32[]{:S(2)}, u32[]{:S(2)}) %collective-permute-start.2) | collective-permute-done | bytes 294944 | tf_op jit(solution)/shard_map/ppermute | solution.py:336
  19.4 0.0 collective-permute-done.3.t0
  19.5 0.9 %first_step.1 = (s16[208,768]{1,0:T(8,128)(2,1)S(1)}, f32[192,768]{1,0:T(8,128)S(1)}) custom-call(s32[2]{0:T(128)S(1)} %pad_add_fusion.where_ref, f32[384,768]{1,0:T(8,128)S(1)} %get-tuple-element.53.mine, f32[192,768]{1,0:T(8,128)S(1)} %collective-permute-done.3.t0, f32[192,768]{1,0:T(8,128)S(1)} %collective-permute-done.4.t1), custom_call_target="tpu_custom_call" | custom-call | flops 1000 | bytes 1000 | tf_op jit(solution)/shard_map/first_step/pallas_call | solution.py:26
  20.4 1.8 %collective-permute-start.7 = (s16[208,768]{1,0:T(8,128)(2,1)S(1)}, s16[208,768]{1,0:T(8,128)(2,1)S(1)}, u32[]{:S(2)}, u32[]{:S(2)}) collective-permute-start(s16[208,768]{1,0:T(8,128)(2,1)S(1)} %get-tuple-element.56), channel_id=1, source_target_pairs={{0,2},{1,3},{2,0},{3,1},{4,6},{5,7},{6,4},{7,5},{8,10},{9,11},{10,... | collective-permute-start | bytes 958472 | tf_op jit(solution)/shard_map/ppermute | solution.py:336
  22.2 6.0 %collective-permute-done.1.rest_8_ = bf16[192,768]{1,0:T(8,128)(2,1)S(1)} collective-permute-done((bf16[192,768]{1,0:T(8,128)(2,1)S(1)}, bf16[192,768]{1,0:T(8,128)(2,1)S(1)}, u32[]{:S(2)}, u32[]{:S(2)}) %collective-permute-start.1) | collective-permute-done | bytes 294944 | tf_op jit(solution)/shard_map/ppermute | solution.py:336
  28.2 0.6 collective-permute-start.5
  28.8 0.0 collective-permute-done.16.rest_6_
  28.8 0.5 collective-permute-start.17
  29.3 1.5 %collective-permute-start.8 = (bf16[192,768]{1,0:T(8,128)(2,1)S(1)}, bf16[192,768]{1,0:T(8,128)(2,1)S(1)}, u32[]{:S(2)}, u32[]{:S(2)}) collective-permute-start(bf16[192,768]{1,0:T(8,128)(2,1)S(1)} %collective-permute-done.1.rest_8_), channel_id=1, source_target_pairs={{0,2},{1,3},{2,0},{3,1},{4,6},{5,7},{6,4},{7,5},{8,10},{9,11},{10,... | collective-permute-start | bytes 884744 | tf_op jit(solution)/shard_map/ppermute | solution.py:336
  30.8 0.0 collective-permute-start.6
  30.8 0.8 second_step.3
  31.7 3.4 %collective-permute-start.10 = (s16[64,768]{1,0:T(8,128)(2,1)S(1)}, s16[64,768]{1,0:T(8,128)(2,1)S(1)}, u32[]{:S(2)}, u32[]{:S(2)}) collective-permute-start(s16[64,768]{1,0:T(8,128)(2,1)S(1)} %get-tuple-element.66), channel_id=1, source_target_pairs={{0,8},{1,9},{2,10},{3,11},{4,12},{5,13},{6,14},{7,15},{8,0},{9,1},... | collective-permute-start | bytes 294920 | tf_op jit(solution)/shard_map/ppermute | solution.py:336
  35.1 1.3 %collective-permute-done.5.rest_10_ = bf16[192,768]{1,0:T(8,128)(2,1)S(1)} collective-permute-done((bf16[192,768]{1,0:T(8,128)(2,1)S(1)}, bf16[192,768]{1,0:T(8,128)(2,1)S(1)}, u32[]{:S(2)}, u32[]{:S(2)}) %collective-permute-start.5) | collective-permute-done | bytes 294944 | tf_op jit(solution)/shard_map/ppermute | solution.py:336
  36.4 5.6 %collective-permute-start.11 = (s16[64,768]{1,0:T(8,128)(2,1)S(1)}, s16[64,768]{1,0:T(8,128)(2,1)S(1)}, u32[]{:S(2)}, u32[]{:S(2)}) collective-permute-start(s16[64,768]{1,0:T(8,128)(2,1)S(1)} %get-tuple-element.67), channel_id=1, source_target_pairs={{0,12},{1,13},{2,14},{3,15},{4,8},{5,9},{6,10},{7,11},{8,4},{9,5},... | collective-permute-start | bytes 294920 | tf_op jit(solution)/shard_map/ppermute | solution.py:336
  42.1 0.4 collective-permute-start.18
  42.5 0.6 cut.3.weights
  43.1 3.5 %attention.1 = (bf16[256,1536]{1,0:T(8,128)(2,1)S(1)}, bf16[256,768]{1,0:T(8,128)(2,1)S(1)}, bf16[256,768]{1,0:T(8,128)(2,1)S(1)}, bf16[256,768]{1,0:T(8,128)(2,1)S(1)}, bf16[256,768]{1,0:T(8,128)(2,1)S(1)}) custom-call(s32[2]{0:T(128)S(1)} %pad_add_fusion.where_ref, bf16[256,1536]{1,0:T(8,128)(2,1)S(1)} %bitcast.16, bf16[256,1536]{1,0:T(8,128)(2,1)S(1)} %bitcast.17, ...), custom_call_target="tpu_custom_call" | custom-call | flops 1000 | bytes 1000 | tf_op jit(solution)/shard_map/attention/pallas_call | solution.py:26
  46.6 0.1 collective-permute-start.12
  46.7 0.5 collective-permute-start.13
  47.2 0.1 collective-permute-start.14
  47.2 0.4 collective-permute-start.15
  47.7 2.4 %collective-permute-done.18.rest_11_ = bf16[192,768]{1,0:T(8,128)(2,1)S(1)} collective-permute-done((bf16[192,768]{1,0:T(8,128)(2,1)S(1)}, bf16[192,768]{1,0:T(8,128)(2,1)S(1)}, u32[]{:S(2)}, u32[]{:S(2)}) %collective-permute-start.18) | collective-permute-done | bytes 294944 | tf_op jit(solution)/shard_map/ppermute | solution.py:336
  50.1 0.6 last_step.3.gram_own
  50.8 2.8 %branch.1 = (f32[512,768]{1,0:T(8,128)S(1)}, f32[512,128]{1,0:T(8,128)S(1)}) custom-call(s32[2]{0:T(128)S(1)} %pad_add_fusion.where_ref, bf16[256,1536]{1,0:T(8,128)(2,1)S(1)} %get-tuple-element.68.mixed_own, bf16[256,1536]{1,0:T(8,128)(2,1)S(1)} %bitcast.13, bf16[256,1536]{1,0:T(8,128)(2,1)S(1)} %bitcast.15, ...), custom_call_target="tpu_custom_call" | custom-call | flops 1000 | bytes 1000 | tf_op jit(solution)/shard_map/branch/pallas_call | solution.py:26
  53.5 0.6 collective-permute-start.19
  54.1 0.1 collective-permute-start.21
  54.2 1.1 %collective-permute-done.19.stats_other = f32[512,128]{1,0:T(8,128)S(1)} collective-permute-done((f32[512,128]{1,0:T(8,128)S(1)}, f32[512,128]{1,0:T(8,128)S(1)}, u32[]{:S(2)}, u32[]{:S(2)}) %collective-permute-start.19) | collective-permute-done | bytes 262176 | tf_op jit(solution)/shard_map/ppermute | solution.py:336
  55.3 0.2 collective-permute-done.21.gram_other
  55.5 1.9 %targets.2 = (f32[256,384]{1,0:T(8,128)S(1)}, f32[256,384]{1,0:T(8,128)S(1)}, s16[400,384]{1,0:T(8,128)(2,1)S(1)}, f32[384,384]{1,0:T(8,128)S(1)}) custom-call(s32[2]{0:T(128)S(1)} %pad_add_fusion.where_ref, f32[512,768]{1,0:T(8,128)S(1)} %get-tuple-element.74.blend, f32[512,128]{1,0:T(8,128)S(1)} %get-tuple-element.75.stats, ...), custom_call_target="tpu_custom_call" | custom-call | flops 1000 | bytes 1000 | tf_op jit(solution)/shard_map/targets/pallas_call | solution.py:26
  57.4 0.4 collective-permute-start.22
  57.8 0.6 collective-permute-start.24
  58.4 0.7 collective-permute-done.22
  59.2 1.9 %targets.3 = (f32[256,384]{1,0:T(8,128)S(1)}, f32[256,384]{1,0:T(8,128)S(1)}, s16[400,384]{1,0:T(8,128)(2,1)S(1)}, f32[384,384]{1,0:T(8,128)S(1)}) custom-call(s32[2]{0:T(128)S(1)} %pad_add_fusion.where_ref, f32[512,768]{1,0:T(8,128)S(1)} %get-tuple-element.74.blend, f32[512,128]{1,0:T(8,128)S(1)} %get-tuple-element.75.stats, ...), custom_call_target="tpu_custom_call" | custom-call | flops 1000 | bytes 1000 | tf_op jit(solution)/shard_map/targets/pallas_call | solution.py:26
  61.1 0.4 collective-permute-start.23
  61.5 0.6 collective-permute-start.28
  62.1 5.8 %collective-permute-done.24.codes = s16[400,384]{1,0:T(8,128)(2,1)S(1)} collective-permute-done((s16[400,384]{1,0:T(8,128)(2,1)S(1)}, s16[400,384]{1,0:T(8,128)(2,1)S(1)}, u32[]{:S(2)}, u32[]{:S(2)}) %collective-permute-start.24) | collective-permute-done | bytes 307232 | tf_op jit(solution)/shard_map/ppermute | solution.py:336
  67.9 0.8 second_step.4
  68.8 1.6 %collective-permute-start.25 = (s16[112,384]{1,0:T(8,128)(2,1)S(1)}, s16[112,384]{1,0:T(8,128)(2,1)S(1)}, u32[]{:S(2)}, u32[]{:S(2)}) collective-permute-start(s16[112,384]{1,0:T(8,128)(2,1)S(1)} %get-tuple-element.85), channel_id=1, source_target_pairs={{0,4},{1,5},{2,6},{3,7},{4,0},{5,1},{6,2},{7,3},{8,12},{9,13},{10,... | collective-permute-start | bytes 258056 | tf_op jit(solution)/shard_map/ppermute | solution.py:336
  70.4 2.1 %collective-permute-start.26 = (s16[112,384]{1,0:T(8,128)(2,1)S(1)}, s16[112,384]{1,0:T(8,128)(2,1)S(1)}, u32[]{:S(2)}, u32[]{:S(2)}) collective-permute-start(s16[112,384]{1,0:T(8,128)(2,1)S(1)} %get-tuple-element.86), channel_id=1, source_target_pairs={{0,8},{1,9},{2,10},{3,11},{4,12},{5,13},{6,14},{7,15},{8,0},{9,1},... | collective-permute-start | bytes 258056 | tf_op jit(solution)/shard_map/ppermute | solution.py:336
  72.5 1.2 %collective-permute-start.27 = (s16[112,384]{1,0:T(8,128)(2,1)S(1)}, s16[112,384]{1,0:T(8,128)(2,1)S(1)}, u32[]{:S(2)}, u32[]{:S(2)}) collective-permute-start(s16[112,384]{1,0:T(8,128)(2,1)S(1)} %get-tuple-element.87), channel_id=1, source_target_pairs={{0,12},{1,13},{2,14},{3,15},{4,8},{5,9},{6,10},{7,11},{8,4},{9,5},... | collective-permute-start | bytes 258056 | tf_op jit(solution)/shard_map/ppermute | solution.py:336
  73.7 0.0 collective-permute-done.28.codes
  73.7 0.8 second_step.5
  74.5 1.6 %collective-permute-start.29 = (s16[112,384]{1,0:T(8,128)(2,1)S(1)}, s16[112,384]{1,0:T(8,128)(2,1)S(1)}, u32[]{:S(2)}, u32[]{:S(2)}) collective-permute-start(s16[112,384]{1,0:T(8,128)(2,1)S(1)} %get-tuple-element.92), channel_id=1, source_target_pairs={{0,4},{1,5},{2,6},{3,7},{4,0},{5,1},{6,2},{7,3},{8,12},{9,13},{10,... | collective-permute-start | bytes 258056 | tf_op jit(solution)/shard_map/ppermute | solution.py:336
  76.1 2.1 %collective-permute-start.30 = (s16[112,384]{1,0:T(8,128)(2,1)S(1)}, s16[112,384]{1,0:T(8,128)(2,1)S(1)}, u32[]{:S(2)}, u32[]{:S(2)}) collective-permute-start(s16[112,384]{1,0:T(8,128)(2,1)S(1)} %get-tuple-element.93), channel_id=1, source_target_pairs={{0,8},{1,9},{2,10},{3,11},{4,12},{5,13},{6,14},{7,15},{8,0},{9,1},... | collective-permute-start | bytes 258056 | tf_op jit(solution)/shard_map/ppermute | solution.py:336
  78.3 1.3 %collective-permute-start.31 = (s16[112,384]{1,0:T(8,128)(2,1)S(1)}, s16[112,384]{1,0:T(8,128)(2,1)S(1)}, u32[]{:S(2)}, u32[]{:S(2)}) collective-permute-start(s16[112,384]{1,0:T(8,128)(2,1)S(1)} %get-tuple-element.94), channel_id=1, source_target_pairs={{0,12},{1,13},{2,14},{3,15},{4,8},{5,9},{6,10},{7,11},{8,4},{9,5},... | collective-permute-start | bytes 258056 | tf_op jit(solution)/shard_map/ppermute | solution.py:336
  79.5 2.5 %maximum_select_fusion = f32[1,256,1536]{2,1,0:T(8,128)} fusion(f32[1,256,384]{2,1,0:T(8,128)} %bitcast.11, f32[1,256,384]{2,1,0:T(8,128)S(1)} %bitcast.22, f32[1,256,384]{2,1,0:T(8,128)S(1)} %bitcast.20, f32[1,256,384]{2,1,0:T(8,128)S(1)} %bitcast.19, pred[]{:T(512)S(6)} %eq.6), kind=kLoop, calls=%fused_computation | loop fusion | flops 2752512 | bytes 3145729 | tf_op jit(solution)/shard_map/jit(_where)/select_n | solution.py:339
  82.0 0.6 last_step.4
  82.6 0.1 collective-permute-start.32
  82.7 3.8 %collective-permute-done.30.c2 = s16[112,384]{1,0:T(8,128)(2,1)S(1)} collective-permute-done((s16[112,384]{1,0:T(8,128)(2,1)S(1)}, s16[112,384]{1,0:T(8,128)(2,1)S(1)}, u32[]{:S(2)}, u32[]{:S(2)}) %collective-permute-start.30) | collective-permute-done | bytes 86048 | tf_op jit(solution)/shard_map/ppermute | solution.py:336
  86.5 0.6 last_step.5
  87.2 0.1 collective-permute-start.33
  87.3 1.2 %collective-permute-done.33 = f32[48,384]{1,0:T(8,128)S(1)} collective-permute-done((f32[48,384]{1,0:T(8,128)S(1)}, f32[48,384]{1,0:T(8,128)S(1)}, u32[]{:S(2)}, u32[]{:S(2)}) %collective-permute-start.33) | collective-permute-done | bytes 73760 | tf_op jit(solution)/shard_map/ppermute | solution.py:336
  88.5 0.7 maximum_select_fusion.1
  (39 shorter events, 0.1 us)
Async XLA Ops:
  0.6 7.9 %collective-permute-start = (bf16[96,1536]{1,0:T(8,128)(2,1)}, bf16[96,1536]{1,0:T(8,128)(2,1)S(1)}, u32[]{:S(2)}, u32[]{:S(2)}) collective-permute-start(bf16[96,1536]{1,0:T(8,128)(2,1)} %own.1), channel_id=1, source_target_pairs={{0,1},{1,0},{2,3},{3,2},{4,5},{5,4},{6,7},{7,6},{8,9},{9,8},{10,11... | collective-permute-start | bytes 884744 | tf_op jit(solution)/shard_map/ppermute | solution.py:336
  1.2 1.9 %copy-start.2 = (bf16[1,8,256,768]{3,2,1,0:T(8,128)(2,1)S(1)}, bf16[1,8,256,768]{3,2,1,0:T(8,128)(2,1)}, u32[]{:S(2)}) copy-start(bf16[1,8,256,768]{3,2,1,0:T(8,128)(2,1)} %hidden_ref.1) | copy-start | bytes 9437188
  3.1 0.7 copy-start.8
  3.8 4.8 %copy-start.6 = (bf16[96,1536]{1,0:T(8,128)(2,1)S(1)}, bf16[96,1536]{1,0:T(8,128)(2,1)}, u32[]{:S(2)}) copy-start(bf16[96,1536]{1,0:T(8,128)(2,1)} %own.1) | copy-start | bytes 884740
  8.0 11.5 %collective-permute-start.3 = (f32[192,768]{1,0:T(8,128)S(1)}, f32[192,768]{1,0:T(8,128)S(1)}, u32[]{:S(2)}, u32[]{:S(2)}) collective-permute-start(f32[192,768]{1,0:T(8,128)S(1)} %get-tuple-element.54), channel_id=1, source_target_pairs={{0,1},{1,0},{2,3},{3,2},{4,5},{5,4},{6,7},{7,6},{8,9},{9,8},{10,11... | collective-permute-start | bytes 1769480 | tf_op jit(solution)/shard_map/ppermute | solution.py:336
  8.1 11.3 %collective-permute-start.4 = (f32[192,768]{1,0:T(8,128)S(1)}, f32[192,768]{1,0:T(8,128)S(1)}, u32[]{:S(2)}, u32[]{:S(2)}) collective-permute-start(f32[192,768]{1,0:T(8,128)S(1)} %get-tuple-element.55), channel_id=1, source_target_pairs={{0,1},{1,0},{2,3},{3,2},{4,5},{5,4},{6,7},{7,6},{8,9},{9,8},{10,11... | collective-permute-start | bytes 1769480 | tf_op jit(solution)/shard_map/ppermute | solution.py:336
  8.6 22.3 %copy-start.7 = (bf16[48,1536]{1,0:T(8,128)(2,1)S(1)}, bf16[48,1536]{1,0:T(8,128)(2,1)}, u32[]{:S(2)}) copy-start(bf16[48,1536]{1,0:T(8,128)(2,1)} %own.2) | copy-start | bytes 442372
  8.6 34.5 %copy-start.5 = (bf16[1,256,1536]{2,1,0:T(8,128)(2,1)S(1)}, bf16[1,256,1536]{2,1,0:T(8,128)(2,1)}, u32[]{:S(2)}) copy-start(bf16[1,256,1536]{2,1,0:T(8,128)(2,1)} %param.11) | copy-start | bytes 2359300
  9.2 10.3 %collective-permute-start.2 = (bf16[192,768]{1,0:T(8,128)(2,1)S(1)}, bf16[192,768]{1,0:T(8,128)(2,1)S(1)}, u32[]{:S(2)}, u32[]{:S(2)}) collective-permute-start(bf16[192,768]{1,0:T(8,128)(2,1)S(1)} %cut.2.rest_4_), channel_id=1, source_target_pairs={{0,2},{1,3},{2,0},{3,1},{4,6},{5,7},{6,4},{7,5},{8,10},{9,11},{10,... | collective-permute-start | bytes 884744 | tf_op jit(solution)/shard_map/ppermute | solution.py:336
  11.8 16.4 %collective-permute-start.1 = (bf16[192,768]{1,0:T(8,128)(2,1)S(1)}, bf16[192,768]{1,0:T(8,128)(2,1)S(1)}, u32[]{:S(2)}, u32[]{:S(2)}) collective-permute-start(bf16[192,768]{1,0:T(8,128)(2,1)S(1)} %cut.2.rest_4_), channel_id=1, source_target_pairs={{0,8},{1,9},{2,10},{3,11},{4,12},{5,13},{6,14},{7,15},{8,0},{9,1},... | collective-permute-start | bytes 884744 | tf_op jit(solution)/shard_map/ppermute | solution.py:336
  14.4 14.4 %collective-permute-start.16 = (bf16[192,768]{1,0:T(8,128)(2,1)S(1)}, bf16[192,768]{1,0:T(8,128)(2,1)S(1)}, u32[]{:S(2)}, u32[]{:S(2)}) collective-permute-start(bf16[192,768]{1,0:T(8,128)(2,1)S(1)} %cut.2.rest_4_), channel_id=1, source_target_pairs={{0,4},{1,5},{2,6},{3,7},{4,0},{5,1},{6,2},{7,3},{8,12},{9,13},{10,... | collective-permute-start | bytes 884744 | tf_op jit(solution)/shard_map/ppermute | solution.py:336
  19.4 23.6 %copy-start = (bf16[1,256,1536]{2,1,0:T(8,128)(2,1)S(1)}, bf16[1,256,1536]{2,1,0:T(8,128)(2,1)}, u32[]{:S(2)}) copy-start(bf16[1,256,1536]{2,1,0:T(8,128)(2,1)} %param.12) | copy-start | bytes 2359300
  19.4 23.6 %copy-start.1 = (bf16[1,256,1536]{2,1,0:T(8,128)(2,1)S(1)}, bf16[1,256,1536]{2,1,0:T(8,128)(2,1)}, u32[]{:S(2)}) copy-start(bf16[1,256,1536]{2,1,0:T(8,128)(2,1)} %param.13) | copy-start | bytes 2359300
  19.4 23.6 %copy-start.3 = (bf16[1,256,1536]{2,1,0:T(8,128)(2,1)S(1)}, bf16[1,256,1536]{2,1,0:T(8,128)(2,1)}, u32[]{:S(2)}) copy-start(bf16[1,256,1536]{2,1,0:T(8,128)(2,1)} %param.9) | copy-start | bytes 2359300
  19.4 23.6 %copy-start.4 = (bf16[1,256,1536]{2,1,0:T(8,128)(2,1)S(1)}, bf16[1,256,1536]{2,1,0:T(8,128)(2,1)}, u32[]{:S(2)}) copy-start(bf16[1,256,1536]{2,1,0:T(8,128)(2,1)} %param.10) | copy-start | bytes 2359300
  20.4 10.4 %collective-permute-start.7 = (s16[208,768]{1,0:T(8,128)(2,1)S(1)}, s16[208,768]{1,0:T(8,128)(2,1)S(1)}, u32[]{:S(2)}, u32[]{:S(2)}) collective-permute-start(s16[208,768]{1,0:T(8,128)(2,1)S(1)} %get-tuple-element.56), channel_id=1, source_target_pairs={{0,2},{1,3},{2,0},{3,1},{4,6},{5,7},{6,4},{7,5},{8,10},{9,11},{10,... | collective-permute-start | bytes 958472 | tf_op jit(solution)/shard_map/ppermute | solution.py:336
  28.2 8.2 %collective-permute-start.5 = (bf16[192,768]{1,0:T(8,128)(2,1)S(1)}, bf16[192,768]{1,0:T(8,128)(2,1)S(1)}, u32[]{:S(2)}, u32[]{:S(2)}) collective-permute-start(bf16[192,768]{1,0:T(8,128)(2,1)S(1)} %collective-permute-done.1.rest_8_), channel_id=1, source_target_pairs={{0,4},{1,5},{2,6},{3,7},{4,0},{5,1},{6,2},{7,3},{8,12},{9,13},{10,... | collective-permute-start | bytes 884744 | tf_op jit(solution)/shard_map/ppermute | solution.py:336
  28.8 13.3 %collective-permute-start.17 = (bf16[192,768]{1,0:T(8,128)(2,1)S(1)}, bf16[192,768]{1,0:T(8,128)(2,1)S(1)}, u32[]{:S(2)}, u32[]{:S(2)}) collective-permute-start(bf16[192,768]{1,0:T(8,128)(2,1)S(1)} %collective-permute-done.16.rest_6_), channel_id=1, source_target_pairs={{0,2},{1,3},{2,0},{3,1},{4,6},{5,7},{6,4},{7,5},{8,10},{9,11},{10,... | collective-permute-start | bytes 884744 | tf_op jit(solution)/shard_map/ppermute | solution.py:336
  29.3 17.3 %collective-permute-start.8 = (bf16[192,768]{1,0:T(8,128)(2,1)S(1)}, bf16[192,768]{1,0:T(8,128)(2,1)S(1)}, u32[]{:S(2)}, u32[]{:S(2)}) collective-permute-start(bf16[192,768]{1,0:T(8,128)(2,1)S(1)} %collective-permute-done.1.rest_8_), channel_id=1, source_target_pairs={{0,2},{1,3},{2,0},{3,1},{4,6},{5,7},{6,4},{7,5},{8,10},{9,11},{10,... | collective-permute-start | bytes 884744 | tf_op jit(solution)/shard_map/ppermute | solution.py:336
  30.8 11.2 %collective-permute-start.6 = (bf16[48,1536]{1,0:T(8,128)(2,1)S(1)}, bf16[48,1536]{1,0:T(8,128)(2,1)S(1)}, u32[]{:S(2)}, u32[]{:S(2)}) collective-permute-start(bf16[48,1536]{1,0:T(8,128)(2,1)S(1)} %copy-done.7), channel_id=1, source_target_pairs={{0,1},{1,0},{2,3},{3,2},{4,5},{5,4},{6,7},{7,6},{8,9},{9,8},{10,11... | collective-permute-start | bytes 442376 | tf_op jit(solution)/shard_map/ppermute | solution.py:336
  31.7 15.0 %collective-permute-start.10 = (s16[64,768]{1,0:T(8,128)(2,1)S(1)}, s16[64,768]{1,0:T(8,128)(2,1)S(1)}, u32[]{:S(2)}, u32[]{:S(2)}) collective-permute-start(s16[64,768]{1,0:T(8,128)(2,1)S(1)} %get-tuple-element.66), channel_id=1, source_target_pairs={{0,8},{1,9},{2,10},{3,11},{4,12},{5,13},{6,14},{7,15},{8,0},{9,1},... | collective-permute-start | bytes 294920 | tf_op jit(solution)/shard_map/ppermute | solution.py:336
  36.4 10.7 %collective-permute-start.11 = (s16[64,768]{1,0:T(8,128)(2,1)S(1)}, s16[64,768]{1,0:T(8,128)(2,1)S(1)}, u32[]{:S(2)}, u32[]{:S(2)}) collective-permute-start(s16[64,768]{1,0:T(8,128)(2,1)S(1)} %get-tuple-element.67), channel_id=1, source_target_pairs={{0,12},{1,13},{2,14},{3,15},{4,8},{5,9},{6,10},{7,11},{8,4},{9,5},... | collective-permute-start | bytes 294920 | tf_op jit(solution)/shard_map/ppermute | solution.py:336
  42.1 5.2 %collective-permute-start.9 = (s16[64,768]{1,0:T(8,128)(2,1)S(1)}, s16[64,768]{1,0:T(8,128)(2,1)S(1)}, u32[]{:S(2)}, u32[]{:S(2)}) collective-permute-start(s16[64,768]{1,0:T(8,128)(2,1)S(1)} %get-tuple-element.65), channel_id=1, source_target_pairs={{0,4},{1,5},{2,6},{3,7},{4,0},{5,1},{6,2},{7,3},{8,12},{9,13},{10,... | collective-permute-start | bytes 294920 | tf_op jit(solution)/shard_map/ppermute | solution.py:336
  42.1 8.0 %collective-permute-start.18 = (bf16[192,768]{1,0:T(8,128)(2,1)S(1)}, bf16[192,768]{1,0:T(8,128)(2,1)S(1)}, u32[]{:S(2)}, u32[]{:S(2)}) collective-permute-start(bf16[192,768]{1,0:T(8,128)(2,1)S(1)} %collective-permute-done.5.rest_10_), channel_id=1, source_target_pairs={{0,2},{1,3},{2,0},{3,1},{4,6},{5,7},{6,4},{7,5},{8,10},{9,11},{10,... | collective-permute-start | bytes 884744 | tf_op jit(solution)/shard_map/ppermute | solution.py:336
  46.6 4.2 %collective-permute-start.12 = (bf16[256,768]{1,0:T(8,128)(2,1)S(1)}, bf16[256,768]{1,0:T(8,128)(2,1)S(1)}, u32[]{:S(2)}, u32[]{:S(2)}) collective-permute-start(bf16[256,768]{1,0:T(8,128)(2,1)S(1)} %get-tuple-element.69), channel_id=1, source_target_pairs={{0,1},{1,0},{2,3},{3,2},{4,5},{5,4},{6,7},{7,6},{8,9},{9,8},{10,11... | collective-permute-start | bytes 1179656 | tf_op jit(solution)/shard_map/ppermute | solution.py:336
  46.7 4.1 %collective-permute-start.13 = (bf16[256,768]{1,0:T(8,128)(2,1)S(1)}, bf16[256,768]{1,0:T(8,128)(2,1)S(1)}, u32[]{:S(2)}, u32[]{:S(2)}) collective-permute-start(bf16[256,768]{1,0:T(8,128)(2,1)S(1)} %get-tuple-element.70), channel_id=1, source_target_pairs={{0,1},{1,0},{2,3},{3,2},{4,5},{5,4},{6,7},{7,6},{8,9},{9,8},{10,11... | collective-permute-start | bytes 1179656 | tf_op jit(solution)/shard_map/ppermute | solution.py:336
  47.2 3.6 %collective-permute-start.14 = (bf16[256,768]{1,0:T(8,128)(2,1)S(1)}, bf16[256,768]{1,0:T(8,128)(2,1)S(1)}, u32[]{:S(2)}, u32[]{:S(2)}) collective-permute-start(bf16[256,768]{1,0:T(8,128)(2,1)S(1)} %get-tuple-element.71), channel_id=1, source_target_pairs={{0,1},{1,0},{2,3},{3,2},{4,5},{5,4},{6,7},{7,6},{8,9},{9,8},{10,11... | collective-permute-start | bytes 1179656 | tf_op jit(solution)/shard_map/ppermute | solution.py:336
  47.2 3.5 %collective-permute-start.15 = (bf16[256,768]{1,0:T(8,128)(2,1)S(1)}, bf16[256,768]{1,0:T(8,128)(2,1)S(1)}, u32[]{:S(2)}, u32[]{:S(2)}) collective-permute-start(bf16[256,768]{1,0:T(8,128)(2,1)S(1)} %get-tuple-element.72), channel_id=1, source_target_pairs={{0,1},{1,0},{2,3},{3,2},{4,5},{5,4},{6,7},{7,6},{8,9},{9,8},{10,11... | collective-permute-start | bytes 1179656 | tf_op jit(solution)/shard_map/ppermute | solution.py:336
  50.1 5.2 %collective-permute-start.20 = (bf16[256,768]{1,0:T(8,128)(2,1)S(1)}, bf16[256,768]{1,0:T(8,128)(2,1)S(1)}, u32[]{:S(2)}, u32[]{:S(2)}) collective-permute-start(bf16[256,768]{1,0:T(8,128)(2,1)S(1)} %get-tuple-element.50.sum_own), channel_id=1, source_target_pairs={{0,1},{1,0},{2,3},{3,2},{4,5},{5,4},{6,7},{7,6},{8,9},{9,8},{10,11... | collective-permute-start | bytes 1179656 | tf_op jit(solution)/shard_map/ppermute | solution.py:336
  53.5 1.7 %collective-permute-start.19 = (f32[512,128]{1,0:T(8,128)S(1)}, f32[512,128]{1,0:T(8,128)S(1)}, u32[]{:S(2)}, u32[]{:S(2)}) collective-permute-start(f32[512,128]{1,0:T(8,128)S(1)} %get-tuple-element.75.stats), channel_id=1, source_target_pairs={{0,1},{1,0},{2,3},{3,2},{4,5},{5,4},{6,7},{7,6},{8,9},{9,8},{10,11... | collective-permute-start | bytes 786440 | tf_op jit(solution)/shard_map/ppermute | solution.py:336
  54.1 1.4 %collective-permute-start.21 = (bf16[96,768]{1,0:T(8,128)(2,1)S(1)}, bf16[96,768]{1,0:T(8,128)(2,1)S(1)}, u32[]{:S(2)}, u32[]{:S(2)}) collective-permute-start(bf16[96,768]{1,0:T(8,128)(2,1)S(1)} %last_step.3.gram_own), channel_id=1, source_target_pairs={{0,1},{1,0},{2,3},{3,2},{4,5},{5,4},{6,7},{7,6},{8,9},{9,8},{10,11... | collective-permute-start | bytes 442376 | tf_op jit(solution)/shard_map/ppermute | solution.py:336
  57.4 1.8 %collective-permute-start.22 = (f32[256,384]{1,0:T(8,128)S(1)}, f32[256,384]{1,0:T(8,128)S(1)}, u32[]{:S(2)}, u32[]{:S(2)}) collective-permute-start(f32[256,384]{1,0:T(8,128)S(1)} %get-tuple-element.77), channel_id=1, source_target_pairs={{0,1},{1,0},{2,3},{3,2},{4,5},{5,4},{6,7},{7,6},{8,9},{9,8},{10,11... | collective-permute-start | bytes 1179656 | tf_op jit(solution)/shard_map/ppermute | solution.py:336
  57.8 10.1 %collective-permute-start.24 = (s16[400,384]{1,0:T(8,128)(2,1)S(1)}, s16[400,384]{1,0:T(8,128)(2,1)S(1)}, u32[]{:S(2)}, u32[]{:S(2)}) collective-permute-start(s16[400,384]{1,0:T(8,128)(2,1)S(1)} %get-tuple-element.82), channel_id=1, source_target_pairs={{0,2},{1,3},{2,0},{3,1},{4,6},{5,7},{6,4},{7,5},{8,10},{9,11},{10,... | collective-permute-start | bytes 921608 | tf_op jit(solution)/shard_map/ppermute | solution.py:336
  61.1 17.2 %collective-permute-start.23 = (f32[256,384]{1,0:T(8,128)S(1)}, f32[256,384]{1,0:T(8,128)}, u32[]{:S(2)}, u32[]{:S(2)}) collective-permute-start(f32[256,384]{1,0:T(8,128)S(1)} %get-tuple-element.80), channel_id=1, source_target_pairs={{0,1},{1,0},{2,3},{3,2},{4,5},{5,4},{6,7},{7,6},{8,9},{9,8},{10,11... | collective-permute-start | bytes 1179656 | tf_op jit(solution)/shard_map/ppermute | solution.py:336
  61.5 12.2 %collective-permute-start.28 = (s16[400,384]{1,0:T(8,128)(2,1)S(1)}, s16[400,384]{1,0:T(8,128)(2,1)S(1)}, u32[]{:S(2)}, u32[]{:S(2)}) collective-permute-start(s16[400,384]{1,0:T(8,128)(2,1)S(1)} %get-tuple-element.90), channel_id=1, source_target_pairs={{0,2},{1,3},{2,0},{3,1},{4,6},{5,7},{6,4},{7,5},{8,10},{9,11},{10,... | collective-permute-start | bytes 921608 | tf_op jit(solution)/shard_map/ppermute | solution.py:336
  68.8 7.4 %collective-permute-start.25 = (s16[112,384]{1,0:T(8,128)(2,1)S(1)}, s16[112,384]{1,0:T(8,128)(2,1)S(1)}, u32[]{:S(2)}, u32[]{:S(2)}) collective-permute-start(s16[112,384]{1,0:T(8,128)(2,1)S(1)} %get-tuple-element.85), channel_id=1, source_target_pairs={{0,4},{1,5},{2,6},{3,7},{4,0},{5,1},{6,2},{7,3},{8,12},{9,13},{10,... | collective-permute-start | bytes 258056 | tf_op jit(solution)/shard_map/ppermute | solution.py:336
  70.4 11.6 %collective-permute-start.26 = (s16[112,384]{1,0:T(8,128)(2,1)S(1)}, s16[112,384]{1,0:T(8,128)(2,1)S(1)}, u32[]{:S(2)}, u32[]{:S(2)}) collective-permute-start(s16[112,384]{1,0:T(8,128)(2,1)S(1)} %get-tuple-element.86), channel_id=1, source_target_pairs={{0,8},{1,9},{2,10},{3,11},{4,12},{5,13},{6,14},{7,15},{8,0},{9,1},... | collective-permute-start | bytes 258056 | tf_op jit(solution)/shard_map/ppermute | solution.py:336
  72.5 9.5 %collective-permute-start.27 = (s16[112,384]{1,0:T(8,128)(2,1)S(1)}, s16[112,384]{1,0:T(8,128)(2,1)S(1)}, u32[]{:S(2)}, u32[]{:S(2)}) collective-permute-start(s16[112,384]{1,0:T(8,128)(2,1)S(1)} %get-tuple-element.87), channel_id=1, source_target_pairs={{0,12},{1,13},{2,14},{3,15},{4,8},{5,9},{6,10},{7,11},{8,4},{9,5},... | collective-permute-start | bytes 258056 | tf_op jit(solution)/shard_map/ppermute | solution.py:336
  74.5 8.2 %collective-permute-start.29 = (s16[112,384]{1,0:T(8,128)(2,1)S(1)}, s16[112,384]{1,0:T(8,128)(2,1)S(1)}, u32[]{:S(2)}, u32[]{:S(2)}) collective-permute-start(s16[112,384]{1,0:T(8,128)(2,1)S(1)} %get-tuple-element.92), channel_id=1, source_target_pairs={{0,4},{1,5},{2,6},{3,7},{4,0},{5,1},{6,2},{7,3},{8,12},{9,13},{10,... | collective-permute-start | bytes 258056 | tf_op jit(solution)/shard_map/ppermute | solution.py:336
  76.1 10.4 %collective-permute-start.30 = (s16[112,384]{1,0:T(8,128)(2,1)S(1)}, s16[112,384]{1,0:T(8,128)(2,1)S(1)}, u32[]{:S(2)}, u32[]{:S(2)}) collective-permute-start(s16[112,384]{1,0:T(8,128)(2,1)S(1)} %get-tuple-element.93), channel_id=1, source_target_pairs={{0,8},{1,9},{2,10},{3,11},{4,12},{5,13},{6,14},{7,15},{8,0},{9,1},... | collective-permute-start | bytes 258056 | tf_op jit(solution)/shard_map/ppermute | solution.py:336
  78.3 8.3 %collective-permute-start.31 = (s16[112,384]{1,0:T(8,128)(2,1)S(1)}, s16[112,384]{1,0:T(8,128)(2,1)S(1)}, u32[]{:S(2)}, u32[]{:S(2)}) collective-permute-start(s16[112,384]{1,0:T(8,128)(2,1)S(1)} %get-tuple-element.94), channel_id=1, source_target_pairs={{0,12},{1,13},{2,14},{3,15},{4,8},{5,9},{6,10},{7,11},{8,4},{9,5},... | collective-permute-start | bytes 258056 | tf_op jit(solution)/shard_map/ppermute | solution.py:336
  82.6 4.6 %collective-permute-start.32 = (f32[48,384]{1,0:T(8,128)S(1)}, f32[48,384]{1,0:T(8,128)S(1)}, u32[]{:S(2)}, u32[]{:S(2)}) collective-permute-start(f32[48,384]{1,0:T(8,128)S(1)} %get-tuple-element.96), channel_id=1, source_target_pairs={{0,1},{1,0},{2,3},{3,2},{4,5},{5,4},{6,7},{7,6},{8,9},{9,8},{10,11... | collective-permute-start | bytes 221192 | tf_op jit(solution)/shard_map/ppermute | solution.py:336
  87.2 1.3 %collective-permute-start.33 = (f32[48,384]{1,0:T(8,128)S(1)}, f32[48,384]{1,0:T(8,128)S(1)}, u32[]{:S(2)}, u32[]{:S(2)}) collective-permute-start(f32[48,384]{1,0:T(8,128)S(1)} %get-tuple-element.97), channel_id=1, source_target_pairs={{0,1},{1,0},{2,3},{3,2},{4,5},{5,4},{6,7},{7,6},{8,9},{9,8},{10,11... | collective-permute-start | bytes 221192 | tf_op jit(solution)/shard_map/ppermute | solution.py:336

commit v6 on v5

--- a/solution.py
+++ b/solution.py
@@ -15,7 +15,6 @@
 COST = 1000
 CORE, NEXT_Y, NEXT_Z, FAR_Z = 1, 2, 4, 8
 LINE = 4
-CUTS = 2
 TAIL = 16
 
 
@@ -205,6 +204,34 @@
     encode(jnp.concatenate(blocks(1 - y), axis=0), send_ref)
 
 
+def halve_z(values, where_ref, send_ref, keep_ref):
+    rows = keep_ref.shape[0] // 2
+    z = where_ref[1] // 2
+
+    def block(of):
+        return values[pl.ds(pl.multiple_of(of * rows, rows), rows), :]
+
+    keep_ref[...] = jnp.concatenate([block(z), block(z ^ 2)], axis=0)
+    encode(jnp.concatenate([block(z ^ 1), block(z ^ 3)], axis=0), send_ref)
+
+
+def halve_pairs(values, where_ref, send_ref, keep_ref):
+    rows = keep_ref.shape[0] // 2
+    y = where_ref[1] % 2
+
+    def blocks(of):
+        return [values[pl.ds(pl.multiple_of((2 * z + of) * rows, rows), rows), :] for z in range(2)]
+
+    keep_ref[...] = jnp.concatenate(blocks(y), axis=0)
+    encode(jnp.concatenate(blocks(1 - y), axis=0), send_ref)
+
+
+def halve_far(values, where_ref, send_ref, keep_ref):
+    rows = keep_ref.shape[0]
+    keep_ref[...] = values[:rows, :]
+    encode(values[rows:, :], send_ref)
+
+
 def halved_shapes(rows, width):
     return [jax.ShapeDtypeStruct((rows // 2 + TAIL, width), jnp.int16), f32(rows // 2, width)]
 
@@ -240,8 +267,22 @@
     return call(second_kernel, shapes, "second_step", scratch)(where, keep, codes)
 
 
-def last_kernel(where_ref, own, c1, c2, c3, *out_refs, scale):
-    total = own[...] + (decode(c1[...]) + (decode(c2[...]) + decode(c3[...])))
+def next_kernel(where_ref, keep, codes, send_ref, keep_ref, total, *, halving):
+    total[...] = keep[...] + decode(codes[...])
+    halving(total, where_ref, send_ref, keep_ref)
+
+
+def next_step(where, keep, codes, halving):
+    scratch = [pltpu.VMEM(keep.shape, jnp.float32)]
+    kernel = functools.partial(next_kernel, halving=halving)
+    return call(kernel, halved_shapes(*keep.shape), "next_step", scratch)(where, keep, codes)
+
+
+def last_kernel(where_ref, own, *rest, scale, count):
+    codes, out_refs = rest[:count], rest[count:]
+    total = own[...]
+    for ref in codes:
+        total = total + decode(ref[...])
     if scale is None:
         (pair,) = out_refs
         rows = total.shape[0]
@@ -260,7 +301,7 @@
 def last_step(where, own, codes, scale=None):
     rows, width = own.shape
     shapes = [bf16(2 * rows, width)] if scale is None else [f32(rows // 2, width)] * 2
-    return call(functools.partial(last_kernel, scale=scale), shapes, "last_step")(where, own, *codes)
+    return call(functools.partial(last_kernel, scale=scale, count=len(codes)), shapes, "last_step")(where, own, *codes)
 
 
 def targets_kernel(where_ref, blend, stats, stats_other, sum_own, sum_other, gram_own, gram_other, weights, own_ref, other_ref, *rest, cut, width):
@@ -287,7 +328,10 @@
         return
     send_ref, keep_ref, total = rest
     total[...] = grad
-    halve(total, where_ref, send_ref, keep_ref)
+    if cut == 0:
+        halve(total, where_ref, send_ref, keep_ref)
+    else:
+        halve_z(total, where_ref, send_ref, keep_ref)
 
 
 def targets_and_term(where, blend, stats, stats_other, sum_own, sum_other, grams, weights, part, coded):
@@ -401,19 +445,21 @@
         send = lax.dynamic_index_in_dim(summed, 1 - core, 0, keepdims=False)
         return targets, side_by_side([keep], [swap(send, CORE)])
 
-    steps, rest, received = [], [], []
-    for j in range(CUTS):
-        steps.append(term((j, CUTS), True, *rest))
-        rest.append(swap(steps[j][1], CORE))
-        received.append(swap(steps[j][2], NEXT_Y))
-    targets = side_by_side([s[0] for s in steps], rest)[None]
+    steps, rest = [], []
+    for j, axis in enumerate((NEXT_Y, NEXT_Z)):
+        target_own, target_other, send, keep = term((j, 2), True, *rest)
+        rest.append(swap(target_other, CORE))
+        steps.append((target_own, keep, swap(send, axis)))
+    targets = side_by_side([x[0] for x in steps], rest)[None]
     mine, theirs = [], []
-    for j in range(CUTS):
-        own, *codes = second_step(where, steps[j][3], received[j])
-        codes = [swap(c, NEXT_Z * (m + 1)) for m, c in enumerate(codes)]
-        if j == 0:
-            own = after(own, targets)
-        keep, send = last_step(where, own, codes, scale)
+    for (_, keep, codes), halving, axis in zip(steps, (halve_z, halve_pairs), (NEXT_Z, NEXT_Y)):
+        send, keep = next_step(where, keep, codes, halving)
+        codes = swap(send, axis)
+        send, keep = next_step(where, keep, codes, halve_far)
+        codes = swap(send, FAR_Z)
+        if not mine:
+            keep = after(keep, targets)
+        keep, send = last_step(where, keep, [codes], scale)
         mine.append(keep)
         theirs.append(swap(send, CORE))
     return targets, side_by_side(mine, theirs)

time: 89.4 us -> 88.2 us (0.987)
  other arithmetic: 3.3 us -> 2.19 us
  starting transfers between devices: 35.7 us -> 34.6 us
  Pallas kernels: 20.5 us -> 21.5 us
    select_n x2, other arithmetic: 3.22 us -> 2.12 us  [side_by_side(): jnp.where(core == 0, jnp.concatenate(mine + theirs, axis=1), jnp.concaten...]
    ppermute x34 -> x32, starting transfers between devices: 35.7 us -> 34.6 us  [swap(): return lax.ppermute(x, AXES, pairs)]
    pallas_call x14 -> x16, Pallas kernels: 20.5 us -> 21.5 us  [run(): pl.pallas_call(kernel, out_shape=tuple(out_shape), in_specs=[pl.BlockSpec...]
    ppermute x34 -> x32, waiting for transfers between devices: 26.3 us -> 26.2 us  [swap(): return lax.ppermute(x, AXES, pairs)]
  transfers between devices with their start and end apart: 34 -> 32, of which waited for: 10 -> 13; matrix products, arithmetic and copies ran while one was open for 3% -> 2% of each run, Pallas kernels for 21% -> 22%
where the time goes in v6:
time: 88.2 us; the launch traced here: 88 us
  starting transfers between devices  34.6 us (39%)
  waiting for transfers between devices  26.2 us (30%)
  Pallas kernels  21.5 us (24%)
  local copies, waits for them, and re-layouts  2.6 us (3%)
  other arithmetic  2.19 us (2%)
  between operations  0.92 us (1%)
    ppermute x32, starting transfers between devices, swap(): return lax.ppermute(x, AXES, pairs)  34.6 us
    ppermute x32, waiting for transfers between devices, swap(): return lax.ppermute(x, AXES, pairs)  26.2 us
    pallas_call x16, Pallas kernels, run(): pl.pallas_call(kernel, out_shape=tuple(out_shape), in_specs=[pl.BlockSpec...  21.5 us
    unnamed x18, local copies, waits for them, and re-layouts  2.6 us
    select_n x2, other arithmetic, side_by_side(): jnp.where(core == 0, jnp.concatenate(mine + theirs, axis=1), jnp.concaten...  2.12 us
  transfers between devices with their start and end apart: 32, of which 13 were waited for; matrix products, arithmetic and copies ran while one was open for 2% of the time, Pallas kernels for 22%

profile of v6, /device:TPU:0, one launch (start us, length us, event | category | flops | bytes accessed | tf_op | source)
XLA Modules:
  0.0 88.0 jit_solution(10102140723595697143)
XLA Ops:
  0.6 0.5 collective-permute-start
  1.1 0.1 pad_add_fusion.where_ref
  1.2 1.9 %copy-done.2 = bf16[1,8,256,768]{3,2,1,0:T(8,128)(2,1)S(1)} copy-done((bf16[1,8,256,768]{3,2,1,0:T(8,128)(2,1)S(1)}, bf16[1,8,256,768]{3,2,1,0:T(8,128)(2,1)}, u32[]{:S(2)}) %copy-start.2) | copy-done | bytes 3145752
  3.1 0.7 copy-done.8
  3.8 4.2 %gram.1 = (f32[384,768]{1,0:T(8,128)S(1)}, f32[192,768]{1,0:T(8,128)S(1)}, f32[192,768]{1,0:T(8,128)S(1)}, bf16[256,768]{1,0:T(8,128)(2,1)S(1)}) custom-call(s32[2]{0:T(128)S(1)} %pad_add_fusion.where_ref, bf16[1,8,256,768]{3,2,1,0:T(8,128)(2,1)S(1)} %copy-done.2, s32[8,64]{1,0:T(8,128)S(1)} %bitcast.21), custom_call_target="tpu_custom_call" | custom-call | flops 1000 | bytes 1000 | tf_op jit(solution)/shard_map/gram/pallas_call | solution.py:25
  8.0 0.1 collective-permute-start.3
  8.1 0.4 collective-permute-start.4
  8.6 0.0 collective-permute-done.other
  8.6 0.6 cut.2.rest_4_
  9.2 2.7 %collective-permute-start.2 = (bf16[192,768]{1,0:T(8,128)(2,1)S(1)}, bf16[192,768]{1,0:T(8,128)(2,1)S(1)}, u32[]{:S(2)}, u32[]{:S(2)}) collective-permute-start(bf16[192,768]{1,0:T(8,128)(2,1)S(1)} %cut.2.rest_4_), channel_id=1, source_target_pairs={{0,2},{1,3},{2,0},{3,1},{4,6},{5,7},{6,4},{7,5},{8,10},{9,11},{10,... | collective-permute-start | bytes 884744 | tf_op jit(solution)/shard_map/ppermute | solution.py:380
  11.8 2.6 %collective-permute-start.1 = (bf16[192,768]{1,0:T(8,128)(2,1)S(1)}, bf16[192,768]{1,0:T(8,128)(2,1)S(1)}, u32[]{:S(2)}, u32[]{:S(2)}) collective-permute-start(bf16[192,768]{1,0:T(8,128)(2,1)S(1)} %cut.2.rest_4_), channel_id=1, source_target_pairs={{0,8},{1,9},{2,10},{3,11},{4,12},{5,13},{6,14},{7,15},{8,0},{9,1},... | collective-permute-start | bytes 884744 | tf_op jit(solution)/shard_map/ppermute | solution.py:380
  14.4 1.6 %collective-permute-start.16 = (bf16[192,768]{1,0:T(8,128)(2,1)S(1)}, bf16[192,768]{1,0:T(8,128)(2,1)S(1)}, u32[]{:S(2)}, u32[]{:S(2)}) collective-permute-start(bf16[192,768]{1,0:T(8,128)(2,1)S(1)} %cut.2.rest_4_), channel_id=1, source_target_pairs={{0,4},{1,5},{2,6},{3,7},{4,0},{5,1},{6,2},{7,3},{8,12},{9,13},{10,... | collective-permute-start | bytes 884744 | tf_op jit(solution)/shard_map/ppermute | solution.py:380
  16.0 3.5 %collective-permute-done.2.rest_5_ = bf16[192,768]{1,0:T(8,128)(2,1)S(1)} collective-permute-done((bf16[192,768]{1,0:T(8,128)(2,1)S(1)}, bf16[192,768]{1,0:T(8,128)(2,1)S(1)}, u32[]{:S(2)}, u32[]{:S(2)}) %collective-permute-start.2) | collective-permute-done | bytes 294944 | tf_op jit(solution)/shard_map/ppermute | solution.py:380
  19.5 0.9 %first_step.1 = (s16[208,768]{1,0:T(8,128)(2,1)S(1)}, f32[192,768]{1,0:T(8,128)S(1)}) custom-call(s32[2]{0:T(128)S(1)} %pad_add_fusion.where_ref, f32[384,768]{1,0:T(8,128)S(1)} %get-tuple-element.53.mine, f32[192,768]{1,0:T(8,128)S(1)} %collective-permute-done.3.t0, f32[192,768]{1,0:T(8,128)S(1)} %collective-permute-done.4.t1), custom_call_target="tpu_custom_call" | custom-call | flops 1000 | bytes 1000 | tf_op jit(solution)/shard_map/first_step/pallas_call | solution.py:25
  20.4 1.8 %collective-permute-start.7 = (s16[208,768]{1,0:T(8,128)(2,1)S(1)}, s16[208,768]{1,0:T(8,128)(2,1)S(1)}, u32[]{:S(2)}, u32[]{:S(2)}) collective-permute-start(s16[208,768]{1,0:T(8,128)(2,1)S(1)} %get-tuple-element.56), channel_id=1, source_target_pairs={{0,2},{1,3},{2,0},{3,1},{4,6},{5,7},{6,4},{7,5},{8,10},{9,11},{10,... | collective-permute-start | bytes 958472 | tf_op jit(solution)/shard_map/ppermute | solution.py:380
  22.2 6.0 %collective-permute-done.1.rest_8_ = bf16[192,768]{1,0:T(8,128)(2,1)S(1)} collective-permute-done((bf16[192,768]{1,0:T(8,128)(2,1)S(1)}, bf16[192,768]{1,0:T(8,128)(2,1)S(1)}, u32[]{:S(2)}, u32[]{:S(2)}) %collective-permute-start.1) | collective-permute-done | bytes 294944 | tf_op jit(solution)/shard_map/ppermute | solution.py:380
  28.2 0.6 collective-permute-start.5
  28.8 0.5 collective-permute-start.17
  29.3 1.5 %collective-permute-start.8 = (bf16[192,768]{1,0:T(8,128)(2,1)S(1)}, bf16[192,768]{1,0:T(8,128)(2,1)S(1)}, u32[]{:S(2)}, u32[]{:S(2)}) collective-permute-start(bf16[192,768]{1,0:T(8,128)(2,1)S(1)} %collective-permute-done.1.rest_8_), channel_id=1, source_target_pairs={{0,2},{1,3},{2,0},{3,1},{4,6},{5,7},{6,4},{7,5},{8,10},{9,11},{10,... | collective-permute-start | bytes 884744 | tf_op jit(solution)/shard_map/ppermute | solution.py:380
  30.8 0.8 second_step.1
  31.7 3.4 %collective-permute-start.10 = (s16[64,768]{1,0:T(8,128)(2,1)S(1)}, s16[64,768]{1,0:T(8,128)(2,1)S(1)}, u32[]{:S(2)}, u32[]{:S(2)}) collective-permute-start(s16[64,768]{1,0:T(8,128)(2,1)S(1)} %get-tuple-element.66), channel_id=1, source_target_pairs={{0,8},{1,9},{2,10},{3,11},{4,12},{5,13},{6,14},{7,15},{8,0},{9,1},... | collective-permute-start | bytes 294920 | tf_op jit(solution)/shard_map/ppermute | solution.py:380
  35.1 1.3 %collective-permute-done.5.rest_10_ = bf16[192,768]{1,0:T(8,128)(2,1)S(1)} collective-permute-done((bf16[192,768]{1,0:T(8,128)(2,1)S(1)}, bf16[192,768]{1,0:T(8,128)(2,1)S(1)}, u32[]{:S(2)}, u32[]{:S(2)}) %collective-permute-start.5) | collective-permute-done | bytes 294944 | tf_op jit(solution)/shard_map/ppermute | solution.py:380
  36.4 5.6 %collective-permute-start.11 = (s16[64,768]{1,0:T(8,128)(2,1)S(1)}, s16[64,768]{1,0:T(8,128)(2,1)S(1)}, u32[]{:S(2)}, u32[]{:S(2)}) collective-permute-start(s16[64,768]{1,0:T(8,128)(2,1)S(1)} %get-tuple-element.67), channel_id=1, source_target_pairs={{0,12},{1,13},{2,14},{3,15},{4,8},{5,9},{6,10},{7,11},{8,4},{9,5},... | collective-permute-start | bytes 294920 | tf_op jit(solution)/shard_map/ppermute | solution.py:380
  42.1 0.4 collective-permute-start.18
  42.5 0.6 cut.3.weights
  43.1 3.5 %attention.1 = (bf16[256,1536]{1,0:T(8,128)(2,1)S(1)}, bf16[256,768]{1,0:T(8,128)(2,1)S(1)}, bf16[256,768]{1,0:T(8,128)(2,1)S(1)}, bf16[256,768]{1,0:T(8,128)(2,1)S(1)}, bf16[256,768]{1,0:T(8,128)(2,1)S(1)}) custom-call(s32[2]{0:T(128)S(1)} %pad_add_fusion.where_ref, bf16[256,1536]{1,0:T(8,128)(2,1)S(1)} %bitcast.16, bf16[256,1536]{1,0:T(8,128)(2,1)S(1)} %bitcast.17, ...), custom_call_target="tpu_custom_call" | custom-call | flops 1000 | bytes 1000 | tf_op jit(solution)/shard_map/attention/pallas_call | solution.py:25
  46.6 0.1 collective-permute-start.12
  46.7 0.5 collective-permute-start.13
  47.2 0.1 collective-permute-start.14
  47.2 0.4 collective-permute-start.15
  47.7 2.4 %collective-permute-done.18.rest_11_ = bf16[192,768]{1,0:T(8,128)(2,1)S(1)} collective-permute-done((bf16[192,768]{1,0:T(8,128)(2,1)S(1)}, bf16[192,768]{1,0:T(8,128)(2,1)S(1)}, u32[]{:S(2)}, u32[]{:S(2)}) %collective-permute-start.18) | collective-permute-done | bytes 294944 | tf_op jit(solution)/shard_map/ppermute | solution.py:380
  50.1 0.6 last_step.3.gram_own
  50.8 2.8 %branch.1 = (f32[512,768]{1,0:T(8,128)S(1)}, f32[512,128]{1,0:T(8,128)S(1)}) custom-call(s32[2]{0:T(128)S(1)} %pad_add_fusion.where_ref, bf16[256,1536]{1,0:T(8,128)(2,1)S(1)} %get-tuple-element.68.mixed_own, bf16[256,1536]{1,0:T(8,128)(2,1)S(1)} %bitcast.13, bf16[256,1536]{1,0:T(8,128)(2,1)S(1)} %bitcast.15, ...), custom_call_target="tpu_custom_call" | custom-call | flops 1000 | bytes 1000 | tf_op jit(solution)/shard_map/branch/pallas_call | solution.py:25
  53.5 0.6 collective-permute-start.19
  54.1 0.1 collective-permute-start.21
  54.2 1.1 %collective-permute-done.19.stats_other = f32[512,128]{1,0:T(8,128)S(1)} collective-permute-done((f32[512,128]{1,0:T(8,128)S(1)}, f32[512,128]{1,0:T(8,128)S(1)}, u32[]{:S(2)}, u32[]{:S(2)}) %collective-permute-start.19) | collective-permute-done | bytes 262176 | tf_op jit(solution)/shard_map/ppermute | solution.py:380
  55.3 0.2 collective-permute-done.21.gram_other
  55.5 1.9 %targets.2 = (f32[256,384]{1,0:T(8,128)S(1)}, f32[256,384]{1,0:T(8,128)S(1)}, s16[400,384]{1,0:T(8,128)(2,1)S(1)}, f32[384,384]{1,0:T(8,128)S(1)}) custom-call(s32[2]{0:T(128)S(1)} %pad_add_fusion.where_ref, f32[512,768]{1,0:T(8,128)S(1)} %get-tuple-element.74.blend, f32[512,128]{1,0:T(8,128)S(1)} %get-tuple-element.75.stats, ...), custom_call_target="tpu_custom_call" | custom-call | flops 1000 | bytes 1000 | tf_op jit(solution)/shard_map/targets/pallas_call | solution.py:25
  57.4 0.4 collective-permute-start.22
  57.8 0.6 collective-permute-start.24
  58.4 0.7 collective-permute-done.22
  59.2 1.8 %targets.3 = (f32[256,384]{1,0:T(8,128)S(1)}, f32[256,384]{1,0:T(8,128)S(1)}, s16[400,384]{1,0:T(8,128)(2,1)S(1)}, f32[384,384]{1,0:T(8,128)S(1)}) custom-call(s32[2]{0:T(128)S(1)} %pad_add_fusion.where_ref, f32[512,768]{1,0:T(8,128)S(1)} %get-tuple-element.74.blend, f32[512,128]{1,0:T(8,128)S(1)} %get-tuple-element.75.stats, ...), custom_call_target="tpu_custom_call" | custom-call | flops 1000 | bytes 1000 | tf_op jit(solution)/shard_map/targets/pallas_call | solution.py:25
  60.9 1.6 %collective-permute-start.27 = (s16[400,384]{1,0:T(8,128)(2,1)S(1)}, s16[400,384]{1,0:T(8,128)(2,1)S(1)}, u32[]{:S(2)}, u32[]{:S(2)}) collective-permute-start(s16[400,384]{1,0:T(8,128)(2,1)S(1)} %get-tuple-element.90), channel_id=1, source_target_pairs={{0,4},{1,5},{2,6},{3,7},{4,0},{5,1},{6,2},{7,3},{8,12},{9,13},{10,... | collective-permute-start | bytes 921608 | tf_op jit(solution)/shard_map/ppermute | solution.py:380
  62.6 0.1 collective-permute-start.23
  62.7 4.5 %collective-permute-done.24.codes = s16[400,384]{1,0:T(8,128)(2,1)S(1)} collective-permute-done((s16[400,384]{1,0:T(8,128)(2,1)S(1)}, s16[400,384]{1,0:T(8,128)(2,1)S(1)}, u32[]{:S(2)}, u32[]{:S(2)}) %collective-permute-start.24) | collective-permute-done | bytes 307232 | tf_op jit(solution)/shard_map/ppermute | solution.py:380
  67.1 0.8 next_step.4
  67.9 1.6 %collective-permute-start.25 = (s16[208,384]{1,0:T(8,128)(2,1)S(1)}, s16[208,384]{1,0:T(8,128)(2,1)S(1)}, u32[]{:S(2)}, u32[]{:S(2)}) collective-permute-start(s16[208,384]{1,0:T(8,128)(2,1)S(1)} %get-tuple-element.84), channel_id=1, source_target_pairs={{0,4},{1,5},{2,6},{3,7},{4,0},{5,1},{6,2},{7,3},{8,12},{9,13},{10,... | collective-permute-start | bytes 479240 | tf_op jit(solution)/shard_map/ppermute | solution.py:380
  69.5 1.6 %collective-permute-done.27.codes = s16[400,384]{1,0:T(8,128)(2,1)S(1)} collective-permute-done((s16[400,384]{1,0:T(8,128)(2,1)S(1)}, s16[400,384]{1,0:T(8,128)(2,1)S(1)}, u32[]{:S(2)}, u32[]{:S(2)}) %collective-permute-start.27) | collective-permute-done | bytes 307232 | tf_op jit(solution)/shard_map/ppermute | solution.py:380
  71.1 0.8 next_step.6
  71.9 0.4 collective-permute-start.28
  72.3 1.6 %collective-permute-done.25.codes = s16[208,384]{1,0:T(8,128)(2,1)S(1)} collective-permute-done((s16[208,384]{1,0:T(8,128)(2,1)S(1)}, s16[208,384]{1,0:T(8,128)(2,1)S(1)}, u32[]{:S(2)}, u32[]{:S(2)}) %collective-permute-start.25) | collective-permute-done | bytes 159776 | tf_op jit(solution)/shard_map/ppermute | solution.py:380
  74.0 0.6 next_step.5
  74.6 3.5 %collective-permute-start.26 = (s16[112,384]{1,0:T(8,128)(2,1)S(1)}, s16[112,384]{1,0:T(8,128)(2,1)S(1)}, u32[]{:S(2)}, u32[]{:S(2)}) collective-permute-start(s16[112,384]{1,0:T(8,128)(2,1)S(1)} %get-tuple-element.87), channel_id=1, source_target_pairs={{0,8},{1,9},{2,10},{3,11},{4,12},{5,13},{6,14},{7,15},{8,0},{9,1},... | collective-permute-start | bytes 258056 | tf_op jit(solution)/shard_map/ppermute | solution.py:380
  78.1 0.6 next_step.7
  78.7 2.6 %collective-permute-start.29 = (s16[112,384]{1,0:T(8,128)(2,1)S(1)}, s16[112,384]{1,0:T(8,128)(2,1)S(1)}, u32[]{:S(2)}, u32[]{:S(2)}) collective-permute-start(s16[112,384]{1,0:T(8,128)(2,1)S(1)} %get-tuple-element.94), channel_id=1, source_target_pairs={{0,8},{1,9},{2,10},{3,11},{4,12},{5,13},{6,14},{7,15},{8,0},{9,1},... | collective-permute-start | bytes 258056 | tf_op jit(solution)/shard_map/ppermute | solution.py:380
  81.3 1.4 %maximum_select_fusion = f32[1,256,1536]{2,1,0:T(8,128)} fusion(f32[1,256,384]{2,1,0:T(8,128)S(1)} %bitcast.23, f32[1,256,384]{2,1,0:T(8,128)S(1)} %bitcast.22, f32[1,256,384]{2,1,0:T(8,128)S(1)} %bitcast.20, f32[1,256,384]{2,1,0:T(8,128)S(1)} %bitcast.19, pred[]{:T(512)S(6)} %eq.6), kind=kLoop, calls=%fused_computation | loop fusion | flops 2752512 | bytes 3145729 | tf_op jit(solution)/shard_map/jit(_where)/select_n | solution.py:383
  82.7 0.3 collective-permute-done.26.rest_0_
  83.1 0.6 last_step.4
  83.6 0.1 collective-permute-start.30
  83.7 1.7 %collective-permute-done.29.rest_0_ = s16[112,384]{1,0:T(8,128)(2,1)S(1)} collective-permute-done((s16[112,384]{1,0:T(8,128)(2,1)S(1)}, s16[112,384]{1,0:T(8,128)(2,1)S(1)}, u32[]{:S(2)}, u32[]{:S(2)}) %collective-permute-start.29) | collective-permute-done | bytes 86048 | tf_op jit(solution)/shard_map/ppermute | solution.py:380
  85.4 0.6 last_step.5
  85.9 0.1 collective-permute-start.31
  86.0 1.2 %collective-permute-done.31 = f32[48,384]{1,0:T(8,128)S(1)} collective-permute-done((f32[48,384]{1,0:T(8,128)S(1)}, f32[48,384]{1,0:T(8,128)S(1)}, u32[]{:S(2)}, u32[]{:S(2)}) %collective-permute-start.31) | collective-permute-done | bytes 73760 | tf_op jit(solution)/shard_map/ppermute | solution.py:380
  87.3 0.7 maximum_select_fusion.1
  (37 shorter events, 0.1 us)
Async XLA Ops:
  0.6 7.9 %collective-permute-start = (bf16[96,1536]{1,0:T(8,128)(2,1)}, bf16[96,1536]{1,0:T(8,128)(2,1)S(1)}, u32[]{:S(2)}, u32[]{:S(2)}) collective-permute-start(bf16[96,1536]{1,0:T(8,128)(2,1)} %own.1), channel_id=1, source_target_pairs={{0,1},{1,0},{2,3},{3,2},{4,5},{5,4},{6,7},{7,6},{8,9},{9,8},{10,11... | collective-permute-start | bytes 884744 | tf_op jit(solution)/shard_map/ppermute | solution.py:380
  1.2 1.9 %copy-start.2 = (bf16[1,8,256,768]{3,2,1,0:T(8,128)(2,1)S(1)}, bf16[1,8,256,768]{3,2,1,0:T(8,128)(2,1)}, u32[]{:S(2)}) copy-start(bf16[1,8,256,768]{3,2,1,0:T(8,128)(2,1)} %hidden_ref.1) | copy-start | bytes 9437188
  3.1 0.7 copy-start.8
  3.8 4.8 %copy-start.6 = (bf16[96,1536]{1,0:T(8,128)(2,1)S(1)}, bf16[96,1536]{1,0:T(8,128)(2,1)}, u32[]{:S(2)}) copy-start(bf16[96,1536]{1,0:T(8,128)(2,1)} %own.1) | copy-start | bytes 884740
  8.0 11.5 %collective-permute-start.3 = (f32[192,768]{1,0:T(8,128)S(1)}, f32[192,768]{1,0:T(8,128)S(1)}, u32[]{:S(2)}, u32[]{:S(2)}) collective-permute-start(f32[192,768]{1,0:T(8,128)S(1)} %get-tuple-element.54), channel_id=1, source_target_pairs={{0,1},{1,0},{2,3},{3,2},{4,5},{5,4},{6,7},{7,6},{8,9},{9,8},{10,11... | collective-permute-start | bytes 1769480 | tf_op jit(solution)/shard_map/ppermute | solution.py:380
  8.1 11.3 %collective-permute-start.4 = (f32[192,768]{1,0:T(8,128)S(1)}, f32[192,768]{1,0:T(8,128)S(1)}, u32[]{:S(2)}, u32[]{:S(2)}) collective-permute-start(f32[192,768]{1,0:T(8,128)S(1)} %get-tuple-element.55), channel_id=1, source_target_pairs={{0,1},{1,0},{2,3},{3,2},{4,5},{5,4},{6,7},{7,6},{8,9},{9,8},{10,11... | collective-permute-start | bytes 1769480 | tf_op jit(solution)/shard_map/ppermute | solution.py:380
  8.6 22.3 %copy-start.7 = (bf16[48,1536]{1,0:T(8,128)(2,1)S(1)}, bf16[48,1536]{1,0:T(8,128)(2,1)}, u32[]{:S(2)}) copy-start(bf16[48,1536]{1,0:T(8,128)(2,1)} %own.2) | copy-start | bytes 442372
  8.6 34.5 %copy-start.5 = (bf16[1,256,1536]{2,1,0:T(8,128)(2,1)S(1)}, bf16[1,256,1536]{2,1,0:T(8,128)(2,1)}, u32[]{:S(2)}) copy-start(bf16[1,256,1536]{2,1,0:T(8,128)(2,1)} %param.11) | copy-start | bytes 2359300
  9.2 10.3 %collective-permute-start.2 = (bf16[192,768]{1,0:T(8,128)(2,1)S(1)}, bf16[192,768]{1,0:T(8,128)(2,1)S(1)}, u32[]{:S(2)}, u32[]{:S(2)}) collective-permute-start(bf16[192,768]{1,0:T(8,128)(2,1)S(1)} %cut.2.rest_4_), channel_id=1, source_target_pairs={{0,2},{1,3},{2,0},{3,1},{4,6},{5,7},{6,4},{7,5},{8,10},{9,11},{10,... | collective-permute-start | bytes 884744 | tf_op jit(solution)/shard_map/ppermute | solution.py:380
  11.8 16.4 %collective-permute-start.1 = (bf16[192,768]{1,0:T(8,128)(2,1)S(1)}, bf16[192,768]{1,0:T(8,128)(2,1)S(1)}, u32[]{:S(2)}, u32[]{:S(2)}) collective-permute-start(bf16[192,768]{1,0:T(8,128)(2,1)S(1)} %cut.2.rest_4_), channel_id=1, source_target_pairs={{0,8},{1,9},{2,10},{3,11},{4,12},{5,13},{6,14},{7,15},{8,0},{9,1},... | collective-permute-start | bytes 884744 | tf_op jit(solution)/shard_map/ppermute | solution.py:380
  14.4 14.4 %collective-permute-start.16 = (bf16[192,768]{1,0:T(8,128)(2,1)S(1)}, bf16[192,768]{1,0:T(8,128)(2,1)S(1)}, u32[]{:S(2)}, u32[]{:S(2)}) collective-permute-start(bf16[192,768]{1,0:T(8,128)(2,1)S(1)} %cut.2.rest_4_), channel_id=1, source_target_pairs={{0,4},{1,5},{2,6},{3,7},{4,0},{5,1},{6,2},{7,3},{8,12},{9,13},{10,... | collective-permute-start | bytes 884744 | tf_op jit(solution)/shard_map/ppermute | solution.py:380
  19.4 23.6 %copy-start = (bf16[1,256,1536]{2,1,0:T(8,128)(2,1)S(1)}, bf16[1,256,1536]{2,1,0:T(8,128)(2,1)}, u32[]{:S(2)}) copy-start(bf16[1,256,1536]{2,1,0:T(8,128)(2,1)} %param.12) | copy-start | bytes 2359300
  19.4 23.6 %copy-start.1 = (bf16[1,256,1536]{2,1,0:T(8,128)(2,1)S(1)}, bf16[1,256,1536]{2,1,0:T(8,128)(2,1)}, u32[]{:S(2)}) copy-start(bf16[1,256,1536]{2,1,0:T(8,128)(2,1)} %param.13) | copy-start | bytes 2359300
  19.4 23.6 %copy-start.3 = (bf16[1,256,1536]{2,1,0:T(8,128)(2,1)S(1)}, bf16[1,256,1536]{2,1,0:T(8,128)(2,1)}, u32[]{:S(2)}) copy-start(bf16[1,256,1536]{2,1,0:T(8,128)(2,1)} %param.9) | copy-start | bytes 2359300
  19.4 23.6 %copy-start.4 = (bf16[1,256,1536]{2,1,0:T(8,128)(2,1)S(1)}, bf16[1,256,1536]{2,1,0:T(8,128)(2,1)}, u32[]{:S(2)}) copy-start(bf16[1,256,1536]{2,1,0:T(8,128)(2,1)} %param.10) | copy-start | bytes 2359300
  20.4 10.4 %collective-permute-start.7 = (s16[208,768]{1,0:T(8,128)(2,1)S(1)}, s16[208,768]{1,0:T(8,128)(2,1)S(1)}, u32[]{:S(2)}, u32[]{:S(2)}) collective-permute-start(s16[208,768]{1,0:T(8,128)(2,1)S(1)} %get-tuple-element.56), channel_id=1, source_target_pairs={{0,2},{1,3},{2,0},{3,1},{4,6},{5,7},{6,4},{7,5},{8,10},{9,11},{10,... | collective-permute-start | bytes 958472 | tf_op jit(solution)/shard_map/ppermute | solution.py:380
  28.2 8.2 %collective-permute-start.5 = (bf16[192,768]{1,0:T(8,128)(2,1)S(1)}, bf16[192,768]{1,0:T(8,128)(2,1)S(1)}, u32[]{:S(2)}, u32[]{:S(2)}) collective-permute-start(bf16[192,768]{1,0:T(8,128)(2,1)S(1)} %collective-permute-done.1.rest_8_), channel_id=1, source_target_pairs={{0,4},{1,5},{2,6},{3,7},{4,0},{5,1},{6,2},{7,3},{8,12},{9,13},{10,... | collective-permute-start | bytes 884744 | tf_op jit(solution)/shard_map/ppermute | solution.py:380
  28.8 13.3 %collective-permute-start.17 = (bf16[192,768]{1,0:T(8,128)(2,1)S(1)}, bf16[192,768]{1,0:T(8,128)(2,1)S(1)}, u32[]{:S(2)}, u32[]{:S(2)}) collective-permute-start(bf16[192,768]{1,0:T(8,128)(2,1)S(1)} %collective-permute-done.16.rest_6_), channel_id=1, source_target_pairs={{0,2},{1,3},{2,0},{3,1},{4,6},{5,7},{6,4},{7,5},{8,10},{9,11},{10,... | collective-permute-start | bytes 884744 | tf_op jit(solution)/shard_map/ppermute | solution.py:380
  29.3 17.3 %collective-permute-start.8 = (bf16[192,768]{1,0:T(8,128)(2,1)S(1)}, bf16[192,768]{1,0:T(8,128)(2,1)S(1)}, u32[]{:S(2)}, u32[]{:S(2)}) collective-permute-start(bf16[192,768]{1,0:T(8,128)(2,1)S(1)} %collective-permute-done.1.rest_8_), channel_id=1, source_target_pairs={{0,2},{1,3},{2,0},{3,1},{4,6},{5,7},{6,4},{7,5},{8,10},{9,11},{10,... | collective-permute-start | bytes 884744 | tf_op jit(solution)/shard_map/ppermute | solution.py:380
  30.8 11.2 %collective-permute-start.6 = (bf16[48,1536]{1,0:T(8,128)(2,1)S(1)}, bf16[48,1536]{1,0:T(8,128)(2,1)S(1)}, u32[]{:S(2)}, u32[]{:S(2)}) collective-permute-start(bf16[48,1536]{1,0:T(8,128)(2,1)S(1)} %copy-done.7), channel_id=1, source_target_pairs={{0,1},{1,0},{2,3},{3,2},{4,5},{5,4},{6,7},{7,6},{8,9},{9,8},{10,11... | collective-permute-start | bytes 442376 | tf_op jit(solution)/shard_map/ppermute | solution.py:380
  31.7 15.0 %collective-permute-start.10 = (s16[64,768]{1,0:T(8,128)(2,1)S(1)}, s16[64,768]{1,0:T(8,128)(2,1)S(1)}, u32[]{:S(2)}, u32[]{:S(2)}) collective-permute-start(s16[64,768]{1,0:T(8,128)(2,1)S(1)} %get-tuple-element.66), channel_id=1, source_target_pairs={{0,8},{1,9},{2,10},{3,11},{4,12},{5,13},{6,14},{7,15},{8,0},{9,1},... | collective-permute-start | bytes 294920 | tf_op jit(solution)/shard_map/ppermute | solution.py:380
  36.4 10.7 %collective-permute-start.11 = (s16[64,768]{1,0:T(8,128)(2,1)S(1)}, s16[64,768]{1,0:T(8,128)(2,1)S(1)}, u32[]{:S(2)}, u32[]{:S(2)}) collective-permute-start(s16[64,768]{1,0:T(8,128)(2,1)S(1)} %get-tuple-element.67), channel_id=1, source_target_pairs={{0,12},{1,13},{2,14},{3,15},{4,8},{5,9},{6,10},{7,11},{8,4},{9,5},... | collective-permute-start | bytes 294920 | tf_op jit(solution)/shard_map/ppermute | solution.py:380
  42.1 5.2 %collective-permute-start.9 = (s16[64,768]{1,0:T(8,128)(2,1)S(1)}, s16[64,768]{1,0:T(8,128)(2,1)S(1)}, u32[]{:S(2)}, u32[]{:S(2)}) collective-permute-start(s16[64,768]{1,0:T(8,128)(2,1)S(1)} %get-tuple-element.65), channel_id=1, source_target_pairs={{0,4},{1,5},{2,6},{3,7},{4,0},{5,1},{6,2},{7,3},{8,12},{9,13},{10,... | collective-permute-start | bytes 294920 | tf_op jit(solution)/shard_map/ppermute | solution.py:380
  42.1 8.0 %collective-permute-start.18 = (bf16[192,768]{1,0:T(8,128)(2,1)S(1)}, bf16[192,768]{1,0:T(8,128)(2,1)S(1)}, u32[]{:S(2)}, u32[]{:S(2)}) collective-permute-start(bf16[192,768]{1,0:T(8,128)(2,1)S(1)} %collective-permute-done.5.rest_10_), channel_id=1, source_target_pairs={{0,2},{1,3},{2,0},{3,1},{4,6},{5,7},{6,4},{7,5},{8,10},{9,11},{10,... | collective-permute-start | bytes 884744 | tf_op jit(solution)/shard_map/ppermute | solution.py:380
  46.6 4.2 %collective-permute-start.12 = (bf16[256,768]{1,0:T(8,128)(2,1)S(1)}, bf16[256,768]{1,0:T(8,128)(2,1)S(1)}, u32[]{:S(2)}, u32[]{:S(2)}) collective-permute-start(bf16[256,768]{1,0:T(8,128)(2,1)S(1)} %get-tuple-element.69), channel_id=1, source_target_pairs={{0,1},{1,0},{2,3},{3,2},{4,5},{5,4},{6,7},{7,6},{8,9},{9,8},{10,11... | collective-permute-start | bytes 1179656 | tf_op jit(solution)/shard_map/ppermute | solution.py:380
  46.7 4.1 %collective-permute-start.13 = (bf16[256,768]{1,0:T(8,128)(2,1)S(1)}, bf16[256,768]{1,0:T(8,128)(2,1)S(1)}, u32[]{:S(2)}, u32[]{:S(2)}) collective-permute-start(bf16[256,768]{1,0:T(8,128)(2,1)S(1)} %get-tuple-element.70), channel_id=1, source_target_pairs={{0,1},{1,0},{2,3},{3,2},{4,5},{5,4},{6,7},{7,6},{8,9},{9,8},{10,11... | collective-permute-start | bytes 1179656 | tf_op jit(solution)/shard_map/ppermute | solution.py:380
  47.2 3.6 %collective-permute-start.14 = (bf16[256,768]{1,0:T(8,128)(2,1)S(1)}, bf16[256,768]{1,0:T(8,128)(2,1)S(1)}, u32[]{:S(2)}, u32[]{:S(2)}) collective-permute-start(bf16[256,768]{1,0:T(8,128)(2,1)S(1)} %get-tuple-element.71), channel_id=1, source_target_pairs={{0,1},{1,0},{2,3},{3,2},{4,5},{5,4},{6,7},{7,6},{8,9},{9,8},{10,11... | collective-permute-start | bytes 1179656 | tf_op jit(solution)/shard_map/ppermute | solution.py:380
  47.2 3.5 %collective-permute-start.15 = (bf16[256,768]{1,0:T(8,128)(2,1)S(1)}, bf16[256,768]{1,0:T(8,128)(2,1)S(1)}, u32[]{:S(2)}, u32[]{:S(2)}) collective-permute-start(bf16[256,768]{1,0:T(8,128)(2,1)S(1)} %get-tuple-element.72), channel_id=1, source_target_pairs={{0,1},{1,0},{2,3},{3,2},{4,5},{5,4},{6,7},{7,6},{8,9},{9,8},{10,11... | collective-permute-start | bytes 1179656 | tf_op jit(solution)/shard_map/ppermute | solution.py:380
  50.1 5.2 %collective-permute-start.20 = (bf16[256,768]{1,0:T(8,128)(2,1)S(1)}, bf16[256,768]{1,0:T(8,128)(2,1)S(1)}, u32[]{:S(2)}, u32[]{:S(2)}) collective-permute-start(bf16[256,768]{1,0:T(8,128)(2,1)S(1)} %get-tuple-element.50.sum_own), channel_id=1, source_target_pairs={{0,1},{1,0},{2,3},{3,2},{4,5},{5,4},{6,7},{7,6},{8,9},{9,8},{10,11... | collective-permute-start | bytes 1179656 | tf_op jit(solution)/shard_map/ppermute | solution.py:380
  53.5 1.7 %collective-permute-start.19 = (f32[512,128]{1,0:T(8,128)S(1)}, f32[512,128]{1,0:T(8,128)S(1)}, u32[]{:S(2)}, u32[]{:S(2)}) collective-permute-start(f32[512,128]{1,0:T(8,128)S(1)} %get-tuple-element.75.stats), channel_id=1, source_target_pairs={{0,1},{1,0},{2,3},{3,2},{4,5},{5,4},{6,7},{7,6},{8,9},{9,8},{10,11... | collective-permute-start | bytes 786440 | tf_op jit(solution)/shard_map/ppermute | solution.py:380
  54.1 1.4 %collective-permute-start.21 = (bf16[96,768]{1,0:T(8,128)(2,1)S(1)}, bf16[96,768]{1,0:T(8,128)(2,1)S(1)}, u32[]{:S(2)}, u32[]{:S(2)}) collective-permute-start(bf16[96,768]{1,0:T(8,128)(2,1)S(1)} %last_step.3.gram_own), channel_id=1, source_target_pairs={{0,1},{1,0},{2,3},{3,2},{4,5},{5,4},{6,7},{7,6},{8,9},{9,8},{10,11... | collective-permute-start | bytes 442376 | tf_op jit(solution)/shard_map/ppermute | solution.py:380
  57.4 1.8 %collective-permute-start.22 = (f32[256,384]{1,0:T(8,128)S(1)}, f32[256,384]{1,0:T(8,128)S(1)}, u32[]{:S(2)}, u32[]{:S(2)}) collective-permute-start(f32[256,384]{1,0:T(8,128)S(1)} %get-tuple-element.77), channel_id=1, source_target_pairs={{0,1},{1,0},{2,3},{3,2},{4,5},{5,4},{6,7},{7,6},{8,9},{9,8},{10,11... | collective-permute-start | bytes 1179656 | tf_op jit(solution)/shard_map/ppermute | solution.py:380
  57.8 9.3 %collective-permute-start.24 = (s16[400,384]{1,0:T(8,128)(2,1)S(1)}, s16[400,384]{1,0:T(8,128)(2,1)S(1)}, u32[]{:S(2)}, u32[]{:S(2)}) collective-permute-start(s16[400,384]{1,0:T(8,128)(2,1)S(1)} %get-tuple-element.82), channel_id=1, source_target_pairs={{0,2},{1,3},{2,0},{3,1},{4,6},{5,7},{6,4},{7,5},{8,10},{9,11},{10,... | collective-permute-start | bytes 921608 | tf_op jit(solution)/shard_map/ppermute | solution.py:380
  60.9 10.2 %collective-permute-start.27 = (s16[400,384]{1,0:T(8,128)(2,1)S(1)}, s16[400,384]{1,0:T(8,128)(2,1)S(1)}, u32[]{:S(2)}, u32[]{:S(2)}) collective-permute-start(s16[400,384]{1,0:T(8,128)(2,1)S(1)} %get-tuple-element.90), channel_id=1, source_target_pairs={{0,4},{1,5},{2,6},{3,7},{4,0},{5,1},{6,2},{7,3},{8,12},{9,13},{10,... | collective-permute-start | bytes 921608 | tf_op jit(solution)/shard_map/ppermute | solution.py:380
  62.6 18.7 %collective-permute-start.23 = (f32[256,384]{1,0:T(8,128)S(1)}, f32[256,384]{1,0:T(8,128)S(1)}, u32[]{:S(2)}, u32[]{:S(2)}) collective-permute-start(f32[256,384]{1,0:T(8,128)S(1)} %get-tuple-element.80), channel_id=1, source_target_pairs={{0,1},{1,0},{2,3},{3,2},{4,5},{5,4},{6,7},{7,6},{8,9},{9,8},{10,11... | collective-permute-start | bytes 1179656 | tf_op jit(solution)/shard_map/ppermute | solution.py:380
  67.9 6.0 %collective-permute-start.25 = (s16[208,384]{1,0:T(8,128)(2,1)S(1)}, s16[208,384]{1,0:T(8,128)(2,1)S(1)}, u32[]{:S(2)}, u32[]{:S(2)}) collective-permute-start(s16[208,384]{1,0:T(8,128)(2,1)S(1)} %get-tuple-element.84), channel_id=1, source_target_pairs={{0,4},{1,5},{2,6},{3,7},{4,0},{5,1},{6,2},{7,3},{8,12},{9,13},{10,... | collective-permute-start | bytes 479240 | tf_op jit(solution)/shard_map/ppermute | solution.py:380
  71.9 6.2 %collective-permute-start.28 = (s16[208,384]{1,0:T(8,128)(2,1)S(1)}, s16[208,384]{1,0:T(8,128)(2,1)S(1)}, u32[]{:S(2)}, u32[]{:S(2)}) collective-permute-start(s16[208,384]{1,0:T(8,128)(2,1)S(1)} %get-tuple-element.92), channel_id=1, source_target_pairs={{0,2},{1,3},{2,0},{3,1},{4,6},{5,7},{6,4},{7,5},{8,10},{9,11},{10,... | collective-permute-start | bytes 479240 | tf_op jit(solution)/shard_map/ppermute | solution.py:380
  74.6 8.4 %collective-permute-start.26 = (s16[112,384]{1,0:T(8,128)(2,1)S(1)}, s16[112,384]{1,0:T(8,128)(2,1)S(1)}, u32[]{:S(2)}, u32[]{:S(2)}) collective-permute-start(s16[112,384]{1,0:T(8,128)(2,1)S(1)} %get-tuple-element.87), channel_id=1, source_target_pairs={{0,8},{1,9},{2,10},{3,11},{4,12},{5,13},{6,14},{7,15},{8,0},{9,1},... | collective-permute-start | bytes 258056 | tf_op jit(solution)/shard_map/ppermute | solution.py:380
  78.7 6.7 %collective-permute-start.29 = (s16[112,384]{1,0:T(8,128)(2,1)S(1)}, s16[112,384]{1,0:T(8,128)(2,1)S(1)}, u32[]{:S(2)}, u32[]{:S(2)}) collective-permute-start(s16[112,384]{1,0:T(8,128)(2,1)S(1)} %get-tuple-element.94), channel_id=1, source_target_pairs={{0,8},{1,9},{2,10},{3,11},{4,12},{5,13},{6,14},{7,15},{8,0},{9,1},... | collective-permute-start | bytes 258056 | tf_op jit(solution)/shard_map/ppermute | solution.py:380
  83.6 2.4 %collective-permute-start.30 = (f32[48,384]{1,0:T(8,128)S(1)}, f32[48,384]{1,0:T(8,128)S(1)}, u32[]{:S(2)}, u32[]{:S(2)}) collective-permute-start(f32[48,384]{1,0:T(8,128)S(1)} %get-tuple-element.96), channel_id=1, source_target_pairs={{0,1},{1,0},{2,3},{3,2},{4,5},{5,4},{6,7},{7,6},{8,9},{9,8},{10,11... | collective-permute-start | bytes 221192 | tf_op jit(solution)/shard_map/ppermute | solution.py:380
  85.9 1.3 %collective-permute-start.31 = (f32[48,384]{1,0:T(8,128)S(1)}, f32[48,384]{1,0:T(8,128)S(1)}, u32[]{:S(2)}, u32[]{:S(2)}) collective-permute-start(f32[48,384]{1,0:T(8,128)S(1)} %get-tuple-element.97), channel_id=1, source_target_pairs={{0,1},{1,0},{2,3},{3,2},{4,5},{5,4},{6,7},{7,6},{8,9},{9,8},{10,11... | collective-permute-start | bytes 221192 | tf_op jit(solution)/shard_map/ppermute | solution.py:380

commit v7 on v6

--- a/solution.py
+++ b/solution.py
@@ -76,6 +76,17 @@
     return call(kernel, shapes, "attention")(where, q, k, v, stream, earlier)
 
 
+def symmetric_product(x, out):
+    width = x.shape[1]
+    block = 256 if width % 256 == 0 else width
+    for at in range(0, width, block):
+        here = slice(at, at + block)
+        strip = contract_rows(x[:, here], x[:, at:])
+        out[here, at:] = strip
+        for later in range(at + block, width, block):
+            out[later : later + block, here] = strip[:, later - at : later - at + block].T
+
+
 def gram_kernel(where_ref, hidden_ref, kept_ref, *rest, parted):
     *gram_refs, sum_ref, rows_all, total = rest
     clones, patches = hidden_ref.shape[1:3]
@@ -91,9 +102,9 @@
         sums = wide if sums is None else sums + wide
     sum_ref[...] = sums.astype(sum_ref.dtype)
     if not parted:
-        gram_refs[0][...] = contract_rows(rows_all[...], rows_all[...])
+        symmetric_product(rows_all, gram_refs[0])
         return
-    total[...] = contract_rows(rows_all[...], rows_all[...])
+    symmetric_product(rows_all, total)
     mine, *theirs = gram_refs
     core = where_ref[0]
     chips, rows = parted
@@ -447,7 +458,7 @@
 
     steps, rest = [], []
     for j, axis in enumerate((NEXT_Y, NEXT_Z)):
-        target_own, target_other, send, keep = term((j, 2), True, *rest)
+        target_own, target_other, send, keep = term((j, 2), True)
         rest.append(swap(target_other, CORE))
         steps.append((target_own, keep, swap(send, axis)))
     targets = side_by_side([x[0] for x in steps], rest)[None]

time: 88.2 us -> 86.6 us (0.982)
  waiting for transfers between devices: 26.2 us -> 24.4 us
  other arithmetic: 2.19 us -> 3.3 us
  Pallas kernels: 21.5 us -> 20.6 us
    ppermute x32, waiting for transfers between devices: 26.2 us -> 24.4 us  [swap(): return lax.ppermute(x, AXES, pairs)]
    select_n x2, other arithmetic: 2.12 us -> 3.22 us  [side_by_side(): jnp.where(core == 0, jnp.concatenate(mine + theirs, axis=1), jnp.concaten...]
    pallas_call x16, Pallas kernels: 21.5 us -> 20.6 us  [run(): pl.pallas_call(kernel, out_shape=tuple(out_shape), in_specs=[pl.BlockSpec...]
  transfers between devices with their start and end apart: 32 -> 32, of which waited for: 13 -> 11; matrix products, arithmetic and copies ran while one was open for 2% -> 3% of each run, Pallas kernels for 22% -> 22%
where the time goes in v7:
time: 86.6 us; the launch traced here: 86.4 us
  starting transfers between devices  34.5 us (40%)
  waiting for transfers between devices  24.4 us (28%)
  Pallas kernels  20.6 us (24%)
  other arithmetic  3.3 us (4%)
  local copies, waits for them, and re-layouts  2.6 us (3%)
  between operations  0.92 us (1%)
    ppermute x32, starting transfers between devices, swap(): return lax.ppermute(x, AXES, pairs)  34.5 us
    ppermute x32, waiting for transfers between devices, swap(): return lax.ppermute(x, AXES, pairs)  24.4 us
    pallas_call x16, Pallas kernels, run(): pl.pallas_call(kernel, out_shape=tuple(out_shape), in_specs=[pl.BlockSpec...  20.6 us
    select_n x2, other arithmetic, side_by_side(): jnp.where(core == 0, jnp.concatenate(mine + theirs, axis=1), jnp.concaten...  3.22 us
    unnamed x18, local copies, waits for them, and re-layouts  2.6 us
  transfers between devices with their start and end apart: 32, of which 11 were waited for; matrix products, arithmetic and copies ran while one was open for 3% of the time, Pallas kernels for 22%

profile of v7, /device:TPU:0, one launch (start us, length us, event | category | flops | bytes accessed | tf_op | source)
XLA Modules:
  0.0 86.4 jit_solution(16040174014503461525)
XLA Ops:
  0.6 0.5 collective-permute-start
  1.1 0.1 pad_add_fusion.where_ref
  1.2 1.9 %copy-done.2 = bf16[1,8,256,768]{3,2,1,0:T(8,128)(2,1)S(1)} copy-done((bf16[1,8,256,768]{3,2,1,0:T(8,128)(2,1)S(1)}, bf16[1,8,256,768]{3,2,1,0:T(8,128)(2,1)}, u32[]{:S(2)}) %copy-start.2) | copy-done | bytes 3145752
  3.1 0.7 copy-done.8
  3.8 3.3 %gram.1 = (f32[384,768]{1,0:T(8,128)S(1)}, f32[192,768]{1,0:T(8,128)S(1)}, f32[192,768]{1,0:T(8,128)S(1)}, bf16[256,768]{1,0:T(8,128)(2,1)S(1)}) custom-call(s32[2]{0:T(128)S(1)} %pad_add_fusion.where_ref, bf16[1,8,256,768]{3,2,1,0:T(8,128)(2,1)S(1)} %copy-done.2, s32[8,64]{1,0:T(8,128)S(1)} %bitcast.21), custom_call_target="tpu_custom_call" | custom-call | flops 1000 | bytes 1000 | tf_op jit(solution)/shard_map/gram/pallas_call | solution.py:25
  7.1 0.1 collective-permute-start.3
  7.2 0.5 collective-permute-start.4
  7.7 0.0 collective-permute-done.other
  7.7 0.6 cut.2.rest_4_
  8.2 2.7 %collective-permute-start.2 = (bf16[192,768]{1,0:T(8,128)(2,1)S(1)}, bf16[192,768]{1,0:T(8,128)(2,1)S(1)}, u32[]{:S(2)}, u32[]{:S(2)}) collective-permute-start(bf16[192,768]{1,0:T(8,128)(2,1)S(1)} %cut.2.rest_4_), channel_id=1, source_target_pairs={{0,2},{1,3},{2,0},{3,1},{4,6},{5,7},{6,4},{7,5},{8,10},{9,11},{10,... | collective-permute-start | bytes 884744 | tf_op jit(solution)/shard_map/ppermute | solution.py:391
  10.9 2.6 %collective-permute-start.1 = (bf16[192,768]{1,0:T(8,128)(2,1)S(1)}, bf16[192,768]{1,0:T(8,128)(2,1)S(1)}, u32[]{:S(2)}, u32[]{:S(2)}) collective-permute-start(bf16[192,768]{1,0:T(8,128)(2,1)S(1)} %cut.2.rest_4_), channel_id=1, source_target_pairs={{0,8},{1,9},{2,10},{3,11},{4,12},{5,13},{6,14},{7,15},{8,0},{9,1},... | collective-permute-start | bytes 884744 | tf_op jit(solution)/shard_map/ppermute | solution.py:391
  13.5 1.6 %collective-permute-start.16 = (bf16[192,768]{1,0:T(8,128)(2,1)S(1)}, bf16[192,768]{1,0:T(8,128)(2,1)S(1)}, u32[]{:S(2)}, u32[]{:S(2)}) collective-permute-start(bf16[192,768]{1,0:T(8,128)(2,1)S(1)} %cut.2.rest_4_), channel_id=1, source_target_pairs={{0,4},{1,5},{2,6},{3,7},{4,0},{5,1},{6,2},{7,3},{8,12},{9,13},{10,... | collective-permute-start | bytes 884744 | tf_op jit(solution)/shard_map/ppermute | solution.py:391
  15.1 3.4 %collective-permute-done.2.rest_5_ = bf16[192,768]{1,0:T(8,128)(2,1)S(1)} collective-permute-done((bf16[192,768]{1,0:T(8,128)(2,1)S(1)}, bf16[192,768]{1,0:T(8,128)(2,1)S(1)}, u32[]{:S(2)}, u32[]{:S(2)}) %collective-permute-start.2) | collective-permute-done | bytes 294944 | tf_op jit(solution)/shard_map/ppermute | solution.py:391
  18.5 0.0 collective-permute-done.3.t0
  18.5 0.9 %first_step.1 = (s16[208,768]{1,0:T(8,128)(2,1)S(1)}, f32[192,768]{1,0:T(8,128)S(1)}) custom-call(s32[2]{0:T(128)S(1)} %pad_add_fusion.where_ref, f32[384,768]{1,0:T(8,128)S(1)} %get-tuple-element.52.mine, f32[192,768]{1,0:T(8,128)S(1)} %collective-permute-done.3.t0, f32[192,768]{1,0:T(8,128)S(1)} %collective-permute-done.4.t1), custom_call_target="tpu_custom_call" | custom-call | flops 1000 | bytes 1000 | tf_op jit(solution)/shard_map/first_step/pallas_call | solution.py:25
  19.5 1.8 %collective-permute-start.7 = (s16[208,768]{1,0:T(8,128)(2,1)S(1)}, s16[208,768]{1,0:T(8,128)(2,1)S(1)}, u32[]{:S(2)}, u32[]{:S(2)}) collective-permute-start(s16[208,768]{1,0:T(8,128)(2,1)S(1)} %get-tuple-element.55), channel_id=1, source_target_pairs={{0,2},{1,3},{2,0},{3,1},{4,6},{5,7},{6,4},{7,5},{8,10},{9,11},{10,... | collective-permute-start | bytes 958472 | tf_op jit(solution)/shard_map/ppermute | solution.py:391
  21.3 6.0 %collective-permute-done.1.rest_8_ = bf16[192,768]{1,0:T(8,128)(2,1)S(1)} collective-permute-done((bf16[192,768]{1,0:T(8,128)(2,1)S(1)}, bf16[192,768]{1,0:T(8,128)(2,1)S(1)}, u32[]{:S(2)}, u32[]{:S(2)}) %collective-permute-start.1) | collective-permute-done | bytes 294944 | tf_op jit(solution)/shard_map/ppermute | solution.py:391
  27.3 0.6 collective-permute-start.5
  27.9 0.5 collective-permute-start.17
  28.4 1.5 %collective-permute-start.8 = (bf16[192,768]{1,0:T(8,128)(2,1)S(1)}, bf16[192,768]{1,0:T(8,128)(2,1)S(1)}, u32[]{:S(2)}, u32[]{:S(2)}) collective-permute-start(bf16[192,768]{1,0:T(8,128)(2,1)S(1)} %collective-permute-done.1.rest_8_), channel_id=1, source_target_pairs={{0,2},{1,3},{2,0},{3,1},{4,6},{5,7},{6,4},{7,5},{8,10},{9,11},{10,... | collective-permute-start | bytes 884744 | tf_op jit(solution)/shard_map/ppermute | solution.py:391
  29.9 0.8 second_step.1
  30.8 3.4 %collective-permute-start.10 = (s16[64,768]{1,0:T(8,128)(2,1)S(1)}, s16[64,768]{1,0:T(8,128)(2,1)S(1)}, u32[]{:S(2)}, u32[]{:S(2)}) collective-permute-start(s16[64,768]{1,0:T(8,128)(2,1)S(1)} %get-tuple-element.65), channel_id=1, source_target_pairs={{0,8},{1,9},{2,10},{3,11},{4,12},{5,13},{6,14},{7,15},{8,0},{9,1},... | collective-permute-start | bytes 294920 | tf_op jit(solution)/shard_map/ppermute | solution.py:391
  34.2 1.3 %collective-permute-done.5.rest_10_ = bf16[192,768]{1,0:T(8,128)(2,1)S(1)} collective-permute-done((bf16[192,768]{1,0:T(8,128)(2,1)S(1)}, bf16[192,768]{1,0:T(8,128)(2,1)S(1)}, u32[]{:S(2)}, u32[]{:S(2)}) %collective-permute-start.5) | collective-permute-done | bytes 294944 | tf_op jit(solution)/shard_map/ppermute | solution.py:391
  35.5 5.7 %collective-permute-start.11 = (s16[64,768]{1,0:T(8,128)(2,1)S(1)}, s16[64,768]{1,0:T(8,128)(2,1)S(1)}, u32[]{:S(2)}, u32[]{:S(2)}) collective-permute-start(s16[64,768]{1,0:T(8,128)(2,1)S(1)} %get-tuple-element.66), channel_id=1, source_target_pairs={{0,12},{1,13},{2,14},{3,15},{4,8},{5,9},{6,10},{7,11},{8,4},{9,5},... | collective-permute-start | bytes 294920 | tf_op jit(solution)/shard_map/ppermute | solution.py:391
  41.2 0.0 collective-permute-done.17.rest_7_
  41.2 0.0 collective-permute-start.9
  41.2 0.4 collective-permute-start.18
  41.6 0.6 cut.3.weights
  42.2 3.5 %attention.1 = (bf16[256,1536]{1,0:T(8,128)(2,1)S(1)}, bf16[256,768]{1,0:T(8,128)(2,1)S(1)}, bf16[256,768]{1,0:T(8,128)(2,1)S(1)}, bf16[256,768]{1,0:T(8,128)(2,1)S(1)}, bf16[256,768]{1,0:T(8,128)(2,1)S(1)}) custom-call(s32[2]{0:T(128)S(1)} %pad_add_fusion.where_ref, bf16[256,1536]{1,0:T(8,128)(2,1)S(1)} %bitcast.16, bf16[256,1536]{1,0:T(8,128)(2,1)S(1)} %bitcast.17, ...), custom_call_target="tpu_custom_call" | custom-call | flops 1000 | bytes 1000 | tf_op jit(solution)/shard_map/attention/pallas_call | solution.py:25
  45.7 0.1 collective-permute-start.12
  45.8 0.5 collective-permute-start.13
  46.3 0.1 collective-permute-start.14
  46.3 0.4 collective-permute-start.15
  46.8 2.4 %collective-permute-done.18.rest_11_ = bf16[192,768]{1,0:T(8,128)(2,1)S(1)} collective-permute-done((bf16[192,768]{1,0:T(8,128)(2,1)S(1)}, bf16[192,768]{1,0:T(8,128)(2,1)S(1)}, u32[]{:S(2)}, u32[]{:S(2)}) %collective-permute-start.18) | collective-permute-done | bytes 294944 | tf_op jit(solution)/shard_map/ppermute | solution.py:391
  49.2 0.6 last_step.3.gram_own
  49.9 2.8 %branch.1 = (f32[512,768]{1,0:T(8,128)S(1)}, f32[512,128]{1,0:T(8,128)S(1)}) custom-call(s32[2]{0:T(128)S(1)} %pad_add_fusion.where_ref, bf16[256,1536]{1,0:T(8,128)(2,1)S(1)} %get-tuple-element.67.mixed_own, bf16[256,1536]{1,0:T(8,128)(2,1)S(1)} %bitcast.13, bf16[256,1536]{1,0:T(8,128)(2,1)S(1)} %bitcast.15, ...), custom_call_target="tpu_custom_call" | custom-call | flops 1000 | bytes 1000 | tf_op jit(solution)/shard_map/branch/pallas_call | solution.py:25
  52.6 0.6 collective-permute-start.19
  53.2 0.1 collective-permute-start.21
  53.3 1.1 %collective-permute-done.19.stats_other = f32[512,128]{1,0:T(8,128)S(1)} collective-permute-done((f32[512,128]{1,0:T(8,128)S(1)}, f32[512,128]{1,0:T(8,128)S(1)}, u32[]{:S(2)}, u32[]{:S(2)}) %collective-permute-start.19) | collective-permute-done | bytes 262176 | tf_op jit(solution)/shard_map/ppermute | solution.py:391
  54.4 0.2 collective-permute-done.21.gram_other
  54.6 1.9 %targets.2 = (f32[256,384]{1,0:T(8,128)S(1)}, f32[256,384]{1,0:T(8,128)S(1)}, s16[400,384]{1,0:T(8,128)(2,1)S(1)}, f32[384,384]{1,0:T(8,128)S(1)}) custom-call(s32[2]{0:T(128)S(1)} %pad_add_fusion.where_ref, f32[512,768]{1,0:T(8,128)S(1)} %get-tuple-element.73.blend, f32[512,128]{1,0:T(8,128)S(1)} %get-tuple-element.74.stats, ...), custom_call_target="tpu_custom_call" | custom-call | flops 1000 | bytes 1000 | tf_op jit(solution)/shard_map/targets/pallas_call | solution.py:25
  56.5 0.9 %collective-permute-start.24 = (s16[400,384]{1,0:T(8,128)(2,1)S(1)}, s16[400,384]{1,0:T(8,128)(2,1)S(1)}, u32[]{:S(2)}, u32[]{:S(2)}) collective-permute-start(s16[400,384]{1,0:T(8,128)(2,1)S(1)} %get-tuple-element.80), channel_id=1, source_target_pairs={{0,2},{1,3},{2,0},{3,1},{4,6},{5,7},{6,4},{7,5},{8,10},{9,11},{10,... | collective-permute-start | bytes 921608 | tf_op jit(solution)/shard_map/ppermute | solution.py:391
  57.4 1.8 %targets.3 = (f32[256,384]{1,0:T(8,128)S(1)}, f32[256,384]{1,0:T(8,128)S(1)}, s16[400,384]{1,0:T(8,128)(2,1)S(1)}, f32[384,384]{1,0:T(8,128)S(1)}) custom-call(s32[2]{0:T(128)S(1)} %pad_add_fusion.where_ref, f32[512,768]{1,0:T(8,128)S(1)} %get-tuple-element.73.blend, f32[512,128]{1,0:T(8,128)S(1)} %get-tuple-element.74.stats, ...), custom_call_target="tpu_custom_call" | custom-call | flops 1000 | bytes 1000 | tf_op jit(solution)/shard_map/targets/pallas_call | solution.py:25
  59.1 2.0 %collective-permute-start.27 = (s16[400,384]{1,0:T(8,128)(2,1)S(1)}, s16[400,384]{1,0:T(8,128)(2,1)S(1)}, u32[]{:S(2)}, u32[]{:S(2)}) collective-permute-start(s16[400,384]{1,0:T(8,128)(2,1)S(1)} %get-tuple-element.88), channel_id=1, source_target_pairs={{0,4},{1,5},{2,6},{3,7},{4,0},{5,1},{6,2},{7,3},{8,12},{9,13},{10,... | collective-permute-start | bytes 921608 | tf_op jit(solution)/shard_map/ppermute | solution.py:391
  61.2 0.5 collective-permute-start.23
  61.7 4.4 %collective-permute-done.24.codes = s16[400,384]{1,0:T(8,128)(2,1)S(1)} collective-permute-done((s16[400,384]{1,0:T(8,128)(2,1)S(1)}, s16[400,384]{1,0:T(8,128)(2,1)S(1)}, u32[]{:S(2)}, u32[]{:S(2)}) %collective-permute-start.24) | collective-permute-done | bytes 307232 | tf_op jit(solution)/shard_map/ppermute | solution.py:391
  66.1 0.8 next_step.4
  66.9 1.6 %collective-permute-start.25 = (s16[208,384]{1,0:T(8,128)(2,1)S(1)}, s16[208,384]{1,0:T(8,128)(2,1)S(1)}, u32[]{:S(2)}, u32[]{:S(2)}) collective-permute-start(s16[208,384]{1,0:T(8,128)(2,1)S(1)} %get-tuple-element.82), channel_id=1, source_target_pairs={{0,4},{1,5},{2,6},{3,7},{4,0},{5,1},{6,2},{7,3},{8,12},{9,13},{10,... | collective-permute-start | bytes 479240 | tf_op jit(solution)/shard_map/ppermute | solution.py:391
  68.5 0.8 next_step.6
  69.3 1.2 %collective-permute-start.28 = (s16[208,384]{1,0:T(8,128)(2,1)S(1)}, s16[208,384]{1,0:T(8,128)(2,1)S(1)}, u32[]{:S(2)}, u32[]{:S(2)}) collective-permute-start(s16[208,384]{1,0:T(8,128)(2,1)S(1)} %get-tuple-element.90), channel_id=1, source_target_pairs={{0,2},{1,3},{2,0},{3,1},{4,6},{5,7},{6,4},{7,5},{8,10},{9,11},{10,... | collective-permute-start | bytes 479240 | tf_op jit(solution)/shard_map/ppermute | solution.py:391
  70.5 2.0 %collective-permute-done.25.codes = s16[208,384]{1,0:T(8,128)(2,1)S(1)} collective-permute-done((s16[208,384]{1,0:T(8,128)(2,1)S(1)}, s16[208,384]{1,0:T(8,128)(2,1)S(1)}, u32[]{:S(2)}, u32[]{:S(2)}) %collective-permute-start.25) | collective-permute-done | bytes 159776 | tf_op jit(solution)/shard_map/ppermute | solution.py:391
  72.5 0.6 next_step.5
  73.2 3.5 %collective-permute-start.26 = (s16[112,384]{1,0:T(8,128)(2,1)S(1)}, s16[112,384]{1,0:T(8,128)(2,1)S(1)}, u32[]{:S(2)}, u32[]{:S(2)}) collective-permute-start(s16[112,384]{1,0:T(8,128)(2,1)S(1)} %get-tuple-element.85), channel_id=1, source_target_pairs={{0,8},{1,9},{2,10},{3,11},{4,12},{5,13},{6,14},{7,15},{8,0},{9,1},... | collective-permute-start | bytes 258056 | tf_op jit(solution)/shard_map/ppermute | solution.py:391
  76.6 0.6 next_step.7
  77.3 1.1 %collective-permute-start.29 = (s16[112,384]{1,0:T(8,128)(2,1)S(1)}, s16[112,384]{1,0:T(8,128)(2,1)S(1)}, u32[]{:S(2)}, u32[]{:S(2)}) collective-permute-start(s16[112,384]{1,0:T(8,128)(2,1)S(1)} %get-tuple-element.92), channel_id=1, source_target_pairs={{0,8},{1,9},{2,10},{3,11},{4,12},{5,13},{6,14},{7,15},{8,0},{9,1},... | collective-permute-start | bytes 258056 | tf_op jit(solution)/shard_map/ppermute | solution.py:391
  78.4 2.5 %maximum_select_fusion = f32[1,256,1536]{2,1,0:T(8,128)} fusion(f32[1,256,384]{2,1,0:T(8,128)} %bitcast.11, f32[1,256,384]{2,1,0:T(8,128)S(1)} %bitcast.22, f32[1,256,384]{2,1,0:T(8,128)S(1)} %bitcast.20, f32[1,256,384]{2,1,0:T(8,128)S(1)} %bitcast.19, pred[]{:T(512)S(6)} %eq.6), kind=kLoop, calls=%fused_computation | loop fusion | flops 2752512 | bytes 3145729 | tf_op jit(solution)/shard_map/jit(_where)/select_n | solution.py:394
  80.9 0.4 collective-permute-done.26.rest_0_
  81.2 0.6 last_step.4
  81.8 0.1 collective-permute-start.30
  81.9 1.8 %collective-permute-done.29.rest_0_ = s16[112,384]{1,0:T(8,128)(2,1)S(1)} collective-permute-done((s16[112,384]{1,0:T(8,128)(2,1)S(1)}, s16[112,384]{1,0:T(8,128)(2,1)S(1)}, u32[]{:S(2)}, u32[]{:S(2)}) %collective-permute-start.29) | collective-permute-done | bytes 86048 | tf_op jit(solution)/shard_map/ppermute | solution.py:391
  83.7 0.6 last_step.5
  84.3 0.1 collective-permute-start.31
  84.4 1.2 %collective-permute-done.31 = f32[48,384]{1,0:T(8,128)S(1)} collective-permute-done((f32[48,384]{1,0:T(8,128)S(1)}, f32[48,384]{1,0:T(8,128)S(1)}, u32[]{:S(2)}, u32[]{:S(2)}) %collective-permute-start.31) | collective-permute-done | bytes 73760 | tf_op jit(solution)/shard_map/ppermute | solution.py:391
  85.6 0.7 maximum_select_fusion.1
  (37 shorter events, 0.1 us)
Async XLA Ops:
  0.6 7.0 %collective-permute-start = (bf16[96,1536]{1,0:T(8,128)(2,1)}, bf16[96,1536]{1,0:T(8,128)(2,1)S(1)}, u32[]{:S(2)}, u32[]{:S(2)}) collective-permute-start(bf16[96,1536]{1,0:T(8,128)(2,1)} %own.1), channel_id=1, source_target_pairs={{0,1},{1,0},{2,3},{3,2},{4,5},{5,4},{6,7},{7,6},{8,9},{9,8},{10,11... | collective-permute-start | bytes 884744 | tf_op jit(solution)/shard_map/ppermute | solution.py:391
  1.2 1.9 %copy-start.2 = (bf16[1,8,256,768]{3,2,1,0:T(8,128)(2,1)S(1)}, bf16[1,8,256,768]{3,2,1,0:T(8,128)(2,1)}, u32[]{:S(2)}) copy-start(bf16[1,8,256,768]{3,2,1,0:T(8,128)(2,1)} %hidden_ref.1) | copy-start | bytes 9437188
  3.1 0.7 copy-start.8
  3.8 3.9 %copy-start.6 = (bf16[96,1536]{1,0:T(8,128)(2,1)S(1)}, bf16[96,1536]{1,0:T(8,128)(2,1)}, u32[]{:S(2)}) copy-start(bf16[96,1536]{1,0:T(8,128)(2,1)} %own.1) | copy-start | bytes 884740
  7.1 11.4 %collective-permute-start.3 = (f32[192,768]{1,0:T(8,128)S(1)}, f32[192,768]{1,0:T(8,128)S(1)}, u32[]{:S(2)}, u32[]{:S(2)}) collective-permute-start(f32[192,768]{1,0:T(8,128)S(1)} %get-tuple-element.53), channel_id=1, source_target_pairs={{0,1},{1,0},{2,3},{3,2},{4,5},{5,4},{6,7},{7,6},{8,9},{9,8},{10,11... | collective-permute-start | bytes 1769480 | tf_op jit(solution)/shard_map/ppermute | solution.py:391
  7.2 11.3 %collective-permute-start.4 = (f32[192,768]{1,0:T(8,128)S(1)}, f32[192,768]{1,0:T(8,128)S(1)}, u32[]{:S(2)}, u32[]{:S(2)}) collective-permute-start(f32[192,768]{1,0:T(8,128)S(1)} %get-tuple-element.54), channel_id=1, source_target_pairs={{0,1},{1,0},{2,3},{3,2},{4,5},{5,4},{6,7},{7,6},{8,9},{9,8},{10,11... | collective-permute-start | bytes 1769480 | tf_op jit(solution)/shard_map/ppermute | solution.py:391
  7.7 22.3 %copy-start.7 = (bf16[48,1536]{1,0:T(8,128)(2,1)S(1)}, bf16[48,1536]{1,0:T(8,128)(2,1)}, u32[]{:S(2)}) copy-start(bf16[48,1536]{1,0:T(8,128)(2,1)} %own.2) | copy-start | bytes 442372
  7.7 34.5 %copy-start.5 = (bf16[1,256,1536]{2,1,0:T(8,128)(2,1)S(1)}, bf16[1,256,1536]{2,1,0:T(8,128)(2,1)}, u32[]{:S(2)}) copy-start(bf16[1,256,1536]{2,1,0:T(8,128)(2,1)} %param.11) | copy-start | bytes 2359300
  8.2 10.3 %collective-permute-start.2 = (bf16[192,768]{1,0:T(8,128)(2,1)S(1)}, bf16[192,768]{1,0:T(8,128)(2,1)S(1)}, u32[]{:S(2)}, u32[]{:S(2)}) collective-permute-start(bf16[192,768]{1,0:T(8,128)(2,1)S(1)} %cut.2.rest_4_), channel_id=1, source_target_pairs={{0,2},{1,3},{2,0},{3,1},{4,6},{5,7},{6,4},{7,5},{8,10},{9,11},{10,... | collective-permute-start | bytes 884744 | tf_op jit(solution)/shard_map/ppermute | solution.py:391
  10.9 16.4 %collective-permute-start.1 = (bf16[192,768]{1,0:T(8,128)(2,1)S(1)}, bf16[192,768]{1,0:T(8,128)(2,1)S(1)}, u32[]{:S(2)}, u32[]{:S(2)}) collective-permute-start(bf16[192,768]{1,0:T(8,128)(2,1)S(1)} %cut.2.rest_4_), channel_id=1, source_target_pairs={{0,8},{1,9},{2,10},{3,11},{4,12},{5,13},{6,14},{7,15},{8,0},{9,1},... | collective-permute-start | bytes 884744 | tf_op jit(solution)/shard_map/ppermute | solution.py:391
  13.5 14.4 %collective-permute-start.16 = (bf16[192,768]{1,0:T(8,128)(2,1)S(1)}, bf16[192,768]{1,0:T(8,128)(2,1)S(1)}, u32[]{:S(2)}, u32[]{:S(2)}) collective-permute-start(bf16[192,768]{1,0:T(8,128)(2,1)S(1)} %cut.2.rest_4_), channel_id=1, source_target_pairs={{0,4},{1,5},{2,6},{3,7},{4,0},{5,1},{6,2},{7,3},{8,12},{9,13},{10,... | collective-permute-start | bytes 884744 | tf_op jit(solution)/shard_map/ppermute | solution.py:391
  18.5 23.6 %copy-start = (bf16[1,256,1536]{2,1,0:T(8,128)(2,1)S(1)}, bf16[1,256,1536]{2,1,0:T(8,128)(2,1)}, u32[]{:S(2)}) copy-start(bf16[1,256,1536]{2,1,0:T(8,128)(2,1)} %param.12) | copy-start | bytes 2359300
  18.5 23.6 %copy-start.1 = (bf16[1,256,1536]{2,1,0:T(8,128)(2,1)S(1)}, bf16[1,256,1536]{2,1,0:T(8,128)(2,1)}, u32[]{:S(2)}) copy-start(bf16[1,256,1536]{2,1,0:T(8,128)(2,1)} %param.13) | copy-start | bytes 2359300
  18.5 23.7 %copy-start.3 = (bf16[1,256,1536]{2,1,0:T(8,128)(2,1)S(1)}, bf16[1,256,1536]{2,1,0:T(8,128)(2,1)}, u32[]{:S(2)}) copy-start(bf16[1,256,1536]{2,1,0:T(8,128)(2,1)} %param.9) | copy-start | bytes 2359300
  18.5 23.7 %copy-start.4 = (bf16[1,256,1536]{2,1,0:T(8,128)(2,1)S(1)}, bf16[1,256,1536]{2,1,0:T(8,128)(2,1)}, u32[]{:S(2)}) copy-start(bf16[1,256,1536]{2,1,0:T(8,128)(2,1)} %param.10) | copy-start | bytes 2359300
  19.5 10.5 %collective-permute-start.7 = (s16[208,768]{1,0:T(8,128)(2,1)S(1)}, s16[208,768]{1,0:T(8,128)(2,1)S(1)}, u32[]{:S(2)}, u32[]{:S(2)}) collective-permute-start(s16[208,768]{1,0:T(8,128)(2,1)S(1)} %get-tuple-element.55), channel_id=1, source_target_pairs={{0,2},{1,3},{2,0},{3,1},{4,6},{5,7},{6,4},{7,5},{8,10},{9,11},{10,... | collective-permute-start | bytes 958472 | tf_op jit(solution)/shard_map/ppermute | solution.py:391
  27.3 8.2 %collective-permute-start.5 = (bf16[192,768]{1,0:T(8,128)(2,1)S(1)}, bf16[192,768]{1,0:T(8,128)(2,1)S(1)}, u32[]{:S(2)}, u32[]{:S(2)}) collective-permute-start(bf16[192,768]{1,0:T(8,128)(2,1)S(1)} %collective-permute-done.1.rest_8_), channel_id=1, source_target_pairs={{0,4},{1,5},{2,6},{3,7},{4,0},{5,1},{6,2},{7,3},{8,12},{9,13},{10,... | collective-permute-start | bytes 884744 | tf_op jit(solution)/shard_map/ppermute | solution.py:391
  27.9 13.3 %collective-permute-start.17 = (bf16[192,768]{1,0:T(8,128)(2,1)S(1)}, bf16[192,768]{1,0:T(8,128)(2,1)S(1)}, u32[]{:S(2)}, u32[]{:S(2)}) collective-permute-start(bf16[192,768]{1,0:T(8,128)(2,1)S(1)} %collective-permute-done.16.rest_6_), channel_id=1, source_target_pairs={{0,2},{1,3},{2,0},{3,1},{4,6},{5,7},{6,4},{7,5},{8,10},{9,11},{10,... | collective-permute-start | bytes 884744 | tf_op jit(solution)/shard_map/ppermute | solution.py:391
  28.4 17.3 %collective-permute-start.8 = (bf16[192,768]{1,0:T(8,128)(2,1)S(1)}, bf16[192,768]{1,0:T(8,128)(2,1)S(1)}, u32[]{:S(2)}, u32[]{:S(2)}) collective-permute-start(bf16[192,768]{1,0:T(8,128)(2,1)S(1)} %collective-permute-done.1.rest_8_), channel_id=1, source_target_pairs={{0,2},{1,3},{2,0},{3,1},{4,6},{5,7},{6,4},{7,5},{8,10},{9,11},{10,... | collective-permute-start | bytes 884744 | tf_op jit(solution)/shard_map/ppermute | solution.py:391
  29.9 11.2 %collective-permute-start.6 = (bf16[48,1536]{1,0:T(8,128)(2,1)S(1)}, bf16[48,1536]{1,0:T(8,128)(2,1)S(1)}, u32[]{:S(2)}, u32[]{:S(2)}) collective-permute-start(bf16[48,1536]{1,0:T(8,128)(2,1)S(1)} %copy-done.7), channel_id=1, source_target_pairs={{0,1},{1,0},{2,3},{3,2},{4,5},{5,4},{6,7},{7,6},{8,9},{9,8},{10,11... | collective-permute-start | bytes 442376 | tf_op jit(solution)/shard_map/ppermute | solution.py:391
  30.8 15.0 %collective-permute-start.10 = (s16[64,768]{1,0:T(8,128)(2,1)S(1)}, s16[64,768]{1,0:T(8,128)(2,1)S(1)}, u32[]{:S(2)}, u32[]{:S(2)}) collective-permute-start(s16[64,768]{1,0:T(8,128)(2,1)S(1)} %get-tuple-element.65), channel_id=1, source_target_pairs={{0,8},{1,9},{2,10},{3,11},{4,12},{5,13},{6,14},{7,15},{8,0},{9,1},... | collective-permute-start | bytes 294920 | tf_op jit(solution)/shard_map/ppermute | solution.py:391
  35.5 10.8 %collective-permute-start.11 = (s16[64,768]{1,0:T(8,128)(2,1)S(1)}, s16[64,768]{1,0:T(8,128)(2,1)S(1)}, u32[]{:S(2)}, u32[]{:S(2)}) collective-permute-start(s16[64,768]{1,0:T(8,128)(2,1)S(1)} %get-tuple-element.66), channel_id=1, source_target_pairs={{0,12},{1,13},{2,14},{3,15},{4,8},{5,9},{6,10},{7,11},{8,4},{9,5},... | collective-permute-start | bytes 294920 | tf_op jit(solution)/shard_map/ppermute | solution.py:391
  41.2 5.2 %collective-permute-start.9 = (s16[64,768]{1,0:T(8,128)(2,1)S(1)}, s16[64,768]{1,0:T(8,128)(2,1)S(1)}, u32[]{:S(2)}, u32[]{:S(2)}) collective-permute-start(s16[64,768]{1,0:T(8,128)(2,1)S(1)} %get-tuple-element.64), channel_id=1, source_target_pairs={{0,4},{1,5},{2,6},{3,7},{4,0},{5,1},{6,2},{7,3},{8,12},{9,13},{10,... | collective-permute-start | bytes 294920 | tf_op jit(solution)/shard_map/ppermute | solution.py:391
  41.2 8.0 %collective-permute-start.18 = (bf16[192,768]{1,0:T(8,128)(2,1)S(1)}, bf16[192,768]{1,0:T(8,128)(2,1)S(1)}, u32[]{:S(2)}, u32[]{:S(2)}) collective-permute-start(bf16[192,768]{1,0:T(8,128)(2,1)S(1)} %collective-permute-done.5.rest_10_), channel_id=1, source_target_pairs={{0,2},{1,3},{2,0},{3,1},{4,6},{5,7},{6,4},{7,5},{8,10},{9,11},{10,... | collective-permute-start | bytes 884744 | tf_op jit(solution)/shard_map/ppermute | solution.py:391
  45.7 4.2 %collective-permute-start.12 = (bf16[256,768]{1,0:T(8,128)(2,1)S(1)}, bf16[256,768]{1,0:T(8,128)(2,1)S(1)}, u32[]{:S(2)}, u32[]{:S(2)}) collective-permute-start(bf16[256,768]{1,0:T(8,128)(2,1)S(1)} %get-tuple-element.68), channel_id=1, source_target_pairs={{0,1},{1,0},{2,3},{3,2},{4,5},{5,4},{6,7},{7,6},{8,9},{9,8},{10,11... | collective-permute-start | bytes 1179656 | tf_op jit(solution)/shard_map/ppermute | solution.py:391
  45.8 4.1 %collective-permute-start.13 = (bf16[256,768]{1,0:T(8,128)(2,1)S(1)}, bf16[256,768]{1,0:T(8,128)(2,1)S(1)}, u32[]{:S(2)}, u32[]{:S(2)}) collective-permute-start(bf16[256,768]{1,0:T(8,128)(2,1)S(1)} %get-tuple-element.69), channel_id=1, source_target_pairs={{0,1},{1,0},{2,3},{3,2},{4,5},{5,4},{6,7},{7,6},{8,9},{9,8},{10,11... | collective-permute-start | bytes 1179656 | tf_op jit(solution)/shard_map/ppermute | solution.py:391
  46.3 3.6 %collective-permute-start.14 = (bf16[256,768]{1,0:T(8,128)(2,1)S(1)}, bf16[256,768]{1,0:T(8,128)(2,1)S(1)}, u32[]{:S(2)}, u32[]{:S(2)}) collective-permute-start(bf16[256,768]{1,0:T(8,128)(2,1)S(1)} %get-tuple-element.70), channel_id=1, source_target_pairs={{0,1},{1,0},{2,3},{3,2},{4,5},{5,4},{6,7},{7,6},{8,9},{9,8},{10,11... | collective-permute-start | bytes 1179656 | tf_op jit(solution)/shard_map/ppermute | solution.py:391
  46.3 3.5 %collective-permute-start.15 = (bf16[256,768]{1,0:T(8,128)(2,1)S(1)}, bf16[256,768]{1,0:T(8,128)(2,1)S(1)}, u32[]{:S(2)}, u32[]{:S(2)}) collective-permute-start(bf16[256,768]{1,0:T(8,128)(2,1)S(1)} %get-tuple-element.71), channel_id=1, source_target_pairs={{0,1},{1,0},{2,3},{3,2},{4,5},{5,4},{6,7},{7,6},{8,9},{9,8},{10,11... | collective-permute-start | bytes 1179656 | tf_op jit(solution)/shard_map/ppermute | solution.py:391
  49.2 5.2 %collective-permute-start.20 = (bf16[256,768]{1,0:T(8,128)(2,1)S(1)}, bf16[256,768]{1,0:T(8,128)(2,1)S(1)}, u32[]{:S(2)}, u32[]{:S(2)}) collective-permute-start(bf16[256,768]{1,0:T(8,128)(2,1)S(1)} %get-tuple-element.49.sum_own), channel_id=1, source_target_pairs={{0,1},{1,0},{2,3},{3,2},{4,5},{5,4},{6,7},{7,6},{8,9},{9,8},{10,11... | collective-permute-start | bytes 1179656 | tf_op jit(solution)/shard_map/ppermute | solution.py:391
  52.6 1.7 %collective-permute-start.19 = (f32[512,128]{1,0:T(8,128)S(1)}, f32[512,128]{1,0:T(8,128)S(1)}, u32[]{:S(2)}, u32[]{:S(2)}) collective-permute-start(f32[512,128]{1,0:T(8,128)S(1)} %get-tuple-element.74.stats), channel_id=1, source_target_pairs={{0,1},{1,0},{2,3},{3,2},{4,5},{5,4},{6,7},{7,6},{8,9},{9,8},{10,11... | collective-permute-start | bytes 786440 | tf_op jit(solution)/shard_map/ppermute | solution.py:391
  53.2 1.4 %collective-permute-start.21 = (bf16[96,768]{1,0:T(8,128)(2,1)S(1)}, bf16[96,768]{1,0:T(8,128)(2,1)S(1)}, u32[]{:S(2)}, u32[]{:S(2)}) collective-permute-start(bf16[96,768]{1,0:T(8,128)(2,1)S(1)} %last_step.3.gram_own), channel_id=1, source_target_pairs={{0,1},{1,0},{2,3},{3,2},{4,5},{5,4},{6,7},{7,6},{8,9},{9,8},{10,11... | collective-permute-start | bytes 442376 | tf_op jit(solution)/shard_map/ppermute | solution.py:391
  56.5 9.6 %collective-permute-start.24 = (s16[400,384]{1,0:T(8,128)(2,1)S(1)}, s16[400,384]{1,0:T(8,128)(2,1)S(1)}, u32[]{:S(2)}, u32[]{:S(2)}) collective-permute-start(s16[400,384]{1,0:T(8,128)(2,1)S(1)} %get-tuple-element.80), channel_id=1, source_target_pairs={{0,2},{1,3},{2,0},{3,1},{4,6},{5,7},{6,4},{7,5},{8,10},{9,11},{10,... | collective-permute-start | bytes 921608 | tf_op jit(solution)/shard_map/ppermute | solution.py:391
  59.1 9.4 %collective-permute-start.27 = (s16[400,384]{1,0:T(8,128)(2,1)S(1)}, s16[400,384]{1,0:T(8,128)(2,1)S(1)}, u32[]{:S(2)}, u32[]{:S(2)}) collective-permute-start(s16[400,384]{1,0:T(8,128)(2,1)S(1)} %get-tuple-element.88), channel_id=1, source_target_pairs={{0,4},{1,5},{2,6},{3,7},{4,0},{5,1},{6,2},{7,3},{8,12},{9,13},{10,... | collective-permute-start | bytes 921608 | tf_op jit(solution)/shard_map/ppermute | solution.py:391
  61.2 17.2 %collective-permute-start.22 = (f32[256,384]{1,0:T(8,128)S(1)}, f32[256,384]{1,0:T(8,128)S(1)}, u32[]{:S(2)}, u32[]{:S(2)}) collective-permute-start(f32[256,384]{1,0:T(8,128)S(1)} %get-tuple-element.77), channel_id=1, source_target_pairs={{0,1},{1,0},{2,3},{3,2},{4,5},{5,4},{6,7},{7,6},{8,9},{9,8},{10,11... | collective-permute-start | bytes 1179656 | tf_op jit(solution)/shard_map/ppermute | solution.py:391
  61.2 17.2 %collective-permute-start.23 = (f32[256,384]{1,0:T(8,128)S(1)}, f32[256,384]{1,0:T(8,128)}, u32[]{:S(2)}, u32[]{:S(2)}) collective-permute-start(f32[256,384]{1,0:T(8,128)S(1)} %get-tuple-element.78), channel_id=1, source_target_pairs={{0,1},{1,0},{2,3},{3,2},{4,5},{5,4},{6,7},{7,6},{8,9},{9,8},{10,11... | collective-permute-start | bytes 1179656 | tf_op jit(solution)/shard_map/ppermute | solution.py:391
  66.9 5.6 %collective-permute-start.25 = (s16[208,384]{1,0:T(8,128)(2,1)S(1)}, s16[208,384]{1,0:T(8,128)(2,1)S(1)}, u32[]{:S(2)}, u32[]{:S(2)}) collective-permute-start(s16[208,384]{1,0:T(8,128)(2,1)S(1)} %get-tuple-element.82), channel_id=1, source_target_pairs={{0,4},{1,5},{2,6},{3,7},{4,0},{5,1},{6,2},{7,3},{8,12},{9,13},{10,... | collective-permute-start | bytes 479240 | tf_op jit(solution)/shard_map/ppermute | solution.py:391
  69.3 7.3 %collective-permute-start.28 = (s16[208,384]{1,0:T(8,128)(2,1)S(1)}, s16[208,384]{1,0:T(8,128)(2,1)S(1)}, u32[]{:S(2)}, u32[]{:S(2)}) collective-permute-start(s16[208,384]{1,0:T(8,128)(2,1)S(1)} %get-tuple-element.90), channel_id=1, source_target_pairs={{0,2},{1,3},{2,0},{3,1},{4,6},{5,7},{6,4},{7,5},{8,10},{9,11},{10,... | collective-permute-start | bytes 479240 | tf_op jit(solution)/shard_map/ppermute | solution.py:391
  73.2 8.1 %collective-permute-start.26 = (s16[112,384]{1,0:T(8,128)(2,1)S(1)}, s16[112,384]{1,0:T(8,128)(2,1)S(1)}, u32[]{:S(2)}, u32[]{:S(2)}) collective-permute-start(s16[112,384]{1,0:T(8,128)(2,1)S(1)} %get-tuple-element.85), channel_id=1, source_target_pairs={{0,8},{1,9},{2,10},{3,11},{4,12},{5,13},{6,14},{7,15},{8,0},{9,1},... | collective-permute-start | bytes 258056 | tf_op jit(solution)/shard_map/ppermute | solution.py:391
  77.3 6.4 %collective-permute-start.29 = (s16[112,384]{1,0:T(8,128)(2,1)S(1)}, s16[112,384]{1,0:T(8,128)(2,1)S(1)}, u32[]{:S(2)}, u32[]{:S(2)}) collective-permute-start(s16[112,384]{1,0:T(8,128)(2,1)S(1)} %get-tuple-element.92), channel_id=1, source_target_pairs={{0,8},{1,9},{2,10},{3,11},{4,12},{5,13},{6,14},{7,15},{8,0},{9,1},... | collective-permute-start | bytes 258056 | tf_op jit(solution)/shard_map/ppermute | solution.py:391
  81.8 2.5 %collective-permute-start.30 = (f32[48,384]{1,0:T(8,128)S(1)}, f32[48,384]{1,0:T(8,128)S(1)}, u32[]{:S(2)}, u32[]{:S(2)}) collective-permute-start(f32[48,384]{1,0:T(8,128)S(1)} %get-tuple-element.94), channel_id=1, source_target_pairs={{0,1},{1,0},{2,3},{3,2},{4,5},{5,4},{6,7},{7,6},{8,9},{9,8},{10,11... | collective-permute-start | bytes 221192 | tf_op jit(solution)/shard_map/ppermute | solution.py:391
  84.3 1.3 %collective-permute-start.31 = (f32[48,384]{1,0:T(8,128)S(1)}, f32[48,384]{1,0:T(8,128)S(1)}, u32[]{:S(2)}, u32[]{:S(2)}) collective-permute-start(f32[48,384]{1,0:T(8,128)S(1)} %get-tuple-element.95), channel_id=1, source_target_pairs={{0,1},{1,0},{2,3},{3,2},{4,5},{5,4},{6,7},{7,6},{8,9},{9,8},{10,11... | collective-permute-start | bytes 221192 | tf_op jit(solution)/shard_map/ppermute | solution.py:391

commit v8 on v7

--- a/solution.py
+++ b/solution.py
@@ -398,12 +398,15 @@
         )
 
     rows = out_weight.shape[0]
+    pred_other = swap(pred_weight, CORE)
     if by_pairs:
-        gram_mine, *gram_theirs, sum_own = gram(where, decoder_hidden, kept_index[0], (chips, dec // parts))
+        gram_mine, *gram_theirs, sum_own = gram(
+            where, decoder_hidden, after(kept_index, pred_other)[0], (chips, dec // parts)
+        )
     else:
         gram_all, sum_own = gram(where, decoder_hidden, kept_index[0], None)
     out_piece = cut(where, after(out_weight, sum_own), swap(out_weight, CORE))
-    pred_piece = cut(where, pred_weight, swap(pred_weight, CORE))
+    pred_piece = cut(where, pred_weight, pred_other)
 
     def attend(*anchors):
         q = after(queries, *anchors) if anchors else queries

time: 86.6 us -> 85.6 us (0.988)
  starting transfers between devices: 34.5 us -> 31.5 us
  waiting for transfers between devices: 24.4 us -> 26.5 us
    ppermute x32, starting transfers between devices: 34.5 us -> 31.5 us  [swap(): return lax.ppermute(x, AXES, pairs)]
    ppermute x32, waiting for transfers between devices: 24.4 us -> 26.5 us  [swap(): return lax.ppermute(x, AXES, pairs)]
  transfers between devices with their start and end apart: 32 -> 32, of which waited for: 11 -> 14; matrix products, arithmetic and copies ran while one was open for 3% -> 3% of each run, Pallas kernels for 22% -> 22%
where the time goes in v8:
time: 85.6 us; the launch traced here: 85.4 us
  starting transfers between devices  31.5 us (37%)
  waiting for transfers between devices  26.5 us (31%)
  Pallas kernels  20.6 us (24%)
  other arithmetic  3.3 us (4%)
  local copies, waits for them, and re-layouts  2.6 us (3%)
  between operations  0.91 us (1%)
    ppermute x32, starting transfers between devices, swap(): return lax.ppermute(x, AXES, pairs)  31.5 us
    ppermute x32, waiting for transfers between devices, swap(): return lax.ppermute(x, AXES, pairs)  26.5 us
    pallas_call x16, Pallas kernels, run(): pl.pallas_call(kernel, out_shape=tuple(out_shape), in_specs=[pl.BlockSpec...  20.6 us
    select_n x2, other arithmetic, side_by_side(): jnp.where(core == 0, jnp.concatenate(mine + theirs, axis=1), jnp.concaten...  3.22 us
    unnamed x18, local copies, waits for them, and re-layouts  2.6 us
  transfers between devices with their start and end apart: 32, of which 14 were waited for; matrix products, arithmetic and copies ran while one was open for 3% of the time, Pallas kernels for 22%

profile of v8, /device:TPU:0, one launch (start us, length us, event | category | flops | bytes accessed | tf_op | source)
XLA Modules:
  0.0 85.4 jit_solution(10775184839739163951)
XLA Ops:
  0.6 0.5 collective-permute-start
  1.1 0.1 collective-permute-start.1
  1.2 0.1 pad_add_fusion.where_ref
  1.3 1.1 %collective-permute-done.other = bf16[48,1536]{1,0:T(8,128)(2,1)S(1)} collective-permute-done((bf16[48,1536]{1,0:T(8,128)(2,1)}, bf16[48,1536]{1,0:T(8,128)(2,1)S(1)}, u32[]{:S(2)}, u32[]{:S(2)}) %collective-permute-start) | collective-permute-done | bytes 147488 | tf_op jit(solution)/shard_map/ppermute | solution.py:391
  2.4 1.9 %copy-done.2 = bf16[1,8,256,768]{3,2,1,0:T(8,128)(2,1)S(1)} copy-done((bf16[1,8,256,768]{3,2,1,0:T(8,128)(2,1)S(1)}, bf16[1,8,256,768]{3,2,1,0:T(8,128)(2,1)}, u32[]{:S(2)}) %copy-start.2) | copy-done | bytes 3145752
  4.3 0.7 copy-done.8
  4.9 3.3 %gram.1 = (f32[384,768]{1,0:T(8,128)S(1)}, f32[192,768]{1,0:T(8,128)S(1)}, f32[192,768]{1,0:T(8,128)S(1)}, bf16[256,768]{1,0:T(8,128)(2,1)S(1)}) custom-call(s32[2]{0:T(128)S(1)} %pad_add_fusion.where_ref, bf16[1,8,256,768]{3,2,1,0:T(8,128)(2,1)S(1)} %copy-done.2, s32[8,64]{1,0:T(8,128)S(1)} %bitcast.21), custom_call_target="tpu_custom_call" | custom-call | flops 1000 | bytes 1000 | tf_op jit(solution)/shard_map/gram/pallas_call | solution.py:25
  8.2 0.4 collective-permute-start.4
  8.7 0.1 collective-permute-start.5
  8.8 0.6 cut.2.rest_4_
  9.4 2.9 %collective-permute-start.3 = (bf16[192,768]{1,0:T(8,128)(2,1)S(1)}, bf16[192,768]{1,0:T(8,128)(2,1)S(1)}, u32[]{:S(2)}, u32[]{:S(2)}) collective-permute-start(bf16[192,768]{1,0:T(8,128)(2,1)S(1)} %cut.2.rest_4_), channel_id=1, source_target_pairs={{0,2},{1,3},{2,0},{3,1},{4,6},{5,7},{6,4},{7,5},{8,10},{9,11},{10,... | collective-permute-start | bytes 884744 | tf_op jit(solution)/shard_map/ppermute | solution.py:391
  12.3 1.6 %collective-permute-start.16 = (bf16[192,768]{1,0:T(8,128)(2,1)S(1)}, bf16[192,768]{1,0:T(8,128)(2,1)S(1)}, u32[]{:S(2)}, u32[]{:S(2)}) collective-permute-start(bf16[192,768]{1,0:T(8,128)(2,1)S(1)} %cut.2.rest_4_), channel_id=1, source_target_pairs={{0,4},{1,5},{2,6},{3,7},{4,0},{5,1},{6,2},{7,3},{8,12},{9,13},{10,... | collective-permute-start | bytes 884744 | tf_op jit(solution)/shard_map/ppermute | solution.py:391
  13.9 2.6 %collective-permute-start.2 = (bf16[192,768]{1,0:T(8,128)(2,1)S(1)}, bf16[192,768]{1,0:T(8,128)(2,1)S(1)}, u32[]{:S(2)}, u32[]{:S(2)}) collective-permute-start(bf16[192,768]{1,0:T(8,128)(2,1)S(1)} %cut.2.rest_4_), channel_id=1, source_target_pairs={{0,8},{1,9},{2,10},{3,11},{4,12},{5,13},{6,14},{7,15},{8,0},{9,1},... | collective-permute-start | bytes 884744 | tf_op jit(solution)/shard_map/ppermute | solution.py:391
  16.5 3.2 %collective-permute-done.3.rest_5_ = bf16[192,768]{1,0:T(8,128)(2,1)S(1)} collective-permute-done((bf16[192,768]{1,0:T(8,128)(2,1)S(1)}, bf16[192,768]{1,0:T(8,128)(2,1)S(1)}, u32[]{:S(2)}, u32[]{:S(2)}) %collective-permute-start.3) | collective-permute-done | bytes 294944 | tf_op jit(solution)/shard_map/ppermute | solution.py:391
  19.7 0.9 %first_step.1 = (s16[208,768]{1,0:T(8,128)(2,1)S(1)}, f32[192,768]{1,0:T(8,128)S(1)}) custom-call(s32[2]{0:T(128)S(1)} %pad_add_fusion.where_ref, f32[384,768]{1,0:T(8,128)S(1)} %get-tuple-element.54.mine, f32[192,768]{1,0:T(8,128)S(1)} %collective-permute-done.4.t0, f32[192,768]{1,0:T(8,128)S(1)} %collective-permute-done.5.t1), custom_call_target="tpu_custom_call" | custom-call | flops 1000 | bytes 1000 | tf_op jit(solution)/shard_map/first_step/pallas_call | solution.py:25
  20.6 1.8 %collective-permute-start.7 = (s16[208,768]{1,0:T(8,128)(2,1)S(1)}, s16[208,768]{1,0:T(8,128)(2,1)S(1)}, u32[]{:S(2)}, u32[]{:S(2)}) collective-permute-start(s16[208,768]{1,0:T(8,128)(2,1)S(1)} %get-tuple-element.57), channel_id=1, source_target_pairs={{0,2},{1,3},{2,0},{3,1},{4,6},{5,7},{6,4},{7,5},{8,10},{9,11},{10,... | collective-permute-start | bytes 958472 | tf_op jit(solution)/shard_map/ppermute | solution.py:391
  22.4 4.9 %collective-permute-done.16.rest_6_ = bf16[192,768]{1,0:T(8,128)(2,1)S(1)} collective-permute-done((bf16[192,768]{1,0:T(8,128)(2,1)S(1)}, bf16[192,768]{1,0:T(8,128)(2,1)S(1)}, u32[]{:S(2)}, u32[]{:S(2)}) %collective-permute-start.16) | collective-permute-done | bytes 294944 | tf_op jit(solution)/shard_map/ppermute | solution.py:391
  27.3 0.4 collective-permute-start.17
  27.7 2.0 %collective-permute-done.2.rest_8_ = bf16[192,768]{1,0:T(8,128)(2,1)S(1)} collective-permute-done((bf16[192,768]{1,0:T(8,128)(2,1)S(1)}, bf16[192,768]{1,0:T(8,128)(2,1)S(1)}, u32[]{:S(2)}, u32[]{:S(2)}) %collective-permute-start.2) | collective-permute-done | bytes 294944 | tf_op jit(solution)/shard_map/ppermute | solution.py:391
  29.7 0.4 collective-permute-start.6
  30.1 0.5 collective-permute-start.8
  30.6 0.8 second_step.1
  31.5 3.4 %collective-permute-start.10 = (s16[64,768]{1,0:T(8,128)(2,1)S(1)}, s16[64,768]{1,0:T(8,128)(2,1)S(1)}, u32[]{:S(2)}, u32[]{:S(2)}) collective-permute-start(s16[64,768]{1,0:T(8,128)(2,1)S(1)} %get-tuple-element.67), channel_id=1, source_target_pairs={{0,8},{1,9},{2,10},{3,11},{4,12},{5,13},{6,14},{7,15},{8,0},{9,1},... | collective-permute-start | bytes 294920 | tf_op jit(solution)/shard_map/ppermute | solution.py:391
  34.8 1.3 %collective-permute-start.11 = (s16[64,768]{1,0:T(8,128)(2,1)S(1)}, s16[64,768]{1,0:T(8,128)(2,1)S(1)}, u32[]{:S(2)}, u32[]{:S(2)}) collective-permute-start(s16[64,768]{1,0:T(8,128)(2,1)S(1)} %get-tuple-element.68), channel_id=1, source_target_pairs={{0,12},{1,13},{2,14},{3,15},{4,8},{5,9},{6,10},{7,11},{8,4},{9,5},... | collective-permute-start | bytes 294920 | tf_op jit(solution)/shard_map/ppermute | solution.py:391
  36.2 1.1 %collective-permute-done.17.rest_7_ = bf16[192,768]{1,0:T(8,128)(2,1)S(1)} collective-permute-done((bf16[192,768]{1,0:T(8,128)(2,1)S(1)}, bf16[192,768]{1,0:T(8,128)(2,1)S(1)}, u32[]{:S(2)}, u32[]{:S(2)}) %collective-permute-start.17) | collective-permute-done | bytes 294944 | tf_op jit(solution)/shard_map/ppermute | solution.py:391
  37.3 2.0 %collective-permute-start.9 = (s16[64,768]{1,0:T(8,128)(2,1)S(1)}, s16[64,768]{1,0:T(8,128)(2,1)S(1)}, u32[]{:S(2)}, u32[]{:S(2)}) collective-permute-start(s16[64,768]{1,0:T(8,128)(2,1)S(1)} %get-tuple-element.66), channel_id=1, source_target_pairs={{0,4},{1,5},{2,6},{3,7},{4,0},{5,1},{6,2},{7,3},{8,12},{9,13},{10,... | collective-permute-start | bytes 294920 | tf_op jit(solution)/shard_map/ppermute | solution.py:391
  39.3 0.9 %collective-permute-done.6.rest_10_ = bf16[192,768]{1,0:T(8,128)(2,1)S(1)} collective-permute-done((bf16[192,768]{1,0:T(8,128)(2,1)S(1)}, bf16[192,768]{1,0:T(8,128)(2,1)S(1)}, u32[]{:S(2)}, u32[]{:S(2)}) %collective-permute-start.6) | collective-permute-done | bytes 294944 | tf_op jit(solution)/shard_map/ppermute | solution.py:391
  40.2 0.6 collective-permute-start.18
  40.8 0.6 cut.3.weights
  41.4 3.5 %attention.1 = (bf16[256,1536]{1,0:T(8,128)(2,1)S(1)}, bf16[256,768]{1,0:T(8,128)(2,1)S(1)}, bf16[256,768]{1,0:T(8,128)(2,1)S(1)}, bf16[256,768]{1,0:T(8,128)(2,1)S(1)}, bf16[256,768]{1,0:T(8,128)(2,1)S(1)}) custom-call(s32[2]{0:T(128)S(1)} %pad_add_fusion.where_ref, bf16[256,1536]{1,0:T(8,128)(2,1)S(1)} %bitcast.16, bf16[256,1536]{1,0:T(8,128)(2,1)S(1)} %bitcast.17, ...), custom_call_target="tpu_custom_call" | custom-call | flops 1000 | bytes 1000 | tf_op jit(solution)/shard_map/attention/pallas_call | solution.py:25
  45.0 0.5 collective-permute-start.13
  45.5 0.1 collective-permute-start.14
  45.6 0.4 collective-permute-start.15
  46.0 2.7 %collective-permute-done.18.rest_11_ = bf16[192,768]{1,0:T(8,128)(2,1)S(1)} collective-permute-done((bf16[192,768]{1,0:T(8,128)(2,1)S(1)}, bf16[192,768]{1,0:T(8,128)(2,1)S(1)}, u32[]{:S(2)}, u32[]{:S(2)}) %collective-permute-start.18) | collective-permute-done | bytes 294944 | tf_op jit(solution)/shard_map/ppermute | solution.py:391
  48.7 0.6 last_step.3.gram_own
  49.4 2.8 %branch.1 = (f32[512,768]{1,0:T(8,128)S(1)}, f32[512,128]{1,0:T(8,128)S(1)}) custom-call(s32[2]{0:T(128)S(1)} %pad_add_fusion.where_ref, bf16[256,1536]{1,0:T(8,128)(2,1)S(1)} %get-tuple-element.69.mixed_own, bf16[256,1536]{1,0:T(8,128)(2,1)S(1)} %bitcast.13, bf16[256,1536]{1,0:T(8,128)(2,1)S(1)} %bitcast.15, ...), custom_call_target="tpu_custom_call" | custom-call | flops 1000 | bytes 1000 | tf_op jit(solution)/shard_map/branch/pallas_call | solution.py:25
  52.2 0.6 collective-permute-start.19
  52.7 0.1 collective-permute-start.21
  52.8 1.1 %collective-permute-done.19.stats_other = f32[512,128]{1,0:T(8,128)S(1)} collective-permute-done((f32[512,128]{1,0:T(8,128)S(1)}, f32[512,128]{1,0:T(8,128)S(1)}, u32[]{:S(2)}, u32[]{:S(2)}) %collective-permute-start.19) | collective-permute-done | bytes 262176 | tf_op jit(solution)/shard_map/ppermute | solution.py:391
  53.9 0.2 collective-permute-done.21.gram_other
  54.1 1.9 %targets.2 = (f32[256,384]{1,0:T(8,128)S(1)}, f32[256,384]{1,0:T(8,128)S(1)}, s16[400,384]{1,0:T(8,128)(2,1)S(1)}, f32[384,384]{1,0:T(8,128)S(1)}) custom-call(s32[2]{0:T(128)S(1)} %pad_add_fusion.where_ref, f32[512,768]{1,0:T(8,128)S(1)} %get-tuple-element.75.blend, f32[512,128]{1,0:T(8,128)S(1)} %get-tuple-element.76.stats, ...), custom_call_target="tpu_custom_call" | custom-call | flops 1000 | bytes 1000 | tf_op jit(solution)/shard_map/targets/pallas_call | solution.py:25
  56.0 1.5 %collective-permute-start.24 = (s16[400,384]{1,0:T(8,128)(2,1)S(1)}, s16[400,384]{1,0:T(8,128)(2,1)S(1)}, u32[]{:S(2)}, u32[]{:S(2)}) collective-permute-start(s16[400,384]{1,0:T(8,128)(2,1)S(1)} %get-tuple-element.82), channel_id=1, source_target_pairs={{0,2},{1,3},{2,0},{3,1},{4,6},{5,7},{6,4},{7,5},{8,10},{9,11},{10,... | collective-permute-start | bytes 921608 | tf_op jit(solution)/shard_map/ppermute | solution.py:391
  57.5 1.8 %targets.3 = (f32[256,384]{1,0:T(8,128)S(1)}, f32[256,384]{1,0:T(8,128)S(1)}, s16[400,384]{1,0:T(8,128)(2,1)S(1)}, f32[384,384]{1,0:T(8,128)S(1)}) custom-call(s32[2]{0:T(128)S(1)} %pad_add_fusion.where_ref, f32[512,768]{1,0:T(8,128)S(1)} %get-tuple-element.75.blend, f32[512,128]{1,0:T(8,128)S(1)} %get-tuple-element.76.stats, ...), custom_call_target="tpu_custom_call" | custom-call | flops 1000 | bytes 1000 | tf_op jit(solution)/shard_map/targets/pallas_call | solution.py:25
  59.3 1.6 %collective-permute-start.27 = (s16[400,384]{1,0:T(8,128)(2,1)S(1)}, s16[400,384]{1,0:T(8,128)(2,1)S(1)}, u32[]{:S(2)}, u32[]{:S(2)}) collective-permute-start(s16[400,384]{1,0:T(8,128)(2,1)S(1)} %get-tuple-element.90), channel_id=1, source_target_pairs={{0,4},{1,5},{2,6},{3,7},{4,0},{5,1},{6,2},{7,3},{8,12},{9,13},{10,... | collective-permute-start | bytes 921608 | tf_op jit(solution)/shard_map/ppermute | solution.py:391
  60.9 0.5 collective-permute-start.23
  61.4 4.2 %collective-permute-done.24.codes = s16[400,384]{1,0:T(8,128)(2,1)S(1)} collective-permute-done((s16[400,384]{1,0:T(8,128)(2,1)S(1)}, s16[400,384]{1,0:T(8,128)(2,1)S(1)}, u32[]{:S(2)}, u32[]{:S(2)}) %collective-permute-start.24) | collective-permute-done | bytes 307232 | tf_op jit(solution)/shard_map/ppermute | solution.py:391
  65.6 0.8 next_step.4
  66.4 1.5 %collective-permute-start.25 = (s16[208,384]{1,0:T(8,128)(2,1)S(1)}, s16[208,384]{1,0:T(8,128)(2,1)S(1)}, u32[]{:S(2)}, u32[]{:S(2)}) collective-permute-start(s16[208,384]{1,0:T(8,128)(2,1)S(1)} %get-tuple-element.84), channel_id=1, source_target_pairs={{0,4},{1,5},{2,6},{3,7},{4,0},{5,1},{6,2},{7,3},{8,12},{9,13},{10,... | collective-permute-start | bytes 479240 | tf_op jit(solution)/shard_map/ppermute | solution.py:391
  68.0 0.6 collective-permute-done.27.codes
  68.6 0.8 next_step.6
  69.4 1.0 %collective-permute-start.28 = (s16[208,384]{1,0:T(8,128)(2,1)S(1)}, s16[208,384]{1,0:T(8,128)(2,1)S(1)}, u32[]{:S(2)}, u32[]{:S(2)}) collective-permute-start(s16[208,384]{1,0:T(8,128)(2,1)S(1)} %get-tuple-element.92), channel_id=1, source_target_pairs={{0,2},{1,3},{2,0},{3,1},{4,6},{5,7},{6,4},{7,5},{8,10},{9,11},{10,... | collective-permute-start | bytes 479240 | tf_op jit(solution)/shard_map/ppermute | solution.py:391
  70.3 1.7 %collective-permute-done.25.codes = s16[208,384]{1,0:T(8,128)(2,1)S(1)} collective-permute-done((s16[208,384]{1,0:T(8,128)(2,1)S(1)}, s16[208,384]{1,0:T(8,128)(2,1)S(1)}, u32[]{:S(2)}, u32[]{:S(2)}) %collective-permute-start.25) | collective-permute-done | bytes 159776 | tf_op jit(solution)/shard_map/ppermute | solution.py:391
  72.1 0.6 next_step.5
  72.7 2.6 %collective-permute-start.26 = (s16[112,384]{1,0:T(8,128)(2,1)S(1)}, s16[112,384]{1,0:T(8,128)(2,1)S(1)}, u32[]{:S(2)}, u32[]{:S(2)}) collective-permute-start(s16[112,384]{1,0:T(8,128)(2,1)S(1)} %get-tuple-element.87), channel_id=1, source_target_pairs={{0,8},{1,9},{2,10},{3,11},{4,12},{5,13},{6,14},{7,15},{8,0},{9,1},... | collective-permute-start | bytes 258056 | tf_op jit(solution)/shard_map/ppermute | solution.py:391
  75.3 0.6 next_step.7
  75.9 2.1 %collective-permute-start.29 = (s16[112,384]{1,0:T(8,128)(2,1)S(1)}, s16[112,384]{1,0:T(8,128)(2,1)S(1)}, u32[]{:S(2)}, u32[]{:S(2)}) collective-permute-start(s16[112,384]{1,0:T(8,128)(2,1)S(1)} %get-tuple-element.94), channel_id=1, source_target_pairs={{0,8},{1,9},{2,10},{3,11},{4,12},{5,13},{6,14},{7,15},{8,0},{9,1},... | collective-permute-start | bytes 258056 | tf_op jit(solution)/shard_map/ppermute | solution.py:391
  78.0 2.5 %maximum_select_fusion = f32[1,256,1536]{2,1,0:T(8,128)} fusion(f32[1,256,384]{2,1,0:T(8,128)} %bitcast.11, f32[1,256,384]{2,1,0:T(8,128)S(1)} %bitcast.22, f32[1,256,384]{2,1,0:T(8,128)S(1)} %bitcast.20, f32[1,256,384]{2,1,0:T(8,128)S(1)} %bitcast.19, pred[]{:T(512)S(6)} %eq.6), kind=kLoop, calls=%fused_computation | loop fusion | flops 2752512 | bytes 3145729 | tf_op jit(solution)/shard_map/jit(_where)/select_n | solution.py:394
  80.5 0.6 last_step.4
  81.1 0.1 collective-permute-start.30
  81.2 1.6 %collective-permute-done.29.rest_0_ = s16[112,384]{1,0:T(8,128)(2,1)S(1)} collective-permute-done((s16[112,384]{1,0:T(8,128)(2,1)S(1)}, s16[112,384]{1,0:T(8,128)(2,1)S(1)}, u32[]{:S(2)}, u32[]{:S(2)}) %collective-permute-start.29) | collective-permute-done | bytes 86048 | tf_op jit(solution)/shard_map/ppermute | solution.py:391
  82.8 0.6 last_step.5
  83.3 0.1 collective-permute-start.31
  83.4 1.2 %collective-permute-done.31 = f32[48,384]{1,0:T(8,128)S(1)} collective-permute-done((f32[48,384]{1,0:T(8,128)S(1)}, f32[48,384]{1,0:T(8,128)S(1)}, u32[]{:S(2)}, u32[]{:S(2)}) %collective-permute-start.31) | collective-permute-done | bytes 73760 | tf_op jit(solution)/shard_map/ppermute | solution.py:391
  84.7 0.7 maximum_select_fusion.1
  (37 shorter events, 0.2 us)
Async XLA Ops:
  0.6 1.7 %collective-permute-start = (bf16[48,1536]{1,0:T(8,128)(2,1)}, bf16[48,1536]{1,0:T(8,128)(2,1)S(1)}, u32[]{:S(2)}, u32[]{:S(2)}) collective-permute-start(bf16[48,1536]{1,0:T(8,128)(2,1)} %own.2), channel_id=1, source_target_pairs={{0,1},{1,0},{2,3},{3,2},{4,5},{5,4},{6,7},{7,6},{8,9},{9,8},{10,11... | collective-permute-start | bytes 442376 | tf_op jit(solution)/shard_map/ppermute | solution.py:391
  1.1 7.7 %collective-permute-start.1 = (bf16[96,1536]{1,0:T(8,128)(2,1)}, bf16[96,1536]{1,0:T(8,128)(2,1)S(1)}, u32[]{:S(2)}, u32[]{:S(2)}) collective-permute-start(bf16[96,1536]{1,0:T(8,128)(2,1)} %own.1), channel_id=1, source_target_pairs={{0,1},{1,0},{2,3},{3,2},{4,5},{5,4},{6,7},{7,6},{8,9},{9,8},{10,11... | collective-permute-start | bytes 884744 | tf_op jit(solution)/shard_map/ppermute | solution.py:391
  2.4 1.9 %copy-start.2 = (bf16[1,8,256,768]{3,2,1,0:T(8,128)(2,1)S(1)}, bf16[1,8,256,768]{3,2,1,0:T(8,128)(2,1)}, u32[]{:S(2)}) copy-start(bf16[1,8,256,768]{3,2,1,0:T(8,128)(2,1)} %hidden_ref.1) | copy-start | bytes 9437188
  4.3 0.7 copy-start.8
  4.9 3.9 %copy-start.6 = (bf16[96,1536]{1,0:T(8,128)(2,1)S(1)}, bf16[96,1536]{1,0:T(8,128)(2,1)}, u32[]{:S(2)}) copy-start(bf16[96,1536]{1,0:T(8,128)(2,1)} %own.1) | copy-start | bytes 884740
  8.2 11.5 %collective-permute-start.4 = (f32[192,768]{1,0:T(8,128)S(1)}, f32[192,768]{1,0:T(8,128)S(1)}, u32[]{:S(2)}, u32[]{:S(2)}) collective-permute-start(f32[192,768]{1,0:T(8,128)S(1)} %get-tuple-element.55), channel_id=1, source_target_pairs={{0,1},{1,0},{2,3},{3,2},{4,5},{5,4},{6,7},{7,6},{8,9},{9,8},{10,11... | collective-permute-start | bytes 1769480 | tf_op jit(solution)/shard_map/ppermute | solution.py:391
  8.7 11.0 %collective-permute-start.5 = (f32[192,768]{1,0:T(8,128)S(1)}, f32[192,768]{1,0:T(8,128)S(1)}, u32[]{:S(2)}, u32[]{:S(2)}) collective-permute-start(f32[192,768]{1,0:T(8,128)S(1)} %get-tuple-element.56), channel_id=1, source_target_pairs={{0,1},{1,0},{2,3},{3,2},{4,5},{5,4},{6,7},{7,6},{8,9},{9,8},{10,11... | collective-permute-start | bytes 1769480 | tf_op jit(solution)/shard_map/ppermute | solution.py:391
  8.8 32.5 %copy-start.5 = (bf16[1,256,1536]{2,1,0:T(8,128)(2,1)S(1)}, bf16[1,256,1536]{2,1,0:T(8,128)(2,1)}, u32[]{:S(2)}) copy-start(bf16[1,256,1536]{2,1,0:T(8,128)(2,1)} %param.11) | copy-start | bytes 2359300
  9.4 10.3 %collective-permute-start.3 = (bf16[192,768]{1,0:T(8,128)(2,1)S(1)}, bf16[192,768]{1,0:T(8,128)(2,1)S(1)}, u32[]{:S(2)}, u32[]{:S(2)}) collective-permute-start(bf16[192,768]{1,0:T(8,128)(2,1)S(1)} %cut.2.rest_4_), channel_id=1, source_target_pairs={{0,2},{1,3},{2,0},{3,1},{4,6},{5,7},{6,4},{7,5},{8,10},{9,11},{10,... | collective-permute-start | bytes 884744 | tf_op jit(solution)/shard_map/ppermute | solution.py:391
  12.3 15.0 %collective-permute-start.16 = (bf16[192,768]{1,0:T(8,128)(2,1)S(1)}, bf16[192,768]{1,0:T(8,128)(2,1)S(1)}, u32[]{:S(2)}, u32[]{:S(2)}) collective-permute-start(bf16[192,768]{1,0:T(8,128)(2,1)S(1)} %cut.2.rest_4_), channel_id=1, source_target_pairs={{0,4},{1,5},{2,6},{3,7},{4,0},{5,1},{6,2},{7,3},{8,12},{9,13},{10,... | collective-permute-start | bytes 884744 | tf_op jit(solution)/shard_map/ppermute | solution.py:391
  13.9 15.8 %collective-permute-start.2 = (bf16[192,768]{1,0:T(8,128)(2,1)S(1)}, bf16[192,768]{1,0:T(8,128)(2,1)S(1)}, u32[]{:S(2)}, u32[]{:S(2)}) collective-permute-start(bf16[192,768]{1,0:T(8,128)(2,1)S(1)} %cut.2.rest_4_), channel_id=1, source_target_pairs={{0,8},{1,9},{2,10},{3,11},{4,12},{5,13},{6,14},{7,15},{8,0},{9,1},... | collective-permute-start | bytes 884744 | tf_op jit(solution)/shard_map/ppermute | solution.py:391
  19.6 21.1 %copy-start.7 = (bf16[48,1536]{1,0:T(8,128)(2,1)S(1)}, bf16[48,1536]{1,0:T(8,128)(2,1)}, u32[]{:S(2)}) copy-start(bf16[48,1536]{1,0:T(8,128)(2,1)} %own.2) | copy-start | bytes 442372
  19.7 21.7 %copy-start = (bf16[1,256,1536]{2,1,0:T(8,128)(2,1)S(1)}, bf16[1,256,1536]{2,1,0:T(8,128)(2,1)}, u32[]{:S(2)}) copy-start(bf16[1,256,1536]{2,1,0:T(8,128)(2,1)} %param.12) | copy-start | bytes 2359300
  19.7 21.7 %copy-start.1 = (bf16[1,256,1536]{2,1,0:T(8,128)(2,1)S(1)}, bf16[1,256,1536]{2,1,0:T(8,128)(2,1)}, u32[]{:S(2)}) copy-start(bf16[1,256,1536]{2,1,0:T(8,128)(2,1)} %param.13) | copy-start | bytes 2359300
  19.7 21.7 %copy-start.3 = (bf16[1,256,1536]{2,1,0:T(8,128)(2,1)S(1)}, bf16[1,256,1536]{2,1,0:T(8,128)(2,1)}, u32[]{:S(2)}) copy-start(bf16[1,256,1536]{2,1,0:T(8,128)(2,1)} %param.9) | copy-start | bytes 2359300
  19.7 21.7 %copy-start.4 = (bf16[1,256,1536]{2,1,0:T(8,128)(2,1)S(1)}, bf16[1,256,1536]{2,1,0:T(8,128)(2,1)}, u32[]{:S(2)}) copy-start(bf16[1,256,1536]{2,1,0:T(8,128)(2,1)} %param.10) | copy-start | bytes 2359300
  20.6 10.0 %collective-permute-start.7 = (s16[208,768]{1,0:T(8,128)(2,1)S(1)}, s16[208,768]{1,0:T(8,128)(2,1)S(1)}, u32[]{:S(2)}, u32[]{:S(2)}) collective-permute-start(s16[208,768]{1,0:T(8,128)(2,1)S(1)} %get-tuple-element.57), channel_id=1, source_target_pairs={{0,2},{1,3},{2,0},{3,1},{4,6},{5,7},{6,4},{7,5},{8,10},{9,11},{10,... | collective-permute-start | bytes 958472 | tf_op jit(solution)/shard_map/ppermute | solution.py:391
  27.3 9.9 %collective-permute-start.17 = (bf16[192,768]{1,0:T(8,128)(2,1)S(1)}, bf16[192,768]{1,0:T(8,128)(2,1)S(1)}, u32[]{:S(2)}, u32[]{:S(2)}) collective-permute-start(bf16[192,768]{1,0:T(8,128)(2,1)S(1)} %collective-permute-done.16.rest_6_), channel_id=1, source_target_pairs={{0,2},{1,3},{2,0},{3,1},{4,6},{5,7},{6,4},{7,5},{8,10},{9,11},{10,... | collective-permute-start | bytes 884744 | tf_op jit(solution)/shard_map/ppermute | solution.py:391
  29.7 10.5 %collective-permute-start.6 = (bf16[192,768]{1,0:T(8,128)(2,1)S(1)}, bf16[192,768]{1,0:T(8,128)(2,1)S(1)}, u32[]{:S(2)}, u32[]{:S(2)}) collective-permute-start(bf16[192,768]{1,0:T(8,128)(2,1)S(1)} %collective-permute-done.2.rest_8_), channel_id=1, source_target_pairs={{0,4},{1,5},{2,6},{3,7},{4,0},{5,1},{6,2},{7,3},{8,12},{9,13},{10,... | collective-permute-start | bytes 884744 | tf_op jit(solution)/shard_map/ppermute | solution.py:391
  30.1 14.8 %collective-permute-start.8 = (bf16[192,768]{1,0:T(8,128)(2,1)S(1)}, bf16[192,768]{1,0:T(8,128)(2,1)S(1)}, u32[]{:S(2)}, u32[]{:S(2)}) collective-permute-start(bf16[192,768]{1,0:T(8,128)(2,1)S(1)} %collective-permute-done.2.rest_8_), channel_id=1, source_target_pairs={{0,2},{1,3},{2,0},{3,1},{4,6},{5,7},{6,4},{7,5},{8,10},{9,11},{10,... | collective-permute-start | bytes 884744 | tf_op jit(solution)/shard_map/ppermute | solution.py:391
  31.5 13.5 %collective-permute-start.10 = (s16[64,768]{1,0:T(8,128)(2,1)S(1)}, s16[64,768]{1,0:T(8,128)(2,1)S(1)}, u32[]{:S(2)}, u32[]{:S(2)}) collective-permute-start(s16[64,768]{1,0:T(8,128)(2,1)S(1)} %get-tuple-element.67), channel_id=1, source_target_pairs={{0,8},{1,9},{2,10},{3,11},{4,12},{5,13},{6,14},{7,15},{8,0},{9,1},... | collective-permute-start | bytes 294920 | tf_op jit(solution)/shard_map/ppermute | solution.py:391
  34.8 10.6 %collective-permute-start.11 = (s16[64,768]{1,0:T(8,128)(2,1)S(1)}, s16[64,768]{1,0:T(8,128)(2,1)S(1)}, u32[]{:S(2)}, u32[]{:S(2)}) collective-permute-start(s16[64,768]{1,0:T(8,128)(2,1)S(1)} %get-tuple-element.68), channel_id=1, source_target_pairs={{0,12},{1,13},{2,14},{3,15},{4,8},{5,9},{6,10},{7,11},{8,4},{9,5},... | collective-permute-start | bytes 294920 | tf_op jit(solution)/shard_map/ppermute | solution.py:391
  37.3 8.3 %collective-permute-start.9 = (s16[64,768]{1,0:T(8,128)(2,1)S(1)}, s16[64,768]{1,0:T(8,128)(2,1)S(1)}, u32[]{:S(2)}, u32[]{:S(2)}) collective-permute-start(s16[64,768]{1,0:T(8,128)(2,1)S(1)} %get-tuple-element.66), channel_id=1, source_target_pairs={{0,4},{1,5},{2,6},{3,7},{4,0},{5,1},{6,2},{7,3},{8,12},{9,13},{10,... | collective-permute-start | bytes 294920 | tf_op jit(solution)/shard_map/ppermute | solution.py:391
  40.2 8.6 %collective-permute-start.18 = (bf16[192,768]{1,0:T(8,128)(2,1)S(1)}, bf16[192,768]{1,0:T(8,128)(2,1)S(1)}, u32[]{:S(2)}, u32[]{:S(2)}) collective-permute-start(bf16[192,768]{1,0:T(8,128)(2,1)S(1)} %collective-permute-done.6.rest_10_), channel_id=1, source_target_pairs={{0,2},{1,3},{2,0},{3,1},{4,6},{5,7},{6,4},{7,5},{8,10},{9,11},{10,... | collective-permute-start | bytes 884744 | tf_op jit(solution)/shard_map/ppermute | solution.py:391
  44.9 4.5 %collective-permute-start.12 = (bf16[256,768]{1,0:T(8,128)(2,1)S(1)}, bf16[256,768]{1,0:T(8,128)(2,1)S(1)}, u32[]{:S(2)}, u32[]{:S(2)}) collective-permute-start(bf16[256,768]{1,0:T(8,128)(2,1)S(1)} %get-tuple-element.70), channel_id=1, source_target_pairs={{0,1},{1,0},{2,3},{3,2},{4,5},{5,4},{6,7},{7,6},{8,9},{9,8},{10,11... | collective-permute-start | bytes 1179656 | tf_op jit(solution)/shard_map/ppermute | solution.py:391
  45.0 4.4 %collective-permute-start.13 = (bf16[256,768]{1,0:T(8,128)(2,1)S(1)}, bf16[256,768]{1,0:T(8,128)(2,1)S(1)}, u32[]{:S(2)}, u32[]{:S(2)}) collective-permute-start(bf16[256,768]{1,0:T(8,128)(2,1)S(1)} %get-tuple-element.71), channel_id=1, source_target_pairs={{0,1},{1,0},{2,3},{3,2},{4,5},{5,4},{6,7},{7,6},{8,9},{9,8},{10,11... | collective-permute-start | bytes 1179656 | tf_op jit(solution)/shard_map/ppermute | solution.py:391
  45.5 3.9 %collective-permute-start.14 = (bf16[256,768]{1,0:T(8,128)(2,1)S(1)}, bf16[256,768]{1,0:T(8,128)(2,1)S(1)}, u32[]{:S(2)}, u32[]{:S(2)}) collective-permute-start(bf16[256,768]{1,0:T(8,128)(2,1)S(1)} %get-tuple-element.72), channel_id=1, source_target_pairs={{0,1},{1,0},{2,3},{3,2},{4,5},{5,4},{6,7},{7,6},{8,9},{9,8},{10,11... | collective-permute-start | bytes 1179656 | tf_op jit(solution)/shard_map/ppermute | solution.py:391
  45.6 3.8 %collective-permute-start.15 = (bf16[256,768]{1,0:T(8,128)(2,1)S(1)}, bf16[256,768]{1,0:T(8,128)(2,1)S(1)}, u32[]{:S(2)}, u32[]{:S(2)}) collective-permute-start(bf16[256,768]{1,0:T(8,128)(2,1)S(1)} %get-tuple-element.73), channel_id=1, source_target_pairs={{0,1},{1,0},{2,3},{3,2},{4,5},{5,4},{6,7},{7,6},{8,9},{9,8},{10,11... | collective-permute-start | bytes 1179656 | tf_op jit(solution)/shard_map/ppermute | solution.py:391
  48.7 5.2 %collective-permute-start.20 = (bf16[256,768]{1,0:T(8,128)(2,1)S(1)}, bf16[256,768]{1,0:T(8,128)(2,1)S(1)}, u32[]{:S(2)}, u32[]{:S(2)}) collective-permute-start(bf16[256,768]{1,0:T(8,128)(2,1)S(1)} %get-tuple-element.51.sum_own), channel_id=1, source_target_pairs={{0,1},{1,0},{2,3},{3,2},{4,5},{5,4},{6,7},{7,6},{8,9},{9,8},{10,11... | collective-permute-start | bytes 1179656 | tf_op jit(solution)/shard_map/ppermute | solution.py:391
  52.2 1.7 %collective-permute-start.19 = (f32[512,128]{1,0:T(8,128)S(1)}, f32[512,128]{1,0:T(8,128)S(1)}, u32[]{:S(2)}, u32[]{:S(2)}) collective-permute-start(f32[512,128]{1,0:T(8,128)S(1)} %get-tuple-element.76.stats), channel_id=1, source_target_pairs={{0,1},{1,0},{2,3},{3,2},{4,5},{5,4},{6,7},{7,6},{8,9},{9,8},{10,11... | collective-permute-start | bytes 786440 | tf_op jit(solution)/shard_map/ppermute | solution.py:391
  52.7 1.4 %collective-permute-start.21 = (bf16[96,768]{1,0:T(8,128)(2,1)S(1)}, bf16[96,768]{1,0:T(8,128)(2,1)S(1)}, u32[]{:S(2)}, u32[]{:S(2)}) collective-permute-start(bf16[96,768]{1,0:T(8,128)(2,1)S(1)} %last_step.3.gram_own), channel_id=1, source_target_pairs={{0,1},{1,0},{2,3},{3,2},{4,5},{5,4},{6,7},{7,6},{8,9},{9,8},{10,11... | collective-permute-start | bytes 442376 | tf_op jit(solution)/shard_map/ppermute | solution.py:391
  56.0 9.6 %collective-permute-start.24 = (s16[400,384]{1,0:T(8,128)(2,1)S(1)}, s16[400,384]{1,0:T(8,128)(2,1)S(1)}, u32[]{:S(2)}, u32[]{:S(2)}) collective-permute-start(s16[400,384]{1,0:T(8,128)(2,1)S(1)} %get-tuple-element.82), channel_id=1, source_target_pairs={{0,2},{1,3},{2,0},{3,1},{4,6},{5,7},{6,4},{7,5},{8,10},{9,11},{10,... | collective-permute-start | bytes 921608 | tf_op jit(solution)/shard_map/ppermute | solution.py:391
  59.3 9.3 %collective-permute-start.27 = (s16[400,384]{1,0:T(8,128)(2,1)S(1)}, s16[400,384]{1,0:T(8,128)(2,1)S(1)}, u32[]{:S(2)}, u32[]{:S(2)}) collective-permute-start(s16[400,384]{1,0:T(8,128)(2,1)S(1)} %get-tuple-element.90), channel_id=1, source_target_pairs={{0,4},{1,5},{2,6},{3,7},{4,0},{5,1},{6,2},{7,3},{8,12},{9,13},{10,... | collective-permute-start | bytes 921608 | tf_op jit(solution)/shard_map/ppermute | solution.py:391
  60.9 17.1 %collective-permute-start.22 = (f32[256,384]{1,0:T(8,128)S(1)}, f32[256,384]{1,0:T(8,128)S(1)}, u32[]{:S(2)}, u32[]{:S(2)}) collective-permute-start(f32[256,384]{1,0:T(8,128)S(1)} %get-tuple-element.79), channel_id=1, source_target_pairs={{0,1},{1,0},{2,3},{3,2},{4,5},{5,4},{6,7},{7,6},{8,9},{9,8},{10,11... | collective-permute-start | bytes 1179656 | tf_op jit(solution)/shard_map/ppermute | solution.py:391
  60.9 17.1 %collective-permute-start.23 = (f32[256,384]{1,0:T(8,128)S(1)}, f32[256,384]{1,0:T(8,128)}, u32[]{:S(2)}, u32[]{:S(2)}) collective-permute-start(f32[256,384]{1,0:T(8,128)S(1)} %get-tuple-element.80), channel_id=1, source_target_pairs={{0,1},{1,0},{2,3},{3,2},{4,5},{5,4},{6,7},{7,6},{8,9},{9,8},{10,11... | collective-permute-start | bytes 1179656 | tf_op jit(solution)/shard_map/ppermute | solution.py:391
  66.4 5.6 %collective-permute-start.25 = (s16[208,384]{1,0:T(8,128)(2,1)S(1)}, s16[208,384]{1,0:T(8,128)(2,1)S(1)}, u32[]{:S(2)}, u32[]{:S(2)}) collective-permute-start(s16[208,384]{1,0:T(8,128)(2,1)S(1)} %get-tuple-element.84), channel_id=1, source_target_pairs={{0,4},{1,5},{2,6},{3,7},{4,0},{5,1},{6,2},{7,3},{8,12},{9,13},{10,... | collective-permute-start | bytes 479240 | tf_op jit(solution)/shard_map/ppermute | solution.py:391
  69.4 5.9 %collective-permute-start.28 = (s16[208,384]{1,0:T(8,128)(2,1)S(1)}, s16[208,384]{1,0:T(8,128)(2,1)S(1)}, u32[]{:S(2)}, u32[]{:S(2)}) collective-permute-start(s16[208,384]{1,0:T(8,128)(2,1)S(1)} %get-tuple-element.92), channel_id=1, source_target_pairs={{0,2},{1,3},{2,0},{3,1},{4,6},{5,7},{6,4},{7,5},{8,10},{9,11},{10,... | collective-permute-start | bytes 479240 | tf_op jit(solution)/shard_map/ppermute | solution.py:391
  72.7 7.8 %collective-permute-start.26 = (s16[112,384]{1,0:T(8,128)(2,1)S(1)}, s16[112,384]{1,0:T(8,128)(2,1)S(1)}, u32[]{:S(2)}, u32[]{:S(2)}) collective-permute-start(s16[112,384]{1,0:T(8,128)(2,1)S(1)} %get-tuple-element.87), channel_id=1, source_target_pairs={{0,8},{1,9},{2,10},{3,11},{4,12},{5,13},{6,14},{7,15},{8,0},{9,1},... | collective-permute-start | bytes 258056 | tf_op jit(solution)/shard_map/ppermute | solution.py:391
  75.9 6.8 %collective-permute-start.29 = (s16[112,384]{1,0:T(8,128)(2,1)S(1)}, s16[112,384]{1,0:T(8,128)(2,1)S(1)}, u32[]{:S(2)}, u32[]{:S(2)}) collective-permute-start(s16[112,384]{1,0:T(8,128)(2,1)S(1)} %get-tuple-element.94), channel_id=1, source_target_pairs={{0,8},{1,9},{2,10},{3,11},{4,12},{5,13},{6,14},{7,15},{8,0},{9,1},... | collective-permute-start | bytes 258056 | tf_op jit(solution)/shard_map/ppermute | solution.py:391
  81.1 2.3 %collective-permute-start.30 = (f32[48,384]{1,0:T(8,128)S(1)}, f32[48,384]{1,0:T(8,128)S(1)}, u32[]{:S(2)}, u32[]{:S(2)}) collective-permute-start(f32[48,384]{1,0:T(8,128)S(1)} %get-tuple-element.96), channel_id=1, source_target_pairs={{0,1},{1,0},{2,3},{3,2},{4,5},{5,4},{6,7},{7,6},{8,9},{9,8},{10,11... | collective-permute-start | bytes 221192 | tf_op jit(solution)/shard_map/ppermute | solution.py:391
  83.3 1.3 %collective-permute-start.31 = (f32[48,384]{1,0:T(8,128)S(1)}, f32[48,384]{1,0:T(8,128)S(1)}, u32[]{:S(2)}, u32[]{:S(2)}) collective-permute-start(f32[48,384]{1,0:T(8,128)S(1)} %get-tuple-element.97), channel_id=1, source_target_pairs={{0,1},{1,0},{2,3},{3,2},{4,5},{5,4},{6,7},{7,6},{8,9},{9,8},{10,11... | collective-permute-start | bytes 221192 | tf_op jit(solution)/shard_map/ppermute | solution.py:391

commit v9 on v8

--- a/solution.py
+++ b/solution.py
@@ -401,7 +401,7 @@
     pred_other = swap(pred_weight, CORE)
     if by_pairs:
         gram_mine, *gram_theirs, sum_own = gram(
-            where, decoder_hidden, after(kept_index, pred_other)[0], (chips, dec // parts)
+            where, decoder_hidden, kept_index[0], (chips, dec // parts)
         )
     else:
         gram_all, sum_own = gram(where, decoder_hidden, kept_index[0], None)
@@ -415,7 +415,7 @@
     if by_pairs:
         z1, z2, y0 = swap(out_piece, NEXT_Z), swap(out_piece, FAR_Z), swap(out_piece, NEXT_Y)
         sum_other = swap(sum_own, CORE)
-        gram_theirs = [swap(g, CORE) for g in gram_theirs]
+        gram_theirs = [swap(after(g, pred_other), CORE) for g in gram_theirs]
         send, keep = first_step(where, after(gram_mine, y0), gram_theirs)
         y1 = swap(z1, NEXT_Y)
         z3 = swap(after(z2, send), NEXT_Z)

time: 85.6 us -> 84.5 us (0.987)
  waiting for transfers between devices: 26.5 us -> 25.5 us
    ppermute x32, waiting for transfers between devices: 26.5 us -> 25.5 us  [swap(): return lax.ppermute(x, AXES, pairs)]
  transfers between devices with their start and end apart: 32 -> 32, of which waited for: 14 -> 13; matrix products, arithmetic and copies ran while one was open for 3% -> 3% of each run, Pallas kernels for 22% -> 22%
where the time goes in v9:
time: 84.5 us; the launch traced here: 84.3 us
  starting transfers between devices  31.4 us (37%)
  waiting for transfers between devices  25.5 us (30%)
  Pallas kernels  20.6 us (24%)
  other arithmetic  3.3 us (4%)
  local copies, waits for them, and re-layouts  2.6 us (3%)
  between operations  0.92 us (1%)
    ppermute x32, starting transfers between devices, swap(): return lax.ppermute(x, AXES, pairs)  31.4 us
    ppermute x32, waiting for transfers between devices, swap(): return lax.ppermute(x, AXES, pairs)  25.5 us
    pallas_call x16, Pallas kernels, run(): pl.pallas_call(kernel, out_shape=tuple(out_shape), in_specs=[pl.BlockSpec...  20.6 us
    select_n x2, other arithmetic, side_by_side(): jnp.where(core == 0, jnp.concatenate(mine + theirs, axis=1), jnp.concaten...  3.22 us
    unnamed x18, local copies, waits for them, and re-layouts  2.6 us
  transfers between devices with their start and end apart: 32, of which 13 were waited for; matrix products, arithmetic and copies ran while one was open for 3% of the time, Pallas kernels for 22%

profile of v9, /device:TPU:0, one launch (start us, length us, event | category | flops | bytes accessed | tf_op | source)
XLA Modules:
  0.0 84.3 jit_solution(2780462462210485897)
XLA Ops:
  0.6 0.5 collective-permute-start.3
  1.1 0.1 collective-permute-start
  1.2 0.1 pad_add_fusion.where_ref
  1.3 1.9 %copy-done.2 = bf16[1,8,256,768]{3,2,1,0:T(8,128)(2,1)S(1)} copy-done((bf16[1,8,256,768]{3,2,1,0:T(8,128)(2,1)S(1)}, bf16[1,8,256,768]{3,2,1,0:T(8,128)(2,1)}, u32[]{:S(2)}) %copy-start.2) | copy-done | bytes 3145752
  3.2 0.7 copy-done.8
  3.9 3.3 %gram.1 = (f32[384,768]{1,0:T(8,128)S(1)}, f32[192,768]{1,0:T(8,128)S(1)}, f32[192,768]{1,0:T(8,128)S(1)}, bf16[256,768]{1,0:T(8,128)(2,1)S(1)}) custom-call(s32[2]{0:T(128)S(1)} %pad_add_fusion.where_ref, bf16[1,8,256,768]{3,2,1,0:T(8,128)(2,1)S(1)} %copy-done.2, s32[8,64]{1,0:T(8,128)S(1)} %bitcast.21), custom_call_target="tpu_custom_call" | custom-call | flops 1000 | bytes 1000 | tf_op jit(solution)/shard_map/gram/pallas_call | solution.py:25
  7.2 0.5 collective-permute-start.4
  7.7 0.1 collective-permute-start.5
  7.8 0.6 cut.2.rest_4_
  8.3 3.0 %collective-permute-start.2 = (bf16[192,768]{1,0:T(8,128)(2,1)S(1)}, bf16[192,768]{1,0:T(8,128)(2,1)S(1)}, u32[]{:S(2)}, u32[]{:S(2)}) collective-permute-start(bf16[192,768]{1,0:T(8,128)(2,1)S(1)} %cut.2.rest_4_), channel_id=1, source_target_pairs={{0,2},{1,3},{2,0},{3,1},{4,6},{5,7},{6,4},{7,5},{8,10},{9,11},{10,... | collective-permute-start | bytes 884744 | tf_op jit(solution)/shard_map/ppermute | solution.py:391
  11.3 1.6 %collective-permute-start.16 = (bf16[192,768]{1,0:T(8,128)(2,1)S(1)}, bf16[192,768]{1,0:T(8,128)(2,1)S(1)}, u32[]{:S(2)}, u32[]{:S(2)}) collective-permute-start(bf16[192,768]{1,0:T(8,128)(2,1)S(1)} %cut.2.rest_4_), channel_id=1, source_target_pairs={{0,4},{1,5},{2,6},{3,7},{4,0},{5,1},{6,2},{7,3},{8,12},{9,13},{10,... | collective-permute-start | bytes 884744 | tf_op jit(solution)/shard_map/ppermute | solution.py:391
  12.9 2.6 %collective-permute-start.1 = (bf16[192,768]{1,0:T(8,128)(2,1)S(1)}, bf16[192,768]{1,0:T(8,128)(2,1)S(1)}, u32[]{:S(2)}, u32[]{:S(2)}) collective-permute-start(bf16[192,768]{1,0:T(8,128)(2,1)S(1)} %cut.2.rest_4_), channel_id=1, source_target_pairs={{0,8},{1,9},{2,10},{3,11},{4,12},{5,13},{6,14},{7,15},{8,0},{9,1},... | collective-permute-start | bytes 884744 | tf_op jit(solution)/shard_map/ppermute | solution.py:391
  15.5 3.1 %collective-permute-done.2.rest_5_ = bf16[192,768]{1,0:T(8,128)(2,1)S(1)} collective-permute-done((bf16[192,768]{1,0:T(8,128)(2,1)S(1)}, bf16[192,768]{1,0:T(8,128)(2,1)S(1)}, u32[]{:S(2)}, u32[]{:S(2)}) %collective-permute-start.2) | collective-permute-done | bytes 294944 | tf_op jit(solution)/shard_map/ppermute | solution.py:391
  18.6 0.9 %first_step.1 = (s16[208,768]{1,0:T(8,128)(2,1)S(1)}, f32[192,768]{1,0:T(8,128)S(1)}) custom-call(s32[2]{0:T(128)S(1)} %pad_add_fusion.where_ref, f32[384,768]{1,0:T(8,128)S(1)} %get-tuple-element.54.mine, f32[192,768]{1,0:T(8,128)S(1)} %collective-permute-done.4.t0, f32[192,768]{1,0:T(8,128)S(1)} %collective-permute-done.5.t1), custom_call_target="tpu_custom_call" | custom-call | flops 1000 | bytes 1000 | tf_op jit(solution)/shard_map/first_step/pallas_call | solution.py:25
  19.6 1.8 %collective-permute-start.7 = (s16[208,768]{1,0:T(8,128)(2,1)S(1)}, s16[208,768]{1,0:T(8,128)(2,1)S(1)}, u32[]{:S(2)}, u32[]{:S(2)}) collective-permute-start(s16[208,768]{1,0:T(8,128)(2,1)S(1)} %get-tuple-element.59), channel_id=1, source_target_pairs={{0,2},{1,3},{2,0},{3,1},{4,6},{5,7},{6,4},{7,5},{8,10},{9,11},{10,... | collective-permute-start | bytes 958472 | tf_op jit(solution)/shard_map/ppermute | solution.py:391
  21.4 4.9 %collective-permute-done.16.rest_6_ = bf16[192,768]{1,0:T(8,128)(2,1)S(1)} collective-permute-done((bf16[192,768]{1,0:T(8,128)(2,1)S(1)}, bf16[192,768]{1,0:T(8,128)(2,1)S(1)}, u32[]{:S(2)}, u32[]{:S(2)}) %collective-permute-start.16) | collective-permute-done | bytes 294944 | tf_op jit(solution)/shard_map/ppermute | solution.py:391
  26.3 0.4 collective-permute-start.17
  26.6 2.0 %collective-permute-done.1.rest_8_ = bf16[192,768]{1,0:T(8,128)(2,1)S(1)} collective-permute-done((bf16[192,768]{1,0:T(8,128)(2,1)S(1)}, bf16[192,768]{1,0:T(8,128)(2,1)S(1)}, u32[]{:S(2)}, u32[]{:S(2)}) %collective-permute-start.1) | collective-permute-done | bytes 294944 | tf_op jit(solution)/shard_map/ppermute | solution.py:391
  28.6 0.5 collective-permute-start.6
  29.1 0.5 collective-permute-start.8
  29.6 0.8 second_step.1
  30.4 3.4 %collective-permute-start.10 = (s16[64,768]{1,0:T(8,128)(2,1)S(1)}, s16[64,768]{1,0:T(8,128)(2,1)S(1)}, u32[]{:S(2)}, u32[]{:S(2)}) collective-permute-start(s16[64,768]{1,0:T(8,128)(2,1)S(1)} %get-tuple-element.69), channel_id=1, source_target_pairs={{0,8},{1,9},{2,10},{3,11},{4,12},{5,13},{6,14},{7,15},{8,0},{9,1},... | collective-permute-start | bytes 294920 | tf_op jit(solution)/shard_map/ppermute | solution.py:391
  33.8 1.3 %collective-permute-start.11 = (s16[64,768]{1,0:T(8,128)(2,1)S(1)}, s16[64,768]{1,0:T(8,128)(2,1)S(1)}, u32[]{:S(2)}, u32[]{:S(2)}) collective-permute-start(s16[64,768]{1,0:T(8,128)(2,1)S(1)} %get-tuple-element.70), channel_id=1, source_target_pairs={{0,12},{1,13},{2,14},{3,15},{4,8},{5,9},{6,10},{7,11},{8,4},{9,5},... | collective-permute-start | bytes 294920 | tf_op jit(solution)/shard_map/ppermute | solution.py:391
  35.1 1.1 %collective-permute-done.17.rest_7_ = bf16[192,768]{1,0:T(8,128)(2,1)S(1)} collective-permute-done((bf16[192,768]{1,0:T(8,128)(2,1)S(1)}, bf16[192,768]{1,0:T(8,128)(2,1)S(1)}, u32[]{:S(2)}, u32[]{:S(2)}) %collective-permute-start.17) | collective-permute-done | bytes 294944 | tf_op jit(solution)/shard_map/ppermute | solution.py:391
  36.2 2.0 %collective-permute-start.9 = (s16[64,768]{1,0:T(8,128)(2,1)S(1)}, s16[64,768]{1,0:T(8,128)(2,1)S(1)}, u32[]{:S(2)}, u32[]{:S(2)}) collective-permute-start(s16[64,768]{1,0:T(8,128)(2,1)S(1)} %get-tuple-element.68), channel_id=1, source_target_pairs={{0,4},{1,5},{2,6},{3,7},{4,0},{5,1},{6,2},{7,3},{8,12},{9,13},{10,... | collective-permute-start | bytes 294920 | tf_op jit(solution)/shard_map/ppermute | solution.py:391
  38.2 1.0 %collective-permute-done.6.rest_10_ = bf16[192,768]{1,0:T(8,128)(2,1)S(1)} collective-permute-done((bf16[192,768]{1,0:T(8,128)(2,1)S(1)}, bf16[192,768]{1,0:T(8,128)(2,1)S(1)}, u32[]{:S(2)}, u32[]{:S(2)}) %collective-permute-start.6) | collective-permute-done | bytes 294944 | tf_op jit(solution)/shard_map/ppermute | solution.py:391
  39.2 0.5 collective-permute-start.18
  39.7 0.6 cut.3.weights
  40.3 3.5 %attention.1 = (bf16[256,1536]{1,0:T(8,128)(2,1)S(1)}, bf16[256,768]{1,0:T(8,128)(2,1)S(1)}, bf16[256,768]{1,0:T(8,128)(2,1)S(1)}, bf16[256,768]{1,0:T(8,128)(2,1)S(1)}, bf16[256,768]{1,0:T(8,128)(2,1)S(1)}) custom-call(s32[2]{0:T(128)S(1)} %pad_add_fusion.where_ref, bf16[256,1536]{1,0:T(8,128)(2,1)S(1)} %bitcast.16, bf16[256,1536]{1,0:T(8,128)(2,1)S(1)} %bitcast.17, ...), custom_call_target="tpu_custom_call" | custom-call | flops 1000 | bytes 1000 | tf_op jit(solution)/shard_map/attention/pallas_call | solution.py:25
  43.8 0.1 collective-permute-start.12
  43.9 0.5 collective-permute-start.13
  44.4 0.1 collective-permute-start.14
  44.5 0.4 collective-permute-start.15
  44.9 2.6 %collective-permute-done.18.rest_11_ = bf16[192,768]{1,0:T(8,128)(2,1)S(1)} collective-permute-done((bf16[192,768]{1,0:T(8,128)(2,1)S(1)}, bf16[192,768]{1,0:T(8,128)(2,1)S(1)}, u32[]{:S(2)}, u32[]{:S(2)}) %collective-permute-start.18) | collective-permute-done | bytes 294944 | tf_op jit(solution)/shard_map/ppermute | solution.py:391
  47.6 0.6 last_step.3.gram_own
  48.3 2.8 %branch.1 = (f32[512,768]{1,0:T(8,128)S(1)}, f32[512,128]{1,0:T(8,128)S(1)}) custom-call(s32[2]{0:T(128)S(1)} %pad_add_fusion.where_ref, bf16[256,1536]{1,0:T(8,128)(2,1)S(1)} %get-tuple-element.71.mixed_own, bf16[256,1536]{1,0:T(8,128)(2,1)S(1)} %bitcast.13, bf16[256,1536]{1,0:T(8,128)(2,1)S(1)} %bitcast.15, ...), custom_call_target="tpu_custom_call" | custom-call | flops 1000 | bytes 1000 | tf_op jit(solution)/shard_map/branch/pallas_call | solution.py:25
  51.0 0.6 collective-permute-start.19
  51.6 0.1 collective-permute-start.21
  51.7 1.1 %collective-permute-done.19.stats_other = f32[512,128]{1,0:T(8,128)S(1)} collective-permute-done((f32[512,128]{1,0:T(8,128)S(1)}, f32[512,128]{1,0:T(8,128)S(1)}, u32[]{:S(2)}, u32[]{:S(2)}) %collective-permute-start.19) | collective-permute-done | bytes 262176 | tf_op jit(solution)/shard_map/ppermute | solution.py:391
  52.8 0.2 collective-permute-done.21.gram_other
  53.0 1.9 %targets.2 = (f32[256,384]{1,0:T(8,128)S(1)}, f32[256,384]{1,0:T(8,128)S(1)}, s16[400,384]{1,0:T(8,128)(2,1)S(1)}, f32[384,384]{1,0:T(8,128)S(1)}) custom-call(s32[2]{0:T(128)S(1)} %pad_add_fusion.where_ref, f32[512,768]{1,0:T(8,128)S(1)} %get-tuple-element.77.blend, f32[512,128]{1,0:T(8,128)S(1)} %get-tuple-element.78.stats, ...), custom_call_target="tpu_custom_call" | custom-call | flops 1000 | bytes 1000 | tf_op jit(solution)/shard_map/targets/pallas_call | solution.py:25
  54.9 1.5 %collective-permute-start.24 = (s16[400,384]{1,0:T(8,128)(2,1)S(1)}, s16[400,384]{1,0:T(8,128)(2,1)S(1)}, u32[]{:S(2)}, u32[]{:S(2)}) collective-permute-start(s16[400,384]{1,0:T(8,128)(2,1)S(1)} %get-tuple-element.84), channel_id=1, source_target_pairs={{0,2},{1,3},{2,0},{3,1},{4,6},{5,7},{6,4},{7,5},{8,10},{9,11},{10,... | collective-permute-start | bytes 921608 | tf_op jit(solution)/shard_map/ppermute | solution.py:391
  56.4 1.8 %targets.3 = (f32[256,384]{1,0:T(8,128)S(1)}, f32[256,384]{1,0:T(8,128)S(1)}, s16[400,384]{1,0:T(8,128)(2,1)S(1)}, f32[384,384]{1,0:T(8,128)S(1)}) custom-call(s32[2]{0:T(128)S(1)} %pad_add_fusion.where_ref, f32[512,768]{1,0:T(8,128)S(1)} %get-tuple-element.77.blend, f32[512,128]{1,0:T(8,128)S(1)} %get-tuple-element.78.stats, ...), custom_call_target="tpu_custom_call" | custom-call | flops 1000 | bytes 1000 | tf_op jit(solution)/shard_map/targets/pallas_call | solution.py:25
  58.1 1.6 %collective-permute-start.27 = (s16[400,384]{1,0:T(8,128)(2,1)S(1)}, s16[400,384]{1,0:T(8,128)(2,1)S(1)}, u32[]{:S(2)}, u32[]{:S(2)}) collective-permute-start(s16[400,384]{1,0:T(8,128)(2,1)S(1)} %get-tuple-element.92), channel_id=1, source_target_pairs={{0,4},{1,5},{2,6},{3,7},{4,0},{5,1},{6,2},{7,3},{8,12},{9,13},{10,... | collective-permute-start | bytes 921608 | tf_op jit(solution)/shard_map/ppermute | solution.py:391
  59.8 0.5 collective-permute-start.23
  60.3 4.2 %collective-permute-done.24.codes = s16[400,384]{1,0:T(8,128)(2,1)S(1)} collective-permute-done((s16[400,384]{1,0:T(8,128)(2,1)S(1)}, s16[400,384]{1,0:T(8,128)(2,1)S(1)}, u32[]{:S(2)}, u32[]{:S(2)}) %collective-permute-start.24) | collective-permute-done | bytes 307232 | tf_op jit(solution)/shard_map/ppermute | solution.py:391
  64.5 0.8 next_step.4
  65.3 1.5 %collective-permute-start.25 = (s16[208,384]{1,0:T(8,128)(2,1)S(1)}, s16[208,384]{1,0:T(8,128)(2,1)S(1)}, u32[]{:S(2)}, u32[]{:S(2)}) collective-permute-start(s16[208,384]{1,0:T(8,128)(2,1)S(1)} %get-tuple-element.86), channel_id=1, source_target_pairs={{0,4},{1,5},{2,6},{3,7},{4,0},{5,1},{6,2},{7,3},{8,12},{9,13},{10,... | collective-permute-start | bytes 479240 | tf_op jit(solution)/shard_map/ppermute | solution.py:391
  66.8 0.6 collective-permute-done.27.codes
  67.5 0.8 next_step.6
  68.2 1.0 %collective-permute-start.28 = (s16[208,384]{1,0:T(8,128)(2,1)S(1)}, s16[208,384]{1,0:T(8,128)(2,1)S(1)}, u32[]{:S(2)}, u32[]{:S(2)}) collective-permute-start(s16[208,384]{1,0:T(8,128)(2,1)S(1)} %get-tuple-element.94), channel_id=1, source_target_pairs={{0,2},{1,3},{2,0},{3,1},{4,6},{5,7},{6,4},{7,5},{8,10},{9,11},{10,... | collective-permute-start | bytes 479240 | tf_op jit(solution)/shard_map/ppermute | solution.py:391
  69.2 1.7 %collective-permute-done.25.codes = s16[208,384]{1,0:T(8,128)(2,1)S(1)} collective-permute-done((s16[208,384]{1,0:T(8,128)(2,1)S(1)}, s16[208,384]{1,0:T(8,128)(2,1)S(1)}, u32[]{:S(2)}, u32[]{:S(2)}) %collective-permute-start.25) | collective-permute-done | bytes 159776 | tf_op jit(solution)/shard_map/ppermute | solution.py:391
  70.9 0.6 next_step.5
  71.6 2.6 %collective-permute-start.26 = (s16[112,384]{1,0:T(8,128)(2,1)S(1)}, s16[112,384]{1,0:T(8,128)(2,1)S(1)}, u32[]{:S(2)}, u32[]{:S(2)}) collective-permute-start(s16[112,384]{1,0:T(8,128)(2,1)S(1)} %get-tuple-element.89), channel_id=1, source_target_pairs={{0,8},{1,9},{2,10},{3,11},{4,12},{5,13},{6,14},{7,15},{8,0},{9,1},... | collective-permute-start | bytes 258056 | tf_op jit(solution)/shard_map/ppermute | solution.py:391
  74.2 0.6 next_step.7
  74.8 2.1 %collective-permute-start.29 = (s16[112,384]{1,0:T(8,128)(2,1)S(1)}, s16[112,384]{1,0:T(8,128)(2,1)S(1)}, u32[]{:S(2)}, u32[]{:S(2)}) collective-permute-start(s16[112,384]{1,0:T(8,128)(2,1)S(1)} %get-tuple-element.96), channel_id=1, source_target_pairs={{0,8},{1,9},{2,10},{3,11},{4,12},{5,13},{6,14},{7,15},{8,0},{9,1},... | collective-permute-start | bytes 258056 | tf_op jit(solution)/shard_map/ppermute | solution.py:391
  76.9 2.5 %maximum_select_fusion = f32[1,256,1536]{2,1,0:T(8,128)} fusion(f32[1,256,384]{2,1,0:T(8,128)} %bitcast.11, f32[1,256,384]{2,1,0:T(8,128)S(1)} %bitcast.22, f32[1,256,384]{2,1,0:T(8,128)S(1)} %bitcast.20, f32[1,256,384]{2,1,0:T(8,128)S(1)} %bitcast.19, pred[]{:T(512)S(6)} %eq.6), kind=kLoop, calls=%fused_computation | loop fusion | flops 2752512 | bytes 3145729 | tf_op jit(solution)/shard_map/jit(_where)/select_n | solution.py:394
  79.4 0.6 last_step.4
  79.9 0.1 collective-permute-start.30
  80.0 1.6 %collective-permute-done.29.rest_0_ = s16[112,384]{1,0:T(8,128)(2,1)S(1)} collective-permute-done((s16[112,384]{1,0:T(8,128)(2,1)S(1)}, s16[112,384]{1,0:T(8,128)(2,1)S(1)}, u32[]{:S(2)}, u32[]{:S(2)}) %collective-permute-start.29) | collective-permute-done | bytes 86048 | tf_op jit(solution)/shard_map/ppermute | solution.py:391
  81.6 0.6 last_step.5
  82.2 0.1 collective-permute-start.31
  82.3 1.2 %collective-permute-done.31 = f32[48,384]{1,0:T(8,128)S(1)} collective-permute-done((f32[48,384]{1,0:T(8,128)S(1)}, f32[48,384]{1,0:T(8,128)S(1)}, u32[]{:S(2)}, u32[]{:S(2)}) %collective-permute-start.31) | collective-permute-done | bytes 73760 | tf_op jit(solution)/shard_map/ppermute | solution.py:391
  83.5 0.7 maximum_select_fusion.1
  (37 shorter events, 0.1 us)
Async XLA Ops:
  0.6 6.5 %collective-permute-start.3 = (bf16[48,1536]{1,0:T(8,128)(2,1)}, bf16[48,1536]{1,0:T(8,128)(2,1)S(1)}, u32[]{:S(2)}, u32[]{:S(2)}) collective-permute-start(bf16[48,1536]{1,0:T(8,128)(2,1)} %own.2), channel_id=1, source_target_pairs={{0,1},{1,0},{2,3},{3,2},{4,5},{5,4},{6,7},{7,6},{8,9},{9,8},{10,11... | collective-permute-start | bytes 442376 | tf_op jit(solution)/shard_map/ppermute | solution.py:391
  1.1 6.6 %collective-permute-start = (bf16[96,1536]{1,0:T(8,128)(2,1)}, bf16[96,1536]{1,0:T(8,128)(2,1)S(1)}, u32[]{:S(2)}, u32[]{:S(2)}) collective-permute-start(bf16[96,1536]{1,0:T(8,128)(2,1)} %own.1), channel_id=1, source_target_pairs={{0,1},{1,0},{2,3},{3,2},{4,5},{5,4},{6,7},{7,6},{8,9},{9,8},{10,11... | collective-permute-start | bytes 884744 | tf_op jit(solution)/shard_map/ppermute | solution.py:391
  1.3 1.9 %copy-start.2 = (bf16[1,8,256,768]{3,2,1,0:T(8,128)(2,1)S(1)}, bf16[1,8,256,768]{3,2,1,0:T(8,128)(2,1)}, u32[]{:S(2)}) copy-start(bf16[1,8,256,768]{3,2,1,0:T(8,128)(2,1)} %hidden_ref.1) | copy-start | bytes 9437188
  3.2 0.7 copy-start.8
  3.9 3.9 %copy-start.6 = (bf16[96,1536]{1,0:T(8,128)(2,1)S(1)}, bf16[96,1536]{1,0:T(8,128)(2,1)}, u32[]{:S(2)}) copy-start(bf16[96,1536]{1,0:T(8,128)(2,1)} %own.1) | copy-start | bytes 884740
  7.2 11.4 %collective-permute-start.4 = (f32[192,768]{1,0:T(8,128)S(1)}, f32[192,768]{1,0:T(8,128)S(1)}, u32[]{:S(2)}, u32[]{:S(2)}) collective-permute-start(f32[192,768]{1,0:T(8,128)S(1)} %get-tuple-element.56), channel_id=1, source_target_pairs={{0,1},{1,0},{2,3},{3,2},{4,5},{5,4},{6,7},{7,6},{8,9},{9,8},{10,11... | collective-permute-start | bytes 1769480 | tf_op jit(solution)/shard_map/ppermute | solution.py:391
  7.7 11.0 %collective-permute-start.5 = (f32[192,768]{1,0:T(8,128)S(1)}, f32[192,768]{1,0:T(8,128)S(1)}, u32[]{:S(2)}, u32[]{:S(2)}) collective-permute-start(f32[192,768]{1,0:T(8,128)S(1)} %get-tuple-element.58), channel_id=1, source_target_pairs={{0,1},{1,0},{2,3},{3,2},{4,5},{5,4},{6,7},{7,6},{8,9},{9,8},{10,11... | collective-permute-start | bytes 1769480 | tf_op jit(solution)/shard_map/ppermute | solution.py:391
  7.8 32.5 %copy-start.5 = (bf16[1,256,1536]{2,1,0:T(8,128)(2,1)S(1)}, bf16[1,256,1536]{2,1,0:T(8,128)(2,1)}, u32[]{:S(2)}) copy-start(bf16[1,256,1536]{2,1,0:T(8,128)(2,1)} %param.11) | copy-start | bytes 2359300
  8.3 10.3 %collective-permute-start.2 = (bf16[192,768]{1,0:T(8,128)(2,1)S(1)}, bf16[192,768]{1,0:T(8,128)(2,1)S(1)}, u32[]{:S(2)}, u32[]{:S(2)}) collective-permute-start(bf16[192,768]{1,0:T(8,128)(2,1)S(1)} %cut.2.rest_4_), channel_id=1, source_target_pairs={{0,2},{1,3},{2,0},{3,1},{4,6},{5,7},{6,4},{7,5},{8,10},{9,11},{10,... | collective-permute-start | bytes 884744 | tf_op jit(solution)/shard_map/ppermute | solution.py:391
  11.3 14.9 %collective-permute-start.16 = (bf16[192,768]{1,0:T(8,128)(2,1)S(1)}, bf16[192,768]{1,0:T(8,128)(2,1)S(1)}, u32[]{:S(2)}, u32[]{:S(2)}) collective-permute-start(bf16[192,768]{1,0:T(8,128)(2,1)S(1)} %cut.2.rest_4_), channel_id=1, source_target_pairs={{0,4},{1,5},{2,6},{3,7},{4,0},{5,1},{6,2},{7,3},{8,12},{9,13},{10,... | collective-permute-start | bytes 884744 | tf_op jit(solution)/shard_map/ppermute | solution.py:391
  12.9 15.7 %collective-permute-start.1 = (bf16[192,768]{1,0:T(8,128)(2,1)S(1)}, bf16[192,768]{1,0:T(8,128)(2,1)S(1)}, u32[]{:S(2)}, u32[]{:S(2)}) collective-permute-start(bf16[192,768]{1,0:T(8,128)(2,1)S(1)} %cut.2.rest_4_), channel_id=1, source_target_pairs={{0,8},{1,9},{2,10},{3,11},{4,12},{5,13},{6,14},{7,15},{8,0},{9,1},... | collective-permute-start | bytes 884744 | tf_op jit(solution)/shard_map/ppermute | solution.py:391
  18.6 21.1 %copy-start.7 = (bf16[48,1536]{1,0:T(8,128)(2,1)S(1)}, bf16[48,1536]{1,0:T(8,128)(2,1)}, u32[]{:S(2)}) copy-start(bf16[48,1536]{1,0:T(8,128)(2,1)} %own.2) | copy-start | bytes 442372
  18.6 21.7 %copy-start = (bf16[1,256,1536]{2,1,0:T(8,128)(2,1)S(1)}, bf16[1,256,1536]{2,1,0:T(8,128)(2,1)}, u32[]{:S(2)}) copy-start(bf16[1,256,1536]{2,1,0:T(8,128)(2,1)} %param.12) | copy-start | bytes 2359300
  18.6 21.7 %copy-start.1 = (bf16[1,256,1536]{2,1,0:T(8,128)(2,1)S(1)}, bf16[1,256,1536]{2,1,0:T(8,128)(2,1)}, u32[]{:S(2)}) copy-start(bf16[1,256,1536]{2,1,0:T(8,128)(2,1)} %param.13) | copy-start | bytes 2359300
  18.6 21.7 %copy-start.3 = (bf16[1,256,1536]{2,1,0:T(8,128)(2,1)S(1)}, bf16[1,256,1536]{2,1,0:T(8,128)(2,1)}, u32[]{:S(2)}) copy-start(bf16[1,256,1536]{2,1,0:T(8,128)(2,1)} %param.9) | copy-start | bytes 2359300
  18.6 21.7 %copy-start.4 = (bf16[1,256,1536]{2,1,0:T(8,128)(2,1)S(1)}, bf16[1,256,1536]{2,1,0:T(8,128)(2,1)}, u32[]{:S(2)}) copy-start(bf16[1,256,1536]{2,1,0:T(8,128)(2,1)} %param.10) | copy-start | bytes 2359300
  19.6 10.0 %collective-permute-start.7 = (s16[208,768]{1,0:T(8,128)(2,1)S(1)}, s16[208,768]{1,0:T(8,128)(2,1)S(1)}, u32[]{:S(2)}, u32[]{:S(2)}) collective-permute-start(s16[208,768]{1,0:T(8,128)(2,1)S(1)} %get-tuple-element.59), channel_id=1, source_target_pairs={{0,2},{1,3},{2,0},{3,1},{4,6},{5,7},{6,4},{7,5},{8,10},{9,11},{10,... | collective-permute-start | bytes 958472 | tf_op jit(solution)/shard_map/ppermute | solution.py:391
  26.3 9.9 %collective-permute-start.17 = (bf16[192,768]{1,0:T(8,128)(2,1)S(1)}, bf16[192,768]{1,0:T(8,128)(2,1)S(1)}, u32[]{:S(2)}, u32[]{:S(2)}) collective-permute-start(bf16[192,768]{1,0:T(8,128)(2,1)S(1)} %collective-permute-done.16.rest_6_), channel_id=1, source_target_pairs={{0,2},{1,3},{2,0},{3,1},{4,6},{5,7},{6,4},{7,5},{8,10},{9,11},{10,... | collective-permute-start | bytes 884744 | tf_op jit(solution)/shard_map/ppermute | solution.py:391
  28.6 10.6 %collective-permute-start.6 = (bf16[192,768]{1,0:T(8,128)(2,1)S(1)}, bf16[192,768]{1,0:T(8,128)(2,1)S(1)}, u32[]{:S(2)}, u32[]{:S(2)}) collective-permute-start(bf16[192,768]{1,0:T(8,128)(2,1)S(1)} %collective-permute-done.1.rest_8_), channel_id=1, source_target_pairs={{0,4},{1,5},{2,6},{3,7},{4,0},{5,1},{6,2},{7,3},{8,12},{9,13},{10,... | collective-permute-start | bytes 884744 | tf_op jit(solution)/shard_map/ppermute | solution.py:391
  29.1 14.8 %collective-permute-start.8 = (bf16[192,768]{1,0:T(8,128)(2,1)S(1)}, bf16[192,768]{1,0:T(8,128)(2,1)S(1)}, u32[]{:S(2)}, u32[]{:S(2)}) collective-permute-start(bf16[192,768]{1,0:T(8,128)(2,1)S(1)} %collective-permute-done.1.rest_8_), channel_id=1, source_target_pairs={{0,2},{1,3},{2,0},{3,1},{4,6},{5,7},{6,4},{7,5},{8,10},{9,11},{10,... | collective-permute-start | bytes 884744 | tf_op jit(solution)/shard_map/ppermute | solution.py:391
  30.4 13.5 %collective-permute-start.10 = (s16[64,768]{1,0:T(8,128)(2,1)S(1)}, s16[64,768]{1,0:T(8,128)(2,1)S(1)}, u32[]{:S(2)}, u32[]{:S(2)}) collective-permute-start(s16[64,768]{1,0:T(8,128)(2,1)S(1)} %get-tuple-element.69), channel_id=1, source_target_pairs={{0,8},{1,9},{2,10},{3,11},{4,12},{5,13},{6,14},{7,15},{8,0},{9,1},... | collective-permute-start | bytes 294920 | tf_op jit(solution)/shard_map/ppermute | solution.py:391
  33.8 10.6 %collective-permute-start.11 = (s16[64,768]{1,0:T(8,128)(2,1)S(1)}, s16[64,768]{1,0:T(8,128)(2,1)S(1)}, u32[]{:S(2)}, u32[]{:S(2)}) collective-permute-start(s16[64,768]{1,0:T(8,128)(2,1)S(1)} %get-tuple-element.70), channel_id=1, source_target_pairs={{0,12},{1,13},{2,14},{3,15},{4,8},{5,9},{6,10},{7,11},{8,4},{9,5},... | collective-permute-start | bytes 294920 | tf_op jit(solution)/shard_map/ppermute | solution.py:391
  36.2 8.3 %collective-permute-start.9 = (s16[64,768]{1,0:T(8,128)(2,1)S(1)}, s16[64,768]{1,0:T(8,128)(2,1)S(1)}, u32[]{:S(2)}, u32[]{:S(2)}) collective-permute-start(s16[64,768]{1,0:T(8,128)(2,1)S(1)} %get-tuple-element.68), channel_id=1, source_target_pairs={{0,4},{1,5},{2,6},{3,7},{4,0},{5,1},{6,2},{7,3},{8,12},{9,13},{10,... | collective-permute-start | bytes 294920 | tf_op jit(solution)/shard_map/ppermute | solution.py:391
  39.2 8.4 %collective-permute-start.18 = (bf16[192,768]{1,0:T(8,128)(2,1)S(1)}, bf16[192,768]{1,0:T(8,128)(2,1)S(1)}, u32[]{:S(2)}, u32[]{:S(2)}) collective-permute-start(bf16[192,768]{1,0:T(8,128)(2,1)S(1)} %collective-permute-done.6.rest_10_), channel_id=1, source_target_pairs={{0,2},{1,3},{2,0},{3,1},{4,6},{5,7},{6,4},{7,5},{8,10},{9,11},{10,... | collective-permute-start | bytes 884744 | tf_op jit(solution)/shard_map/ppermute | solution.py:391
  43.8 4.4 %collective-permute-start.12 = (bf16[256,768]{1,0:T(8,128)(2,1)S(1)}, bf16[256,768]{1,0:T(8,128)(2,1)S(1)}, u32[]{:S(2)}, u32[]{:S(2)}) collective-permute-start(bf16[256,768]{1,0:T(8,128)(2,1)S(1)} %get-tuple-element.72), channel_id=1, source_target_pairs={{0,1},{1,0},{2,3},{3,2},{4,5},{5,4},{6,7},{7,6},{8,9},{9,8},{10,11... | collective-permute-start | bytes 1179656 | tf_op jit(solution)/shard_map/ppermute | solution.py:391
  43.9 4.3 %collective-permute-start.13 = (bf16[256,768]{1,0:T(8,128)(2,1)S(1)}, bf16[256,768]{1,0:T(8,128)(2,1)S(1)}, u32[]{:S(2)}, u32[]{:S(2)}) collective-permute-start(bf16[256,768]{1,0:T(8,128)(2,1)S(1)} %get-tuple-element.73), channel_id=1, source_target_pairs={{0,1},{1,0},{2,3},{3,2},{4,5},{5,4},{6,7},{7,6},{8,9},{9,8},{10,11... | collective-permute-start | bytes 1179656 | tf_op jit(solution)/shard_map/ppermute | solution.py:391
  44.4 3.8 %collective-permute-start.14 = (bf16[256,768]{1,0:T(8,128)(2,1)S(1)}, bf16[256,768]{1,0:T(8,128)(2,1)S(1)}, u32[]{:S(2)}, u32[]{:S(2)}) collective-permute-start(bf16[256,768]{1,0:T(8,128)(2,1)S(1)} %get-tuple-element.74), channel_id=1, source_target_pairs={{0,1},{1,0},{2,3},{3,2},{4,5},{5,4},{6,7},{7,6},{8,9},{9,8},{10,11... | collective-permute-start | bytes 1179656 | tf_op jit(solution)/shard_map/ppermute | solution.py:391
  44.5 3.7 %collective-permute-start.15 = (bf16[256,768]{1,0:T(8,128)(2,1)S(1)}, bf16[256,768]{1,0:T(8,128)(2,1)S(1)}, u32[]{:S(2)}, u32[]{:S(2)}) collective-permute-start(bf16[256,768]{1,0:T(8,128)(2,1)S(1)} %get-tuple-element.75), channel_id=1, source_target_pairs={{0,1},{1,0},{2,3},{3,2},{4,5},{5,4},{6,7},{7,6},{8,9},{9,8},{10,11... | collective-permute-start | bytes 1179656 | tf_op jit(solution)/shard_map/ppermute | solution.py:391
  47.6 5.2 %collective-permute-start.20 = (bf16[256,768]{1,0:T(8,128)(2,1)S(1)}, bf16[256,768]{1,0:T(8,128)(2,1)S(1)}, u32[]{:S(2)}, u32[]{:S(2)}) collective-permute-start(bf16[256,768]{1,0:T(8,128)(2,1)S(1)} %get-tuple-element.51.sum_own), channel_id=1, source_target_pairs={{0,1},{1,0},{2,3},{3,2},{4,5},{5,4},{6,7},{7,6},{8,9},{9,8},{10,11... | collective-permute-start | bytes 1179656 | tf_op jit(solution)/shard_map/ppermute | solution.py:391
  51.0 1.7 %collective-permute-start.19 = (f32[512,128]{1,0:T(8,128)S(1)}, f32[512,128]{1,0:T(8,128)S(1)}, u32[]{:S(2)}, u32[]{:S(2)}) collective-permute-start(f32[512,128]{1,0:T(8,128)S(1)} %get-tuple-element.78.stats), channel_id=1, source_target_pairs={{0,1},{1,0},{2,3},{3,2},{4,5},{5,4},{6,7},{7,6},{8,9},{9,8},{10,11... | collective-permute-start | bytes 786440 | tf_op jit(solution)/shard_map/ppermute | solution.py:391
  51.6 1.4 %collective-permute-start.21 = (bf16[96,768]{1,0:T(8,128)(2,1)S(1)}, bf16[96,768]{1,0:T(8,128)(2,1)S(1)}, u32[]{:S(2)}, u32[]{:S(2)}) collective-permute-start(bf16[96,768]{1,0:T(8,128)(2,1)S(1)} %last_step.3.gram_own), channel_id=1, source_target_pairs={{0,1},{1,0},{2,3},{3,2},{4,5},{5,4},{6,7},{7,6},{8,9},{9,8},{10,11... | collective-permute-start | bytes 442376 | tf_op jit(solution)/shard_map/ppermute | solution.py:391
  54.9 9.6 %collective-permute-start.24 = (s16[400,384]{1,0:T(8,128)(2,1)S(1)}, s16[400,384]{1,0:T(8,128)(2,1)S(1)}, u32[]{:S(2)}, u32[]{:S(2)}) collective-permute-start(s16[400,384]{1,0:T(8,128)(2,1)S(1)} %get-tuple-element.84), channel_id=1, source_target_pairs={{0,2},{1,3},{2,0},{3,1},{4,6},{5,7},{6,4},{7,5},{8,10},{9,11},{10,... | collective-permute-start | bytes 921608 | tf_op jit(solution)/shard_map/ppermute | solution.py:391
  58.1 9.3 %collective-permute-start.27 = (s16[400,384]{1,0:T(8,128)(2,1)S(1)}, s16[400,384]{1,0:T(8,128)(2,1)S(1)}, u32[]{:S(2)}, u32[]{:S(2)}) collective-permute-start(s16[400,384]{1,0:T(8,128)(2,1)S(1)} %get-tuple-element.92), channel_id=1, source_target_pairs={{0,4},{1,5},{2,6},{3,7},{4,0},{5,1},{6,2},{7,3},{8,12},{9,13},{10,... | collective-permute-start | bytes 921608 | tf_op jit(solution)/shard_map/ppermute | solution.py:391
  59.8 17.1 %collective-permute-start.22 = (f32[256,384]{1,0:T(8,128)S(1)}, f32[256,384]{1,0:T(8,128)S(1)}, u32[]{:S(2)}, u32[]{:S(2)}) collective-permute-start(f32[256,384]{1,0:T(8,128)S(1)} %get-tuple-element.81), channel_id=1, source_target_pairs={{0,1},{1,0},{2,3},{3,2},{4,5},{5,4},{6,7},{7,6},{8,9},{9,8},{10,11... | collective-permute-start | bytes 1179656 | tf_op jit(solution)/shard_map/ppermute | solution.py:391
  59.8 17.1 %collective-permute-start.23 = (f32[256,384]{1,0:T(8,128)S(1)}, f32[256,384]{1,0:T(8,128)}, u32[]{:S(2)}, u32[]{:S(2)}) collective-permute-start(f32[256,384]{1,0:T(8,128)S(1)} %get-tuple-element.82), channel_id=1, source_target_pairs={{0,1},{1,0},{2,3},{3,2},{4,5},{5,4},{6,7},{7,6},{8,9},{9,8},{10,11... | collective-permute-start | bytes 1179656 | tf_op jit(solution)/shard_map/ppermute | solution.py:391
  65.3 5.6 %collective-permute-start.25 = (s16[208,384]{1,0:T(8,128)(2,1)S(1)}, s16[208,384]{1,0:T(8,128)(2,1)S(1)}, u32[]{:S(2)}, u32[]{:S(2)}) collective-permute-start(s16[208,384]{1,0:T(8,128)(2,1)S(1)} %get-tuple-element.86), channel_id=1, source_target_pairs={{0,4},{1,5},{2,6},{3,7},{4,0},{5,1},{6,2},{7,3},{8,12},{9,13},{10,... | collective-permute-start | bytes 479240 | tf_op jit(solution)/shard_map/ppermute | solution.py:391
  68.2 5.9 %collective-permute-start.28 = (s16[208,384]{1,0:T(8,128)(2,1)S(1)}, s16[208,384]{1,0:T(8,128)(2,1)S(1)}, u32[]{:S(2)}, u32[]{:S(2)}) collective-permute-start(s16[208,384]{1,0:T(8,128)(2,1)S(1)} %get-tuple-element.94), channel_id=1, source_target_pairs={{0,2},{1,3},{2,0},{3,1},{4,6},{5,7},{6,4},{7,5},{8,10},{9,11},{10,... | collective-permute-start | bytes 479240 | tf_op jit(solution)/shard_map/ppermute | solution.py:391
  71.6 7.8 %collective-permute-start.26 = (s16[112,384]{1,0:T(8,128)(2,1)S(1)}, s16[112,384]{1,0:T(8,128)(2,1)S(1)}, u32[]{:S(2)}, u32[]{:S(2)}) collective-permute-start(s16[112,384]{1,0:T(8,128)(2,1)S(1)} %get-tuple-element.89), channel_id=1, source_target_pairs={{0,8},{1,9},{2,10},{3,11},{4,12},{5,13},{6,14},{7,15},{8,0},{9,1},... | collective-permute-start | bytes 258056 | tf_op jit(solution)/shard_map/ppermute | solution.py:391
  74.8 6.8 %collective-permute-start.29 = (s16[112,384]{1,0:T(8,128)(2,1)S(1)}, s16[112,384]{1,0:T(8,128)(2,1)S(1)}, u32[]{:S(2)}, u32[]{:S(2)}) collective-permute-start(s16[112,384]{1,0:T(8,128)(2,1)S(1)} %get-tuple-element.96), channel_id=1, source_target_pairs={{0,8},{1,9},{2,10},{3,11},{4,12},{5,13},{6,14},{7,15},{8,0},{9,1},... | collective-permute-start | bytes 258056 | tf_op jit(solution)/shard_map/ppermute | solution.py:391
  79.9 2.3 %collective-permute-start.30 = (f32[48,384]{1,0:T(8,128)S(1)}, f32[48,384]{1,0:T(8,128)S(1)}, u32[]{:S(2)}, u32[]{:S(2)}) collective-permute-start(f32[48,384]{1,0:T(8,128)S(1)} %get-tuple-element.98), channel_id=1, source_target_pairs={{0,1},{1,0},{2,3},{3,2},{4,5},{5,4},{6,7},{7,6},{8,9},{9,8},{10,11... | collective-permute-start | bytes 221192 | tf_op jit(solution)/shard_map/ppermute | solution.py:391
  82.2 1.3 %collective-permute-start.31 = (f32[48,384]{1,0:T(8,128)S(1)}, f32[48,384]{1,0:T(8,128)S(1)}, u32[]{:S(2)}, u32[]{:S(2)}) collective-permute-start(f32[48,384]{1,0:T(8,128)S(1)} %get-tuple-element.99), channel_id=1, source_target_pairs={{0,1},{1,0},{2,3},{3,2},{4,5},{5,4},{6,7},{7,6},{8,9},{9,8},{10,11... | collective-permute-start | bytes 221192 | tf_op jit(solution)/shard_map/ppermute | solution.py:391

commit v10 on v9

--- a/solution.py
+++ b/solution.py
@@ -315,11 +315,11 @@
     return call(functools.partial(last_kernel, scale=scale, count=len(codes)), shapes, "last_step")(where, own, *codes)
 
 
-def targets_kernel(where_ref, blend, stats, stats_other, sum_own, sum_other, gram_own, gram_other, weights, own_ref, other_ref, *rest, cut, width):
+def targets_kernel(where_ref, blend, stats, stats_other, sum_own, sum_other, gram_own, gram_other, weight_own, weight_other, own_ref, other_ref, *rest, cut, width):
     patches, columns = own_ref.shape
     cols = slice(cut * columns, (cut + 1) * columns)
-    rows = weights.shape[0] // 2
-    mine, theirs = weights[:rows, cols], weights[rows:, cols]
+    there = pl.ds(pl.multiple_of(where_ref[0] * (width // 2) + cut * columns, columns), columns)
+    mine, theirs = weight_own[:, there], weight_other[:, there]
     grad = contract_rows(
         jnp.concatenate([gram_own[...], gram_other[...]], axis=0),
         jnp.concatenate([mine, mine, theirs, theirs], axis=0),
@@ -354,7 +354,7 @@
     kernel = functools.partial(targets_kernel, cut=j, width=2 * blend.shape[1])
     scratch = [pltpu.VMEM((dec, columns), jnp.float32)] if coded else []
     return call(kernel, shapes, "targets", scratch)(
-        where, blend, stats, stats_other, sum_own, sum_other, *grams, weights
+        where, blend, stats, stats_other, sum_own, sum_other, *grams, *weights
     )
 
 
@@ -406,7 +406,7 @@
     else:
         gram_all, sum_own = gram(where, decoder_hidden, kept_index[0], None)
     out_piece = cut(where, after(out_weight, sum_own), swap(out_weight, CORE))
-    pred_piece = cut(where, pred_weight, pred_other)
+    weights = [pred_weight, pred_other]
 
     def attend(*anchors):
         q = after(queries, *anchors) if anchors else queries
@@ -423,7 +423,7 @@
         own, *codes = second_step(where, after(keep, z2), swap(send, NEXT_Y))
         y3 = swap(after(z3, y1, own), NEXT_Y)
         out_pieces = [out_piece, y0, z1, y1, z2, y2, z3, y3]
-        mixed_own, *bundle = attend(z3, pred_piece)
+        mixed_own, *bundle = attend(z3)
         others = [swap(b, CORE) for b in bundle]
         codes = [swap(c, NEXT_Z * (m + 1)) for m, c in enumerate(codes)]
         (gram_rows,) = last_step(where, after(own, y2), codes)
@@ -445,7 +445,7 @@
 
     def term(part, coded, *before):
         return targets_and_term(
-            where, blend, stats, after(stats_other, *before), sum_own, sum_other, grams, pred_piece, part, coded
+            where, blend, stats, after(stats_other, *before), sum_own, sum_other, grams, weights, part, coded
         )
 
     if not by_pairs:

time: 84.5 us -> 84.5 us (level)
    pallas_call x16 -> x15, Pallas kernels: 20.6 us -> 20.1 us  [run(): pl.pallas_call(kernel, out_shape=tuple(out_shape), in_specs=[pl.BlockSpec...]
where the time goes in v10:
time: 84.5 us; the launch traced here: 84.3 us
  starting transfers between devices  31.3 us (37%)
  waiting for transfers between devices  26.1 us (31%)
  Pallas kernels  20.1 us (24%)
  other arithmetic  3.3 us (4%)
  local copies, waits for them, and re-layouts  2.6 us (3%)
  between operations  0.89 us (1%)
    ppermute x32, starting transfers between devices, swap(): return lax.ppermute(x, AXES, pairs)  31.3 us
    ppermute x32, waiting for transfers between devices, swap(): return lax.ppermute(x, AXES, pairs)  26.1 us
    pallas_call x15, Pallas kernels, run(): pl.pallas_call(kernel, out_shape=tuple(out_shape), in_specs=[pl.BlockSpec...  20.1 us
    select_n x2, other arithmetic, side_by_side(): jnp.where(core == 0, jnp.concatenate(mine + theirs, axis=1), jnp.concaten...  3.22 us
    unnamed x18, local copies, waits for them, and re-layouts  2.6 us
  transfers between devices with their start and end apart: 32, of which 13 were waited for; matrix products, arithmetic and copies ran while one was open for 3% of the time, Pallas kernels for 22%

profile of v10, /device:TPU:0, one launch (start us, length us, event | category | flops | bytes accessed | tf_op | source)
XLA Modules:
  0.0 84.3 jit_solution(15648688749936569163)
XLA Ops:
  0.6 0.5 collective-permute-start.3
  1.1 0.1 collective-permute-start
  1.2 0.1 pad_add_fusion.where_ref
  1.3 1.9 %copy-done.2 = bf16[1,8,256,768]{3,2,1,0:T(8,128)(2,1)S(1)} copy-done((bf16[1,8,256,768]{3,2,1,0:T(8,128)(2,1)S(1)}, bf16[1,8,256,768]{3,2,1,0:T(8,128)(2,1)}, u32[]{:S(2)}) %copy-start.2) | copy-done | bytes 3145752
  3.2 0.7 copy-done.8
  3.9 3.3 %gram.1 = (f32[384,768]{1,0:T(8,128)S(1)}, f32[192,768]{1,0:T(8,128)S(1)}, f32[192,768]{1,0:T(8,128)S(1)}, bf16[256,768]{1,0:T(8,128)(2,1)S(1)}) custom-call(s32[2]{0:T(128)S(1)} %pad_add_fusion.where_ref, bf16[1,8,256,768]{3,2,1,0:T(8,128)(2,1)S(1)} %copy-done.2, s32[8,64]{1,0:T(8,128)S(1)} %bitcast.21), custom_call_target="tpu_custom_call" | custom-call | flops 1000 | bytes 1000 | tf_op jit(solution)/shard_map/gram/pallas_call | solution.py:25
  7.2 0.5 collective-permute-start.4
  7.7 0.1 collective-permute-start.5
  7.8 0.6 cut.1.rest_4_
  8.3 3.0 %collective-permute-start.2 = (bf16[192,768]{1,0:T(8,128)(2,1)S(1)}, bf16[192,768]{1,0:T(8,128)(2,1)S(1)}, u32[]{:S(2)}, u32[]{:S(2)}) collective-permute-start(bf16[192,768]{1,0:T(8,128)(2,1)S(1)} %cut.1.rest_4_), channel_id=1, source_target_pairs={{0,2},{1,3},{2,0},{3,1},{4,6},{5,7},{6,4},{7,5},{8,10},{9,11},{10,... | collective-permute-start | bytes 884744 | tf_op jit(solution)/shard_map/ppermute | solution.py:391
  11.3 1.6 %collective-permute-start.16 = (bf16[192,768]{1,0:T(8,128)(2,1)S(1)}, bf16[192,768]{1,0:T(8,128)(2,1)S(1)}, u32[]{:S(2)}, u32[]{:S(2)}) collective-permute-start(bf16[192,768]{1,0:T(8,128)(2,1)S(1)} %cut.1.rest_4_), channel_id=1, source_target_pairs={{0,4},{1,5},{2,6},{3,7},{4,0},{5,1},{6,2},{7,3},{8,12},{9,13},{10,... | collective-permute-start | bytes 884744 | tf_op jit(solution)/shard_map/ppermute | solution.py:391
  12.9 2.6 %collective-permute-start.1 = (bf16[192,768]{1,0:T(8,128)(2,1)S(1)}, bf16[192,768]{1,0:T(8,128)(2,1)S(1)}, u32[]{:S(2)}, u32[]{:S(2)}) collective-permute-start(bf16[192,768]{1,0:T(8,128)(2,1)S(1)} %cut.1.rest_4_), channel_id=1, source_target_pairs={{0,8},{1,9},{2,10},{3,11},{4,12},{5,13},{6,14},{7,15},{8,0},{9,1},... | collective-permute-start | bytes 884744 | tf_op jit(solution)/shard_map/ppermute | solution.py:391
  15.5 3.1 %collective-permute-done.2.rest_5_ = bf16[192,768]{1,0:T(8,128)(2,1)S(1)} collective-permute-done((bf16[192,768]{1,0:T(8,128)(2,1)S(1)}, bf16[192,768]{1,0:T(8,128)(2,1)S(1)}, u32[]{:S(2)}, u32[]{:S(2)}) %collective-permute-start.2) | collective-permute-done | bytes 294944 | tf_op jit(solution)/shard_map/ppermute | solution.py:391
  18.6 0.9 %first_step.1 = (s16[208,768]{1,0:T(8,128)(2,1)S(1)}, f32[192,768]{1,0:T(8,128)S(1)}) custom-call(s32[2]{0:T(128)S(1)} %pad_add_fusion.where_ref, f32[384,768]{1,0:T(8,128)S(1)} %get-tuple-element.54.mine, f32[192,768]{1,0:T(8,128)S(1)} %collective-permute-done.4.t0, f32[192,768]{1,0:T(8,128)S(1)} %collective-permute-done.5.t1), custom_call_target="tpu_custom_call" | custom-call | flops 1000 | bytes 1000 | tf_op jit(solution)/shard_map/first_step/pallas_call | solution.py:25
  19.5 1.8 %collective-permute-start.7 = (s16[208,768]{1,0:T(8,128)(2,1)S(1)}, s16[208,768]{1,0:T(8,128)(2,1)S(1)}, u32[]{:S(2)}, u32[]{:S(2)}) collective-permute-start(s16[208,768]{1,0:T(8,128)(2,1)S(1)} %get-tuple-element.59), channel_id=1, source_target_pairs={{0,2},{1,3},{2,0},{3,1},{4,6},{5,7},{6,4},{7,5},{8,10},{9,11},{10,... | collective-permute-start | bytes 958472 | tf_op jit(solution)/shard_map/ppermute | solution.py:391
  21.4 4.9 %collective-permute-done.16.rest_6_ = bf16[192,768]{1,0:T(8,128)(2,1)S(1)} collective-permute-done((bf16[192,768]{1,0:T(8,128)(2,1)S(1)}, bf16[192,768]{1,0:T(8,128)(2,1)S(1)}, u32[]{:S(2)}, u32[]{:S(2)}) %collective-permute-start.16) | collective-permute-done | bytes 294944 | tf_op jit(solution)/shard_map/ppermute | solution.py:391
  26.3 0.4 collective-permute-start.17
  26.6 2.0 %collective-permute-done.1.rest_8_ = bf16[192,768]{1,0:T(8,128)(2,1)S(1)} collective-permute-done((bf16[192,768]{1,0:T(8,128)(2,1)S(1)}, bf16[192,768]{1,0:T(8,128)(2,1)S(1)}, u32[]{:S(2)}, u32[]{:S(2)}) %collective-permute-start.1) | collective-permute-done | bytes 294944 | tf_op jit(solution)/shard_map/ppermute | solution.py:391
  28.6 0.5 collective-permute-start.6
  29.1 0.5 collective-permute-start.8
  29.6 0.8 second_step.1
  30.4 3.4 %collective-permute-start.10 = (s16[64,768]{1,0:T(8,128)(2,1)S(1)}, s16[64,768]{1,0:T(8,128)(2,1)S(1)}, u32[]{:S(2)}, u32[]{:S(2)}) collective-permute-start(s16[64,768]{1,0:T(8,128)(2,1)S(1)} %get-tuple-element.69), channel_id=1, source_target_pairs={{0,8},{1,9},{2,10},{3,11},{4,12},{5,13},{6,14},{7,15},{8,0},{9,1},... | collective-permute-start | bytes 294920 | tf_op jit(solution)/shard_map/ppermute | solution.py:391
  33.8 1.3 %collective-permute-start.11 = (s16[64,768]{1,0:T(8,128)(2,1)S(1)}, s16[64,768]{1,0:T(8,128)(2,1)S(1)}, u32[]{:S(2)}, u32[]{:S(2)}) collective-permute-start(s16[64,768]{1,0:T(8,128)(2,1)S(1)} %get-tuple-element.70), channel_id=1, source_target_pairs={{0,12},{1,13},{2,14},{3,15},{4,8},{5,9},{6,10},{7,11},{8,4},{9,5},... | collective-permute-start | bytes 294920 | tf_op jit(solution)/shard_map/ppermute | solution.py:391
  35.1 1.1 %collective-permute-done.17.rest_7_ = bf16[192,768]{1,0:T(8,128)(2,1)S(1)} collective-permute-done((bf16[192,768]{1,0:T(8,128)(2,1)S(1)}, bf16[192,768]{1,0:T(8,128)(2,1)S(1)}, u32[]{:S(2)}, u32[]{:S(2)}) %collective-permute-start.17) | collective-permute-done | bytes 294944 | tf_op jit(solution)/shard_map/ppermute | solution.py:391
  36.2 2.0 %collective-permute-start.9 = (s16[64,768]{1,0:T(8,128)(2,1)S(1)}, s16[64,768]{1,0:T(8,128)(2,1)S(1)}, u32[]{:S(2)}, u32[]{:S(2)}) collective-permute-start(s16[64,768]{1,0:T(8,128)(2,1)S(1)} %get-tuple-element.68), channel_id=1, source_target_pairs={{0,4},{1,5},{2,6},{3,7},{4,0},{5,1},{6,2},{7,3},{8,12},{9,13},{10,... | collective-permute-start | bytes 294920 | tf_op jit(solution)/shard_map/ppermute | solution.py:391
  38.2 1.0 %collective-permute-done.6.rest_10_ = bf16[192,768]{1,0:T(8,128)(2,1)S(1)} collective-permute-done((bf16[192,768]{1,0:T(8,128)(2,1)S(1)}, bf16[192,768]{1,0:T(8,128)(2,1)S(1)}, u32[]{:S(2)}, u32[]{:S(2)}) %collective-permute-start.6) | collective-permute-done | bytes 294944 | tf_op jit(solution)/shard_map/ppermute | solution.py:391
  39.2 0.5 collective-permute-start.18
  39.7 3.5 %attention.1 = (bf16[256,1536]{1,0:T(8,128)(2,1)S(1)}, bf16[256,768]{1,0:T(8,128)(2,1)S(1)}, bf16[256,768]{1,0:T(8,128)(2,1)S(1)}, bf16[256,768]{1,0:T(8,128)(2,1)S(1)}, bf16[256,768]{1,0:T(8,128)(2,1)S(1)}) custom-call(s32[2]{0:T(128)S(1)} %pad_add_fusion.where_ref, bf16[256,1536]{1,0:T(8,128)(2,1)S(1)} %bitcast.16, bf16[256,1536]{1,0:T(8,128)(2,1)S(1)} %bitcast.17, ...), custom_call_target="tpu_custom_call" | custom-call | flops 1000 | bytes 1000 | tf_op jit(solution)/shard_map/attention/pallas_call | solution.py:25
  43.2 0.1 collective-permute-start.12
  43.3 0.5 collective-permute-start.13
  43.8 0.1 collective-permute-start.14
  43.9 0.4 collective-permute-start.15
  44.3 3.2 %collective-permute-done.18.rest_11_ = bf16[192,768]{1,0:T(8,128)(2,1)S(1)} collective-permute-done((bf16[192,768]{1,0:T(8,128)(2,1)S(1)}, bf16[192,768]{1,0:T(8,128)(2,1)S(1)}, u32[]{:S(2)}, u32[]{:S(2)}) %collective-permute-start.18) | collective-permute-done | bytes 294944 | tf_op jit(solution)/shard_map/ppermute | solution.py:391
  47.6 0.6 last_step.3.gram_own
  48.2 0.0 copy-start.6
  48.3 2.8 %branch.1 = (f32[512,768]{1,0:T(8,128)S(1)}, f32[512,128]{1,0:T(8,128)S(1)}) custom-call(s32[2]{0:T(128)S(1)} %pad_add_fusion.where_ref, bf16[256,1536]{1,0:T(8,128)(2,1)S(1)} %get-tuple-element.71.mixed_own, bf16[256,1536]{1,0:T(8,128)(2,1)S(1)} %bitcast.13, bf16[256,1536]{1,0:T(8,128)(2,1)S(1)} %bitcast.15, ...), custom_call_target="tpu_custom_call" | custom-call | flops 1000 | bytes 1000 | tf_op jit(solution)/shard_map/branch/pallas_call | solution.py:25
  51.0 0.6 collective-permute-start.19
  51.6 0.1 collective-permute-start.21
  51.7 1.1 %collective-permute-done.19.stats_other = f32[512,128]{1,0:T(8,128)S(1)} collective-permute-done((f32[512,128]{1,0:T(8,128)S(1)}, f32[512,128]{1,0:T(8,128)S(1)}, u32[]{:S(2)}, u32[]{:S(2)}) %collective-permute-start.19) | collective-permute-done | bytes 262176 | tf_op jit(solution)/shard_map/ppermute | solution.py:391
  52.8 0.2 collective-permute-done.21.gram_other
  53.0 1.9 %targets.2 = (f32[256,384]{1,0:T(8,128)S(1)}, f32[256,384]{1,0:T(8,128)S(1)}, s16[400,384]{1,0:T(8,128)(2,1)S(1)}, f32[384,384]{1,0:T(8,128)S(1)}) custom-call(s32[2]{0:T(128)S(1)} %pad_add_fusion.where_ref, f32[512,768]{1,0:T(8,128)S(1)} %get-tuple-element.77.blend, f32[512,128]{1,0:T(8,128)S(1)} %get-tuple-element.78.stats, ...), custom_call_target="tpu_custom_call" | custom-call | flops 1000 | bytes 1000 | tf_op jit(solution)/shard_map/targets/pallas_call | solution.py:25
  54.9 1.5 %collective-permute-start.24 = (s16[400,384]{1,0:T(8,128)(2,1)S(1)}, s16[400,384]{1,0:T(8,128)(2,1)S(1)}, u32[]{:S(2)}, u32[]{:S(2)}) collective-permute-start(s16[400,384]{1,0:T(8,128)(2,1)S(1)} %get-tuple-element.84), channel_id=1, source_target_pairs={{0,2},{1,3},{2,0},{3,1},{4,6},{5,7},{6,4},{7,5},{8,10},{9,11},{10,... | collective-permute-start | bytes 921608 | tf_op jit(solution)/shard_map/ppermute | solution.py:391
  56.4 1.8 %targets.3 = (f32[256,384]{1,0:T(8,128)S(1)}, f32[256,384]{1,0:T(8,128)S(1)}, s16[400,384]{1,0:T(8,128)(2,1)S(1)}, f32[384,384]{1,0:T(8,128)S(1)}) custom-call(s32[2]{0:T(128)S(1)} %pad_add_fusion.where_ref, f32[512,768]{1,0:T(8,128)S(1)} %get-tuple-element.77.blend, f32[512,128]{1,0:T(8,128)S(1)} %get-tuple-element.78.stats, ...), custom_call_target="tpu_custom_call" | custom-call | flops 1000 | bytes 1000 | tf_op jit(solution)/shard_map/targets/pallas_call | solution.py:25
  58.2 1.6 %collective-permute-start.27 = (s16[400,384]{1,0:T(8,128)(2,1)S(1)}, s16[400,384]{1,0:T(8,128)(2,1)S(1)}, u32[]{:S(2)}, u32[]{:S(2)}) collective-permute-start(s16[400,384]{1,0:T(8,128)(2,1)S(1)} %get-tuple-element.92), channel_id=1, source_target_pairs={{0,4},{1,5},{2,6},{3,7},{4,0},{5,1},{6,2},{7,3},{8,12},{9,13},{10,... | collective-permute-start | bytes 921608 | tf_op jit(solution)/shard_map/ppermute | solution.py:391
  59.8 0.5 collective-permute-start.23
  60.3 4.2 %collective-permute-done.24.codes = s16[400,384]{1,0:T(8,128)(2,1)S(1)} collective-permute-done((s16[400,384]{1,0:T(8,128)(2,1)S(1)}, s16[400,384]{1,0:T(8,128)(2,1)S(1)}, u32[]{:S(2)}, u32[]{:S(2)}) %collective-permute-start.24) | collective-permute-done | bytes 307232 | tf_op jit(solution)/shard_map/ppermute | solution.py:391
  64.5 0.8 next_step.4
  65.3 1.5 %collective-permute-start.25 = (s16[208,384]{1,0:T(8,128)(2,1)S(1)}, s16[208,384]{1,0:T(8,128)(2,1)S(1)}, u32[]{:S(2)}, u32[]{:S(2)}) collective-permute-start(s16[208,384]{1,0:T(8,128)(2,1)S(1)} %get-tuple-element.86), channel_id=1, source_target_pairs={{0,4},{1,5},{2,6},{3,7},{4,0},{5,1},{6,2},{7,3},{8,12},{9,13},{10,... | collective-permute-start | bytes 479240 | tf_op jit(solution)/shard_map/ppermute | solution.py:391
  66.8 0.6 collective-permute-done.27.codes
  67.5 0.8 next_step.6
  68.3 0.9 %collective-permute-start.28 = (s16[208,384]{1,0:T(8,128)(2,1)S(1)}, s16[208,384]{1,0:T(8,128)(2,1)S(1)}, u32[]{:S(2)}, u32[]{:S(2)}) collective-permute-start(s16[208,384]{1,0:T(8,128)(2,1)S(1)} %get-tuple-element.94), channel_id=1, source_target_pairs={{0,2},{1,3},{2,0},{3,1},{4,6},{5,7},{6,4},{7,5},{8,10},{9,11},{10,... | collective-permute-start | bytes 479240 | tf_op jit(solution)/shard_map/ppermute | solution.py:391
  69.2 1.7 %collective-permute-done.25.codes = s16[208,384]{1,0:T(8,128)(2,1)S(1)} collective-permute-done((s16[208,384]{1,0:T(8,128)(2,1)S(1)}, s16[208,384]{1,0:T(8,128)(2,1)S(1)}, u32[]{:S(2)}, u32[]{:S(2)}) %collective-permute-start.25) | collective-permute-done | bytes 159776 | tf_op jit(solution)/shard_map/ppermute | solution.py:391
  70.9 0.6 next_step.5
  71.6 2.6 %collective-permute-start.26 = (s16[112,384]{1,0:T(8,128)(2,1)S(1)}, s16[112,384]{1,0:T(8,128)(2,1)S(1)}, u32[]{:S(2)}, u32[]{:S(2)}) collective-permute-start(s16[112,384]{1,0:T(8,128)(2,1)S(1)} %get-tuple-element.89), channel_id=1, source_target_pairs={{0,8},{1,9},{2,10},{3,11},{4,12},{5,13},{6,14},{7,15},{8,0},{9,1},... | collective-permute-start | bytes 258056 | tf_op jit(solution)/shard_map/ppermute | solution.py:391
  74.2 0.6 next_step.7
  74.8 2.1 %collective-permute-start.29 = (s16[112,384]{1,0:T(8,128)(2,1)S(1)}, s16[112,384]{1,0:T(8,128)(2,1)S(1)}, u32[]{:S(2)}, u32[]{:S(2)}) collective-permute-start(s16[112,384]{1,0:T(8,128)(2,1)S(1)} %get-tuple-element.96), channel_id=1, source_target_pairs={{0,8},{1,9},{2,10},{3,11},{4,12},{5,13},{6,14},{7,15},{8,0},{9,1},... | collective-permute-start | bytes 258056 | tf_op jit(solution)/shard_map/ppermute | solution.py:391
  76.9 2.5 %maximum_select_fusion = f32[1,256,1536]{2,1,0:T(8,128)} fusion(f32[1,256,384]{2,1,0:T(8,128)} %bitcast.11, f32[1,256,384]{2,1,0:T(8,128)S(1)} %bitcast.22, f32[1,256,384]{2,1,0:T(8,128)S(1)} %bitcast.20, f32[1,256,384]{2,1,0:T(8,128)S(1)} %bitcast.19, pred[]{:T(512)S(6)} %eq.6), kind=kLoop, calls=%fused_computation | loop fusion | flops 2752512 | bytes 3145729 | tf_op jit(solution)/shard_map/jit(_where)/select_n | solution.py:394
  79.4 0.6 last_step.4
  80.0 0.1 collective-permute-start.30
  80.0 1.6 %collective-permute-done.29.rest_0_ = s16[112,384]{1,0:T(8,128)(2,1)S(1)} collective-permute-done((s16[112,384]{1,0:T(8,128)(2,1)S(1)}, s16[112,384]{1,0:T(8,128)(2,1)S(1)}, u32[]{:S(2)}, u32[]{:S(2)}) %collective-permute-start.29) | collective-permute-done | bytes 86048 | tf_op jit(solution)/shard_map/ppermute | solution.py:391
  81.6 0.6 last_step.5
  82.2 0.1 collective-permute-start.31
  82.3 1.2 %collective-permute-done.31 = f32[48,384]{1,0:T(8,128)S(1)} collective-permute-done((f32[48,384]{1,0:T(8,128)S(1)}, f32[48,384]{1,0:T(8,128)S(1)}, u32[]{:S(2)}, u32[]{:S(2)}) %collective-permute-start.31) | collective-permute-done | bytes 73760 | tf_op jit(solution)/shard_map/ppermute | solution.py:391
  83.5 0.7 maximum_select_fusion.1
  (36 shorter events, 0.1 us)
Async XLA Ops:
  0.6 6.5 %collective-permute-start.3 = (bf16[48,1536]{1,0:T(8,128)(2,1)}, bf16[48,1536]{1,0:T(8,128)(2,1)S(1)}, u32[]{:S(2)}, u32[]{:S(2)}) collective-permute-start(bf16[48,1536]{1,0:T(8,128)(2,1)} %weight_own.3), channel_id=1, source_target_pairs={{0,1},{1,0},{2,3},{3,2},{4,5},{5,4},{6,7},{7,6},{8,9},{9,8},{10,11... | collective-permute-start | bytes 442376 | tf_op jit(solution)/shard_map/ppermute | solution.py:391
  1.1 6.6 %collective-permute-start = (bf16[96,1536]{1,0:T(8,128)(2,1)}, bf16[96,1536]{1,0:T(8,128)(2,1)S(1)}, u32[]{:S(2)}, u32[]{:S(2)}) collective-permute-start(bf16[96,1536]{1,0:T(8,128)(2,1)} %own), channel_id=1, source_target_pairs={{0,1},{1,0},{2,3},{3,2},{4,5},{5,4},{6,7},{7,6},{8,9},{9,8},{10,11... | collective-permute-start | bytes 884744 | tf_op jit(solution)/shard_map/ppermute | solution.py:391
  1.3 1.9 %copy-start.2 = (bf16[1,8,256,768]{3,2,1,0:T(8,128)(2,1)S(1)}, bf16[1,8,256,768]{3,2,1,0:T(8,128)(2,1)}, u32[]{:S(2)}) copy-start(bf16[1,8,256,768]{3,2,1,0:T(8,128)(2,1)} %hidden_ref.1) | copy-start | bytes 9437188
  3.2 0.7 copy-start.8
  3.9 3.9 %copy-start.7 = (bf16[96,1536]{1,0:T(8,128)(2,1)S(1)}, bf16[96,1536]{1,0:T(8,128)(2,1)}, u32[]{:S(2)}) copy-start(bf16[96,1536]{1,0:T(8,128)(2,1)} %own) | copy-start | bytes 884740
  7.2 11.4 %collective-permute-start.4 = (f32[192,768]{1,0:T(8,128)S(1)}, f32[192,768]{1,0:T(8,128)S(1)}, u32[]{:S(2)}, u32[]{:S(2)}) collective-permute-start(f32[192,768]{1,0:T(8,128)S(1)} %get-tuple-element.56), channel_id=1, source_target_pairs={{0,1},{1,0},{2,3},{3,2},{4,5},{5,4},{6,7},{7,6},{8,9},{9,8},{10,11... | collective-permute-start | bytes 1769480 | tf_op jit(solution)/shard_map/ppermute | solution.py:391
  7.7 10.9 %collective-permute-start.5 = (f32[192,768]{1,0:T(8,128)S(1)}, f32[192,768]{1,0:T(8,128)S(1)}, u32[]{:S(2)}, u32[]{:S(2)}) collective-permute-start(f32[192,768]{1,0:T(8,128)S(1)} %get-tuple-element.58), channel_id=1, source_target_pairs={{0,1},{1,0},{2,3},{3,2},{4,5},{5,4},{6,7},{7,6},{8,9},{9,8},{10,11... | collective-permute-start | bytes 1769480 | tf_op jit(solution)/shard_map/ppermute | solution.py:391
  7.8 32.0 %copy-start.5 = (bf16[1,256,1536]{2,1,0:T(8,128)(2,1)S(1)}, bf16[1,256,1536]{2,1,0:T(8,128)(2,1)}, u32[]{:S(2)}) copy-start(bf16[1,256,1536]{2,1,0:T(8,128)(2,1)} %param.11) | copy-start | bytes 2359300
  8.3 10.3 %collective-permute-start.2 = (bf16[192,768]{1,0:T(8,128)(2,1)S(1)}, bf16[192,768]{1,0:T(8,128)(2,1)S(1)}, u32[]{:S(2)}, u32[]{:S(2)}) collective-permute-start(bf16[192,768]{1,0:T(8,128)(2,1)S(1)} %cut.1.rest_4_), channel_id=1, source_target_pairs={{0,2},{1,3},{2,0},{3,1},{4,6},{5,7},{6,4},{7,5},{8,10},{9,11},{10,... | collective-permute-start | bytes 884744 | tf_op jit(solution)/shard_map/ppermute | solution.py:391
  11.3 14.9 %collective-permute-start.16 = (bf16[192,768]{1,0:T(8,128)(2,1)S(1)}, bf16[192,768]{1,0:T(8,128)(2,1)S(1)}, u32[]{:S(2)}, u32[]{:S(2)}) collective-permute-start(bf16[192,768]{1,0:T(8,128)(2,1)S(1)} %cut.1.rest_4_), channel_id=1, source_target_pairs={{0,4},{1,5},{2,6},{3,7},{4,0},{5,1},{6,2},{7,3},{8,12},{9,13},{10,... | collective-permute-start | bytes 884744 | tf_op jit(solution)/shard_map/ppermute | solution.py:391
  12.9 15.7 %collective-permute-start.1 = (bf16[192,768]{1,0:T(8,128)(2,1)S(1)}, bf16[192,768]{1,0:T(8,128)(2,1)S(1)}, u32[]{:S(2)}, u32[]{:S(2)}) collective-permute-start(bf16[192,768]{1,0:T(8,128)(2,1)S(1)} %cut.1.rest_4_), channel_id=1, source_target_pairs={{0,8},{1,9},{2,10},{3,11},{4,12},{5,13},{6,14},{7,15},{8,0},{9,1},... | collective-permute-start | bytes 884744 | tf_op jit(solution)/shard_map/ppermute | solution.py:391
  18.6 21.1 %copy-start = (bf16[1,256,1536]{2,1,0:T(8,128)(2,1)S(1)}, bf16[1,256,1536]{2,1,0:T(8,128)(2,1)}, u32[]{:S(2)}) copy-start(bf16[1,256,1536]{2,1,0:T(8,128)(2,1)} %param.12) | copy-start | bytes 2359300
  18.6 21.1 %copy-start.1 = (bf16[1,256,1536]{2,1,0:T(8,128)(2,1)S(1)}, bf16[1,256,1536]{2,1,0:T(8,128)(2,1)}, u32[]{:S(2)}) copy-start(bf16[1,256,1536]{2,1,0:T(8,128)(2,1)} %param.13) | copy-start | bytes 2359300
  18.6 21.1 %copy-start.3 = (bf16[1,256,1536]{2,1,0:T(8,128)(2,1)S(1)}, bf16[1,256,1536]{2,1,0:T(8,128)(2,1)}, u32[]{:S(2)}) copy-start(bf16[1,256,1536]{2,1,0:T(8,128)(2,1)} %param.9) | copy-start | bytes 2359300
  18.6 21.1 %copy-start.4 = (bf16[1,256,1536]{2,1,0:T(8,128)(2,1)S(1)}, bf16[1,256,1536]{2,1,0:T(8,128)(2,1)}, u32[]{:S(2)}) copy-start(bf16[1,256,1536]{2,1,0:T(8,128)(2,1)} %param.10) | copy-start | bytes 2359300
  19.5 10.0 %collective-permute-start.7 = (s16[208,768]{1,0:T(8,128)(2,1)S(1)}, s16[208,768]{1,0:T(8,128)(2,1)S(1)}, u32[]{:S(2)}, u32[]{:S(2)}) collective-permute-start(s16[208,768]{1,0:T(8,128)(2,1)S(1)} %get-tuple-element.59), channel_id=1, source_target_pairs={{0,2},{1,3},{2,0},{3,1},{4,6},{5,7},{6,4},{7,5},{8,10},{9,11},{10,... | collective-permute-start | bytes 958472 | tf_op jit(solution)/shard_map/ppermute | solution.py:391
  26.3 9.9 %collective-permute-start.17 = (bf16[192,768]{1,0:T(8,128)(2,1)S(1)}, bf16[192,768]{1,0:T(8,128)(2,1)S(1)}, u32[]{:S(2)}, u32[]{:S(2)}) collective-permute-start(bf16[192,768]{1,0:T(8,128)(2,1)S(1)} %collective-permute-done.16.rest_6_), channel_id=1, source_target_pairs={{0,2},{1,3},{2,0},{3,1},{4,6},{5,7},{6,4},{7,5},{8,10},{9,11},{10,... | collective-permute-start | bytes 884744 | tf_op jit(solution)/shard_map/ppermute | solution.py:391
  28.6 10.6 %collective-permute-start.6 = (bf16[192,768]{1,0:T(8,128)(2,1)S(1)}, bf16[192,768]{1,0:T(8,128)(2,1)S(1)}, u32[]{:S(2)}, u32[]{:S(2)}) collective-permute-start(bf16[192,768]{1,0:T(8,128)(2,1)S(1)} %collective-permute-done.1.rest_8_), channel_id=1, source_target_pairs={{0,4},{1,5},{2,6},{3,7},{4,0},{5,1},{6,2},{7,3},{8,12},{9,13},{10,... | collective-permute-start | bytes 884744 | tf_op jit(solution)/shard_map/ppermute | solution.py:391
  29.1 14.2 %collective-permute-start.8 = (bf16[192,768]{1,0:T(8,128)(2,1)S(1)}, bf16[192,768]{1,0:T(8,128)(2,1)S(1)}, u32[]{:S(2)}, u32[]{:S(2)}) collective-permute-start(bf16[192,768]{1,0:T(8,128)(2,1)S(1)} %collective-permute-done.1.rest_8_), channel_id=1, source_target_pairs={{0,2},{1,3},{2,0},{3,1},{4,6},{5,7},{6,4},{7,5},{8,10},{9,11},{10,... | collective-permute-start | bytes 884744 | tf_op jit(solution)/shard_map/ppermute | solution.py:391
  30.4 12.9 %collective-permute-start.10 = (s16[64,768]{1,0:T(8,128)(2,1)S(1)}, s16[64,768]{1,0:T(8,128)(2,1)S(1)}, u32[]{:S(2)}, u32[]{:S(2)}) collective-permute-start(s16[64,768]{1,0:T(8,128)(2,1)S(1)} %get-tuple-element.69), channel_id=1, source_target_pairs={{0,8},{1,9},{2,10},{3,11},{4,12},{5,13},{6,14},{7,15},{8,0},{9,1},... | collective-permute-start | bytes 294920 | tf_op jit(solution)/shard_map/ppermute | solution.py:391
  33.8 10.0 %collective-permute-start.11 = (s16[64,768]{1,0:T(8,128)(2,1)S(1)}, s16[64,768]{1,0:T(8,128)(2,1)S(1)}, u32[]{:S(2)}, u32[]{:S(2)}) collective-permute-start(s16[64,768]{1,0:T(8,128)(2,1)S(1)} %get-tuple-element.70), channel_id=1, source_target_pairs={{0,12},{1,13},{2,14},{3,15},{4,8},{5,9},{6,10},{7,11},{8,4},{9,5},... | collective-permute-start | bytes 294920 | tf_op jit(solution)/shard_map/ppermute | solution.py:391
  36.2 7.7 %collective-permute-start.9 = (s16[64,768]{1,0:T(8,128)(2,1)S(1)}, s16[64,768]{1,0:T(8,128)(2,1)S(1)}, u32[]{:S(2)}, u32[]{:S(2)}) collective-permute-start(s16[64,768]{1,0:T(8,128)(2,1)S(1)} %get-tuple-element.68), channel_id=1, source_target_pairs={{0,4},{1,5},{2,6},{3,7},{4,0},{5,1},{6,2},{7,3},{8,12},{9,13},{10,... | collective-permute-start | bytes 294920 | tf_op jit(solution)/shard_map/ppermute | solution.py:391
  39.2 8.3 %collective-permute-start.18 = (bf16[192,768]{1,0:T(8,128)(2,1)S(1)}, bf16[192,768]{1,0:T(8,128)(2,1)S(1)}, u32[]{:S(2)}, u32[]{:S(2)}) collective-permute-start(bf16[192,768]{1,0:T(8,128)(2,1)S(1)} %collective-permute-done.6.rest_10_), channel_id=1, source_target_pairs={{0,2},{1,3},{2,0},{3,1},{4,6},{5,7},{6,4},{7,5},{8,10},{9,11},{10,... | collective-permute-start | bytes 884744 | tf_op jit(solution)/shard_map/ppermute | solution.py:391
  43.2 5.0 %collective-permute-start.12 = (bf16[256,768]{1,0:T(8,128)(2,1)S(1)}, bf16[256,768]{1,0:T(8,128)(2,1)S(1)}, u32[]{:S(2)}, u32[]{:S(2)}) collective-permute-start(bf16[256,768]{1,0:T(8,128)(2,1)S(1)} %get-tuple-element.72), channel_id=1, source_target_pairs={{0,1},{1,0},{2,3},{3,2},{4,5},{5,4},{6,7},{7,6},{8,9},{9,8},{10,11... | collective-permute-start | bytes 1179656 | tf_op jit(solution)/shard_map/ppermute | solution.py:391
  43.3 4.9 %collective-permute-start.13 = (bf16[256,768]{1,0:T(8,128)(2,1)S(1)}, bf16[256,768]{1,0:T(8,128)(2,1)S(1)}, u32[]{:S(2)}, u32[]{:S(2)}) collective-permute-start(bf16[256,768]{1,0:T(8,128)(2,1)S(1)} %get-tuple-element.73), channel_id=1, source_target_pairs={{0,1},{1,0},{2,3},{3,2},{4,5},{5,4},{6,7},{7,6},{8,9},{9,8},{10,11... | collective-permute-start | bytes 1179656 | tf_op jit(solution)/shard_map/ppermute | solution.py:391
  43.8 4.4 %collective-permute-start.14 = (bf16[256,768]{1,0:T(8,128)(2,1)S(1)}, bf16[256,768]{1,0:T(8,128)(2,1)S(1)}, u32[]{:S(2)}, u32[]{:S(2)}) collective-permute-start(bf16[256,768]{1,0:T(8,128)(2,1)S(1)} %get-tuple-element.74), channel_id=1, source_target_pairs={{0,1},{1,0},{2,3},{3,2},{4,5},{5,4},{6,7},{7,6},{8,9},{9,8},{10,11... | collective-permute-start | bytes 1179656 | tf_op jit(solution)/shard_map/ppermute | solution.py:391
  43.9 4.4 %collective-permute-start.15 = (bf16[256,768]{1,0:T(8,128)(2,1)S(1)}, bf16[256,768]{1,0:T(8,128)(2,1)S(1)}, u32[]{:S(2)}, u32[]{:S(2)}) collective-permute-start(bf16[256,768]{1,0:T(8,128)(2,1)S(1)} %get-tuple-element.75), channel_id=1, source_target_pairs={{0,1},{1,0},{2,3},{3,2},{4,5},{5,4},{6,7},{7,6},{8,9},{9,8},{10,11... | collective-permute-start | bytes 1179656 | tf_op jit(solution)/shard_map/ppermute | solution.py:391
  47.6 5.2 %collective-permute-start.20 = (bf16[256,768]{1,0:T(8,128)(2,1)S(1)}, bf16[256,768]{1,0:T(8,128)(2,1)S(1)}, u32[]{:S(2)}, u32[]{:S(2)}) collective-permute-start(bf16[256,768]{1,0:T(8,128)(2,1)S(1)} %get-tuple-element.51.sum_own), channel_id=1, source_target_pairs={{0,1},{1,0},{2,3},{3,2},{4,5},{5,4},{6,7},{7,6},{8,9},{9,8},{10,11... | collective-permute-start | bytes 1179656 | tf_op jit(solution)/shard_map/ppermute | solution.py:391
  48.2 4.8 %copy-start.6 = (bf16[48,1536]{1,0:T(8,128)(2,1)S(1)}, bf16[48,1536]{1,0:T(8,128)(2,1)}, u32[]{:S(2)}) copy-start(bf16[48,1536]{1,0:T(8,128)(2,1)} %weight_own.3) | copy-start | bytes 442372
  51.0 1.7 %collective-permute-start.19 = (f32[512,128]{1,0:T(8,128)S(1)}, f32[512,128]{1,0:T(8,128)S(1)}, u32[]{:S(2)}, u32[]{:S(2)}) collective-permute-start(f32[512,128]{1,0:T(8,128)S(1)} %get-tuple-element.78.stats), channel_id=1, source_target_pairs={{0,1},{1,0},{2,3},{3,2},{4,5},{5,4},{6,7},{7,6},{8,9},{9,8},{10,11... | collective-permute-start | bytes 786440 | tf_op jit(solution)/shard_map/ppermute | solution.py:391
  51.6 1.4 %collective-permute-start.21 = (bf16[96,768]{1,0:T(8,128)(2,1)S(1)}, bf16[96,768]{1,0:T(8,128)(2,1)S(1)}, u32[]{:S(2)}, u32[]{:S(2)}) collective-permute-start(bf16[96,768]{1,0:T(8,128)(2,1)S(1)} %last_step.3.gram_own), channel_id=1, source_target_pairs={{0,1},{1,0},{2,3},{3,2},{4,5},{5,4},{6,7},{7,6},{8,9},{9,8},{10,11... | collective-permute-start | bytes 442376 | tf_op jit(solution)/shard_map/ppermute | solution.py:391
  54.9 9.6 %collective-permute-start.24 = (s16[400,384]{1,0:T(8,128)(2,1)S(1)}, s16[400,384]{1,0:T(8,128)(2,1)S(1)}, u32[]{:S(2)}, u32[]{:S(2)}) collective-permute-start(s16[400,384]{1,0:T(8,128)(2,1)S(1)} %get-tuple-element.84), channel_id=1, source_target_pairs={{0,2},{1,3},{2,0},{3,1},{4,6},{5,7},{6,4},{7,5},{8,10},{9,11},{10,... | collective-permute-start | bytes 921608 | tf_op jit(solution)/shard_map/ppermute | solution.py:391
  58.2 9.3 %collective-permute-start.27 = (s16[400,384]{1,0:T(8,128)(2,1)S(1)}, s16[400,384]{1,0:T(8,128)(2,1)S(1)}, u32[]{:S(2)}, u32[]{:S(2)}) collective-permute-start(s16[400,384]{1,0:T(8,128)(2,1)S(1)} %get-tuple-element.92), channel_id=1, source_target_pairs={{0,4},{1,5},{2,6},{3,7},{4,0},{5,1},{6,2},{7,3},{8,12},{9,13},{10,... | collective-permute-start | bytes 921608 | tf_op jit(solution)/shard_map/ppermute | solution.py:391
  59.8 17.1 %collective-permute-start.22 = (f32[256,384]{1,0:T(8,128)S(1)}, f32[256,384]{1,0:T(8,128)S(1)}, u32[]{:S(2)}, u32[]{:S(2)}) collective-permute-start(f32[256,384]{1,0:T(8,128)S(1)} %get-tuple-element.81), channel_id=1, source_target_pairs={{0,1},{1,0},{2,3},{3,2},{4,5},{5,4},{6,7},{7,6},{8,9},{9,8},{10,11... | collective-permute-start | bytes 1179656 | tf_op jit(solution)/shard_map/ppermute | solution.py:391
  59.8 17.1 %collective-permute-start.23 = (f32[256,384]{1,0:T(8,128)S(1)}, f32[256,384]{1,0:T(8,128)}, u32[]{:S(2)}, u32[]{:S(2)}) collective-permute-start(f32[256,384]{1,0:T(8,128)S(1)} %get-tuple-element.82), channel_id=1, source_target_pairs={{0,1},{1,0},{2,3},{3,2},{4,5},{5,4},{6,7},{7,6},{8,9},{9,8},{10,11... | collective-permute-start | bytes 1179656 | tf_op jit(solution)/shard_map/ppermute | solution.py:391
  65.3 5.6 %collective-permute-start.25 = (s16[208,384]{1,0:T(8,128)(2,1)S(1)}, s16[208,384]{1,0:T(8,128)(2,1)S(1)}, u32[]{:S(2)}, u32[]{:S(2)}) collective-permute-start(s16[208,384]{1,0:T(8,128)(2,1)S(1)} %get-tuple-element.86), channel_id=1, source_target_pairs={{0,4},{1,5},{2,6},{3,7},{4,0},{5,1},{6,2},{7,3},{8,12},{9,13},{10,... | collective-permute-start | bytes 479240 | tf_op jit(solution)/shard_map/ppermute | solution.py:391
  68.3 5.9 %collective-permute-start.28 = (s16[208,384]{1,0:T(8,128)(2,1)S(1)}, s16[208,384]{1,0:T(8,128)(2,1)S(1)}, u32[]{:S(2)}, u32[]{:S(2)}) collective-permute-start(s16[208,384]{1,0:T(8,128)(2,1)S(1)} %get-tuple-element.94), channel_id=1, source_target_pairs={{0,2},{1,3},{2,0},{3,1},{4,6},{5,7},{6,4},{7,5},{8,10},{9,11},{10,... | collective-permute-start | bytes 479240 | tf_op jit(solution)/shard_map/ppermute | solution.py:391
  71.6 7.8 %collective-permute-start.26 = (s16[112,384]{1,0:T(8,128)(2,1)S(1)}, s16[112,384]{1,0:T(8,128)(2,1)S(1)}, u32[]{:S(2)}, u32[]{:S(2)}) collective-permute-start(s16[112,384]{1,0:T(8,128)(2,1)S(1)} %get-tuple-element.89), channel_id=1, source_target_pairs={{0,8},{1,9},{2,10},{3,11},{4,12},{5,13},{6,14},{7,15},{8,0},{9,1},... | collective-permute-start | bytes 258056 | tf_op jit(solution)/shard_map/ppermute | solution.py:391
  74.8 6.8 %collective-permute-start.29 = (s16[112,384]{1,0:T(8,128)(2,1)S(1)}, s16[112,384]{1,0:T(8,128)(2,1)S(1)}, u32[]{:S(2)}, u32[]{:S(2)}) collective-permute-start(s16[112,384]{1,0:T(8,128)(2,1)S(1)} %get-tuple-element.96), channel_id=1, source_target_pairs={{0,8},{1,9},{2,10},{3,11},{4,12},{5,13},{6,14},{7,15},{8,0},{9,1},... | collective-permute-start | bytes 258056 | tf_op jit(solution)/shard_map/ppermute | solution.py:391
  80.0 2.3 %collective-permute-start.30 = (f32[48,384]{1,0:T(8,128)S(1)}, f32[48,384]{1,0:T(8,128)S(1)}, u32[]{:S(2)}, u32[]{:S(2)}) collective-permute-start(f32[48,384]{1,0:T(8,128)S(1)} %get-tuple-element.98), channel_id=1, source_target_pairs={{0,1},{1,0},{2,3},{3,2},{4,5},{5,4},{6,7},{7,6},{8,9},{9,8},{10,11... | collective-permute-start | bytes 221192 | tf_op jit(solution)/shard_map/ppermute | solution.py:391
  82.2 1.3 %collective-permute-start.31 = (f32[48,384]{1,0:T(8,128)S(1)}, f32[48,384]{1,0:T(8,128)S(1)}, u32[]{:S(2)}, u32[]{:S(2)}) collective-permute-start(f32[48,384]{1,0:T(8,128)S(1)} %get-tuple-element.99), channel_id=1, source_target_pairs={{0,1},{1,0},{2,3},{3,2},{4,5},{5,4},{6,7},{7,6},{8,9},{9,8},{10,11... | collective-permute-start | bytes 221192 | tf_op jit(solution)/shard_map/ppermute | solution.py:391

commit v11 on v10

--- a/solution.py
+++ b/solution.py
@@ -401,7 +401,7 @@
     pred_other = swap(pred_weight, CORE)
     if by_pairs:
         gram_mine, *gram_theirs, sum_own = gram(
-            where, decoder_hidden, kept_index[0], (chips, dec // parts)
+            where, decoder_hidden, jnp.maximum(kept_index[0], 0), (chips, dec // parts)
         )
     else:
         gram_all, sum_own = gram(where, decoder_hidden, kept_index[0], None)
@@ -427,7 +427,7 @@
         others = [swap(b, CORE) for b in bundle]
         codes = [swap(c, NEXT_Z * (m + 1)) for m, c in enumerate(codes)]
         (gram_rows,) = last_step(where, after(own, y2), codes)
-        mixed_own = after(mixed_own, gram_rows)
+        mixed_own = after(mixed_own, *codes)
     else:
         got = lax.all_gather(out_piece, "dp", axis_index_groups=same_core).reshape(chips, 2, rows, half)
         out_pieces = [jnp.where(core == 0, got, got[:, ::-1]).reshape(width, half)]

time: 84.5 us -> 84.2 us (level)
  waiting for transfers between devices: 26.1 us -> 24 us
  starting transfers between devices: 31.3 us -> 33.3 us
    ppermute x32, waiting for transfers between devices: 26.1 us -> 24 us  [swap(): return lax.ppermute(x, AXES, pairs)]
    ppermute x32, starting transfers between devices: 31.3 us -> 33.3 us  [swap(): return lax.ppermute(x, AXES, pairs)]
    unnamed x18 -> x16, local copies, waits for them, and re-layouts: 2.6 us -> 1.91 us
  transfers between devices with their start and end apart: 32 -> 32, of which waited for: 13 -> 13; matrix products, arithmetic and copies ran while one was open for 3% -> 4% of each run, Pallas kernels for 22% -> 22%
where the time goes in v11:
time: 84.2 us; the launch traced here: 84 us
  starting transfers between devices  33.3 us (40%)
  waiting for transfers between devices  24 us (29%)
  Pallas kernels  20 us (24%)
  other arithmetic  3.99 us (5%)
  local copies, waits for them, and re-layouts  1.91 us (2%)
  between operations  0.87 us (1%)
    ppermute x32, starting transfers between devices, swap(): return lax.ppermute(x, AXES, pairs)  33.3 us
    ppermute x32, waiting for transfers between devices, swap(): return lax.ppermute(x, AXES, pairs)  24 us
    pallas_call x15, Pallas kernels, run(): pl.pallas_call(kernel, out_shape=tuple(out_shape), in_specs=[pl.BlockSpec...  20 us
    select_n x2, other arithmetic, side_by_side(): jnp.where(core == 0, jnp.concatenate(mine + theirs, axis=1), jnp.concaten...  3.22 us
    unnamed x16, local copies, waits for them, and re-layouts  1.91 us
  transfers between devices with their start and end apart: 32, of which 13 were waited for; matrix products, arithmetic and copies ran while one was open for 4% of the time, Pallas kernels for 22%

profile of v11, /device:TPU:0, one launch (start us, length us, event | category | flops | bytes accessed | tf_op | source)
XLA Modules:
  0.0 84.0 jit_solution(13197668911730035956)
XLA Ops:
  0.6 0.5 collective-permute-start
  1.1 0.1 collective-permute-start.3
  1.2 0.7 maximum_bitcast_fusion.kept_ref
  1.9 0.1 pad_add_fusion.where_ref
  2.0 1.9 %copy-done.2 = bf16[1,8,256,768]{3,2,1,0:T(8,128)(2,1)S(1)} copy-done((bf16[1,8,256,768]{3,2,1,0:T(8,128)(2,1)S(1)}, bf16[1,8,256,768]{3,2,1,0:T(8,128)(2,1)}, u32[]{:S(2)}) %copy-start.2) | copy-done | bytes 3145752
  3.9 3.3 %gram.1 = (f32[384,768]{1,0:T(8,128)S(1)}, f32[192,768]{1,0:T(8,128)S(1)}, f32[192,768]{1,0:T(8,128)S(1)}, bf16[256,768]{1,0:T(8,128)(2,1)S(1)}) custom-call(s32[2]{0:T(128)S(1)} %pad_add_fusion.where_ref, bf16[1,8,256,768]{3,2,1,0:T(8,128)(2,1)S(1)} %copy-done.2, s32[8,64]{1,0:T(8,128)S(1)} %maximum_bitcast_fusion.kept_ref), custom_call_target="tpu_custom_call" | custom-call | flops 1000 | bytes 1000 | tf_op jit(solution)/shard_map/gram/pallas_call | solution.py:25
  7.2 0.5 collective-permute-start.4
  7.7 0.1 collective-permute-start.5
  7.8 0.0 collective-permute-done.other
  7.8 0.6 cut.1.rest_4_
  8.3 3.0 %collective-permute-start.2 = (bf16[192,768]{1,0:T(8,128)(2,1)S(1)}, bf16[192,768]{1,0:T(8,128)(2,1)S(1)}, u32[]{:S(2)}, u32[]{:S(2)}) collective-permute-start(bf16[192,768]{1,0:T(8,128)(2,1)S(1)} %cut.1.rest_4_), channel_id=1, source_target_pairs={{0,2},{1,3},{2,0},{3,1},{4,6},{5,7},{6,4},{7,5},{8,10},{9,11},{10,... | collective-permute-start | bytes 884744 | tf_op jit(solution)/shard_map/ppermute | solution.py:391
  11.3 1.6 %collective-permute-start.15 = (bf16[192,768]{1,0:T(8,128)(2,1)S(1)}, bf16[192,768]{1,0:T(8,128)(2,1)S(1)}, u32[]{:S(2)}, u32[]{:S(2)}) collective-permute-start(bf16[192,768]{1,0:T(8,128)(2,1)S(1)} %cut.1.rest_4_), channel_id=1, source_target_pairs={{0,4},{1,5},{2,6},{3,7},{4,0},{5,1},{6,2},{7,3},{8,12},{9,13},{10,... | collective-permute-start | bytes 884744 | tf_op jit(solution)/shard_map/ppermute | solution.py:391
  12.9 2.6 %collective-permute-start.1 = (bf16[192,768]{1,0:T(8,128)(2,1)S(1)}, bf16[192,768]{1,0:T(8,128)(2,1)S(1)}, u32[]{:S(2)}, u32[]{:S(2)}) collective-permute-start(bf16[192,768]{1,0:T(8,128)(2,1)S(1)} %cut.1.rest_4_), channel_id=1, source_target_pairs={{0,8},{1,9},{2,10},{3,11},{4,12},{5,13},{6,14},{7,15},{8,0},{9,1},... | collective-permute-start | bytes 884744 | tf_op jit(solution)/shard_map/ppermute | solution.py:391
  15.5 3.1 %collective-permute-done.2.rest_5_ = bf16[192,768]{1,0:T(8,128)(2,1)S(1)} collective-permute-done((bf16[192,768]{1,0:T(8,128)(2,1)S(1)}, bf16[192,768]{1,0:T(8,128)(2,1)S(1)}, u32[]{:S(2)}, u32[]{:S(2)}) %collective-permute-start.2) | collective-permute-done | bytes 294944 | tf_op jit(solution)/shard_map/ppermute | solution.py:391
  18.6 0.0 collective-permute-done.4.t0
  18.6 0.9 %first_step.1 = (s16[208,768]{1,0:T(8,128)(2,1)S(1)}, f32[192,768]{1,0:T(8,128)S(1)}) custom-call(s32[2]{0:T(128)S(1)} %pad_add_fusion.where_ref, f32[384,768]{1,0:T(8,128)S(1)} %get-tuple-element.54.mine, f32[192,768]{1,0:T(8,128)S(1)} %collective-permute-done.4.t0, f32[192,768]{1,0:T(8,128)S(1)} %collective-permute-done.5.t1), custom_call_target="tpu_custom_call" | custom-call | flops 1000 | bytes 1000 | tf_op jit(solution)/shard_map/first_step/pallas_call | solution.py:25
  19.5 1.8 %collective-permute-start.7 = (s16[208,768]{1,0:T(8,128)(2,1)S(1)}, s16[208,768]{1,0:T(8,128)(2,1)S(1)}, u32[]{:S(2)}, u32[]{:S(2)}) collective-permute-start(s16[208,768]{1,0:T(8,128)(2,1)S(1)} %get-tuple-element.59), channel_id=1, source_target_pairs={{0,2},{1,3},{2,0},{3,1},{4,6},{5,7},{6,4},{7,5},{8,10},{9,11},{10,... | collective-permute-start | bytes 958472 | tf_op jit(solution)/shard_map/ppermute | solution.py:391
  21.4 4.9 %collective-permute-done.15.rest_6_ = bf16[192,768]{1,0:T(8,128)(2,1)S(1)} collective-permute-done((bf16[192,768]{1,0:T(8,128)(2,1)S(1)}, bf16[192,768]{1,0:T(8,128)(2,1)S(1)}, u32[]{:S(2)}, u32[]{:S(2)}) %collective-permute-start.15) | collective-permute-done | bytes 294944 | tf_op jit(solution)/shard_map/ppermute | solution.py:391
  26.3 0.4 collective-permute-start.16
  26.6 2.0 %collective-permute-done.1.rest_8_ = bf16[192,768]{1,0:T(8,128)(2,1)S(1)} collective-permute-done((bf16[192,768]{1,0:T(8,128)(2,1)S(1)}, bf16[192,768]{1,0:T(8,128)(2,1)S(1)}, u32[]{:S(2)}, u32[]{:S(2)}) %collective-permute-start.1) | collective-permute-done | bytes 294944 | tf_op jit(solution)/shard_map/ppermute | solution.py:391
  28.6 0.4 collective-permute-start.6
  29.1 0.5 collective-permute-start.17
  29.6 0.8 second_step.1
  30.4 4.4 %collective-permute-start.10 = (s16[64,768]{1,0:T(8,128)(2,1)S(1)}, s16[64,768]{1,0:T(8,128)(2,1)S(1)}, u32[]{:S(2)}, u32[]{:S(2)}) collective-permute-start(s16[64,768]{1,0:T(8,128)(2,1)S(1)} %get-tuple-element.67), channel_id=1, source_target_pairs={{0,12},{1,13},{2,14},{3,15},{4,8},{5,9},{6,10},{7,11},{8,4},{9,5},... | collective-permute-start | bytes 294920 | tf_op jit(solution)/shard_map/ppermute | solution.py:391
  34.8 1.4 %collective-permute-done.16.rest_7_ = bf16[192,768]{1,0:T(8,128)(2,1)S(1)} collective-permute-done((bf16[192,768]{1,0:T(8,128)(2,1)S(1)}, bf16[192,768]{1,0:T(8,128)(2,1)S(1)}, u32[]{:S(2)}, u32[]{:S(2)}) %collective-permute-start.16) | collective-permute-done | bytes 294944 | tf_op jit(solution)/shard_map/ppermute | solution.py:391
  36.2 3.0 %collective-permute-start.9 = (s16[64,768]{1,0:T(8,128)(2,1)S(1)}, s16[64,768]{1,0:T(8,128)(2,1)S(1)}, u32[]{:S(2)}, u32[]{:S(2)}) collective-permute-start(s16[64,768]{1,0:T(8,128)(2,1)S(1)} %get-tuple-element.66), channel_id=1, source_target_pairs={{0,8},{1,9},{2,10},{3,11},{4,12},{5,13},{6,14},{7,15},{8,0},{9,1},... | collective-permute-start | bytes 294920 | tf_op jit(solution)/shard_map/ppermute | solution.py:391
  39.2 1.5 %collective-permute-start.18 = (bf16[192,768]{1,0:T(8,128)(2,1)S(1)}, bf16[192,768]{1,0:T(8,128)(2,1)S(1)}, u32[]{:S(2)}, u32[]{:S(2)}) collective-permute-start(bf16[192,768]{1,0:T(8,128)(2,1)S(1)} %collective-permute-done.6.rest_10_), channel_id=1, source_target_pairs={{0,2},{1,3},{2,0},{3,1},{4,6},{5,7},{6,4},{7,5},{8,10},{9,11},{10,... | collective-permute-start | bytes 884744 | tf_op jit(solution)/shard_map/ppermute | solution.py:391
  40.8 3.5 %attention.1 = (bf16[256,1536]{1,0:T(8,128)(2,1)S(1)}, bf16[256,768]{1,0:T(8,128)(2,1)S(1)}, bf16[256,768]{1,0:T(8,128)(2,1)S(1)}, bf16[256,768]{1,0:T(8,128)(2,1)S(1)}, bf16[256,768]{1,0:T(8,128)(2,1)S(1)}) custom-call(s32[2]{0:T(128)S(1)} %pad_add_fusion.where_ref, bf16[256,1536]{1,0:T(8,128)(2,1)S(1)} %bitcast.17, bf16[256,1536]{1,0:T(8,128)(2,1)S(1)} %bitcast.18, ...), custom_call_target="tpu_custom_call" | custom-call | flops 1000 | bytes 1000 | tf_op jit(solution)/shard_map/attention/pallas_call | solution.py:25
  44.2 0.1 collective-permute-start.11
  44.3 0.5 collective-permute-start.12
  44.8 0.1 collective-permute-start.13
  44.9 0.4 collective-permute-start.14
  45.3 2.2 %collective-permute-done.18.rest_11_ = bf16[192,768]{1,0:T(8,128)(2,1)S(1)} collective-permute-done((bf16[192,768]{1,0:T(8,128)(2,1)S(1)}, bf16[192,768]{1,0:T(8,128)(2,1)S(1)}, u32[]{:S(2)}, u32[]{:S(2)}) %collective-permute-start.18) | collective-permute-done | bytes 294944 | tf_op jit(solution)/shard_map/ppermute | solution.py:391
  47.6 0.1 collective-permute-done.14.rest_3_
  47.7 2.8 %branch.1 = (f32[512,768]{1,0:T(8,128)S(1)}, f32[512,128]{1,0:T(8,128)S(1)}) custom-call(s32[2]{0:T(128)S(1)} %pad_add_fusion.where_ref, bf16[256,1536]{1,0:T(8,128)(2,1)S(1)} %get-tuple-element.68.mixed_own, bf16[256,1536]{1,0:T(8,128)(2,1)S(1)} %bitcast.14, bf16[256,1536]{1,0:T(8,128)(2,1)S(1)} %bitcast.16, ...), custom_call_target="tpu_custom_call" | custom-call | flops 1000 | bytes 1000 | tf_op jit(solution)/shard_map/branch/pallas_call | solution.py:25
  50.5 0.5 collective-permute-start.19
  51.0 0.6 last_step.3.gram_own
  51.6 0.2 collective-permute-start.21
  51.8 0.4 collective-permute-done.19.stats_other
  52.1 0.9 %collective-permute-done.21.gram_other = bf16[96,768]{1,0:T(8,128)(2,1)S(1)} collective-permute-done((bf16[96,768]{1,0:T(8,128)(2,1)S(1)}, bf16[96,768]{1,0:T(8,128)(2,1)S(1)}, u32[]{:S(2)}, u32[]{:S(2)}) %collective-permute-start.21) | collective-permute-done | bytes 147488 | tf_op jit(solution)/shard_map/ppermute | solution.py:391
  53.0 1.9 %targets.2 = (f32[256,384]{1,0:T(8,128)S(1)}, f32[256,384]{1,0:T(8,128)S(1)}, s16[400,384]{1,0:T(8,128)(2,1)S(1)}, f32[384,384]{1,0:T(8,128)S(1)}) custom-call(s32[2]{0:T(128)S(1)} %pad_add_fusion.where_ref, f32[512,768]{1,0:T(8,128)S(1)} %get-tuple-element.76.blend, f32[512,128]{1,0:T(8,128)S(1)} %get-tuple-element.77.stats, ...), custom_call_target="tpu_custom_call" | custom-call | flops 1000 | bytes 1000 | tf_op jit(solution)/shard_map/targets/pallas_call | solution.py:25
  54.9 1.5 %collective-permute-start.24 = (s16[400,384]{1,0:T(8,128)(2,1)S(1)}, s16[400,384]{1,0:T(8,128)(2,1)S(1)}, u32[]{:S(2)}, u32[]{:S(2)}) collective-permute-start(s16[400,384]{1,0:T(8,128)(2,1)S(1)} %get-tuple-element.84), channel_id=1, source_target_pairs={{0,2},{1,3},{2,0},{3,1},{4,6},{5,7},{6,4},{7,5},{8,10},{9,11},{10,... | collective-permute-start | bytes 921608 | tf_op jit(solution)/shard_map/ppermute | solution.py:391
  56.4 1.8 %targets.3 = (f32[256,384]{1,0:T(8,128)S(1)}, f32[256,384]{1,0:T(8,128)S(1)}, s16[400,384]{1,0:T(8,128)(2,1)S(1)}, f32[384,384]{1,0:T(8,128)S(1)}) custom-call(s32[2]{0:T(128)S(1)} %pad_add_fusion.where_ref, f32[512,768]{1,0:T(8,128)S(1)} %get-tuple-element.76.blend, f32[512,128]{1,0:T(8,128)S(1)} %get-tuple-element.77.stats, ...), custom_call_target="tpu_custom_call" | custom-call | flops 1000 | bytes 1000 | tf_op jit(solution)/shard_map/targets/pallas_call | solution.py:25
  58.2 1.6 %collective-permute-start.27 = (s16[400,384]{1,0:T(8,128)(2,1)S(1)}, s16[400,384]{1,0:T(8,128)(2,1)S(1)}, u32[]{:S(2)}, u32[]{:S(2)}) collective-permute-start(s16[400,384]{1,0:T(8,128)(2,1)S(1)} %get-tuple-element.92), channel_id=1, source_target_pairs={{0,4},{1,5},{2,6},{3,7},{4,0},{5,1},{6,2},{7,3},{8,12},{9,13},{10,... | collective-permute-start | bytes 921608 | tf_op jit(solution)/shard_map/ppermute | solution.py:391
  59.8 0.5 collective-permute-start.23
  60.3 4.0 %collective-permute-done.24.codes = s16[400,384]{1,0:T(8,128)(2,1)S(1)} collective-permute-done((s16[400,384]{1,0:T(8,128)(2,1)S(1)}, s16[400,384]{1,0:T(8,128)(2,1)S(1)}, u32[]{:S(2)}, u32[]{:S(2)}) %collective-permute-start.24) | collective-permute-done | bytes 307232 | tf_op jit(solution)/shard_map/ppermute | solution.py:391
  64.3 0.8 next_step.4
  65.1 1.6 %collective-permute-start.25 = (s16[208,384]{1,0:T(8,128)(2,1)S(1)}, s16[208,384]{1,0:T(8,128)(2,1)S(1)}, u32[]{:S(2)}, u32[]{:S(2)}) collective-permute-start(s16[208,384]{1,0:T(8,128)(2,1)S(1)} %get-tuple-element.86), channel_id=1, source_target_pairs={{0,4},{1,5},{2,6},{3,7},{4,0},{5,1},{6,2},{7,3},{8,12},{9,13},{10,... | collective-permute-start | bytes 479240 | tf_op jit(solution)/shard_map/ppermute | solution.py:391
  66.7 0.7 collective-permute-done.27.codes
  67.4 0.8 next_step.6
  68.2 0.8 %collective-permute-start.28 = (s16[208,384]{1,0:T(8,128)(2,1)S(1)}, s16[208,384]{1,0:T(8,128)(2,1)S(1)}, u32[]{:S(2)}, u32[]{:S(2)}) collective-permute-start(s16[208,384]{1,0:T(8,128)(2,1)S(1)} %get-tuple-element.94), channel_id=1, source_target_pairs={{0,2},{1,3},{2,0},{3,1},{4,6},{5,7},{6,4},{7,5},{8,10},{9,11},{10,... | collective-permute-start | bytes 479240 | tf_op jit(solution)/shard_map/ppermute | solution.py:391
  69.0 1.7 %collective-permute-done.25.codes = s16[208,384]{1,0:T(8,128)(2,1)S(1)} collective-permute-done((s16[208,384]{1,0:T(8,128)(2,1)S(1)}, s16[208,384]{1,0:T(8,128)(2,1)S(1)}, u32[]{:S(2)}, u32[]{:S(2)}) %collective-permute-start.25) | collective-permute-done | bytes 159776 | tf_op jit(solution)/shard_map/ppermute | solution.py:391
  70.7 0.6 next_step.5
  71.3 2.7 %collective-permute-start.26 = (s16[112,384]{1,0:T(8,128)(2,1)S(1)}, s16[112,384]{1,0:T(8,128)(2,1)S(1)}, u32[]{:S(2)}, u32[]{:S(2)}) collective-permute-start(s16[112,384]{1,0:T(8,128)(2,1)S(1)} %get-tuple-element.89), channel_id=1, source_target_pairs={{0,8},{1,9},{2,10},{3,11},{4,12},{5,13},{6,14},{7,15},{8,0},{9,1},... | collective-permute-start | bytes 258056 | tf_op jit(solution)/shard_map/ppermute | solution.py:391
  74.0 0.6 next_step.7
  74.6 2.3 %collective-permute-start.29 = (s16[112,384]{1,0:T(8,128)(2,1)S(1)}, s16[112,384]{1,0:T(8,128)(2,1)S(1)}, u32[]{:S(2)}, u32[]{:S(2)}) collective-permute-start(s16[112,384]{1,0:T(8,128)(2,1)S(1)} %get-tuple-element.96), channel_id=1, source_target_pairs={{0,8},{1,9},{2,10},{3,11},{4,12},{5,13},{6,14},{7,15},{8,0},{9,1},... | collective-permute-start | bytes 258056 | tf_op jit(solution)/shard_map/ppermute | solution.py:391
  76.9 2.5 %maximum_select_fusion = f32[1,256,1536]{2,1,0:T(8,128)} fusion(f32[1,256,384]{2,1,0:T(8,128)} %bitcast.11, f32[1,256,384]{2,1,0:T(8,128)S(1)} %bitcast.22, f32[1,256,384]{2,1,0:T(8,128)S(1)} %bitcast.21, f32[1,256,384]{2,1,0:T(8,128)S(1)} %bitcast.20, pred[]{:T(512)S(6)} %eq.6), kind=kLoop, calls=%fused_computation | loop fusion | flops 2752512 | bytes 3145729 | tf_op jit(solution)/shard_map/jit(_where)/select_n | solution.py:394
  79.4 0.6 last_step.4
  80.0 0.1 collective-permute-start.30
  80.1 1.3 %collective-permute-done.29.rest_0_ = s16[112,384]{1,0:T(8,128)(2,1)S(1)} collective-permute-done((s16[112,384]{1,0:T(8,128)(2,1)S(1)}, s16[112,384]{1,0:T(8,128)(2,1)S(1)}, u32[]{:S(2)}, u32[]{:S(2)}) %collective-permute-start.29) | collective-permute-done | bytes 86048 | tf_op jit(solution)/shard_map/ppermute | solution.py:391
  81.4 0.6 last_step.5
  82.0 0.1 collective-permute-start.31
  82.1 1.2 %collective-permute-done.31 = f32[48,384]{1,0:T(8,128)S(1)} collective-permute-done((f32[48,384]{1,0:T(8,128)S(1)}, f32[48,384]{1,0:T(8,128)S(1)}, u32[]{:S(2)}, u32[]{:S(2)}) %collective-permute-start.31) | collective-permute-done | bytes 73760 | tf_op jit(solution)/shard_map/ppermute | solution.py:391
  83.3 0.7 maximum_select_fusion.1
  (35 shorter events, 0.1 us)
Async XLA Ops:
  0.6 7.1 %collective-permute-start = (bf16[96,1536]{1,0:T(8,128)(2,1)}, bf16[96,1536]{1,0:T(8,128)(2,1)S(1)}, u32[]{:S(2)}, u32[]{:S(2)}) collective-permute-start(bf16[96,1536]{1,0:T(8,128)(2,1)} %own), channel_id=1, source_target_pairs={{0,1},{1,0},{2,3},{3,2},{4,5},{5,4},{6,7},{7,6},{8,9},{9,8},{10,11... | collective-permute-start | bytes 884744 | tf_op jit(solution)/shard_map/ppermute | solution.py:391
  1.1 6.0 %collective-permute-start.3 = (bf16[48,1536]{1,0:T(8,128)(2,1)}, bf16[48,1536]{1,0:T(8,128)(2,1)S(1)}, u32[]{:S(2)}, u32[]{:S(2)}) collective-permute-start(bf16[48,1536]{1,0:T(8,128)(2,1)} %weight_own.3), channel_id=1, source_target_pairs={{0,1},{1,0},{2,3},{3,2},{4,5},{5,4},{6,7},{7,6},{8,9},{9,8},{10,11... | collective-permute-start | bytes 442376 | tf_op jit(solution)/shard_map/ppermute | solution.py:391
  2.0 1.9 %copy-start.2 = (bf16[1,8,256,768]{3,2,1,0:T(8,128)(2,1)S(1)}, bf16[1,8,256,768]{3,2,1,0:T(8,128)(2,1)}, u32[]{:S(2)}) copy-start(bf16[1,8,256,768]{3,2,1,0:T(8,128)(2,1)} %hidden_ref.1) | copy-start | bytes 9437188
  3.9 3.9 %copy-start.7 = (bf16[96,1536]{1,0:T(8,128)(2,1)S(1)}, bf16[96,1536]{1,0:T(8,128)(2,1)}, u32[]{:S(2)}) copy-start(bf16[96,1536]{1,0:T(8,128)(2,1)} %own) | copy-start | bytes 884740
  7.2 11.4 %collective-permute-start.4 = (f32[192,768]{1,0:T(8,128)S(1)}, f32[192,768]{1,0:T(8,128)S(1)}, u32[]{:S(2)}, u32[]{:S(2)}) collective-permute-start(f32[192,768]{1,0:T(8,128)S(1)} %get-tuple-element.56), channel_id=1, source_target_pairs={{0,1},{1,0},{2,3},{3,2},{4,5},{5,4},{6,7},{7,6},{8,9},{9,8},{10,11... | collective-permute-start | bytes 1769480 | tf_op jit(solution)/shard_map/ppermute | solution.py:391
  7.7 10.9 %collective-permute-start.5 = (f32[192,768]{1,0:T(8,128)S(1)}, f32[192,768]{1,0:T(8,128)S(1)}, u32[]{:S(2)}, u32[]{:S(2)}) collective-permute-start(f32[192,768]{1,0:T(8,128)S(1)} %get-tuple-element.58), channel_id=1, source_target_pairs={{0,1},{1,0},{2,3},{3,2},{4,5},{5,4},{6,7},{7,6},{8,9},{9,8},{10,11... | collective-permute-start | bytes 1769480 | tf_op jit(solution)/shard_map/ppermute | solution.py:391
  7.8 33.0 %copy-start.5 = (bf16[1,256,1536]{2,1,0:T(8,128)(2,1)S(1)}, bf16[1,256,1536]{2,1,0:T(8,128)(2,1)}, u32[]{:S(2)}) copy-start(bf16[1,256,1536]{2,1,0:T(8,128)(2,1)} %param.11) | copy-start | bytes 2359300
  8.3 10.3 %collective-permute-start.2 = (bf16[192,768]{1,0:T(8,128)(2,1)S(1)}, bf16[192,768]{1,0:T(8,128)(2,1)S(1)}, u32[]{:S(2)}, u32[]{:S(2)}) collective-permute-start(bf16[192,768]{1,0:T(8,128)(2,1)S(1)} %cut.1.rest_4_), channel_id=1, source_target_pairs={{0,2},{1,3},{2,0},{3,1},{4,6},{5,7},{6,4},{7,5},{8,10},{9,11},{10,... | collective-permute-start | bytes 884744 | tf_op jit(solution)/shard_map/ppermute | solution.py:391
  11.3 14.9 %collective-permute-start.15 = (bf16[192,768]{1,0:T(8,128)(2,1)S(1)}, bf16[192,768]{1,0:T(8,128)(2,1)S(1)}, u32[]{:S(2)}, u32[]{:S(2)}) collective-permute-start(bf16[192,768]{1,0:T(8,128)(2,1)S(1)} %cut.1.rest_4_), channel_id=1, source_target_pairs={{0,4},{1,5},{2,6},{3,7},{4,0},{5,1},{6,2},{7,3},{8,12},{9,13},{10,... | collective-permute-start | bytes 884744 | tf_op jit(solution)/shard_map/ppermute | solution.py:391
  12.9 15.7 %collective-permute-start.1 = (bf16[192,768]{1,0:T(8,128)(2,1)S(1)}, bf16[192,768]{1,0:T(8,128)(2,1)S(1)}, u32[]{:S(2)}, u32[]{:S(2)}) collective-permute-start(bf16[192,768]{1,0:T(8,128)(2,1)S(1)} %cut.1.rest_4_), channel_id=1, source_target_pairs={{0,8},{1,9},{2,10},{3,11},{4,12},{5,13},{6,14},{7,15},{8,0},{9,1},... | collective-permute-start | bytes 884744 | tf_op jit(solution)/shard_map/ppermute | solution.py:391
  18.6 22.1 %copy-start = (bf16[1,256,1536]{2,1,0:T(8,128)(2,1)S(1)}, bf16[1,256,1536]{2,1,0:T(8,128)(2,1)}, u32[]{:S(2)}) copy-start(bf16[1,256,1536]{2,1,0:T(8,128)(2,1)} %param.12) | copy-start | bytes 2359300
  18.6 22.1 %copy-start.1 = (bf16[1,256,1536]{2,1,0:T(8,128)(2,1)S(1)}, bf16[1,256,1536]{2,1,0:T(8,128)(2,1)}, u32[]{:S(2)}) copy-start(bf16[1,256,1536]{2,1,0:T(8,128)(2,1)} %param.13) | copy-start | bytes 2359300
  18.6 22.1 %copy-start.3 = (bf16[1,256,1536]{2,1,0:T(8,128)(2,1)S(1)}, bf16[1,256,1536]{2,1,0:T(8,128)(2,1)}, u32[]{:S(2)}) copy-start(bf16[1,256,1536]{2,1,0:T(8,128)(2,1)} %param.9) | copy-start | bytes 2359300
  18.6 22.1 %copy-start.4 = (bf16[1,256,1536]{2,1,0:T(8,128)(2,1)S(1)}, bf16[1,256,1536]{2,1,0:T(8,128)(2,1)}, u32[]{:S(2)}) copy-start(bf16[1,256,1536]{2,1,0:T(8,128)(2,1)} %param.10) | copy-start | bytes 2359300
  19.5 10.0 %collective-permute-start.7 = (s16[208,768]{1,0:T(8,128)(2,1)S(1)}, s16[208,768]{1,0:T(8,128)(2,1)S(1)}, u32[]{:S(2)}, u32[]{:S(2)}) collective-permute-start(s16[208,768]{1,0:T(8,128)(2,1)S(1)} %get-tuple-element.59), channel_id=1, source_target_pairs={{0,2},{1,3},{2,0},{3,1},{4,6},{5,7},{6,4},{7,5},{8,10},{9,11},{10,... | collective-permute-start | bytes 958472 | tf_op jit(solution)/shard_map/ppermute | solution.py:391
  26.3 9.9 %collective-permute-start.16 = (bf16[192,768]{1,0:T(8,128)(2,1)S(1)}, bf16[192,768]{1,0:T(8,128)(2,1)S(1)}, u32[]{:S(2)}, u32[]{:S(2)}) collective-permute-start(bf16[192,768]{1,0:T(8,128)(2,1)S(1)} %collective-permute-done.15.rest_6_), channel_id=1, source_target_pairs={{0,2},{1,3},{2,0},{3,1},{4,6},{5,7},{6,4},{7,5},{8,10},{9,11},{10,... | collective-permute-start | bytes 884744 | tf_op jit(solution)/shard_map/ppermute | solution.py:391
  28.6 10.6 %collective-permute-start.6 = (bf16[192,768]{1,0:T(8,128)(2,1)S(1)}, bf16[192,768]{1,0:T(8,128)(2,1)S(1)}, u32[]{:S(2)}, u32[]{:S(2)}) collective-permute-start(bf16[192,768]{1,0:T(8,128)(2,1)S(1)} %collective-permute-done.1.rest_8_), channel_id=1, source_target_pairs={{0,4},{1,5},{2,6},{3,7},{4,0},{5,1},{6,2},{7,3},{8,12},{9,13},{10,... | collective-permute-start | bytes 884744 | tf_op jit(solution)/shard_map/ppermute | solution.py:391
  29.1 15.2 %collective-permute-start.17 = (bf16[192,768]{1,0:T(8,128)(2,1)S(1)}, bf16[192,768]{1,0:T(8,128)(2,1)S(1)}, u32[]{:S(2)}, u32[]{:S(2)}) collective-permute-start(bf16[192,768]{1,0:T(8,128)(2,1)S(1)} %collective-permute-done.1.rest_8_), channel_id=1, source_target_pairs={{0,2},{1,3},{2,0},{3,1},{4,6},{5,7},{6,4},{7,5},{8,10},{9,11},{10,... | collective-permute-start | bytes 884744 | tf_op jit(solution)/shard_map/ppermute | solution.py:391
  30.4 13.9 %collective-permute-start.10 = (s16[64,768]{1,0:T(8,128)(2,1)S(1)}, s16[64,768]{1,0:T(8,128)(2,1)S(1)}, u32[]{:S(2)}, u32[]{:S(2)}) collective-permute-start(s16[64,768]{1,0:T(8,128)(2,1)S(1)} %get-tuple-element.67), channel_id=1, source_target_pairs={{0,12},{1,13},{2,14},{3,15},{4,8},{5,9},{6,10},{7,11},{8,4},{9,5},... | collective-permute-start | bytes 294920 | tf_op jit(solution)/shard_map/ppermute | solution.py:391
  34.8 10.0 %collective-permute-start.8 = (s16[64,768]{1,0:T(8,128)(2,1)S(1)}, s16[64,768]{1,0:T(8,128)(2,1)S(1)}, u32[]{:S(2)}, u32[]{:S(2)}) collective-permute-start(s16[64,768]{1,0:T(8,128)(2,1)S(1)} %get-tuple-element.65), channel_id=1, source_target_pairs={{0,4},{1,5},{2,6},{3,7},{4,0},{5,1},{6,2},{7,3},{8,12},{9,13},{10,... | collective-permute-start | bytes 294920 | tf_op jit(solution)/shard_map/ppermute | solution.py:391
  36.2 8.7 %collective-permute-start.9 = (s16[64,768]{1,0:T(8,128)(2,1)S(1)}, s16[64,768]{1,0:T(8,128)(2,1)S(1)}, u32[]{:S(2)}, u32[]{:S(2)}) collective-permute-start(s16[64,768]{1,0:T(8,128)(2,1)S(1)} %get-tuple-element.66), channel_id=1, source_target_pairs={{0,8},{1,9},{2,10},{3,11},{4,12},{5,13},{6,14},{7,15},{8,0},{9,1},... | collective-permute-start | bytes 294920 | tf_op jit(solution)/shard_map/ppermute | solution.py:391
  39.2 8.4 %collective-permute-start.18 = (bf16[192,768]{1,0:T(8,128)(2,1)S(1)}, bf16[192,768]{1,0:T(8,128)(2,1)S(1)}, u32[]{:S(2)}, u32[]{:S(2)}) collective-permute-start(bf16[192,768]{1,0:T(8,128)(2,1)S(1)} %collective-permute-done.6.rest_10_), channel_id=1, source_target_pairs={{0,2},{1,3},{2,0},{3,1},{4,6},{5,7},{6,4},{7,5},{8,10},{9,11},{10,... | collective-permute-start | bytes 884744 | tf_op jit(solution)/shard_map/ppermute | solution.py:391
  44.2 3.3 %collective-permute-start.11 = (bf16[256,768]{1,0:T(8,128)(2,1)S(1)}, bf16[256,768]{1,0:T(8,128)(2,1)S(1)}, u32[]{:S(2)}, u32[]{:S(2)}) collective-permute-start(bf16[256,768]{1,0:T(8,128)(2,1)S(1)} %get-tuple-element.69), channel_id=1, source_target_pairs={{0,1},{1,0},{2,3},{3,2},{4,5},{5,4},{6,7},{7,6},{8,9},{9,8},{10,11... | collective-permute-start | bytes 1179656 | tf_op jit(solution)/shard_map/ppermute | solution.py:391
  44.3 3.2 %collective-permute-start.12 = (bf16[256,768]{1,0:T(8,128)(2,1)S(1)}, bf16[256,768]{1,0:T(8,128)(2,1)S(1)}, u32[]{:S(2)}, u32[]{:S(2)}) collective-permute-start(bf16[256,768]{1,0:T(8,128)(2,1)S(1)} %get-tuple-element.70), channel_id=1, source_target_pairs={{0,1},{1,0},{2,3},{3,2},{4,5},{5,4},{6,7},{7,6},{8,9},{9,8},{10,11... | collective-permute-start | bytes 1179656 | tf_op jit(solution)/shard_map/ppermute | solution.py:391
  44.8 2.8 %collective-permute-start.13 = (bf16[256,768]{1,0:T(8,128)(2,1)S(1)}, bf16[256,768]{1,0:T(8,128)(2,1)S(1)}, u32[]{:S(2)}, u32[]{:S(2)}) collective-permute-start(bf16[256,768]{1,0:T(8,128)(2,1)S(1)} %get-tuple-element.71), channel_id=1, source_target_pairs={{0,1},{1,0},{2,3},{3,2},{4,5},{5,4},{6,7},{7,6},{8,9},{9,8},{10,11... | collective-permute-start | bytes 1179656 | tf_op jit(solution)/shard_map/ppermute | solution.py:391
  44.9 2.8 %collective-permute-start.14 = (bf16[256,768]{1,0:T(8,128)(2,1)S(1)}, bf16[256,768]{1,0:T(8,128)(2,1)S(1)}, u32[]{:S(2)}, u32[]{:S(2)}) collective-permute-start(bf16[256,768]{1,0:T(8,128)(2,1)S(1)} %get-tuple-element.72), channel_id=1, source_target_pairs={{0,1},{1,0},{2,3},{3,2},{4,5},{5,4},{6,7},{7,6},{8,9},{9,8},{10,11... | collective-permute-start | bytes 1179656 | tf_op jit(solution)/shard_map/ppermute | solution.py:391
  47.6 4.6 %collective-permute-start.20 = (bf16[256,768]{1,0:T(8,128)(2,1)S(1)}, bf16[256,768]{1,0:T(8,128)(2,1)S(1)}, u32[]{:S(2)}, u32[]{:S(2)}) collective-permute-start(bf16[256,768]{1,0:T(8,128)(2,1)S(1)} %get-tuple-element.51.sum_own), channel_id=1, source_target_pairs={{0,1},{1,0},{2,3},{3,2},{4,5},{5,4},{6,7},{7,6},{8,9},{9,8},{10,11... | collective-permute-start | bytes 1179656 | tf_op jit(solution)/shard_map/ppermute | solution.py:391
  47.6 5.5 %copy-start.6 = (bf16[48,1536]{1,0:T(8,128)(2,1)S(1)}, bf16[48,1536]{1,0:T(8,128)(2,1)}, u32[]{:S(2)}) copy-start(bf16[48,1536]{1,0:T(8,128)(2,1)} %weight_own.3) | copy-start | bytes 442372
  50.5 1.6 %collective-permute-start.19 = (f32[512,128]{1,0:T(8,128)S(1)}, f32[512,128]{1,0:T(8,128)S(1)}, u32[]{:S(2)}, u32[]{:S(2)}) collective-permute-start(f32[512,128]{1,0:T(8,128)S(1)} %get-tuple-element.77.stats), channel_id=1, source_target_pairs={{0,1},{1,0},{2,3},{3,2},{4,5},{5,4},{6,7},{7,6},{8,9},{9,8},{10,11... | collective-permute-start | bytes 786440 | tf_op jit(solution)/shard_map/ppermute | solution.py:391
  51.6 1.4 %collective-permute-start.21 = (bf16[96,768]{1,0:T(8,128)(2,1)S(1)}, bf16[96,768]{1,0:T(8,128)(2,1)S(1)}, u32[]{:S(2)}, u32[]{:S(2)}) collective-permute-start(bf16[96,768]{1,0:T(8,128)(2,1)S(1)} %last_step.3.gram_own), channel_id=1, source_target_pairs={{0,1},{1,0},{2,3},{3,2},{4,5},{5,4},{6,7},{7,6},{8,9},{9,8},{10,11... | collective-permute-start | bytes 442376 | tf_op jit(solution)/shard_map/ppermute | solution.py:391
  54.9 9.4 %collective-permute-start.24 = (s16[400,384]{1,0:T(8,128)(2,1)S(1)}, s16[400,384]{1,0:T(8,128)(2,1)S(1)}, u32[]{:S(2)}, u32[]{:S(2)}) collective-permute-start(s16[400,384]{1,0:T(8,128)(2,1)S(1)} %get-tuple-element.84), channel_id=1, source_target_pairs={{0,2},{1,3},{2,0},{3,1},{4,6},{5,7},{6,4},{7,5},{8,10},{9,11},{10,... | collective-permute-start | bytes 921608 | tf_op jit(solution)/shard_map/ppermute | solution.py:391
  58.2 9.2 %collective-permute-start.27 = (s16[400,384]{1,0:T(8,128)(2,1)S(1)}, s16[400,384]{1,0:T(8,128)(2,1)S(1)}, u32[]{:S(2)}, u32[]{:S(2)}) collective-permute-start(s16[400,384]{1,0:T(8,128)(2,1)S(1)} %get-tuple-element.92), channel_id=1, source_target_pairs={{0,4},{1,5},{2,6},{3,7},{4,0},{5,1},{6,2},{7,3},{8,12},{9,13},{10,... | collective-permute-start | bytes 921608 | tf_op jit(solution)/shard_map/ppermute | solution.py:391
  59.8 17.1 %collective-permute-start.22 = (f32[256,384]{1,0:T(8,128)S(1)}, f32[256,384]{1,0:T(8,128)S(1)}, u32[]{:S(2)}, u32[]{:S(2)}) collective-permute-start(f32[256,384]{1,0:T(8,128)S(1)} %get-tuple-element.81), channel_id=1, source_target_pairs={{0,1},{1,0},{2,3},{3,2},{4,5},{5,4},{6,7},{7,6},{8,9},{9,8},{10,11... | collective-permute-start | bytes 1179656 | tf_op jit(solution)/shard_map/ppermute | solution.py:391
  59.8 17.1 %collective-permute-start.23 = (f32[256,384]{1,0:T(8,128)S(1)}, f32[256,384]{1,0:T(8,128)}, u32[]{:S(2)}, u32[]{:S(2)}) collective-permute-start(f32[256,384]{1,0:T(8,128)S(1)} %get-tuple-element.82), channel_id=1, source_target_pairs={{0,1},{1,0},{2,3},{3,2},{4,5},{5,4},{6,7},{7,6},{8,9},{9,8},{10,11... | collective-permute-start | bytes 1179656 | tf_op jit(solution)/shard_map/ppermute | solution.py:391
  65.1 5.6 %collective-permute-start.25 = (s16[208,384]{1,0:T(8,128)(2,1)S(1)}, s16[208,384]{1,0:T(8,128)(2,1)S(1)}, u32[]{:S(2)}, u32[]{:S(2)}) collective-permute-start(s16[208,384]{1,0:T(8,128)(2,1)S(1)} %get-tuple-element.86), channel_id=1, source_target_pairs={{0,4},{1,5},{2,6},{3,7},{4,0},{5,1},{6,2},{7,3},{8,12},{9,13},{10,... | collective-permute-start | bytes 479240 | tf_op jit(solution)/shard_map/ppermute | solution.py:391
  68.2 5.8 %collective-permute-start.28 = (s16[208,384]{1,0:T(8,128)(2,1)S(1)}, s16[208,384]{1,0:T(8,128)(2,1)S(1)}, u32[]{:S(2)}, u32[]{:S(2)}) collective-permute-start(s16[208,384]{1,0:T(8,128)(2,1)S(1)} %get-tuple-element.94), channel_id=1, source_target_pairs={{0,2},{1,3},{2,0},{3,1},{4,6},{5,7},{6,4},{7,5},{8,10},{9,11},{10,... | collective-permute-start | bytes 479240 | tf_op jit(solution)/shard_map/ppermute | solution.py:391
  71.3 8.1 %collective-permute-start.26 = (s16[112,384]{1,0:T(8,128)(2,1)S(1)}, s16[112,384]{1,0:T(8,128)(2,1)S(1)}, u32[]{:S(2)}, u32[]{:S(2)}) collective-permute-start(s16[112,384]{1,0:T(8,128)(2,1)S(1)} %get-tuple-element.89), channel_id=1, source_target_pairs={{0,8},{1,9},{2,10},{3,11},{4,12},{5,13},{6,14},{7,15},{8,0},{9,1},... | collective-permute-start | bytes 258056 | tf_op jit(solution)/shard_map/ppermute | solution.py:391
  74.6 6.8 %collective-permute-start.29 = (s16[112,384]{1,0:T(8,128)(2,1)S(1)}, s16[112,384]{1,0:T(8,128)(2,1)S(1)}, u32[]{:S(2)}, u32[]{:S(2)}) collective-permute-start(s16[112,384]{1,0:T(8,128)(2,1)S(1)} %get-tuple-element.96), channel_id=1, source_target_pairs={{0,8},{1,9},{2,10},{3,11},{4,12},{5,13},{6,14},{7,15},{8,0},{9,1},... | collective-permute-start | bytes 258056 | tf_op jit(solution)/shard_map/ppermute | solution.py:391
  80.0 2.0 %collective-permute-start.30 = (f32[48,384]{1,0:T(8,128)S(1)}, f32[48,384]{1,0:T(8,128)S(1)}, u32[]{:S(2)}, u32[]{:S(2)}) collective-permute-start(f32[48,384]{1,0:T(8,128)S(1)} %get-tuple-element.98), channel_id=1, source_target_pairs={{0,1},{1,0},{2,3},{3,2},{4,5},{5,4},{6,7},{7,6},{8,9},{9,8},{10,11... | collective-permute-start | bytes 221192 | tf_op jit(solution)/shard_map/ppermute | solution.py:391
  82.0 1.3 %collective-permute-start.31 = (f32[48,384]{1,0:T(8,128)S(1)}, f32[48,384]{1,0:T(8,128)S(1)}, u32[]{:S(2)}, u32[]{:S(2)}) collective-permute-start(f32[48,384]{1,0:T(8,128)S(1)} %get-tuple-element.99), channel_id=1, source_target_pairs={{0,1},{1,0},{2,3},{3,2},{4,5},{5,4},{6,7},{7,6},{8,9},{9,8},{10,11... | collective-permute-start | bytes 221192 | tf_op jit(solution)/shard_map/ppermute | solution.py:391
